TPU v7x, 32 devices: a whole 2x2x4 slice. The times are simulated.
32 devices in a mesh: groups: 2 (over y), dp: 4 (over z), mp: 2 (over x), sub: 2 (over core).
Axes of the slice: x: 2, y: 2, z: 4, core: 2. Of those that a mesh axis runs over, the one named last changes fastest.
Arguments:
- context: bfloat16 [8, 256, 3072], P('groups', 'dp', ('mp', 'sub')), parts along dimension 0, may hold values from -8 to 8
- resid: bfloat16 [8, 256, 6144], P('groups', 'dp', ('mp', 'sub')), parts along dimension 0, may hold values from -60 to 60
- w_out: bfloat16 [3072, 6144], P('dp', ('mp', 'sub')), may hold values from -0.109375 to 0.109375
- b_out: float32 [6144], P(('mp', 'sub')), may hold values from -3 to 3
- ln_gain: float32 [6144], replicated, may hold values from 0.1 to 1.9
- w_proj: bfloat16 [6144, 4096], P('dp', ('mp', 'sub')), may hold values from -0.078125 to 0.078125
Outputs:
- projected: bfloat16 [8, 256, 4096], P(('groups', 'dp'), None, ('mp', 'sub')), parts along dimension 0
There are 2 independent parts, one for each index of `groups`. A program takes and returns all parts, laid end to end along the dimension named above; an argument that names none is the same for every part. Nothing has to cross between parts.
All inputs are finite; a program needn't handle non-finite values.
Results may differ from a plain program's by a relative error of at most 0.0057.
Values may be sent and summed in bfloat16 or wider, within the bound.
No kernel may reach another device: no remote copies, remote signals or barrier semaphores. Data moves between devices by JAX's collectives and lax.ppermute only.
A program may use at most 128 MiB of HBM per device.

v0:
```python
import jax
import jax.numpy as jnp
from jax import lax
from jax.sharding import PartitionSpec as P


def normalize(values, ln_gain):
    floats = lax.optimization_barrier(values).astype(jnp.float32)
    shard_cols = values.shape[2]
    full_width = shard_cols * lax.axis_size(("mp", "sub"))
    totals, squares = lax.psum(
        (jnp.sum(floats, axis=-1, keepdims=True), jnp.sum(floats * floats, axis=-1, keepdims=True)),
        ("mp", "sub"),
    )
    center = totals / full_width
    spread = squares / full_width - center * center
    gain_share = lax.dynamic_slice_in_dim(
        ln_gain, lax.axis_index(("mp", "sub")) * shard_cols, shard_cols
    )
    shard_norm = ((floats - center) * lax.rsqrt(spread + 1e-06) * gain_share).astype(jnp.bfloat16)
    normed = lax.all_gather(shard_norm, ("mp", "sub"), axis=2, tiled=True)
    return normed.reshape(-1, normed.shape[2])


def project(normed, w_proj):
    summed_proj = jnp.dot(
        normed, lax.all_gather(w_proj, "dp", axis=0, tiled=True), preferred_element_type=jnp.float32
    )
    return summed_proj.astype(jnp.bfloat16)


def local(context, resid, w_out, b_out, ln_gain, w_proj):
    images, part_rows, head_cols = context.shape
    width_cols = resid.shape[2]
    tok_rows = context.reshape(images * part_rows, head_cols)
    heads_all = lax.all_gather(tok_rows, ("mp", "sub"), axis=1, tiled=True)
    attended = jnp.dot(
        heads_all,
        lax.all_gather(w_out, "dp", axis=0, tiled=True),
        preferred_element_type=jnp.float32,
    )
    summed = (resid.reshape(-1, width_cols).astype(jnp.float32) + attended + b_out).astype(
        jnp.bfloat16
    )
    summed = summed.reshape(images, part_rows, width_cols)
    moved = lax.all_to_all(summed, "dp", split_axis=0, concat_axis=1, tiled=True)
    normed = normalize(moved, ln_gain)
    result = project(normed, w_proj).reshape(moved.shape[0], moved.shape[1], w_proj.shape[1])
    return result


def solution(mesh):
    in_specs = (
        P("groups", "dp", ("mp", "sub")),
        P("groups", "dp", ("mp", "sub")),
        P("dp", ("mp", "sub")),
        P(("mp", "sub")),
        P(),
        P("dp", ("mp", "sub")),
    )
    out_specs = P(("groups", "dp"), None, ("mp", "sub"))
    return jax.shard_map(local, mesh=mesh, in_specs=in_specs, out_specs=out_specs, check_vma=False)
```

profile of v0, /device:TPU:0, one launch (start us, length us, event | category | flops | bytes accessed | tf_op | source)
XLA Modules:
  0.0 479.1 jit_solution(4246408482786452595)
XLA Ops:
  6.5 0.0 all-gather.5.cloned.1.call-start
  6.5 0.7 all-gather.5.cloned.1.call-update
  7.3 0.0 all-gather.7.cloned.1.call-start
  7.3 0.7 all-gather.7.cloned.1.call-update
  8.0 0.0 copy-start
  8.0 0.0 copy-start.1
  8.0 0.0 all-gather.11.cloned.1.call-start
  8.1 0.7 all-gather.11.cloned.1.call-update
  8.8 22.5 %all-gather.5.cloned.1.call-done = bf16[256,3072]{1,0:T(8,128)(2,1)} async-done(((bf16[256,768]{1,0:T(8,128)(2,1)}), bf16[256,3072]{1,0:T(8,128)(2,1)}) %all-gather.5.cloned.1.call-update) | async-done | bytes 1572880 | tf_op jit(solution)/shard_map/all_gather | solution.py:36
  31.3 168.4 %all-gather.7.cloned.1.call-done = bf16[3072,1536]{1,0:T(8,128)(2,1)} async-done(((bf16[768,1536]{1,0:T(8,128)(2,1)}), bf16[3072,1536]{1,0:T(8,128)(2,1)}) %all-gather.7.cloned.1.call-update) | async-done | bytes 9437200 | tf_op jit(solution)/shard_map/all_gather | solution.py:39
  199.7 0.0 copy-done
  199.7 0.0 copy-done.1
  199.7 7.6 %fusion.3 = bf16[256,1536]{1,0:T(8,128)(2,1)} fusion(bf16[256,3072]{1,0:T(8,128)(2,1)} %all-gather.5.cloned.1.call-done, bf16[3072,1536]{1,0:T(8,128)(2,1)} %all-gather.7.cloned.1.call-done, bf16[256,1536]{1,0:T(8,128)(2,1)S(1)} %bitcast.28, f32[1536]{0:T(1024)S(1)} %copy-done.1), kind=kOutput, calls=%fused_computation.4 | convolution fusion | flops 2417491968 | bytes 12589056 | tf_op jit(solution)/shard_map/dot_general | solution.py:37
  207.3 3.6 all-to-all-start
  210.9 0.0 all-gather.9.cloned.1.call-start
  211.0 0.8 dynamic_slice.3
  211.8 45.1 %all-to-all-done = bf16[4,64,1536]{2,1,0:T(8,128)(2,1)S(1)} async-done(((bf16[4,64,1536]{2,1,0:T(8,128)(2,1)}), bf16[4,64,1536]{2,1,0:T(8,128)(2,1)S(1)}, u32[]{:S(2)}, u32[]{:S(2)}) %all-to-all-start) | async-done | bytes 786464 | tf_op jit(solution)/shard_map/all_to_all | solution.py:46
  256.8 0.3 convert_reduce_fusion
  257.2 6.9 %all-reduce = (f32[1,256,1]{1,2,0:T(1,128)S(1)}, f32[1,256,1]{1,2,0:T(1,128)S(1)}) all-reduce(f32[1,256,1]{1,2,0:T(1,128)S(1)} %bitcast.25, f32[1,256,1]{1,2,0:T(1,128)S(1)} %bitcast.24), channel_id=1, replica_groups=mesh['groups'=2,'dp'=4,'mp'=2,'sub'=2] {'mp','sub'}, use_global_device_ids=true, to_apply=%region_3.0 | all-reduce | flops 512 | bytes 4096 | tf_op jit(solution)/shard_map/psum | solution.py:11
  264.1 1.2 fusion.6
  265.4 0.0 all-gather.9.cloned.1.call-update
  265.4 169.1 %all-gather.11.cloned.1.call-done = bf16[6144,1024]{1,0:T(8,128)(2,1)} async-done(((bf16[1536,1024]{1,0:T(8,128)(2,1)}), bf16[6144,1024]{1,0:T(8,128)(2,1)}) %all-gather.11.cloned.1.call-update) | async-done | bytes 12582928 | tf_op jit(solution)/shard_map/all_gather | solution.py:27
  434.5 28.3 %all-gather.9.cloned.1.call-done = bf16[1,256,6144]{2,1,0:T(8,128)(2,1)} async-done(((bf16[1,256,1536]{2,1,0:T(8,128)(2,1)}), bf16[1,256,6144]{2,1,0:T(8,128)(2,1)}) %all-gather.9.cloned.1.call-update) | async-done | bytes 3145744 | tf_op jit(solution)/shard_map/all_gather | solution.py:21
  462.8 9.7 %fusion.11 = bf16[1,256,1024]{2,1,0:T(8,128)(2,1)} fusion(bf16[6144,1024]{1,0:T(8,128)(2,1)} %all-gather.11.cloned.1.call-done, bf16[1,256,6144]{2,1,0:T(8,128)(2,1)} %all-gather.9.cloned.1.call-done), kind=kOutput, calls=%fused_computation.13 | convolution fusion | flops 3221487616 | bytes 16252928 | tf_op jit(solution)/shard_map/dot_general | solution.py:26
  (1 shorter events, 0.0 us)
Async XLA Ops:
  6.5 24.8 %all-gather.5.cloned.1.call-start = ((), (), s32[]{:S(2)}) async-start(), calls=%async_computation.1 | async-start | bytes 1966080 | tf_op jit(solution)/shard_map/all_gather | solution.py:36
  7.3 192.4 %all-gather.7.cloned.1.call-start = ((), (), s32[]{:S(2)}) async-start(), calls=%async_computation.2 | async-start | bytes 11796480 | tf_op jit(solution)/shard_map/all_gather | solution.py:39
  8.0 191.7 %copy-start = (bf16[4,64,1536]{2,1,0:T(8,128)(2,1)S(1)}, bf16[4,64,1536]{2,1,0:T(8,128)(2,1)}, u32[]{:S(2)}) copy-start(bf16[4,64,1536]{2,1,0:T(8,128)(2,1)} %param.7) | copy-start | bytes 2359300
  8.0 191.7 %copy-start.1 = (f32[1536]{0:T(1024)S(1)}, f32[1536]{0:T(1024)}, u32[]{:S(2)}) copy-start(f32[1536]{0:T(1024)} %param.9) | copy-start | bytes 18436
  8.0 426.5 %all-gather.11.cloned.1.call-start = ((), (), s32[]{:S(2)}) async-start(), calls=%async_computation.4 | async-start | bytes 15728640 | tf_op jit(solution)/shard_map/all_gather | solution.py:27
  207.3 49.5 %all-to-all-start = ((bf16[4,64,1536]{2,1,0:T(8,128)(2,1)}), bf16[4,64,1536]{2,1,0:T(8,128)(2,1)S(1)}, u32[]{:S(2)}, u32[]{:S(2)}) async-start(bf16[4,64,1536]{2,1,0:T(8,128)(2,1)} %bitcast.2), calls=%async_computation | async-start | bytes 1572864 | tf_op jit(solution)/shard_map/all_to_all | solution.py:46
  210.9 251.9 %all-gather.9.cloned.1.call-start = ((), (), s32[]{:S(2)}) async-start(), calls=%async_computation.3 | async-start | bytes 3932160 | tf_op jit(solution)/shard_map/all_gather | solution.py:21
Sparse Core Ops, SparseCore 0:
  8.9 22.3 all-gather.4
  32.9 166.7 all-gather.6
  201.3 233.1 all-gather.10
  435.9 26.8 all-gather.8
where the time goes:
time: 479 us
  waiting for transfers between devices  436 us (91%)
  matrix products  17.4 us (4%)
  between operations  13.2 us (3%)
  blocking collectives  6.94 us (1%)
    all_gather x1, waiting for transfers between devices, project(): lax.all_gather(w_proj, 'dp', axis=0, tiled=True)  169 us
    all_gather x1, waiting for transfers between devices, local(): lax.all_gather(w_out, 'dp', axis=0, tiled=True)  168 us
    all_to_all x1, waiting for transfers between devices, local(): lax.all_to_all(summed, 'dp', split_axis=0, concat_axis=1, tiled=True)  45.1 us
    all_gather x1, waiting for transfers between devices, normalize(): normed = lax.all_gather(shard_norm, ('mp', 'sub'), axis=2, tiled=True)  28.3 us
    all_gather x1, waiting for transfers between devices, local(): heads_all = lax.all_gather(tok_rows, ('mp', 'sub'), axis=1, tiled=True)  22.5 us
    dot_general x1, matrix products, project(): jnp.dot(normed, lax.all_gather(w_proj, 'dp', axis=0, tiled=True), preferr...  9.73 us
  transfers between devices with their start and end apart: 5, of which 5 were waited for; matrix products, arithmetic and copies ran while one was open for 2% of the time, Pallas kernels for 0%

commit v1 on v0

--- a/solution.py
+++ b/solution.py
@@ -2,6 +2,9 @@
 import jax.numpy as jnp
 from jax import lax
 from jax.sharding import PartitionSpec as P
+
+EPS = 1e-06
+CHUNKS = 1
 
 
 def normalize(values, ln_gain):
@@ -17,7 +20,7 @@
     gain_share = lax.dynamic_slice_in_dim(
         ln_gain, lax.axis_index(("mp", "sub")) * shard_cols, shard_cols
     )
-    shard_norm = ((floats - center) * lax.rsqrt(spread + 1e-06) * gain_share).astype(jnp.bfloat16)
+    shard_norm = ((floats - center) * lax.rsqrt(spread + EPS) * gain_share).astype(jnp.bfloat16)
     normed = lax.all_gather(shard_norm, ("mp", "sub"), axis=2, tiled=True)
     return normed.reshape(-1, normed.shape[2])
 
@@ -29,7 +32,7 @@
     return summed_proj.astype(jnp.bfloat16)
 
 
-def local(context, resid, w_out, b_out, ln_gain, w_proj):
+def gathered(context, resid, w_out, b_out, ln_gain, w_proj):
     images, part_rows, head_cols = context.shape
     width_cols = resid.shape[2]
     tok_rows = context.reshape(images * part_rows, head_cols)
@@ -45,8 +48,119 @@
     summed = summed.reshape(images, part_rows, width_cols)
     moved = lax.all_to_all(summed, "dp", split_axis=0, concat_axis=1, tiled=True)
     normed = normalize(moved, ln_gain)
-    result = project(normed, w_proj).reshape(moved.shape[0], moved.shape[1], w_proj.shape[1])
-    return result
+    return project(normed, w_proj).reshape(moved.shape[0], moved.shape[1], w_proj.shape[1])
+
+
+GRID = ("dp", "mp", "sub")
+
+
+def swap(value, step):
+    count = lax.axis_size(("mp", "sub"))
+    return lax.ppermute(value, ("mp", "sub"), [(a, a ^ step) for a in range(count)])
+
+
+def turn(value, step, count):
+    pairs = [
+        (row * count + col, col * count + (row ^ col ^ step))
+        for row in range(count)
+        for col in range(count)
+    ]
+    return lax.ppermute(value, GRID, pairs)
+
+
+def columns(value, sub):
+    blocks = [value]
+    while len(blocks) < lax.axis_size(("mp", "sub")):
+        if len(blocks) < sub:
+            blocks = blocks + [swap(b, len(blocks)) for b in blocks]
+        else:
+            far = swap(value, len(blocks))
+            near = [far]
+            while len(near) < len(blocks):
+                near = near + [swap(b, len(near)) for b in near]
+            blocks = blocks + near
+    return blocks
+
+
+def pick(stack, index):
+    return lax.dynamic_index_in_dim(stack, index, 0, keepdims=False)
+
+
+def stationary(context, resid, w_out, b_out, ln_gain, w_proj):
+    count, sub = lax.axis_size("dp"), lax.axis_size("sub")
+    row, col = lax.axis_index("dp"), lax.axis_index(("mp", "sub"))
+    images, part_rows, head_cols = context.shape
+    width_cols, out_cols = resid.shape[2], w_proj.shape[1]
+    each = images // count
+    patches = part_rows * count
+    span = patches // CHUNKS
+
+    by_image = context.reshape(count, each, part_rows, head_cols)
+    came = jnp.stack([turn(pick(by_image, row ^ col ^ r), r, count) for r in range(count)])
+    own = jnp.stack([pick(came, row ^ col ^ s) for s in range(count)], axis=1)
+    own = own.reshape(each, patches, head_cols)
+    heads = jnp.stack(columns(own, sub))
+
+    gain = lax.dynamic_slice_in_dim(ln_gain, row * width_cols, width_cols)
+    gain_proj = jnp.sum(gain[:, None] * w_proj.astype(jnp.float32), axis=0)
+    gain_projs = lax.all_gather(gain_proj, "dp", axis=0)
+
+    resid = resid.reshape(count, each, part_rows, width_cols)
+    bias = jnp.where(row == 0, b_out, jnp.zeros_like(b_out))
+    here = (jnp.arange(count) == row).reshape(1, count, 1, 1)
+
+    sums = [0.0] * CHUNKS
+    for c in range(CHUNKS):
+        for r in range(count):
+            rows = pick(heads, row ^ r)[:, c * span : (c + 1) * span]
+            part = jnp.dot(
+                rows.reshape(-1, head_cols), w_out, preferred_element_type=jnp.float32
+            ).reshape(each, -1, part_rows, width_cols)
+            mine = here[:, c * (span // part_rows) : (c + 1) * (span // part_rows)]
+            old = pick(resid, row ^ col ^ r).astype(jnp.float32)[:, None]
+            part = (part + bias + jnp.where(mine, old, 0.0)).astype(jnp.bfloat16)
+            sums[c] = sums[c] + turn(part, r, count).astype(jnp.float32)
+
+    outs = []
+    for c in range(CHUNKS):
+        summed = sums[c].astype(jnp.bfloat16).astype(jnp.float32).reshape(each * span, width_cols)
+        mean = jnp.mean(summed, axis=1, keepdims=True)
+        off = summed - mean
+        square = jnp.sum(off * off, axis=1, keepdims=True)
+        scaled = (off * gain).astype(jnp.bfloat16)
+        stats = jnp.concatenate([mean, square], axis=1)
+        stats = lax.ppermute(
+            stats, GRID, [(a * count + b, b * count + a) for a in range(count) for b in range(count)]
+        )
+        stats = jnp.stack(columns(stats, sub))
+        stats = jnp.stack([pick(stats, col ^ s) for s in range(count)])
+        means, squares = stats[..., 0], stats[..., 1]
+        center = jnp.mean(means, axis=0)
+        shift = means - center
+        spread = (jnp.sum(squares, axis=0) + width_cols * jnp.sum(shift * shift, axis=0)) / (
+            width_cols * count
+        )
+
+        wide = jnp.stack(columns(scaled, sub))
+        total = 0.0
+        for e in reversed(range(count)):
+            part = jnp.dot(pick(wide, row ^ e ^ col), w_proj, preferred_element_type=jnp.float32)
+            if e:
+                part = lax.ppermute(
+                    part.astype(jnp.bfloat16), "dp", [(a, a ^ e) for a in range(count)]
+                )
+            total = total + part.astype(jnp.float32)
+        fix = jnp.sum(shift[:, :, None] * gain_projs[:, None, :], axis=0)
+        total = (total + fix) * lax.rsqrt(spread + EPS)[:, None]
+        outs.append(total.astype(jnp.bfloat16).reshape(each, span, out_cols))
+    return jnp.concatenate(outs, axis=1)
+
+
+def local(context, *rest):
+    count = lax.axis_size("dp")
+    square = count == lax.axis_size(("mp", "sub")) and count & (count - 1) == 0
+    whole = context.shape[0] % count == 0 and rest[1].shape[0] == context.shape[2]
+    return (stationary if square and whole else gathered)(context, *rest)
 
 
 def solution(mesh):

time: 479 us -> 266 us (0.56)
  waiting for transfers between devices: 436 us -> 167 us
  starting transfers between devices: 3.69 us -> 55.4 us
  between operations: 13.2 us -> 0.39 us
  other arithmetic: 1.6 us -> 14.1 us
  blocking collectives: 6.94 us -> 13.1 us
  matrix products: 17.4 us -> 11.6 us
    all_gather x4 -> x0, waiting for transfers between devices: 388 us -> none  [the longest x1 169 us: project(): lax.all_gather(w_proj, 'dp', axis=0, tiled=True)]
    ppermute x0 -> x21, waiting for transfers between devices: none -> 167 us  [the longest x8 112 us: turn(): return lax.ppermute(value, GRID, pairs)]
    ppermute x0 -> x21, starting transfers between devices: none -> 55.4 us  [the longest x8 29.8 us: turn(): return lax.ppermute(value, GRID, pairs)]
    all_to_all x1 -> x0, waiting for transfers between devices: 45.1 us -> none  [local(): lax.all_to_all(summed, 'dp', split_axis=0, concat_axis=1, tiled=True)]
    all_gather x0 -> x1, blocking collectives: none -> 13.1 us  [stationary(): gain_projs = lax.all_gather(gain_proj, 'dp', axis=0)]
    reduce_sum x1 -> x6, other arithmetic: 0.35 us -> 7.82 us  [the longest x1 3.16 us: stationary(): mean = jnp.mean(summed, axis=1, keepdims=True)]
    psum x1 -> x0, blocking collectives: 6.94 us -> none  [normalize(): lax.psum((jnp.sum(floats, axis=-1, keepdims=True), jnp.sum(floats * float...]
    dot_general x2 -> x8, matrix products: 17.4 us -> 11.6 us  [the longest x4 6.78 us: stationary(): jnp.dot(rows.reshape(-1, head_cols), w_out, preferred_element_type=jnp.fl...]
  transfers between devices with their start and end apart: 5 -> 21, of which waited for: 5 -> 8; matrix products, arithmetic and copies ran while one was open for 2% -> 5% of each run, Pallas kernels for 0% -> 0%
where the time goes in v1:
time: 266 us; the launch traced here: 265 us
  waiting for transfers between devices  167 us (63%)
  starting transfers between devices  55.4 us (21%)
  other arithmetic  14.1 us (5%)
  blocking collectives  13.1 us (5%)
  matrix products  11.6 us (4%)
  local copies, waits for them, and re-layouts  3.92 us (1%)
    ppermute x8, waiting for transfers between devices, turn(): return lax.ppermute(value, GRID, pairs)  112 us
    ppermute x3, waiting for transfers between devices, stationary(): lax.ppermute(part.astype(jnp.bfloat16), 'dp', [(a, a ^ e) for a in range(...  41.5 us
    ppermute x8, starting transfers between devices, turn(): return lax.ppermute(value, GRID, pairs)  29.8 us
    ppermute x9, starting transfers between devices, swap(): lax.ppermute(value, ('mp', 'sub'), [(a, a ^ step) for a in range(count)])  20.4 us
    ppermute x9, waiting for transfers between devices, swap(): lax.ppermute(value, ('mp', 'sub'), [(a, a ^ step) for a in range(count)])  13.5 us
    all_gather x1, blocking collectives, stationary(): gain_projs = lax.all_gather(gain_proj, 'dp', axis=0)  13.1 us
    dot_general x4, matrix products, stationary(): jnp.dot(rows.reshape(-1, head_cols), w_out, preferred_element_type=jnp.fl...  6.78 us
  transfers between devices with their start and end apart: 21, of which 8 were waited for; matrix products, arithmetic and copies ran while one was open for 5% of the time, Pallas kernels for 0%

profile of v1, /device:TPU:0, one launch (start us, length us, event | category | flops | bytes accessed | tf_op | source)
XLA Modules:
  0.0 265.5 jit_solution(10706451648154554241)
XLA Ops:
  0.0 1.2 constant_dynamic-slice_fusion.15
  1.9 5.7 %collective-permute-start.1 = (bf16[1,64,768]{2,1,0:T(8,128)(2,1)S(1)}, bf16[1,64,768]{2,1,0:T(8,128)(2,1)S(1)}, u32[]{:S(2)}, u32[]{:S(2)}) collective-permute-start(bf16[1,64,768]{2,1,0:T(8,128)(2,1)S(1)} %get-tuple-element.22), channel_id=1, source_target_pairs={{0,1},{1,4},{2,11},{3,14},{4,0},{5,5},{6,10},{7,15},{8,3},{9,6},{1... | collective-permute-start | bytes 294920 | tf_op jit(solution)/shard_map/ppermute | solution.py:68
  7.6 5.6 %collective-permute-start.2 = (bf16[1,64,768]{2,1,0:T(8,128)(2,1)S(1)}, bf16[1,64,768]{2,1,0:T(8,128)(2,1)S(1)}, u32[]{:S(2)}, u32[]{:S(2)}) collective-permute-start(bf16[1,64,768]{2,1,0:T(8,128)(2,1)S(1)} %get-tuple-element.24), channel_id=1, source_target_pairs={{0,2},{1,7},{2,8},{3,13},{4,3},{5,6},{6,9},{7,12},{8,0},{9,5},{10,... | collective-permute-start | bytes 294920 | tf_op jit(solution)/shard_map/ppermute | solution.py:68
  13.2 5.2 %collective-permute-start.3 = (bf16[1,64,768]{2,1,0:T(8,128)(2,1)S(1)}, bf16[1,64,768]{2,1,0:T(8,128)(2,1)S(1)}, u32[]{:S(2)}, u32[]{:S(2)}) collective-permute-start(bf16[1,64,768]{2,1,0:T(8,128)(2,1)S(1)} %get-tuple-element.23), channel_id=1, source_target_pairs={{0,3},{1,6},{2,9},{3,12},{4,2},{5,7},{6,8},{7,13},{8,1},{9,4},{10,... | collective-permute-start | bytes 294920 | tf_op jit(solution)/shard_map/ppermute | solution.py:68
  18.4 6.5 %collective-permute-done.2 = bf16[1,64,768]{2,1,0:T(8,128)(2,1)S(1)} collective-permute-done((bf16[1,64,768]{2,1,0:T(8,128)(2,1)S(1)}, bf16[1,64,768]{2,1,0:T(8,128)(2,1)S(1)}, u32[]{:S(2)}, u32[]{:S(2)}) %collective-permute-start.2) | collective-permute-done | bytes 98336 | tf_op jit(solution)/shard_map/ppermute | solution.py:68
  26.1 11.0 %collective-permute-done.5 = bf16[1,256,768]{2,1,0:T(8,128)(2,1)} collective-permute-done((bf16[1,256,768]{2,1,0:T(8,128)(2,1)S(1)}, bf16[1,256,768]{2,1,0:T(8,128)(2,1)}, u32[]{:S(2)}, u32[]{:S(2)}) %collective-permute-start.5) | collective-permute-done | bytes 393248 | tf_op jit(solution)/shard_map/ppermute | solution.py:59
  37.4 1.8 collective-permute-done.6
  39.2 1.4 pad_maximum_fusion.1
  40.8 1.7 fusion.11
  42.5 1.8 collective-permute-start.7
  44.2 1.7 fusion.10
  45.9 2.2 collective-permute-start.8
  48.1 1.7 fusion.9
  49.8 5.5 %collective-permute-start.9 = (bf16[1,4,64,1536]{3,2,1,0:T(8,128)(2,1)}, bf16[1,4,64,1536]{3,2,1,0:T(8,128)(2,1)}, u32[]{:S(2)}, u32[]{:S(2)}) collective-permute-start(bf16[1,4,64,1536]{3,2,1,0:T(8,128)(2,1)} %fusion.9), channel_id=1, source_target_pairs={{0,2},{1,7},{2,8},{3,13},{4,3},{5,6},{6,9},{7,12},{8,0},{9,5},{10,... | collective-permute-start | bytes 2359304 | tf_op jit(solution)/shard_map/ppermute | solution.py:68
  55.3 1.7 fusion.8
  57.0 3.1 %collective-permute-start.10 = (bf16[1,4,64,1536]{3,2,1,0:T(8,128)(2,1)}, bf16[1,4,64,1536]{3,2,1,0:T(8,128)(2,1)}, u32[]{:S(2)}, u32[]{:S(2)}) collective-permute-start(bf16[1,4,64,1536]{3,2,1,0:T(8,128)(2,1)} %fusion.8), channel_id=1, source_target_pairs={{0,3},{1,6},{2,9},{3,12},{4,2},{5,7},{6,8},{7,13},{8,1},{9,4},{10,... | collective-permute-start | bytes 2359304 | tf_op jit(solution)/shard_map/ppermute | solution.py:68
  60.9 19.1 %collective-permute-done.8 = bf16[1,4,64,1536]{3,2,1,0:T(8,128)(2,1)} collective-permute-done((bf16[1,4,64,1536]{3,2,1,0:T(8,128)(2,1)}, bf16[1,4,64,1536]{3,2,1,0:T(8,128)(2,1)}, u32[]{:S(2)}, u32[]{:S(2)}) %collective-permute-start.8) | collective-permute-done | bytes 786464 | tf_op jit(solution)/shard_map/ppermute | solution.py:68
  80.1 86.4 %collective-permute-done.9 = bf16[1,4,64,1536]{3,2,1,0:T(8,128)(2,1)} collective-permute-done((bf16[1,4,64,1536]{3,2,1,0:T(8,128)(2,1)}, bf16[1,4,64,1536]{3,2,1,0:T(8,128)(2,1)}, u32[]{:S(2)}, u32[]{:S(2)}) %collective-permute-start.9) | collective-permute-done | bytes 786464 | tf_op jit(solution)/shard_map/ppermute | solution.py:68
  166.5 3.2 %fusion.41 = (f32[4,64]{1,0:T(4,128)S(1)}, f32[1,4,64,1536]{3,2,1,0:T(8,128)}) fusion(bf16[1,4,64,1536]{3,2,1,0:T(8,128)(2,1)} %collective-permute-done.10, bf16[1,4,64,1536]{3,2,1,0:T(8,128)(2,1)} %collective-permute-done.9, bf16[1,4,64,1536]{3,2,1,0:T(8,128)(2,1)} %collective-permute-done.8, bf16[1,4,64,1536]{3,2,1,0:T(8,128)(2,1)S(1)} %collective-permute-done.7), kind=kLoop, calls=%fused_computation.87 | loop fusion | flops 3931904 | bytes 4719616 | tf_op jit(solution)/shard_map/reduce_sum | solution.py:127
  169.8 2.5 fusion.17
  172.3 1.7 multiply_reduce_fusion.2
  174.8 2.6 multiply_reduce_fusion
  177.4 18.3 %collective-permute-start.19 = (f32[256,2]{0,1:T(2,128)S(1)}, f32[256,2]{0,1:T(2,128)S(1)}, u32[]{:S(2)}, u32[]{:S(2)}) collective-permute-start(f32[256,2]{0,1:T(2,128)S(1)} %collective-permute-done.17), channel_id=1, source_target_pairs={{0,2},{1,3},{2,0},{3,1},{4,6},{5,7},{6,4},{7,5},{8,10},{9,11},{10,... | collective-permute-start | bytes 6152 | tf_op jit(solution)/shard_map/ppermute | solution.py:59
  195.6 13.1 %all-gather = f32[4096]{0:T(1024)S(1)} all-gather(f32[1024]{0:T(1024)S(1)} %multiply_reduce_fusion), channel_id=2, replica_groups=mesh['groups'=2,'dp'=4,'mp'=2,'sub'=2] {'dp'}, dimensions={0}, use_global_device_ids=true | all-gather | bytes 20480 | tf_op jit(solution)/shard_map/all_gather | solution.py:106
  209.9 1.6 fusion.19
  212.7 1.5 copy-done.1
  215.2 3.0 %collective-permute-start.14 = (bf16[256,1024]{1,0:T(8,128)(2,1)S(1)}, bf16[256,1024]{1,0:T(8,128)(2,1)S(1)}, u32[]{:S(2)}, u32[]{:S(2)}) collective-permute-start(bf16[256,1024]{1,0:T(8,128)(2,1)S(1)} %convolution_convert_fusion.2), channel_id=1, source_target_pairs={{0,12},{4,8},{8,4},{12,0},{1,13},{5,9},{9,5},{13,1},{2,14},{6,10},... | collective-permute-start | bytes 1572872 | tf_op jit(solution)/shard_map/ppermute | solution.py:149
  219.3 1.0 convolution_convert_fusion
  220.3 1.5 collective-permute-start.16
  222.1 9.8 %collective-permute-done.14 = bf16[256,1024]{1,0:T(8,128)(2,1)S(1)} collective-permute-done((bf16[256,1024]{1,0:T(8,128)(2,1)S(1)}, bf16[256,1024]{1,0:T(8,128)(2,1)S(1)}, u32[]{:S(2)}, u32[]{:S(2)}) %collective-permute-start.14) | collective-permute-done | bytes 524320 | tf_op jit(solution)/shard_map/ppermute | solution.py:149
  231.9 31.6 %collective-permute-done.15 = bf16[256,1024]{1,0:T(8,128)(2,1)S(1)} collective-permute-done((bf16[256,1024]{1,0:T(8,128)(2,1)S(1)}, bf16[256,1024]{1,0:T(8,128)(2,1)S(1)}, u32[]{:S(2)}, u32[]{:S(2)}) %collective-permute-start.15) | collective-permute-done | bytes 524320 | tf_op jit(solution)/shard_map/ppermute | solution.py:149
  263.6 1.9 fusion.25
  (62 shorter events, 8.5 us)
Async XLA Ops:
  0.0 40.7 %copy-start = (bf16[768,1536]{1,0:T(8,128)(2,1)S(1)}, bf16[768,1536]{1,0:T(8,128)(2,1)}, u32[]{:S(2)}) copy-start(bf16[768,1536]{1,0:T(8,128)(2,1)} %param.8) | copy-start | bytes 7077892
  0.0 37.1 %copy-start.3 = (f32[1536]{0:T(1024)S(1)}, f32[1536]{0:T(1024)}, u32[]{:S(2)}) copy-start(f32[1536]{0:T(1024)} %param.9) | copy-start | bytes 18436
  0.0 37.2 %copy-start.2 = (bf16[4,64,1536]{2,1,0:T(8,128)(2,1)S(1)}, bf16[4,64,1536]{2,1,0:T(8,128)(2,1)}, u32[]{:S(2)}) copy-start(bf16[4,64,1536]{2,1,0:T(8,128)(2,1)} %param.7) | copy-start | bytes 2359300
  1.2 17.2 %collective-permute-start = (bf16[1,64,768]{2,1,0:T(8,128)(2,1)S(1)}, bf16[1,64,768]{2,1,0:T(8,128)(2,1)S(1)}, u32[]{:S(2)}, u32[]{:S(2)}) collective-permute-start(bf16[1,64,768]{2,1,0:T(8,128)(2,1)S(1)} %get-tuple-element.21), channel_id=1, source_target_pairs={{0,0},{1,5},{2,10},{3,15},{4,1},{5,4},{6,11},{7,14},{8,2},{9,7},{1... | collective-permute-start | bytes 294920 | tf_op jit(solution)/shard_map/ppermute | solution.py:68
  1.9 16.5 %collective-permute-start.1 = (bf16[1,64,768]{2,1,0:T(8,128)(2,1)S(1)}, bf16[1,64,768]{2,1,0:T(8,128)(2,1)S(1)}, u32[]{:S(2)}, u32[]{:S(2)}) collective-permute-start(bf16[1,64,768]{2,1,0:T(8,128)(2,1)S(1)} %get-tuple-element.22), channel_id=1, source_target_pairs={{0,1},{1,4},{2,11},{3,14},{4,0},{5,5},{6,10},{7,15},{8,3},{9,6},{1... | collective-permute-start | bytes 294920 | tf_op jit(solution)/shard_map/ppermute | solution.py:68
  7.6 17.3 %collective-permute-start.2 = (bf16[1,64,768]{2,1,0:T(8,128)(2,1)S(1)}, bf16[1,64,768]{2,1,0:T(8,128)(2,1)S(1)}, u32[]{:S(2)}, u32[]{:S(2)}) collective-permute-start(bf16[1,64,768]{2,1,0:T(8,128)(2,1)S(1)} %get-tuple-element.24), channel_id=1, source_target_pairs={{0,2},{1,7},{2,8},{3,13},{4,3},{5,6},{6,9},{7,12},{8,0},{9,5},{10,... | collective-permute-start | bytes 294920 | tf_op jit(solution)/shard_map/ppermute | solution.py:68
  13.2 11.7 %collective-permute-start.3 = (bf16[1,64,768]{2,1,0:T(8,128)(2,1)S(1)}, bf16[1,64,768]{2,1,0:T(8,128)(2,1)S(1)}, u32[]{:S(2)}, u32[]{:S(2)}) collective-permute-start(bf16[1,64,768]{2,1,0:T(8,128)(2,1)S(1)} %get-tuple-element.23), channel_id=1, source_target_pairs={{0,3},{1,6},{2,9},{3,12},{4,2},{5,7},{6,8},{7,13},{8,1},{9,4},{10,... | collective-permute-start | bytes 294920 | tf_op jit(solution)/shard_map/ppermute | solution.py:68
  25.1 12.1 %collective-permute-start.5 = (bf16[1,256,768]{2,1,0:T(8,128)(2,1)S(1)}, bf16[1,256,768]{2,1,0:T(8,128)(2,1)}, u32[]{:S(2)}, u32[]{:S(2)}) collective-permute-start(bf16[1,256,768]{2,1,0:T(8,128)(2,1)S(1)} %bitcast.96), channel_id=1, source_target_pairs={{0,2},{1,3},{2,0},{3,1},{4,6},{5,7},{6,4},{7,5},{8,10},{9,11},{10,... | collective-permute-start | bytes 1179656 | tf_op jit(solution)/shard_map/ppermute | solution.py:59
  25.4 12.0 %collective-permute-start.4 = (bf16[1,256,768]{2,1,0:T(8,128)(2,1)S(1)}, bf16[1,256,768]{2,1,0:T(8,128)(2,1)}, u32[]{:S(2)}, u32[]{:S(2)}) collective-permute-start(bf16[1,256,768]{2,1,0:T(8,128)(2,1)S(1)} %bitcast.97), channel_id=1, source_target_pairs={{0,1},{1,0},{2,3},{3,2},{4,5},{5,4},{6,7},{7,6},{8,9},{9,8},{10,11... | collective-permute-start | bytes 1179656 | tf_op jit(solution)/shard_map/ppermute | solution.py:59
  37.1 2.1 collective-permute-start.6
  42.5 18.5 %collective-permute-start.7 = (bf16[1,4,64,1536]{3,2,1,0:T(8,128)(2,1)}, bf16[1,4,64,1536]{3,2,1,0:T(8,128)(2,1)S(1)}, u32[]{:S(2)}, u32[]{:S(2)}) collective-permute-start(bf16[1,4,64,1536]{3,2,1,0:T(8,128)(2,1)} %fusion.11), channel_id=1, source_target_pairs={{0,0},{1,5},{2,10},{3,15},{4,1},{5,4},{6,11},{7,14},{8,2},{9,7},{1... | collective-permute-start | bytes 2359304 | tf_op jit(solution)/shard_map/ppermute | solution.py:68
  45.9 34.1 %collective-permute-start.8 = (bf16[1,4,64,1536]{3,2,1,0:T(8,128)(2,1)}, bf16[1,4,64,1536]{3,2,1,0:T(8,128)(2,1)}, u32[]{:S(2)}, u32[]{:S(2)}) collective-permute-start(bf16[1,4,64,1536]{3,2,1,0:T(8,128)(2,1)} %fusion.10), channel_id=1, source_target_pairs={{0,1},{1,4},{2,11},{3,14},{4,0},{5,5},{6,10},{7,15},{8,3},{9,6},{1... | collective-permute-start | bytes 2359304 | tf_op jit(solution)/shard_map/ppermute | solution.py:68
  49.8 116.7 %collective-permute-start.9 = (bf16[1,4,64,1536]{3,2,1,0:T(8,128)(2,1)}, bf16[1,4,64,1536]{3,2,1,0:T(8,128)(2,1)}, u32[]{:S(2)}, u32[]{:S(2)}) collective-permute-start(bf16[1,4,64,1536]{3,2,1,0:T(8,128)(2,1)} %fusion.9), channel_id=1, source_target_pairs={{0,2},{1,7},{2,8},{3,13},{4,3},{5,6},{6,9},{7,12},{8,0},{9,5},{10,... | collective-permute-start | bytes 2359304 | tf_op jit(solution)/shard_map/ppermute | solution.py:68
  57.0 109.5 %collective-permute-start.10 = (bf16[1,4,64,1536]{3,2,1,0:T(8,128)(2,1)}, bf16[1,4,64,1536]{3,2,1,0:T(8,128)(2,1)}, u32[]{:S(2)}, u32[]{:S(2)}) collective-permute-start(bf16[1,4,64,1536]{3,2,1,0:T(8,128)(2,1)} %fusion.8), channel_id=1, source_target_pairs={{0,3},{1,6},{2,9},{3,12},{4,2},{5,7},{6,8},{7,13},{8,1},{9,4},{10,... | collective-permute-start | bytes 2359304 | tf_op jit(solution)/shard_map/ppermute | solution.py:68
  172.2 37.3 %collective-permute-start.12 = (bf16[256,1536]{1,0:T(8,128)(2,1)}, bf16[256,1536]{1,0:T(8,128)(2,1)S(1)}, u32[]{:S(2)}, u32[]{:S(2)}) collective-permute-start(bf16[256,1536]{1,0:T(8,128)(2,1)} %fusion.17), channel_id=1, source_target_pairs={{0,2},{1,3},{2,0},{3,1},{4,6},{5,7},{6,4},{7,5},{8,10},{9,11},{10,... | collective-permute-start | bytes 2359304 | tf_op jit(solution)/shard_map/ppermute | solution.py:59
  174.1 3.2 %collective-permute-start.17 = (f32[256,2]{0,1:T(2,128)S(1)}, f32[256,2]{0,1:T(2,128)S(1)}, u32[]{:S(2)}, u32[]{:S(2)}) collective-permute-start(f32[256,2]{0,1:T(2,128)S(1)} %pad_maximum_fusion.6), channel_id=1, source_target_pairs={{0,0},{1,4},{2,8},{3,12},{4,1},{5,5},{6,9},{7,13},{8,2},{9,6},{10,... | collective-permute-start | bytes 6152 | tf_op jit(solution)/shard_map/ppermute | solution.py:132
  177.4 32.0 %collective-permute-start.19 = (f32[256,2]{0,1:T(2,128)S(1)}, f32[256,2]{0,1:T(2,128)S(1)}, u32[]{:S(2)}, u32[]{:S(2)}) collective-permute-start(f32[256,2]{0,1:T(2,128)S(1)} %collective-permute-done.17), channel_id=1, source_target_pairs={{0,2},{1,3},{2,0},{3,1},{4,6},{5,7},{6,4},{7,5},{8,10},{9,11},{10,... | collective-permute-start | bytes 6152 | tf_op jit(solution)/shard_map/ppermute | solution.py:59
  208.8 2.9 %collective-permute-start.11 = (bf16[256,1536]{1,0:T(8,128)(2,1)}, bf16[256,1536]{1,0:T(8,128)(2,1)S(1)}, u32[]{:S(2)}, u32[]{:S(2)}) collective-permute-start(bf16[256,1536]{1,0:T(8,128)(2,1)} %fusion.17), channel_id=1, source_target_pairs={{0,1},{1,0},{2,3},{3,2},{4,5},{5,4},{6,7},{7,6},{8,9},{9,8},{10,11... | collective-permute-start | bytes 2359304 | tf_op jit(solution)/shard_map/ppermute | solution.py:59
  209.0 2.5 collective-permute-start.18
  209.4 2.2 collective-permute-start.20
  209.5 2.8 %collective-permute-start.13 = (bf16[256,1536]{1,0:T(8,128)(2,1)S(1)}, bf16[256,1536]{1,0:T(8,128)(2,1)S(1)}, u32[]{:S(2)}, u32[]{:S(2)}) collective-permute-start(bf16[256,1536]{1,0:T(8,128)(2,1)S(1)} %collective-permute-done.12), channel_id=1, source_target_pairs={{0,1},{1,0},{2,3},{3,2},{4,5},{5,4},{6,7},{7,6},{8,9},{9,8},{10,11... | collective-permute-start | bytes 2359304 | tf_op jit(solution)/shard_map/ppermute | solution.py:59
  212.3 1.9 copy-start.1
  215.2 16.8 %collective-permute-start.14 = (bf16[256,1024]{1,0:T(8,128)(2,1)S(1)}, bf16[256,1024]{1,0:T(8,128)(2,1)S(1)}, u32[]{:S(2)}, u32[]{:S(2)}) collective-permute-start(bf16[256,1024]{1,0:T(8,128)(2,1)S(1)} %convolution_convert_fusion.2), channel_id=1, source_target_pairs={{0,12},{4,8},{8,4},{12,0},{1,13},{5,9},{9,5},{13,1},{2,14},{6,10},... | collective-permute-start | bytes 1572872 | tf_op jit(solution)/shard_map/ppermute | solution.py:149
  219.2 44.4 %collective-permute-start.15 = (bf16[256,1024]{1,0:T(8,128)(2,1)S(1)}, bf16[256,1024]{1,0:T(8,128)(2,1)S(1)}, u32[]{:S(2)}, u32[]{:S(2)}) collective-permute-start(bf16[256,1024]{1,0:T(8,128)(2,1)S(1)} %convolution_convert_fusion.1), channel_id=1, source_target_pairs={{0,8},{4,12},{8,0},{12,4},{1,9},{5,13},{9,1},{13,5},{2,10},{6,14},... | collective-permute-start | bytes 1572872 | tf_op jit(solution)/shard_map/ppermute | solution.py:149
  220.3 43.3 %collective-permute-start.16 = (bf16[256,1024]{1,0:T(8,128)(2,1)S(1)}, bf16[256,1024]{1,0:T(8,128)(2,1)S(1)}, u32[]{:S(2)}, u32[]{:S(2)}) collective-permute-start(bf16[256,1024]{1,0:T(8,128)(2,1)S(1)} %convolution_convert_fusion), channel_id=1, source_target_pairs={{0,4},{4,0},{8,12},{12,8},{1,5},{5,1},{9,13},{13,9},{2,6},{6,2},{1... | collective-permute-start | bytes 1572872 | tf_op jit(solution)/shard_map/ppermute | solution.py:149

commit v2 on v0

--- a/solution.py
+++ b/solution.py
@@ -2,6 +2,9 @@
 import jax.numpy as jnp
 from jax import lax
 from jax.sharding import PartitionSpec as P
+
+EPS = 1e-06
+CHUNKS = 2
 
 
 def normalize(values, ln_gain):
@@ -17,7 +20,7 @@
     gain_share = lax.dynamic_slice_in_dim(
         ln_gain, lax.axis_index(("mp", "sub")) * shard_cols, shard_cols
     )
-    shard_norm = ((floats - center) * lax.rsqrt(spread + 1e-06) * gain_share).astype(jnp.bfloat16)
+    shard_norm = ((floats - center) * lax.rsqrt(spread + EPS) * gain_share).astype(jnp.bfloat16)
     normed = lax.all_gather(shard_norm, ("mp", "sub"), axis=2, tiled=True)
     return normed.reshape(-1, normed.shape[2])
 
@@ -29,7 +32,7 @@
     return summed_proj.astype(jnp.bfloat16)
 
 
-def local(context, resid, w_out, b_out, ln_gain, w_proj):
+def gathered(context, resid, w_out, b_out, ln_gain, w_proj):
     images, part_rows, head_cols = context.shape
     width_cols = resid.shape[2]
     tok_rows = context.reshape(images * part_rows, head_cols)
@@ -45,8 +48,152 @@
     summed = summed.reshape(images, part_rows, width_cols)
     moved = lax.all_to_all(summed, "dp", split_axis=0, concat_axis=1, tiled=True)
     normed = normalize(moved, ln_gain)
-    result = project(normed, w_proj).reshape(moved.shape[0], moved.shape[1], w_proj.shape[1])
-    return result
+    return project(normed, w_proj).reshape(moved.shape[0], moved.shape[1], w_proj.shape[1])
+
+
+SWAP = [(0, 1), (1, 0)]
+FOLD = [(0, 1), (3, 2)]
+CROSS = [(1, 2), (2, 1)]
+FAR = [(0, 2), (3, 1)]
+SPREAD = [(1, 0), (2, 3)]
+LEAP = [(1, 3), (2, 0)]
+
+
+def along(value, axis, pairs):
+    return lax.ppermute(value, axis, pairs)
+
+
+def after(value, *earlier):
+    return lax.optimization_barrier((value, *earlier))[0]
+
+
+def pick(stack, index):
+    return lax.dynamic_index_in_dim(stack, index, 0, keepdims=False)
+
+
+def either(test, first, second):
+    return jnp.where(test, first, second), jnp.where(test, second, first)
+
+
+def centred(context, resid, w_out, b_out, ln_gain, w_proj):
+    row, group = lax.axis_index("dp"), lax.axis_index("groups")
+    x, core = lax.axis_index("mp"), lax.axis_index("sub")
+    col = 2 * x + core
+    low = row < 2
+    images, part, heads = context.shape
+    wide, out_cols = resid.shape[2], w_proj.shape[1]
+    half = wide // 2
+    span = part // CHUNKS
+    tokens = images * 4 * span
+    inner, outer = jnp.where(low, 0, half), jnp.where(low, half, 0)
+
+    def cut(array, start, axis, size=half):
+        return lax.dynamic_slice_in_dim(array, start, size, axis)
+
+    def swapped(came):
+        return jnp.concatenate(either(group == 0, came, along(came, "groups", SWAP)), axis=0)
+
+    share = heads // 2
+    out_outer, out_inner = cut(w_out, outer, 1), cut(w_out, inner, 1)
+    fold_outer = along(cut(out_outer, group * share, 0, share), "dp", FOLD)
+
+    kept, sent = either(x == 0, context[: images // 2], context[images // 2 :])
+    first, second = either(x == 0, kept, along(sent, "mp", SWAP))
+    near, away = either(low, first, second)
+    mine = [along(near, "dp", FOLD), near, along(away, "dp", CROSS), along(away, "dp", FAR)]
+    mine = jnp.where(low, jnp.stack(mine, 1), jnp.stack(mine[::-1], 1))
+
+    old_outer, old_inner = cut(resid, outer, 2), cut(resid, inner, 2)
+    came_outer = along(after(old_outer, fold_outer), "dp", FOLD)
+    weight_outer = jnp.concatenate([swapped(fold_outer), out_outer], axis=0)
+
+    fold_inner = along(after(cut(out_inner, group * share, 0, share), mine), "dp", FOLD)
+    came_inner = along(after(old_inner, mine), "dp", FOLD)
+    weight_inner = jnp.concatenate([swapped(fold_inner), out_inner], axis=0)
+
+    share = half // 2
+    proj_inner, proj_outer = cut(w_proj, inner, 0), cut(w_proj, outer, 0)
+    sent_inner = cut(proj_inner, group * share, 0, share)
+    sent_outer = cut(proj_outer, group * share, 0, share)
+    proj_cross = along(after(sent_outer, mine), "dp", CROSS)
+    proj_fold = along(after(sent_inner, fold_inner, came_inner), "dp", FOLD)
+    proj_far = along(after(sent_outer, fold_inner, came_inner), "dp", FAR)
+    slices = [swapped(proj_fold), proj_inner, swapped(proj_cross), swapped(proj_far)]
+    slices = jnp.where(low, jnp.stack(slices), jnp.stack(slices[::-1]))
+    slices = jnp.stack([pick(slices, col ^ d) for d in range(4)])
+    gains = ln_gain.reshape(4, 2, half)
+    gains = pick(gains.transpose(1, 0, 2), jnp.where(low, 0, 1))
+    gains = jnp.stack([pick(gains, col ^ d) for d in range(4)])
+    gain_proj = jnp.sum(gains[:, :, None] * slices.astype(jnp.float32), axis=1)
+
+    bias = jnp.where(low, b_out, jnp.zeros_like(b_out))
+    bias_outer, bias_inner = cut(bias, outer, 0), cut(bias, inner, 0)
+
+    def attend(rows, weight, own, came, bias, k):
+        own, came = (v[:, k * span : (k + 1) * span].astype(jnp.float32) for v in (own, came))
+        none = jnp.zeros_like(own)
+        old = jnp.where(
+            low, jnp.stack([came, own, none, none], 1), jnp.stack([none, none, own, came], 1)
+        )
+        total = jnp.dot(rows, weight, preferred_element_type=jnp.float32)
+        return total + old.reshape(tokens, half) + bias
+
+    sums = []
+    for k in range(CHUNKS):
+        own = mine[:, :, k * span : (k + 1) * span]
+        both = jnp.concatenate(either(x == 0, own, along(own, "mp", SWAP)), axis=0)
+        both = both.reshape(tokens, heads)
+        rows = jnp.concatenate(
+            either(low == (core == 0), both, along(both, "sub", SWAP)), axis=1
+        )
+        sends = attend(rows, weight_outer, old_outer, came_outer, bias_outer, k)
+        came = along(sends.astype(jnp.bfloat16), "dp", CROSS)
+        keeps = attend(rows, weight_inner, old_inner, came_inner, bias_inner, k)
+        sums.append((keeps + came.astype(jnp.float32)).astype(jnp.bfloat16))
+
+    outs = []
+    for k in range(CHUNKS):
+        summed = sums[k].astype(jnp.float32)
+        mean = jnp.mean(summed, axis=1)
+        off = summed - mean[:, None]
+        square = jnp.sum(off * off, axis=1)
+        scaled = (off * gains[0]).astype(jnp.bfloat16)
+        over = along(scaled, "mp", SWAP)
+        all_scaled = [scaled, along(scaled, "sub", SWAP), over, along(over, "sub", SWAP)]
+
+        stats = jnp.stack([mean, square])[None]
+        stats = jnp.concatenate([stats, along(stats, "sub", SWAP)])
+        stats = jnp.concatenate([stats, along(stats, "mp", SWAP)])
+        middle = jnp.mean(stats[:, 0], axis=0)
+        square = jnp.sum(stats[:, 1] + half * (stats[:, 0] - middle) ** 2, axis=0)
+        there = along(jnp.stack([middle, square]), "dp", CROSS)
+        center = 0.5 * (middle + there[0])
+        gap = 0.5 * (middle - there[0])
+        spread = (square + there[1]) / (8 * half) + gap * gap
+        shift = stats[:, 0] - center
+        scale = lax.rsqrt(spread + EPS)
+
+        total = jnp.sum(shift[:, :, None] * gain_proj[:, None, :], axis=0)
+        for d in range(4):
+            total = total + jnp.dot(all_scaled[d], slices[d], preferred_element_type=jnp.float32)
+        total = (total * scale[:, None]).reshape(images, 4 * span, out_cols)
+        travel = total.astype(jnp.bfloat16)
+        own = jnp.where((row == 1) | (row == 2), pick(total, row), 0.0)
+        for pairs, image in (
+            (LEAP, jnp.where(low, 3, 0)),
+            (CROSS, jnp.where(low, 2, 1)),
+            (SPREAD, jnp.where(low, 0, 3)),
+        ):
+            own = own + along(pick(travel, image), "dp", pairs).astype(jnp.float32)
+        outs.append(own.astype(jnp.bfloat16).reshape(4, span, out_cols))
+    return jnp.stack(outs, axis=1).reshape(1, 4 * part, out_cols)
+
+
+def local(context, resid, w_out, b_out, ln_gain, w_proj):
+    grid = [lax.axis_size(name) for name in ("groups", "dp", "mp", "sub")]
+    fits = grid == [2, 4, 2, 2] and context.shape[0] == 4 and context.shape[1] % CHUNKS == 0
+    plan = centred if fits else gathered
+    return plan(context, resid, w_out, b_out, ln_gain, w_proj)
 
 
 def solution(mesh):

time: 479 us -> 233 us (0.49)
  waiting for transfers between devices: 436 us -> 129 us
  starting transfers between devices: 3.69 us -> 56.1 us
  other arithmetic: 1.6 us -> 18.4 us
  local copies, waits for them, and re-layouts: 0.8 us -> 13.8 us
  between operations: 13.2 us -> 0.86 us
  blocking collectives: 6.94 us -> 0 us
    all_gather x4 -> x0, waiting for transfers between devices: 388 us -> none  [the longest x1 169 us: project(): lax.all_gather(w_proj, 'dp', axis=0, tiled=True)]
    ppermute x0 -> x40, waiting for transfers between devices: none -> 129 us  [along(): return lax.ppermute(value, axis, pairs)]
    ppermute x0 -> x40, starting transfers between devices: none -> 56.1 us  [along(): return lax.ppermute(value, axis, pairs)]
    all_to_all x1 -> x0, waiting for transfers between devices: 45.1 us -> none  [local(): lax.all_to_all(summed, 'dp', split_axis=0, concat_axis=1, tiled=True)]
    select_n x0 -> x15, other arithmetic: none -> 7.3 us  [the longest x10 4.91 us: either(): return (jnp.where(test, first, second), jnp.where(test, second, first))]
    psum x1 -> x0, blocking collectives: 6.94 us -> none  [normalize(): lax.psum((jnp.sum(floats, axis=-1, keepdims=True), jnp.sum(floats * float...]
    dynamic_slice x1 -> x7, local copies, waits for them, and re-layouts: 0.8 us -> 7.29 us  [the longest x5 5.8 us: cut(): return lax.dynamic_slice_in_dim(array, start, size, axis)]
    unnamed x4 -> x24, local copies, waits for them, and re-layouts: 0.01 us -> 4.83 us
  transfers between devices with their start and end apart: 5 -> 40, of which waited for: 5 -> 16; matrix products, arithmetic and copies ran while one was open for 2% -> 15% of each run, Pallas kernels for 0% -> 0%
where the time goes in v2:
time: 233 us; the launch traced here: 232 us
  waiting for transfers between devices  129 us (55%)
  starting transfers between devices  56.1 us (24%)
  other arithmetic  18.4 us (8%)
  matrix products  14.1 us (6%)
  local copies, waits for them, and re-layouts  13.8 us (6%)
    ppermute x40, waiting for transfers between devices, along(): return lax.ppermute(value, axis, pairs)  129 us
    ppermute x40, starting transfers between devices, along(): return lax.ppermute(value, axis, pairs)  56.1 us
    dot_general x8, matrix products, centred(): jnp.dot(all_scaled[d], slices[d], preferred_element_type=jnp.float32)  8.19 us
    dot_general x4, matrix products, attend(): total = jnp.dot(rows, weight, preferred_element_type=jnp.float32)  5.89 us
    dynamic_slice x5, local copies, waits for them, and re-layouts, cut(): return lax.dynamic_slice_in_dim(array, start, size, axis)  5.8 us
    select_n x10, other arithmetic, either(): return (jnp.where(test, first, second), jnp.where(test, second, first))  4.91 us
    unnamed x24, local copies, waits for them, and re-layouts  4.83 us
  transfers between devices with their start and end apart: 40, of which 16 were waited for; matrix products, arithmetic and copies ran while one was open for 15% of the time, Pallas kernels for 0%

profile of v2, /device:TPU:0, one launch (start us, length us, event | category | flops | bytes accessed | tf_op | source)
XLA Modules:
  0.0 232.3 jit_solution(3437671773652369815)
XLA Ops:
  0.0 1.7 broadcast_select_fusion.20
  1.7 2.9 %collective-permute-start = (bf16[2,64,768]{2,1,0:T(8,128)(2,1)}, bf16[2,64,768]{2,1,0:T(8,128)(2,1)}, u32[]{:S(2)}, u32[]{:S(2)}) collective-permute-start(bf16[2,64,768]{2,1,0:T(8,128)(2,1)} %broadcast_select_fusion.20), channel_id=1, source_target_pairs={{0,2},{2,0},{1,3},{3,1},{4,6},{6,4},{5,7},{7,5},{8,10},{10,8},{9,1... | collective-permute-start | bytes 589832 | tf_op jit(solution)/shard_map/ppermute | solution.py:63
  4.7 3.0 %fusion.71 = (bf16[384,768]{1,0:T(8,128)(2,1)}, bf16[384,768]{1,0:T(8,128)(2,1)}) fusion(bf16[768,1536]{1,0:T(8,128)(2,1)} %param.8, s32[]{:T(128)S(6)} %select_n.299, s32[]{:T(128)S(6)} %select_n.301, s32[]{:T(128)S(6)} %select_n.310), kind=kLoop, calls=%fused_computation.185 | loop fusion | bytes 2359308 | tf_op jit(solution)/shard_map/dynamic_slice | solution.py:91
  7.6 4.3 %collective-permute-start.9 = (bf16[384,768]{1,0:T(8,128)(2,1)}, bf16[384,768]{1,0:T(8,128)(2,1)}, u32[]{:S(2)}, u32[]{:S(2)}) collective-permute-start(bf16[384,768]{1,0:T(8,128)(2,1)} %get-tuple-element.26), channel_id=1, source_target_pairs={{0,4},{12,8},{1,5},{13,9},{2,6},{14,10},{3,7},{15,11},{16,20},{28,... | collective-permute-start | bytes 1769480 | tf_op jit(solution)/shard_map/ppermute | solution.py:63
  11.9 2.2 constant_dynamic-slice_fusion.10
  14.1 2.3 fusion.50
  21.2 3.2 %collective-permute-start.3 = (bf16[2,64,768]{2,1,0:T(8,128)(2,1)S(1)}, bf16[2,64,768]{2,1,0:T(8,128)(2,1)S(1)}, u32[]{:S(2)}, u32[]{:S(2)}) collective-permute-start(bf16[2,64,768]{2,1,0:T(8,128)(2,1)S(1)} %get-tuple-element.68), channel_id=1, source_target_pairs={{0,8},{12,4},{1,9},{13,5},{2,10},{14,6},{3,11},{15,7},{16,24},{28,... | collective-permute-start | bytes 589832 | tf_op jit(solution)/shard_map/ppermute | solution.py:63
  25.9 6.4 %collective-permute-done.1 = bf16[2,64,768]{2,1,0:T(8,128)(2,1)S(1)} collective-permute-done((bf16[2,64,768]{2,1,0:T(8,128)(2,1)S(1)}, bf16[2,64,768]{2,1,0:T(8,128)(2,1)S(1)}, u32[]{:S(2)}, u32[]{:S(2)}) %collective-permute-start.1) | collective-permute-done | bytes 196640 | tf_op jit(solution)/shard_map/ppermute | solution.py:63
  35.9 4.4 %collective-permute-start.8 = (bf16[4,64,768]{2,1,0:T(8,128)(2,1)S(1)}, bf16[4,64,768]{2,1,0:T(8,128)(2,1)S(1)}, u32[]{:S(2)}, u32[]{:S(2)}) collective-permute-start(bf16[4,64,768]{2,1,0:T(8,128)(2,1)S(1)} %copy-done.9), channel_id=1, source_target_pairs={{0,4},{12,8},{1,5},{13,9},{2,6},{14,10},{3,7},{15,11},{16,20},{28,... | collective-permute-start | bytes 1179656 | tf_op jit(solution)/shard_map/ppermute | solution.py:63
  42.4 4.0 %collective-permute-start.11 = (bf16[4,64,768]{2,1,0:T(8,128)(2,1)S(1)}, bf16[4,64,768]{2,1,0:T(8,128)(2,1)S(1)}, u32[]{:S(2)}, u32[]{:S(2)}) collective-permute-start(bf16[4,64,768]{2,1,0:T(8,128)(2,1)S(1)} %copy-done.8), channel_id=1, source_target_pairs={{0,4},{12,8},{1,5},{13,9},{2,6},{14,10},{3,7},{15,11},{16,20},{28,... | collective-permute-start | bytes 1179656 | tf_op jit(solution)/shard_map/ppermute | solution.py:63
  46.4 1.6 collective-permute-start.10
  48.1 1.6 collective-permute-done.8
  50.1 12.3 %collective-permute-done.6 = bf16[384,768]{1,0:T(8,128)(2,1)S(1)} collective-permute-done((bf16[384,768]{1,0:T(8,128)(2,1)S(1)}, bf16[384,768]{1,0:T(8,128)(2,1)S(1)}, u32[]{:S(2)}, u32[]{:S(2)}) %collective-permute-start.6) | collective-permute-done | bytes 589856 | tf_op jit(solution)/shard_map/ppermute | solution.py:63
  63.9 4.0 %collective-permute-done.11 = bf16[4,64,768]{2,1,0:T(8,128)(2,1)S(1)} collective-permute-done((bf16[4,64,768]{2,1,0:T(8,128)(2,1)S(1)}, bf16[4,64,768]{2,1,0:T(8,128)(2,1)S(1)}, u32[]{:S(2)}, u32[]{:S(2)}) %collective-permute-start.11) | collective-permute-done | bytes 393248 | tf_op jit(solution)/shard_map/ppermute | solution.py:63
  68.0 4.4 %collective-permute-start.16 = (bf16[384,1024]{1,0:T(8,128)(2,1)S(1)}, bf16[384,1024]{1,0:T(8,128)(2,1)S(1)}, u32[]{:S(2)}, u32[]{:S(2)}) collective-permute-start(bf16[384,1024]{1,0:T(8,128)(2,1)S(1)} %get-tuple-element.14), channel_id=1, source_target_pairs={{0,4},{12,8},{1,5},{13,9},{2,6},{14,10},{3,7},{15,11},{16,20},{28,... | collective-permute-start | bytes 2359304 | tf_op jit(solution)/shard_map/ppermute | solution.py:63
  72.9 2.7 %collective-permute-start.20 = (bf16[384,1024]{1,0:T(8,128)(2,1)S(1)}, bf16[384,1024]{1,0:T(8,128)(2,1)S(1)}, u32[]{:S(2)}, u32[]{:S(2)}) collective-permute-start(bf16[384,1024]{1,0:T(8,128)(2,1)S(1)} %get-tuple-element.15), channel_id=1, source_target_pairs={{0,8},{12,4},{1,9},{13,5},{2,10},{14,6},{3,11},{15,7},{16,24},{28,... | collective-permute-start | bytes 2359304 | tf_op jit(solution)/shard_map/ppermute | solution.py:63
  75.8 1.6 collective-permute-start.7
  80.8 11.4 %collective-permute-done.7 = bf16[384,768]{1,0:T(8,128)(2,1)S(1)} collective-permute-done((bf16[384,768]{1,0:T(8,128)(2,1)S(1)}, bf16[384,768]{1,0:T(8,128)(2,1)S(1)}, u32[]{:S(2)}, u32[]{:S(2)}) %collective-permute-start.7) | collective-permute-done | bytes 589856 | tf_op jit(solution)/shard_map/ppermute | solution.py:63
  93.0 1.6 collective-permute-start.17
  94.5 8.8 %collective-permute-done.20 = bf16[384,1024]{1,0:T(8,128)(2,1)S(1)} collective-permute-done((bf16[384,1024]{1,0:T(8,128)(2,1)S(1)}, bf16[384,1024]{1,0:T(8,128)(2,1)S(1)}, u32[]{:S(2)}, u32[]{:S(2)}) %collective-permute-start.20) | collective-permute-done | bytes 786464 | tf_op jit(solution)/shard_map/ppermute | solution.py:63
  107.4 1.6 convert_reduce_fusion.1
  108.9 16.9 %collective-permute-done.17 = bf16[384,1024]{1,0:T(8,128)(2,1)S(1)} collective-permute-done((bf16[384,1024]{1,0:T(8,128)(2,1)S(1)}, bf16[384,1024]{1,0:T(8,128)(2,1)S(1)}, u32[]{:S(2)}, u32[]{:S(2)}) %collective-permute-start.17) | collective-permute-done | bytes 786464 | tf_op jit(solution)/shard_map/ppermute | solution.py:63
  126.2 12.0 %collective-permute-done.21 = bf16[384,1024]{1,0:T(8,128)(2,1)S(1)} collective-permute-done((bf16[384,1024]{1,0:T(8,128)(2,1)S(1)}, bf16[384,1024]{1,0:T(8,128)(2,1)S(1)}, u32[]{:S(2)}, u32[]{:S(2)}) %collective-permute-start.21) | collective-permute-done | bytes 786464 | tf_op jit(solution)/shard_map/ppermute | solution.py:63
  138.8 1.6 maximum_select_fusion
  141.1 1.6 multiply_reduce_fusion
  153.4 29.8 %collective-permute-done.14 = f32[2,2,512]{2,0,1:T(2,128)S(1)} collective-permute-done((f32[2,2,512]{2,0,1:T(2,128)S(1)}, f32[2,2,512]{2,0,1:T(2,128)S(1)}, u32[]{:S(2)}, u32[]{:S(2)}) %collective-permute-start.14) | collective-permute-done | bytes 8224 | tf_op jit(solution)/shard_map/ppermute | solution.py:63
  184.7 2.1 collective-permute-done.32
  188.6 1.7 multiply_reduce_fusion.2
  205.5 8.1 %collective-permute-done.25 = bf16[128,1024]{1,0:T(8,128)(2,1)S(1)} collective-permute-done((bf16[128,1024]{1,0:T(8,128)(2,1)S(1)}, bf16[128,1024]{1,0:T(8,128)(2,1)S(1)}, u32[]{:S(2)}, u32[]{:S(2)}) %collective-permute-start.25) | collective-permute-done | bytes 262176 | tf_op jit(solution)/shard_map/ppermute | solution.py:63
  215.6 3.7 %collective-permute-done.27 = bf16[128,1024]{1,0:T(8,128)(2,1)} collective-permute-done((bf16[128,1024]{1,0:T(8,128)(2,1)S(1)}, bf16[128,1024]{1,0:T(8,128)(2,1)}, u32[]{:S(2)}, u32[]{:S(2)}) %collective-permute-start.27) | collective-permute-done | bytes 262176 | tf_op jit(solution)/shard_map/ppermute | solution.py:63
  220.6 4.4 %collective-permute-done.37 = bf16[128,1024]{1,0:T(8,128)(2,1)} collective-permute-done((bf16[128,1024]{1,0:T(8,128)(2,1)S(1)}, bf16[128,1024]{1,0:T(8,128)(2,1)}, u32[]{:S(2)}, u32[]{:S(2)}) %collective-permute-start.37) | collective-permute-done | bytes 262176 | tf_op jit(solution)/shard_map/ppermute | solution.py:63
  225.0 5.0 %collective-permute-done.39 = bf16[128,1024]{1,0:T(8,128)(2,1)} collective-permute-done((bf16[128,1024]{1,0:T(8,128)(2,1)S(1)}, bf16[128,1024]{1,0:T(8,128)(2,1)}, u32[]{:S(2)}, u32[]{:S(2)}) %collective-permute-start.39) | collective-permute-done | bytes 262176 | tf_op jit(solution)/shard_map/ppermute | solution.py:63
  (152 shorter events, 58.5 us)
Async XLA Ops:
  1.7 17.0 %collective-permute-start = (bf16[2,64,768]{2,1,0:T(8,128)(2,1)}, bf16[2,64,768]{2,1,0:T(8,128)(2,1)}, u32[]{:S(2)}, u32[]{:S(2)}) collective-permute-start(bf16[2,64,768]{2,1,0:T(8,128)(2,1)} %broadcast_select_fusion.20), channel_id=1, source_target_pairs={{0,2},{2,0},{1,3},{3,1},{4,6},{6,4},{5,7},{7,5},{8,10},{10,8},{9,1... | collective-permute-start | bytes 589832 | tf_op jit(solution)/shard_map/ppermute | solution.py:63
  7.6 34.7 %collective-permute-start.9 = (bf16[384,768]{1,0:T(8,128)(2,1)}, bf16[384,768]{1,0:T(8,128)(2,1)}, u32[]{:S(2)}, u32[]{:S(2)}) collective-permute-start(bf16[384,768]{1,0:T(8,128)(2,1)} %get-tuple-element.26), channel_id=1, source_target_pairs={{0,4},{12,8},{1,5},{13,9},{2,6},{14,10},{3,7},{15,11},{16,20},{28,... | collective-permute-start | bytes 1769480 | tf_op jit(solution)/shard_map/ppermute | solution.py:63
  20.6 11.7 %collective-permute-start.2 = (bf16[2,64,768]{2,1,0:T(8,128)(2,1)S(1)}, bf16[2,64,768]{2,1,0:T(8,128)(2,1)S(1)}, u32[]{:S(2)}, u32[]{:S(2)}) collective-permute-start(bf16[2,64,768]{2,1,0:T(8,128)(2,1)S(1)} %get-tuple-element.68), channel_id=1, source_target_pairs={{4,8},{8,4},{5,9},{9,5},{6,10},{10,6},{7,11},{11,7},{20,24},{24,20... | collective-permute-start | bytes 589832 | tf_op jit(solution)/shard_map/ppermute | solution.py:63
  21.2 11.1 %collective-permute-start.3 = (bf16[2,64,768]{2,1,0:T(8,128)(2,1)S(1)}, bf16[2,64,768]{2,1,0:T(8,128)(2,1)S(1)}, u32[]{:S(2)}, u32[]{:S(2)}) collective-permute-start(bf16[2,64,768]{2,1,0:T(8,128)(2,1)S(1)} %get-tuple-element.68), channel_id=1, source_target_pairs={{0,8},{12,4},{1,9},{13,5},{2,10},{14,6},{3,11},{15,7},{16,24},{28,... | collective-permute-start | bytes 589832 | tf_op jit(solution)/shard_map/ppermute | solution.py:63
  32.5 13.9 %collective-permute-start.4 = (bf16[2,4,32,768]{3,2,1,0:T(8,128)(2,1)S(1)}, bf16[2,4,32,768]{3,2,1,0:T(8,128)(2,1)S(1)}, u32[]{:S(2)}, u32[]{:S(2)}) collective-permute-start(bf16[2,4,32,768]{3,2,1,0:T(8,128)(2,1)S(1)} %slice.86), channel_id=1, source_target_pairs={{0,2},{2,0},{1,3},{3,1},{4,6},{6,4},{5,7},{7,5},{8,10},{10,8},{9,1... | collective-permute-start | bytes 1179656 | tf_op jit(solution)/shard_map/ppermute | solution.py:63
  35.9 13.9 %collective-permute-start.8 = (bf16[4,64,768]{2,1,0:T(8,128)(2,1)S(1)}, bf16[4,64,768]{2,1,0:T(8,128)(2,1)S(1)}, u32[]{:S(2)}, u32[]{:S(2)}) collective-permute-start(bf16[4,64,768]{2,1,0:T(8,128)(2,1)S(1)} %copy-done.9), channel_id=1, source_target_pairs={{0,4},{12,8},{1,5},{13,9},{2,6},{14,10},{3,7},{15,11},{16,20},{28,... | collective-permute-start | bytes 1179656 | tf_op jit(solution)/shard_map/ppermute | solution.py:63
  40.3 22.2 %collective-permute-start.6 = (bf16[384,768]{1,0:T(8,128)(2,1)S(1)}, bf16[384,768]{1,0:T(8,128)(2,1)S(1)}, u32[]{:S(2)}, u32[]{:S(2)}) collective-permute-start(bf16[384,768]{1,0:T(8,128)(2,1)S(1)} %copy-done.7), channel_id=1, source_target_pairs={{0,4},{12,8},{1,5},{13,9},{2,6},{14,10},{3,7},{15,11},{16,20},{28,... | collective-permute-start | bytes 1769480 | tf_op jit(solution)/shard_map/ppermute | solution.py:63
  41.6 36.9 %collective-permute-start.18 = (bf16[384,1024]{1,0:T(8,128)(2,1)S(1)}, bf16[384,1024]{1,0:T(8,128)(2,1)S(1)}, u32[]{:S(2)}, u32[]{:S(2)}) collective-permute-start(bf16[384,1024]{1,0:T(8,128)(2,1)S(1)} %get-tuple-element.15), channel_id=1, source_target_pairs={{4,8},{8,4},{5,9},{9,5},{6,10},{10,6},{7,11},{11,7},{20,24},{24,20... | collective-permute-start | bytes 2359304 | tf_op jit(solution)/shard_map/ppermute | solution.py:63
  42.4 25.6 %collective-permute-start.11 = (bf16[4,64,768]{2,1,0:T(8,128)(2,1)S(1)}, bf16[4,64,768]{2,1,0:T(8,128)(2,1)S(1)}, u32[]{:S(2)}, u32[]{:S(2)}) collective-permute-start(bf16[4,64,768]{2,1,0:T(8,128)(2,1)S(1)} %copy-done.8), channel_id=1, source_target_pairs={{0,4},{12,8},{1,5},{13,9},{2,6},{14,10},{3,7},{15,11},{16,20},{28,... | collective-permute-start | bytes 1179656 | tf_op jit(solution)/shard_map/ppermute | solution.py:63
  46.4 29.4 %collective-permute-start.10 = (bf16[384,768]{1,0:T(8,128)(2,1)}, bf16[384,768]{1,0:T(8,128)(2,1)S(1)}, u32[]{:S(2)}, u32[]{:S(2)}) collective-permute-start(bf16[384,768]{1,0:T(8,128)(2,1)} %collective-permute-done.9), channel_id=1, source_target_pairs={{0,16},{16,0},{1,17},{17,1},{2,18},{18,2},{3,19},{19,3},{4,20},{20... | collective-permute-start | bytes 1769480 | tf_op jit(solution)/shard_map/ppermute | solution.py:63
  49.8 28.8 %collective-permute-start.5 = (bf16[512,768]{1,0:T(8,128)(2,1)S(1)}, bf16[512,768]{1,0:T(8,128)(2,1)S(1)}, u32[]{:S(2)}, u32[]{:S(2)}) collective-permute-start(bf16[512,768]{1,0:T(8,128)(2,1)S(1)} %bitcast.245), channel_id=1, source_target_pairs={{0,1},{1,0},{2,3},{3,2},{4,5},{5,4},{6,7},{7,6},{8,9},{9,8},{10,11... | collective-permute-start | bytes 2359304 | tf_op jit(solution)/shard_map/ppermute | solution.py:63
  62.4 10.5 %collective-permute-start.28 = (bf16[2,4,32,768]{3,2,1,0:T(8,128)(2,1)S(1)}, bf16[2,4,32,768]{3,2,1,0:T(8,128)(2,1)S(1)}, u32[]{:S(2)}, u32[]{:S(2)}) collective-permute-start(bf16[2,4,32,768]{3,2,1,0:T(8,128)(2,1)S(1)} %get-tuple-element.57), channel_id=1, source_target_pairs={{0,2},{2,0},{1,3},{3,1},{4,6},{6,4},{5,7},{7,5},{8,10},{10,8},{9,1... | collective-permute-start | bytes 1179656 | tf_op jit(solution)/shard_map/ppermute | solution.py:63
  68.0 25.0 %collective-permute-start.16 = (bf16[384,1024]{1,0:T(8,128)(2,1)S(1)}, bf16[384,1024]{1,0:T(8,128)(2,1)S(1)}, u32[]{:S(2)}, u32[]{:S(2)}) collective-permute-start(bf16[384,1024]{1,0:T(8,128)(2,1)S(1)} %get-tuple-element.14), channel_id=1, source_target_pairs={{0,4},{12,8},{1,5},{13,9},{2,6},{14,10},{3,7},{15,11},{16,20},{28,... | collective-permute-start | bytes 2359304 | tf_op jit(solution)/shard_map/ppermute | solution.py:63
  72.9 30.4 %collective-permute-start.20 = (bf16[384,1024]{1,0:T(8,128)(2,1)S(1)}, bf16[384,1024]{1,0:T(8,128)(2,1)S(1)}, u32[]{:S(2)}, u32[]{:S(2)}) collective-permute-start(bf16[384,1024]{1,0:T(8,128)(2,1)S(1)} %get-tuple-element.15), channel_id=1, source_target_pairs={{0,8},{12,4},{1,9},{13,5},{2,10},{14,6},{3,11},{15,7},{16,24},{28,... | collective-permute-start | bytes 2359304 | tf_op jit(solution)/shard_map/ppermute | solution.py:63
  75.8 16.3 %collective-permute-start.7 = (bf16[384,768]{1,0:T(8,128)(2,1)S(1)}, bf16[384,768]{1,0:T(8,128)(2,1)S(1)}, u32[]{:S(2)}, u32[]{:S(2)}) collective-permute-start(bf16[384,768]{1,0:T(8,128)(2,1)S(1)} %collective-permute-done.6), channel_id=1, source_target_pairs={{0,16},{16,0},{1,17},{17,1},{2,18},{18,2},{3,19},{19,3},{4,20},{20... | collective-permute-start | bytes 1769480 | tf_op jit(solution)/shard_map/ppermute | solution.py:63
  78.5 26.3 %collective-permute-start.29 = (bf16[512,768]{1,0:T(8,128)(2,1)S(1)}, bf16[512,768]{1,0:T(8,128)(2,1)S(1)}, u32[]{:S(2)}, u32[]{:S(2)}) collective-permute-start(bf16[512,768]{1,0:T(8,128)(2,1)S(1)} %bitcast.246), channel_id=1, source_target_pairs={{0,1},{1,0},{2,3},{3,2},{4,5},{5,4},{6,7},{7,6},{8,9},{9,8},{10,11... | collective-permute-start | bytes 2359304 | tf_op jit(solution)/shard_map/ppermute | solution.py:63
  78.6 47.5 %collective-permute-start.19 = (bf16[384,1024]{1,0:T(8,128)(2,1)S(1)}, bf16[384,1024]{1,0:T(8,128)(2,1)S(1)}, u32[]{:S(2)}, u32[]{:S(2)}) collective-permute-start(bf16[384,1024]{1,0:T(8,128)(2,1)S(1)} %collective-permute-done.18), channel_id=1, source_target_pairs={{0,16},{16,0},{1,17},{17,1},{2,18},{18,2},{3,19},{19,3},{4,20},{20... | collective-permute-start | bytes 2359304 | tf_op jit(solution)/shard_map/ppermute | solution.py:63
  92.1 15.2 %collective-permute-start.12 = (bf16[512,768]{1,0:T(8,128)(2,1)S(1)}, bf16[512,768]{1,0:T(8,128)(2,1)S(1)}, u32[]{:S(2)}, u32[]{:S(2)}) collective-permute-start(bf16[512,768]{1,0:T(8,128)(2,1)S(1)} %fusion.36), channel_id=1, source_target_pairs={{4,8},{8,4},{5,9},{9,5},{6,10},{10,6},{7,11},{11,7},{20,24},{24,20... | collective-permute-start | bytes 2359304 | tf_op jit(solution)/shard_map/ppermute | solution.py:63
  93.0 32.9 %collective-permute-start.17 = (bf16[384,1024]{1,0:T(8,128)(2,1)S(1)}, bf16[384,1024]{1,0:T(8,128)(2,1)S(1)}, u32[]{:S(2)}, u32[]{:S(2)}) collective-permute-start(bf16[384,1024]{1,0:T(8,128)(2,1)S(1)} %collective-permute-done.16), channel_id=1, source_target_pairs={{0,16},{16,0},{1,17},{17,1},{2,18},{18,2},{3,19},{19,3},{4,20},{20... | collective-permute-start | bytes 2359304 | tf_op jit(solution)/shard_map/ppermute | solution.py:63
  103.4 34.8 %collective-permute-start.21 = (bf16[384,1024]{1,0:T(8,128)(2,1)S(1)}, bf16[384,1024]{1,0:T(8,128)(2,1)S(1)}, u32[]{:S(2)}, u32[]{:S(2)}) collective-permute-start(bf16[384,1024]{1,0:T(8,128)(2,1)S(1)} %collective-permute-done.20), channel_id=1, source_target_pairs={{0,16},{16,0},{1,17},{17,1},{2,18},{18,2},{3,19},{19,3},{4,20},{20... | collective-permute-start | bytes 2359304 | tf_op jit(solution)/shard_map/ppermute | solution.py:63
  106.5 36.3 %collective-permute-start.30 = (bf16[512,768]{1,0:T(8,128)(2,1)S(1)}, bf16[512,768]{1,0:T(8,128)(2,1)S(1)}, u32[]{:S(2)}, u32[]{:S(2)}) collective-permute-start(bf16[512,768]{1,0:T(8,128)(2,1)S(1)} %fusion.17), channel_id=1, source_target_pairs={{4,8},{8,4},{5,9},{9,5},{6,10},{10,6},{7,11},{11,7},{20,24},{24,20... | collective-permute-start | bytes 2359304 | tf_op jit(solution)/shard_map/ppermute | solution.py:63
  146.1 46.8 %collective-permute-start.22 = (bf16[512,768]{1,0:T(8,128)(2,1)S(1)}, bf16[512,768]{1,0:T(8,128)(2,1)S(1)}, u32[]{:S(2)}, u32[]{:S(2)}) collective-permute-start(bf16[512,768]{1,0:T(8,128)(2,1)S(1)} %get-tuple-element.81), channel_id=1, source_target_pairs={{0,1},{1,0},{2,3},{3,2},{4,5},{5,4},{6,7},{7,6},{8,9},{9,8},{10,11... | collective-permute-start | bytes 2359304 | tf_op jit(solution)/shard_map/ppermute | solution.py:63
  146.2 44.1 %collective-permute-start.23 = (bf16[512,768]{1,0:T(8,128)(2,1)S(1)}, bf16[512,768]{1,0:T(8,128)(2,1)S(1)}, u32[]{:S(2)}, u32[]{:S(2)}) collective-permute-start(bf16[512,768]{1,0:T(8,128)(2,1)S(1)} %get-tuple-element.81), channel_id=1, source_target_pairs={{0,2},{2,0},{1,3},{3,1},{4,6},{6,4},{5,7},{7,5},{8,10},{10,8},{9,1... | collective-permute-start | bytes 2359304 | tf_op jit(solution)/shard_map/ppermute | solution.py:63
  148.7 45.2 %collective-permute-start.34 = (bf16[512,768]{1,0:T(8,128)(2,1)S(1)}, bf16[512,768]{1,0:T(8,128)(2,1)S(1)}, u32[]{:S(2)}, u32[]{:S(2)}) collective-permute-start(bf16[512,768]{1,0:T(8,128)(2,1)S(1)} %get-tuple-element.56), channel_id=1, source_target_pairs={{0,1},{1,0},{2,3},{3,2},{4,5},{5,4},{6,7},{7,6},{8,9},{9,8},{10,11... | collective-permute-start | bytes 2359304 | tf_op jit(solution)/shard_map/ppermute | solution.py:63
  149.0 42.4 %collective-permute-start.35 = (bf16[512,768]{1,0:T(8,128)(2,1)S(1)}, bf16[512,768]{1,0:T(8,128)(2,1)S(1)}, u32[]{:S(2)}, u32[]{:S(2)}) collective-permute-start(bf16[512,768]{1,0:T(8,128)(2,1)S(1)} %get-tuple-element.56), channel_id=1, source_target_pairs={{0,2},{2,0},{1,3},{3,1},{4,6},{6,4},{5,7},{7,5},{8,10},{10,8},{9,1... | collective-permute-start | bytes 2359304 | tf_op jit(solution)/shard_map/ppermute | solution.py:63
  152.3 30.9 %collective-permute-start.14 = (f32[2,2,512]{2,0,1:T(2,128)S(1)}, f32[2,2,512]{2,0,1:T(2,128)S(1)}, u32[]{:S(2)}, u32[]{:S(2)}) collective-permute-start(f32[2,2,512]{2,0,1:T(2,128)S(1)} %pad_maximum_fusion.26), channel_id=1, source_target_pairs={{0,2},{2,0},{1,3},{3,1},{4,6},{6,4},{5,7},{7,5},{8,10},{10,8},{9,1... | collective-permute-start | bytes 24584 | tf_op jit(solution)/shard_map/ppermute | solution.py:63
  196.3 17.3 %collective-permute-start.25 = (bf16[128,1024]{1,0:T(8,128)(2,1)S(1)}, bf16[128,1024]{1,0:T(8,128)(2,1)S(1)}, u32[]{:S(2)}, u32[]{:S(2)}) collective-permute-start(bf16[128,1024]{1,0:T(8,128)(2,1)S(1)} %get-tuple-element.47), channel_id=1, source_target_pairs={{4,12},{8,0},{5,13},{9,1},{6,14},{10,2},{7,15},{11,3},{20,28},{24,... | collective-permute-start | bytes 786440 | tf_op jit(solution)/shard_map/ppermute | solution.py:63
  197.6 18.1 %collective-permute-start.26 = (bf16[128,1024]{1,0:T(8,128)(2,1)S(1)}, bf16[128,1024]{1,0:T(8,128)(2,1)}, u32[]{:S(2)}, u32[]{:S(2)}) collective-permute-start(bf16[128,1024]{1,0:T(8,128)(2,1)S(1)} %get-tuple-element.49), channel_id=1, source_target_pairs={{4,8},{8,4},{5,9},{9,5},{6,10},{10,6},{7,11},{11,7},{20,24},{24,20... | collective-permute-start | bytes 786440 | tf_op jit(solution)/shard_map/ppermute | solution.py:63
  199.0 20.4 %collective-permute-start.27 = (bf16[128,1024]{1,0:T(8,128)(2,1)S(1)}, bf16[128,1024]{1,0:T(8,128)(2,1)}, u32[]{:S(2)}, u32[]{:S(2)}) collective-permute-start(bf16[128,1024]{1,0:T(8,128)(2,1)S(1)} %get-tuple-element.48), channel_id=1, source_target_pairs={{4,0},{8,12},{5,1},{9,13},{6,2},{10,14},{7,3},{11,15},{20,16},{24,... | collective-permute-start | bytes 786440 | tf_op jit(solution)/shard_map/ppermute | solution.py:63
  202.9 22.2 %collective-permute-start.37 = (bf16[128,1024]{1,0:T(8,128)(2,1)S(1)}, bf16[128,1024]{1,0:T(8,128)(2,1)}, u32[]{:S(2)}, u32[]{:S(2)}) collective-permute-start(bf16[128,1024]{1,0:T(8,128)(2,1)S(1)} %get-tuple-element.50), channel_id=1, source_target_pairs={{4,12},{8,0},{5,13},{9,1},{6,14},{10,2},{7,15},{11,3},{20,28},{24,... | collective-permute-start | bytes 786440 | tf_op jit(solution)/shard_map/ppermute | solution.py:63
  204.2 20.9 %collective-permute-start.38 = (bf16[128,1024]{1,0:T(8,128)(2,1)S(1)}, bf16[128,1024]{1,0:T(8,128)(2,1)}, u32[]{:S(2)}, u32[]{:S(2)}) collective-permute-start(bf16[128,1024]{1,0:T(8,128)(2,1)S(1)} %get-tuple-element.52), channel_id=1, source_target_pairs={{4,8},{8,4},{5,9},{9,5},{6,10},{10,6},{7,11},{11,7},{20,24},{24,20... | collective-permute-start | bytes 786440 | tf_op jit(solution)/shard_map/ppermute | solution.py:63
  214.3 15.6 %collective-permute-start.39 = (bf16[128,1024]{1,0:T(8,128)(2,1)S(1)}, bf16[128,1024]{1,0:T(8,128)(2,1)}, u32[]{:S(2)}, u32[]{:S(2)}) collective-permute-start(bf16[128,1024]{1,0:T(8,128)(2,1)S(1)} %get-tuple-element.51), channel_id=1, source_target_pairs={{4,0},{8,12},{5,1},{9,13},{6,2},{10,14},{7,3},{11,15},{20,16},{24,... | collective-permute-start | bytes 786440 | tf_op jit(solution)/shard_map/ppermute | solution.py:63
  (20 other events, 106.8 us)

commit v3 on v0

--- a/solution.py
+++ b/solution.py
@@ -1,7 +1,12 @@
 import jax
 import jax.numpy as jnp
 from jax import lax
+from jax.experimental import pallas as pl
+from jax.experimental.pallas import tpu as pltpu
 from jax.sharding import PartitionSpec as P
+
+EPS = 1e-06
+CHUNKS = 2
 
 
 def normalize(values, ln_gain):
@@ -17,7 +22,7 @@
     gain_share = lax.dynamic_slice_in_dim(
         ln_gain, lax.axis_index(("mp", "sub")) * shard_cols, shard_cols
     )
-    shard_norm = ((floats - center) * lax.rsqrt(spread + 1e-06) * gain_share).astype(jnp.bfloat16)
+    shard_norm = ((floats - center) * lax.rsqrt(spread + EPS) * gain_share).astype(jnp.bfloat16)
     normed = lax.all_gather(shard_norm, ("mp", "sub"), axis=2, tiled=True)
     return normed.reshape(-1, normed.shape[2])
 
@@ -29,7 +34,7 @@
     return summed_proj.astype(jnp.bfloat16)
 
 
-def local(context, resid, w_out, b_out, ln_gain, w_proj):
+def gathered(context, resid, w_out, b_out, ln_gain, w_proj):
     images, part_rows, head_cols = context.shape
     width_cols = resid.shape[2]
     tok_rows = context.reshape(images * part_rows, head_cols)
@@ -45,8 +50,390 @@
     summed = summed.reshape(images, part_rows, width_cols)
     moved = lax.all_to_all(summed, "dp", split_axis=0, concat_axis=1, tiled=True)
     normed = normalize(moved, ln_gain)
-    result = project(normed, w_proj).reshape(moved.shape[0], moved.shape[1], w_proj.shape[1])
-    return result
+    return project(normed, w_proj).reshape(moved.shape[0], moved.shape[1], w_proj.shape[1])
+
+
+SWAP = [(0, 1), (1, 0)]
+FOLD = [(0, 1), (3, 2)]
+CROSS = [(1, 2), (2, 1)]
+FAR = [(0, 2), (3, 1)]
+SPREAD = [(1, 0), (2, 3)]
+LEAP = [(1, 3), (2, 0)]
+
+
+def along(value, axis, pairs):
+    return lax.ppermute(value, axis, pairs)
+
+
+def pick(stack, index):
+    return lax.dynamic_index_in_dim(stack, index, 0, keepdims=False)
+
+
+def either(test, first, second):
+    return jnp.where(test, first, second), jnp.where(test, second, first)
+
+
+LIMIT = 48 * 1024 * 1024
+ANY = pl.BlockSpec(memory_space=pl.ANY)
+EXTRA = 16
+
+
+def call(kernel, place, grid, ins, outs, shapes, scratch, args, flops=0):
+    moved = sum(v.size * v.dtype.itemsize for v in (*args, *jax.tree.leaves(shapes)))
+    return pl.pallas_call(
+        kernel,
+        grid_spec=pltpu.PrefetchScalarGridSpec(
+            num_scalar_prefetch=1, grid=grid, in_specs=ins, out_specs=outs, scratch_shapes=scratch
+        ),
+        out_shape=shapes,
+        compiler_params=pltpu.CompilerParams(vmem_limit_bytes=LIMIT),
+        cost_estimate=pl.CostEstimate(flops=flops, bytes_accessed=moved, transcendentals=0),
+    )(place, *args)
+
+
+def cuts(place, blocks, *released):
+    def kernel(place_ref, *refs):
+        for src, dst in zip(refs[: len(blocks)], refs[-len(blocks) :]):
+            dst[...] = src[...]
+
+    def spec(block, index=None):
+        return pl.BlockSpec(block, index or (lambda i, p: (0,) * len(block)))
+
+    return call(
+        kernel,
+        place,
+        (1,),
+        [spec(block, index) for _, block, index in blocks] + [ANY] * len(released),
+        [spec(block) for _, block, _ in blocks],
+        [jax.ShapeDtypeStruct(block, array.dtype) for array, block, _ in blocks],
+        [],
+        [array for array, _, _ in blocks] + list(released),
+    )
+
+
+def terms(value):
+    high = value.astype(jnp.bfloat16)
+    rest = value - high.astype(jnp.float32)
+    mid = rest.astype(jnp.bfloat16)
+    return [high, mid, (rest - mid.astype(jnp.float32)).astype(jnp.bfloat16)]
+
+
+def added(rows, first):
+    high, mid, low = (rows[first + i : first + i + 1].astype(jnp.float32) for i in range(3))
+    return high + (mid + low)
+
+
+def packed(rows):
+    parts = [term for row in rows for term in terms(row)]
+    parts.append(jnp.zeros((EXTRA - len(parts), rows[0].shape[1]), jnp.bfloat16))
+    return jnp.concatenate(parts, axis=0)
+
+
+def upright(rows):
+    rows = jnp.concatenate(rows, axis=0)
+    fill = jnp.zeros((128 - rows.shape[0], rows.shape[1]), jnp.float32)
+    return jnp.concatenate([rows, fill], axis=0).T
+
+
+def attend(place, both, other, w_out, fold, swapped, resid, came, bias, part, inner, dtype):
+    tokens, heads = both.shape
+    half, share = fold.shape[1], fold.shape[0]
+    images, span = resid.shape[0], tokens // resid.shape[0] // 4
+    tile = 256 if half % 256 == 0 else half
+    tiles = half // tile
+
+    def kernel(p, both, other, own, fold, swapped, old, came, bias, out, total):
+        low = p[0] == 1
+        turn = low == (p[2] == 0)
+        here = jnp.where(turn, other[...], both[...])
+        folded = jnp.where(turn, both[...], other[...])
+        first = jnp.where(p[1] == 0, fold[...], swapped[...])
+        second = jnp.where(p[1] == 0, swapped[...], fold[...])
+        value = jnp.dot(here, own[...], preferred_element_type=jnp.float32)
+        value = value + jnp.dot(folded[:, :share], first, preferred_element_type=jnp.float32)
+        value = value + jnp.dot(folded[:, share:], second, preferred_element_type=jnp.float32)
+        total[...] = value + jnp.where(low, bias[...], jnp.zeros_like(bias[...]))
+        own_at, came_at = jnp.where(low, span, 2 * span), jnp.where(low, 0, 3 * span)
+        for image in range(images):
+            for at, source in ((own_at, old), (came_at, came)):
+                rows = pl.ds(pl.multiple_of(image * 4 * span + at, span), span)
+                total[rows, :] = total[rows, :] + source[image].astype(jnp.float32)
+        out[...] = total[...].astype(dtype)
+
+    def column(p, t):
+        return jnp.where((p[0] == 1) == inner, 0, tiles) + t
+
+    whole = pl.BlockSpec((tokens, heads), lambda t, p: (0, 0))
+    piece = pl.BlockSpec((share, tile), lambda t, p: (0, t))
+    return call(
+        kernel,
+        place,
+        (tiles,),
+        [
+            whole,
+            whole,
+            pl.BlockSpec((heads, tile), lambda t, p: (0, column(p, t))),
+            piece,
+            piece,
+            pl.BlockSpec((images, span, tile), lambda t, p: (0, part, column(p, t))),
+            pl.BlockSpec((images, span, tile), lambda t, p: (0, part, t)),
+            pl.BlockSpec((1, tile), lambda t, p: (0, column(p, t))),
+        ],
+        pl.BlockSpec((tokens, tile), lambda t, p: (0, t)),
+        jax.ShapeDtypeStruct((tokens, half), dtype),
+        [pltpu.VMEM((tokens, tile), jnp.float32)],
+        [both, other, w_out, fold, swapped, resid, came, bias.reshape(1, -1)],
+        flops=4 * tokens * heads * half,
+    )
+
+
+def scale_up(place, keeps, came, gain):
+    tokens, half = keeps.shape
+
+    def kernel(p, keeps, came, gain, out):
+        step = pl.program_id(0)
+        summed = (keeps[...] + came[...].astype(jnp.float32)).astype(jnp.bfloat16)
+        summed = summed.astype(jnp.float32)
+        mean = jnp.sum(summed, axis=1, keepdims=True) / half
+        off = summed - mean
+        square = jnp.sum(off * off, axis=1, keepdims=True)
+        at = pl.multiple_of(step * 128, 128)
+        out[pl.ds(at, 128), :] = (off * gain[...]).astype(jnp.bfloat16)
+        lane = lax.broadcasted_iota(jnp.int32, (128, 128), 1)
+        stats = jnp.where(lane == 0, mean, jnp.where(lane == 1, square, 0.0)).T
+        out[tokens:, pl.ds(at, 128)] = packed([stats[0:1], stats[1:2]])
+
+    row = pl.BlockSpec((128, half), lambda i, p: (i, 0))
+    return call(
+        kernel,
+        place,
+        (tokens // 128,),
+        [row, row, pl.BlockSpec((1, half), lambda i, p: (0, 0))],
+        pl.BlockSpec((tokens + EXTRA, half), lambda i, p: (0, 0)),
+        jax.ShapeDtypeStruct((tokens + EXTRA, half), jnp.bfloat16),
+        [],
+        [keeps, came, gain],
+    )
+
+
+def project_up(place, scaled, slices, gain_proj):
+    rows, half = scaled[0].shape
+    tokens, out_cols = rows - EXTRA, slices.shape[1]
+    size = tokens // 4
+    tile = 256 if out_cols % 256 == 0 else out_cols
+
+    def kernel(p, s0, s1, s2, s3, slices, gain_proj, o0, o1, o2, o3, shifts, stats, total):
+        @pl.when(pl.program_id(0) == 0)
+        def _():
+            last = [s[tokens:, :tokens] for s in (s0, s1, s2, s3)]
+            means = [added(v, 0) for v in last]
+            middle = 0.25 * (means[0] + means[1] + means[2] + means[3])
+            shift = [v - middle for v in means]
+            square = sum(added(v, 3) + half * (d * d) for v, d in zip(last, shift))
+            shifts[...] = upright(shift)
+            for image in range(4):
+                at = slice(image * size, (image + 1) * size)
+                stats[image] = jnp.concatenate([middle[:, at], square[:, at]], axis=0)
+
+        value = jnp.zeros(total.shape, jnp.float32)
+        for d, s in enumerate((s0, s1, s2, s3)):
+            value = value + jnp.dot(
+                s[:tokens, :],
+                slices[d * half : (d + 1) * half, :],
+                preferred_element_type=jnp.float32,
+            )
+            value = value + shifts[:, d : d + 1] * gain_proj[d : d + 1, :]
+        total[...] = value
+        gains = jnp.sum(gain_proj[...], axis=0, keepdims=True)
+        for role, out in enumerate((o0, o1, o2, o3)):
+            image = jnp.where(p[0] == 1, role, 3 - role)
+            at = pl.ds(pl.multiple_of(image * size, size), size)
+            out[:size, :] = total[at, :].astype(jnp.bfloat16)
+            here = stats[image]
+            here = jnp.concatenate([here] * (gains.shape[1] // size), axis=1)
+            out[size:, :] = packed([here[0:1], here[1:2], gains])
+
+    whole = pl.BlockSpec((rows, half), lambda t, p: (0, 0))
+    message = pl.BlockSpec((size + EXTRA, tile), lambda t, p: (0, t))
+    return call(
+        kernel,
+        place,
+        (out_cols // tile,),
+        [whole] * 4
+        + [
+            pl.BlockSpec((4 * half, tile), lambda t, p: (0, t)),
+            pl.BlockSpec((4, tile), lambda t, p: (0, t)),
+        ],
+        [message] * 4,
+        [jax.ShapeDtypeStruct((size + EXTRA, out_cols), jnp.bfloat16)] * 4,
+        [
+            pltpu.VMEM((tokens, 128), jnp.float32),
+            pltpu.VMEM((4, 2, size), jnp.float32),
+            pltpu.VMEM((tokens, tile), jnp.float32),
+        ],
+        [*scaled, slices, gain_proj],
+        flops=8 * tokens * half * out_cols,
+    )
+
+
+def finish(place, parts, count):
+    rows, out_cols = parts[0][0].shape
+    size = rows - EXTRA
+    span = size // 4
+
+    def kernel(p, *refs):
+        out = refs[-1]
+        middle = (p[3] == 1) | (p[3] == 2)
+        for k in range(len(parts)):
+            own, cross, spread, leap = refs[4 * k : 4 * k + 4]
+            one = jnp.where(middle, own[...], spread[...])
+            two = jnp.where(middle, cross[...], leap[...])
+            ends = [one[size:], two[size:]]
+            means = [added(v, 0)[:, :size] for v in ends]
+            squares = [added(v, 3)[:, :size] for v in ends]
+            gap = 0.5 * (means[0] - means[1])
+            spread_of = (squares[0] + squares[1]) / count + gap * gap
+            turned = upright([gap, lax.rsqrt(spread_of + EPS)])
+            value = one[:size].astype(jnp.float32) + two[:size].astype(jnp.float32)
+            value = value + turned[:, 0:1] * (added(ends[0], 6) - added(ends[1], 6))
+            value = (value * turned[:, 1:2]).astype(jnp.bfloat16)
+            for row in range(4):
+                at = (row * len(parts) + k) * span
+                out[at : at + span, :] = value[row * span : (row + 1) * span]
+
+    args = [v for part in parts for v in part]
+    return call(
+        kernel,
+        place,
+        (1,),
+        [pl.BlockSpec((rows, out_cols), lambda i, p: (0, 0))] * len(args),
+        pl.BlockSpec((size * len(parts), out_cols), lambda i, p: (0, 0)),
+        jax.ShapeDtypeStruct((size * len(parts), out_cols), jnp.bfloat16),
+        [],
+        args,
+    )
+
+
+def centred(context, resid, w_out, b_out, ln_gain, w_proj):
+    row, group = lax.axis_index("dp"), lax.axis_index("groups")
+    x, core = lax.axis_index("mp"), lax.axis_index("sub")
+    col = 2 * x + core
+    low = row < 2
+    place = jnp.stack([low.astype(jnp.int32), group, core, row])
+    images, part, heads = context.shape
+    wide, out_cols = resid.shape[2], w_proj.shape[1]
+    half = wide // 2
+    span = part // CHUNKS
+
+    def halves(came, swap):
+        return jnp.concatenate(either(group == 0, came, swap), axis=0)
+
+    def inner(p):
+        return 1 - p[0]
+
+    def outer(p):
+        return p[0]
+
+    share, share2 = heads // 2, half // 2
+    sent_outer, sent_cross = cuts(
+        place,
+        [
+            (w_out, (share, half), lambda i, p: (p[1], outer(p))),
+            (w_proj, (share2, out_cols), lambda i, p: (2 * outer(p) + p[1], 0)),
+        ],
+    )
+    kept, sent = either(x == 0, context[: images // 2], context[images // 2 :])
+    got = along(sent, "mp", SWAP)
+    fold_outer = along(sent_outer, "dp", FOLD)
+    proj_cross = along(sent_cross, "dp", CROSS)
+
+    first, second = either(x == 0, kept, got)
+    near, away = either(low, first, second)
+    mine = [along(near, "dp", FOLD), near, along(away, "dp", CROSS), along(away, "dp", FAR)]
+    mine = jnp.where(low, jnp.stack(mine, 1), jnp.stack(mine[::-1], 1))
+
+    old = (images, part, half)
+    sent_inner, sent_old = cuts(
+        place,
+        [
+            (w_out, (share, half), lambda i, p: (p[1], inner(p))),
+            (resid, old, lambda i, p: (0, 0, outer(p))),
+        ],
+        got,
+    )
+    old_outer = along(sent_old, "dp", FOLD)
+    fold_inner = along(sent_inner, "dp", FOLD)
+    swap_outer = along(fold_outer, "groups", SWAP)
+    swap_inner = along(fold_inner, "groups", SWAP)
+
+    sent_fold, sent_old = cuts(
+        place,
+        [
+            (w_proj, (share2, out_cols), lambda i, p: (2 * inner(p) + p[1], 0)),
+            (resid, old, lambda i, p: (0, 0, inner(p))),
+        ],
+        mine,
+    )
+    old_inner = along(sent_old, "dp", FOLD)
+    proj_fold = along(sent_fold, "dp", FOLD)
+    (sent_far,) = cuts(
+        place,
+        [(w_proj, (share2, out_cols), lambda i, p: (2 * outer(p) + p[1], 0))],
+        fold_inner,
+    )
+    proj_far = along(sent_far, "dp", FAR)
+
+    sends, keeps = [], []
+    for k in range(CHUNKS):
+        own = mine[:, :, k * span : (k + 1) * span]
+        both = jnp.concatenate(either(x == 0, own, along(own, "mp", SWAP)), axis=0)
+        both = both.reshape(images * 4 * span, heads)
+        other = along(both, "sub", SWAP)
+        common = (place, both, other, w_out)
+        sends.append(
+            attend(*common, fold_outer, swap_outer, resid, old_outer, b_out, k, False, jnp.bfloat16)
+        )
+        keeps.append(
+            attend(*common, fold_inner, swap_inner, resid, old_inner, b_out, k, True, jnp.float32)
+        )
+
+    gains = ln_gain.reshape(4, 2, half)
+    gains = pick(gains.transpose(1, 0, 2), jnp.where(low, 0, 1))
+    gains = jnp.stack([pick(gains, col ^ d) for d in range(4)])
+    came = [along(v, "dp", CROSS) for v in sends]
+    scaled = []
+    for k in range(CHUNKS):
+        near = scale_up(place, keeps[k], came[k], gains[:1])
+        far = along(near, "mp", SWAP)
+        scaled.append([near, along(near, "sub", SWAP), far, along(far, "sub", SWAP)])
+
+    proj_own = lax.dynamic_slice_in_dim(w_proj, jnp.where(low, 0, half), half, 0)
+    slices = [
+        halves(proj_fold, along(proj_fold, "groups", SWAP)),
+        proj_own,
+        halves(proj_cross, along(proj_cross, "groups", SWAP)),
+        halves(proj_far, along(proj_far, "groups", SWAP)),
+    ]
+    slices = jnp.where(low, jnp.stack(slices), jnp.stack(slices[::-1]))
+    slices = jnp.stack([pick(slices, col ^ d) for d in range(4)])
+    gain_proj = jnp.sum(gains[:, :, None] * slices.astype(jnp.float32), axis=1)
+    slices = slices.reshape(4 * half, out_cols)
+
+    parts = []
+    for k in range(CHUNKS):
+        spread, own, cross, leap = project_up(place, scaled[k], slices, gain_proj)
+        leap = along(leap, "dp", LEAP)
+        cross = along(cross, "dp", CROSS)
+        spread = along(spread, "dp", SPREAD)
+        parts.append([own, cross, spread, leap])
+    return finish(place, parts, 8 * half).reshape(1, 4 * part, out_cols)
+
+
+def local(context, resid, w_out, b_out, ln_gain, w_proj):
+    grid = [lax.axis_size(name) for name in ("groups", "dp", "mp", "sub")]
+    fits = grid == [2, 4, 2, 2] and context.shape[0] == 4 and context.shape[1] % CHUNKS == 0
+    plan = centred if fits else gathered
+    return plan(context, resid, w_out, b_out, ln_gain, w_proj)
 
 
 def solution(mesh):

time: 479 us -> 221 us (0.46)
  waiting for transfers between devices: 436 us -> 97.1 us
  starting transfers between devices: 3.69 us -> 53.2 us
  Pallas kernels: 0 us -> 46.1 us
  matrix products: 17.4 us -> 0 us
  other arithmetic: 1.6 us -> 16 us
  between operations: 13.2 us -> 0.44 us
  blocking collectives: 6.94 us -> 0 us
  local copies, waits for them, and re-layouts: 0.8 us -> 6.79 us
    all_gather x4 -> x0, waiting for transfers between devices: 388 us -> none  [the longest x1 169 us: project(): lax.all_gather(w_proj, 'dp', axis=0, tiled=True)]
    ppermute x0 -> x34, waiting for transfers between devices: none -> 97.1 us  [along(): return lax.ppermute(value, axis, pairs)]
    ppermute x0 -> x34, starting transfers between devices: none -> 53.2 us  [along(): return lax.ppermute(value, axis, pairs)]
    pallas_call x0 -> x13, Pallas kernels: none -> 46.1 us  [call(): pl.pallas_call(kernel, grid_spec=pltpu.PrefetchScalarGridSpec(num_scalar_...]
    all_to_all x1 -> x0, waiting for transfers between devices: 45.1 us -> none  [local(): lax.all_to_all(summed, 'dp', split_axis=0, concat_axis=1, tiled=True)]
    dot_general x2 -> x0, matrix products: 17.4 us -> none  [the longest x1 9.73 us: project(): jnp.dot(normed, lax.all_gather(w_proj, 'dp', axis=0, tiled=True), preferr...]
    select_n x0 -> x9, other arithmetic: none -> 9.12 us  [the longest x7 7.42 us: either(): return (jnp.where(test, first, second), jnp.where(test, second, first))]
    psum x1 -> x0, blocking collectives: 6.94 us -> none  [normalize(): lax.psum((jnp.sum(floats, axis=-1, keepdims=True), jnp.sum(floats * float...]
  transfers between devices with their start and end apart: 5 -> 34, of which waited for: 5 -> 12; matrix products, arithmetic and copies ran while one was open for 2% -> 8% of each run, Pallas kernels for 0% -> 20%
where the time goes in v3:
time: 221 us; the launch traced here: 220 us
  waiting for transfers between devices  97.1 us (44%)
  starting transfers between devices  53.2 us (24%)
  Pallas kernels  46.1 us (21%)
  other arithmetic  16 us (7%)
  local copies, waits for them, and re-layouts  6.79 us (3%)
    ppermute x34, waiting for transfers between devices, along(): return lax.ppermute(value, axis, pairs)  97.1 us
    ppermute x34, starting transfers between devices, along(): return lax.ppermute(value, axis, pairs)  53.2 us
    pallas_call x13, Pallas kernels, call(): pl.pallas_call(kernel, grid_spec=pltpu.PrefetchScalarGridSpec(num_scalar_...  46.1 us
    select_n x7, other arithmetic, either(): return (jnp.where(test, first, second), jnp.where(test, second, first))  7.42 us
  transfers between devices with their start and end apart: 34, of which 12 were waited for; matrix products, arithmetic and copies ran while one was open for 8% of the time, Pallas kernels for 20%

profile of v3, /device:TPU:0, one launch (start us, length us, event | category | flops | bytes accessed | tf_op | source)
XLA Modules:
  0.0 219.6 jit_solution(12165459126771770221)
XLA Ops:
  1.2 3.0 %collective-permute-start = (bf16[2,64,768]{2,1,0:T(8,128)(2,1)S(1)}, bf16[2,64,768]{2,1,0:T(8,128)(2,1)S(1)}, u32[]{:S(2)}, u32[]{:S(2)}) collective-permute-start(bf16[2,64,768]{2,1,0:T(8,128)(2,1)S(1)} %broadcast_select_fusion.12), channel_id=1, source_target_pairs={{0,2},{2,0},{1,3},{3,1},{4,6},{6,4},{5,7},{7,5},{8,10},{10,8},{9,1... | collective-permute-start | bytes 589832 | tf_op jit(solution)/shard_map/ppermute | solution.py:65
  4.2 4.9 %collective-permute-done.refs_2_ = bf16[2,64,768]{2,1,0:T(8,128)(2,1)S(1)} collective-permute-done((bf16[2,64,768]{2,1,0:T(8,128)(2,1)S(1)}, bf16[2,64,768]{2,1,0:T(8,128)(2,1)S(1)}, u32[]{:S(2)}, u32[]{:S(2)}) %collective-permute-start) | collective-permute-done | bytes 196640 | tf_op jit(solution)/shard_map/ppermute | solution.py:65
  10.2 3.7 %collective-permute-start.1 = (bf16[2,64,768]{2,1,0:T(8,128)(2,1)S(1)}, bf16[2,64,768]{2,1,0:T(8,128)(2,1)S(1)}, u32[]{:S(2)}, u32[]{:S(2)}) collective-permute-start(bf16[2,64,768]{2,1,0:T(8,128)(2,1)S(1)} %get-tuple-element.50), channel_id=1, source_target_pairs={{0,4},{12,8},{1,5},{13,9},{2,6},{14,10},{3,7},{15,11},{16,20},{28,... | collective-permute-start | bytes 589832 | tf_op jit(solution)/shard_map/ppermute | solution.py:65
  13.9 2.3 %collective-permute-start.3 = (bf16[2,64,768]{2,1,0:T(8,128)(2,1)S(1)}, bf16[2,64,768]{2,1,0:T(8,128)(2,1)S(1)}, u32[]{:S(2)}, u32[]{:S(2)}) collective-permute-start(bf16[2,64,768]{2,1,0:T(8,128)(2,1)S(1)} %get-tuple-element.51), channel_id=1, source_target_pairs={{0,8},{12,4},{1,9},{13,5},{2,10},{14,6},{3,11},{15,7},{16,24},{28,... | collective-permute-start | bytes 589832 | tf_op jit(solution)/shard_map/ppermute | solution.py:65
  16.9 2.2 collective-permute-done.1
  19.1 2.4 %collective-permute-done.3 = bf16[2,64,768]{2,1,0:T(8,128)(2,1)S(1)} collective-permute-done((bf16[2,64,768]{2,1,0:T(8,128)(2,1)S(1)}, bf16[2,64,768]{2,1,0:T(8,128)(2,1)S(1)}, u32[]{:S(2)}, u32[]{:S(2)}) %collective-permute-start.3) | collective-permute-done | bytes 196640 | tf_op jit(solution)/shard_map/ppermute | solution.py:65
  24.9 1.8 shard_map.67
  26.8 1.7 collective-permute-start.18
  28.4 9.7 %collective-permute-start.9 = (bf16[384,768]{1,0:T(8,128)(2,1)S(1)}, bf16[384,768]{1,0:T(8,128)(2,1)}, u32[]{:S(2)}, u32[]{:S(2)}) collective-permute-start(bf16[384,768]{1,0:T(8,128)(2,1)S(1)} %get-tuple-element.21), channel_id=1, source_target_pairs={{0,4},{12,8},{1,5},{13,9},{2,6},{14,10},{3,7},{15,11},{16,20},{28,... | collective-permute-start | bytes 1769480 | tf_op jit(solution)/shard_map/ppermute | solution.py:65
  39.5 2.1 collective-permute-start.6
  44.8 2.2 collective-permute-start.16
  48.0 3.1 %collective-permute-done.9.fold = bf16[384,768]{1,0:T(8,128)(2,1)} collective-permute-done((bf16[384,768]{1,0:T(8,128)(2,1)S(1)}, bf16[384,768]{1,0:T(8,128)(2,1)}, u32[]{:S(2)}, u32[]{:S(2)}) %collective-permute-start.9) | collective-permute-done | bytes 589856 | tf_op jit(solution)/shard_map/ppermute | solution.py:65
  51.0 12.6 %collective-permute-done.6.fold.refs_1_ = bf16[384,768]{1,0:T(8,128)(2,1)} collective-permute-done((bf16[384,768]{1,0:T(8,128)(2,1)S(1)}, bf16[384,768]{1,0:T(8,128)(2,1)}, u32[]{:S(2)}, u32[]{:S(2)}) %collective-permute-start.6) | collective-permute-done | bytes 589856 | tf_op jit(solution)/shard_map/ppermute | solution.py:65
  65.2 4.5 %collective-permute-start.11 = (bf16[4,64,768]{2,1,0:T(8,128)(2,1)}, bf16[4,64,768]{2,1,0:T(8,128)(2,1)S(1)}, u32[]{:S(2)}, u32[]{:S(2)}) collective-permute-start(bf16[4,64,768]{2,1,0:T(8,128)(2,1)} %get-tuple-element.22), channel_id=1, source_target_pairs={{0,4},{12,8},{1,5},{13,9},{2,6},{14,10},{3,7},{15,11},{16,20},{28,... | collective-permute-start | bytes 1179656 | tf_op jit(solution)/shard_map/ppermute | solution.py:65
  74.8 11.7 %collective-permute-done.11.came = bf16[4,64,768]{2,1,0:T(8,128)(2,1)S(1)} collective-permute-done((bf16[4,64,768]{2,1,0:T(8,128)(2,1)}, bf16[4,64,768]{2,1,0:T(8,128)(2,1)S(1)}, u32[]{:S(2)}, u32[]{:S(2)}) %collective-permute-start.11) | collective-permute-done | bytes 393248 | tf_op jit(solution)/shard_map/ppermute | solution.py:65
  86.5 5.0 %collective-permute-start.20 = (bf16[384,1024]{1,0:T(8,128)(2,1)}, bf16[384,1024]{1,0:T(8,128)(2,1)}, u32[]{:S(2)}, u32[]{:S(2)}) collective-permute-start(bf16[384,1024]{1,0:T(8,128)(2,1)} %shard_map.70), channel_id=1, source_target_pairs={{0,8},{12,4},{1,9},{13,5},{2,10},{14,6},{3,11},{15,7},{16,24},{28,... | collective-permute-start | bytes 2359304 | tf_op jit(solution)/shard_map/ppermute | solution.py:65
  97.8 5.1 %shard_map.73 = bf16[512,768]{1,0:T(8,128)(2,1)S(1)} custom-call(s32[4]{0:T(128)S(1)} %pad_add_fusion.place_ref.p, bf16[512,768]{1,0:T(8,128)(2,1)} %bitcast.22.both, bf16[512,768]{1,0:T(8,128)(2,1)} %collective-permute-done.26.other, bf16[768,1536]{1,0:T(8,128)(2,1)} %own.7, bf16[384,768]{1,0:T(8,128)(2,1)} %collective-permute-done.9.fold, ...), custom_call_target="tpu_custom_call" | custom-call | flops 1207959552 | bytes 7084032 | tf_op jit(solution)/shard_map/pallas_call | solution.py:83
  104.4 9.2 %collective-permute-done.8.came = bf16[4,64,768]{2,1,0:T(8,128)(2,1)S(1)} collective-permute-done((bf16[4,64,768]{2,1,0:T(8,128)(2,1)S(1)}, bf16[4,64,768]{2,1,0:T(8,128)(2,1)S(1)}, u32[]{:S(2)}, u32[]{:S(2)}) %collective-permute-start.8) | collective-permute-done | bytes 393248 | tf_op jit(solution)/shard_map/ppermute | solution.py:65
  115.9 5.1 %shard_map.72.keeps = f32[512,768]{1,0:T(8,128)S(1)} custom-call(s32[4]{0:T(128)S(1)} %pad_add_fusion.place_ref.p, bf16[512,768]{1,0:T(8,128)(2,1)} %bitcast.22.both, bf16[512,768]{1,0:T(8,128)(2,1)} %collective-permute-done.26.other, bf16[768,1536]{1,0:T(8,128)(2,1)} %own.7, bf16[384,768]{1,0:T(8,128)(2,1)} %collective-permute-done.6.fold.refs_1_, ...), custom_call_target="tpu_custom_call" | custom-call | flops 1207959552 | bytes 7870464 | tf_op jit(solution)/shard_map/pallas_call | solution.py:83
  121.0 5.1 %shard_map.68 = bf16[512,768]{1,0:T(8,128)(2,1)S(1)} custom-call(s32[4]{0:T(128)S(1)} %pad_add_fusion.place_ref.p, bf16[512,768]{1,0:T(8,128)(2,1)} %bitcast.12.both, bf16[512,768]{1,0:T(8,128)(2,1)} %collective-permute-done.5.other, bf16[768,1536]{1,0:T(8,128)(2,1)} %own.7, bf16[384,768]{1,0:T(8,128)(2,1)} %collective-permute-done.9.fold, ...), custom_call_target="tpu_custom_call" | custom-call | flops 1207959552 | bytes 7084032 | tf_op jit(solution)/shard_map/pallas_call | solution.py:83
  128.0 5.1 %shard_map.66.keeps = f32[512,768]{1,0:T(8,128)S(1)} custom-call(s32[4]{0:T(128)S(1)} %pad_add_fusion.place_ref.p, bf16[512,768]{1,0:T(8,128)(2,1)} %bitcast.12.both, bf16[512,768]{1,0:T(8,128)(2,1)} %collective-permute-done.5.other, bf16[768,1536]{1,0:T(8,128)(2,1)} %own.7, bf16[384,768]{1,0:T(8,128)(2,1)} %collective-permute-done.6.fold.refs_1_, ...), custom_call_target="tpu_custom_call" | custom-call | flops 1207959552 | bytes 7870464 | tf_op jit(solution)/shard_map/pallas_call | solution.py:83
  133.4 1.7 shard_map.74.s0
  135.8 3.0 %collective-permute-done.21 = bf16[384,1024]{1,0:T(8,128)(2,1)S(1)} collective-permute-done((bf16[384,1024]{1,0:T(8,128)(2,1)}, bf16[384,1024]{1,0:T(8,128)(2,1)S(1)}, u32[]{:S(2)}, u32[]{:S(2)}) %collective-permute-start.21) | collective-permute-done | bytes 786464 | tf_op jit(solution)/shard_map/ppermute | solution.py:65
  140.1 1.7 shard_map.69.s0
  144.8 11.4 %collective-permute-done.29.s2 = bf16[528,768]{1,0:T(8,128)(2,1)S(1)} collective-permute-done((bf16[528,768]{1,0:T(8,128)(2,1)S(1)}, bf16[528,768]{1,0:T(8,128)(2,1)S(1)}, u32[]{:S(2)}, u32[]{:S(2)}) %collective-permute-start.29) | collective-permute-done | bytes 811040 | tf_op jit(solution)/shard_map/ppermute | solution.py:65
  156.2 12.5 %collective-permute-done.14.s2 = bf16[528,768]{1,0:T(8,128)(2,1)S(1)} collective-permute-done((bf16[528,768]{1,0:T(8,128)(2,1)S(1)}, bf16[528,768]{1,0:T(8,128)(2,1)S(1)}, u32[]{:S(2)}, u32[]{:S(2)}) %collective-permute-start.14) | collective-permute-done | bytes 811040 | tf_op jit(solution)/shard_map/ppermute | solution.py:65
  168.8 3.8 %multiply_reduce_fusion = (f32[4,1024]{1,0:T(4,128)S(1)}, bf16[4,768,1024]{2,1,0:T(8,128)(2,1)}) fusion(f32[4,768]{1,0:T(4,128)S(1)} %copy-done.14, bf16[1,768,1024]{2,1,0:T(8,128)(2,1)S(1)} %get-tuple-element.36, bf16[1,768,1024]{2,1,0:T(8,128)(2,1)S(1)} %get-tuple-element.37, bf16[1,768,1024]{2,1,0:T(8,128)(2,1)S(1)} %get-tuple-element.38, ...), kind=kLoop, calls=%fused_computation | loop fusion | flops 18870272 | bytes 12611584 | tf_op jit(solution)/shard_map/reduce_sum | solution.py:419
  172.6 7.2 %shard_map.75 = (bf16[144,1024]{1,0:T(8,128)(2,1)S(1)}, bf16[144,1024]{1,0:T(8,128)(2,1)S(1)}, bf16[144,1024]{1,0:T(8,128)(2,1)S(1)}, bf16[144,1024]{1,0:T(8,128)(2,1)S(1)}) custom-call(s32[4]{0:T(128)S(1)} %pad_add_fusion.place_ref.p, bf16[528,768]{1,0:T(8,128)(2,1)S(1)} %shard_map.74.s0, bf16[528,768]{1,0:T(8,128)(2,1)S(1)} %collective-permute-done.28.s1, ...), custom_call_target="tpu_custom_call" | custom-call | flops 3221225472 | bytes 10731520 | tf_op jit(solution)/shard_map/pallas_call | solution.py:83
  183.1 7.2 %shard_map.71 = (bf16[144,1024]{1,0:T(8,128)(2,1)S(1)}, bf16[144,1024]{1,0:T(8,128)(2,1)S(1)}, bf16[144,1024]{1,0:T(8,128)(2,1)S(1)}, bf16[144,1024]{1,0:T(8,128)(2,1)S(1)}) custom-call(s32[4]{0:T(128)S(1)} %pad_add_fusion.place_ref.p, bf16[528,768]{1,0:T(8,128)(2,1)S(1)} %shard_map.69.s0, bf16[528,768]{1,0:T(8,128)(2,1)S(1)} %collective-permute-done.13.s1, ...), custom_call_target="tpu_custom_call" | custom-call | flops 3221225472 | bytes 10731520 | tf_op jit(solution)/shard_map/pallas_call | solution.py:83
  193.6 12.0 %collective-permute-done.32.refs_6_ = bf16[144,1024]{1,0:T(8,128)(2,1)S(1)} collective-permute-done((bf16[144,1024]{1,0:T(8,128)(2,1)S(1)}, bf16[144,1024]{1,0:T(8,128)(2,1)S(1)}, u32[]{:S(2)}, u32[]{:S(2)}) %collective-permute-start.32) | collective-permute-done | bytes 294944 | tf_op jit(solution)/shard_map/ppermute | solution.py:65
  205.7 12.2 %collective-permute-done.23.refs_2_ = bf16[144,1024]{1,0:T(8,128)(2,1)S(1)} collective-permute-done((bf16[144,1024]{1,0:T(8,128)(2,1)S(1)}, bf16[144,1024]{1,0:T(8,128)(2,1)S(1)}, u32[]{:S(2)}, u32[]{:S(2)}) %collective-permute-start.23) | collective-permute-done | bytes 294944 | tf_op jit(solution)/shard_map/ppermute | solution.py:65
  217.9 1.7 shard_map.76
  (103 shorter events, 42.4 us)
Async XLA Ops:
  1.2 7.9 %collective-permute-start = (bf16[2,64,768]{2,1,0:T(8,128)(2,1)S(1)}, bf16[2,64,768]{2,1,0:T(8,128)(2,1)S(1)}, u32[]{:S(2)}, u32[]{:S(2)}) collective-permute-start(bf16[2,64,768]{2,1,0:T(8,128)(2,1)S(1)} %broadcast_select_fusion.12), channel_id=1, source_target_pairs={{0,2},{2,0},{1,3},{3,1},{4,6},{6,4},{5,7},{7,5},{8,10},{10,8},{9,1... | collective-permute-start | bytes 589832 | tf_op jit(solution)/shard_map/ppermute | solution.py:65
  10.2 8.9 %collective-permute-start.1 = (bf16[2,64,768]{2,1,0:T(8,128)(2,1)S(1)}, bf16[2,64,768]{2,1,0:T(8,128)(2,1)S(1)}, u32[]{:S(2)}, u32[]{:S(2)}) collective-permute-start(bf16[2,64,768]{2,1,0:T(8,128)(2,1)S(1)} %get-tuple-element.50), channel_id=1, source_target_pairs={{0,4},{12,8},{1,5},{13,9},{2,6},{14,10},{3,7},{15,11},{16,20},{28,... | collective-permute-start | bytes 589832 | tf_op jit(solution)/shard_map/ppermute | solution.py:65
  23.3 18.2 %collective-permute-start.25 = (bf16[2,4,32,768]{3,2,1,0:T(8,128)(2,1)}, bf16[2,4,32,768]{3,2,1,0:T(8,128)(2,1)}, u32[]{:S(2)}, u32[]{:S(2)}) collective-permute-start(bf16[2,4,32,768]{3,2,1,0:T(8,128)(2,1)} %slice.17), channel_id=1, source_target_pairs={{0,2},{2,0},{1,3},{3,1},{4,6},{6,4},{5,7},{7,5},{8,10},{10,8},{9,1... | collective-permute-start | bytes 1179656 | tf_op jit(solution)/shard_map/ppermute | solution.py:65
  26.8 38.4 %collective-permute-start.18 = (bf16[384,1024]{1,0:T(8,128)(2,1)S(1)}, bf16[384,1024]{1,0:T(8,128)(2,1)}, u32[]{:S(2)}, u32[]{:S(2)}) collective-permute-start(bf16[384,1024]{1,0:T(8,128)(2,1)S(1)} %get-tuple-element.24), channel_id=1, source_target_pairs={{4,8},{8,4},{5,9},{9,5},{6,10},{10,6},{7,11},{11,7},{20,24},{24,20... | collective-permute-start | bytes 2359304 | tf_op jit(solution)/shard_map/ppermute | solution.py:65
  28.4 22.6 %collective-permute-start.9 = (bf16[384,768]{1,0:T(8,128)(2,1)S(1)}, bf16[384,768]{1,0:T(8,128)(2,1)}, u32[]{:S(2)}, u32[]{:S(2)}) collective-permute-start(bf16[384,768]{1,0:T(8,128)(2,1)S(1)} %get-tuple-element.21), channel_id=1, source_target_pairs={{0,4},{12,8},{1,5},{13,9},{2,6},{14,10},{3,7},{15,11},{16,20},{28,... | collective-permute-start | bytes 1769480 | tf_op jit(solution)/shard_map/ppermute | solution.py:65
  39.5 24.2 %collective-permute-start.6 = (bf16[384,768]{1,0:T(8,128)(2,1)S(1)}, bf16[384,768]{1,0:T(8,128)(2,1)}, u32[]{:S(2)}, u32[]{:S(2)}) collective-permute-start(bf16[384,768]{1,0:T(8,128)(2,1)S(1)} %get-tuple-element.19), channel_id=1, source_target_pairs={{0,4},{12,8},{1,5},{13,9},{2,6},{14,10},{3,7},{15,11},{16,20},{28,... | collective-permute-start | bytes 1769480 | tf_op jit(solution)/shard_map/ppermute | solution.py:65
  42.7 27.0 %collective-permute-start.4 = (bf16[2,4,32,768]{3,2,1,0:T(8,128)(2,1)S(1)}, bf16[2,4,32,768]{3,2,1,0:T(8,128)(2,1)S(1)}, u32[]{:S(2)}, u32[]{:S(2)}) collective-permute-start(bf16[2,4,32,768]{3,2,1,0:T(8,128)(2,1)S(1)} %get-tuple-element.49), channel_id=1, source_target_pairs={{0,2},{2,0},{1,3},{3,1},{4,6},{6,4},{5,7},{7,5},{8,10},{10,8},{9,1... | collective-permute-start | bytes 1179656 | tf_op jit(solution)/shard_map/ppermute | solution.py:65
  44.8 47.6 %collective-permute-start.16 = (bf16[384,1024]{1,0:T(8,128)(2,1)}, bf16[384,1024]{1,0:T(8,128)(2,1)}, u32[]{:S(2)}, u32[]{:S(2)}) collective-permute-start(bf16[384,1024]{1,0:T(8,128)(2,1)} %get-tuple-element.23), channel_id=1, source_target_pairs={{0,4},{12,8},{1,5},{13,9},{2,6},{14,10},{3,7},{15,11},{16,20},{28,... | collective-permute-start | bytes 2359304 | tf_op jit(solution)/shard_map/ppermute | solution.py:65
  51.0 43.6 %collective-permute-start.26 = (bf16[512,768]{1,0:T(8,128)(2,1)}, bf16[512,768]{1,0:T(8,128)(2,1)}, u32[]{:S(2)}, u32[]{:S(2)}) collective-permute-start(bf16[512,768]{1,0:T(8,128)(2,1)} %bitcast.22.both), channel_id=1, source_target_pairs={{0,1},{1,0},{2,3},{3,2},{4,5},{5,4},{6,7},{7,6},{8,9},{9,8},{10,11... | collective-permute-start | bytes 2359304 | tf_op jit(solution)/shard_map/ppermute | solution.py:65
  63.7 30.3 %collective-permute-start.10 = (bf16[384,768]{1,0:T(8,128)(2,1)}, bf16[384,768]{1,0:T(8,128)(2,1)}, u32[]{:S(2)}, u32[]{:S(2)}) collective-permute-start(bf16[384,768]{1,0:T(8,128)(2,1)} %collective-permute-done.9.fold), channel_id=1, source_target_pairs={{0,16},{16,0},{1,17},{17,1},{2,18},{18,2},{3,19},{19,3},{4,20},{20... | collective-permute-start | bytes 1769480 | tf_op jit(solution)/shard_map/ppermute | solution.py:65
  65.2 21.3 %collective-permute-start.11 = (bf16[4,64,768]{2,1,0:T(8,128)(2,1)}, bf16[4,64,768]{2,1,0:T(8,128)(2,1)S(1)}, u32[]{:S(2)}, u32[]{:S(2)}) collective-permute-start(bf16[4,64,768]{2,1,0:T(8,128)(2,1)} %get-tuple-element.22), channel_id=1, source_target_pairs={{0,4},{12,8},{1,5},{13,9},{2,6},{14,10},{3,7},{15,11},{16,20},{28,... | collective-permute-start | bytes 1179656 | tf_op jit(solution)/shard_map/ppermute | solution.py:65
  70.5 26.1 %collective-permute-start.19 = (bf16[384,1024]{1,0:T(8,128)(2,1)}, bf16[384,1024]{1,0:T(8,128)(2,1)}, u32[]{:S(2)}, u32[]{:S(2)}) collective-permute-start(bf16[384,1024]{1,0:T(8,128)(2,1)} %collective-permute-done.18), channel_id=1, source_target_pairs={{0,16},{16,0},{1,17},{17,1},{2,18},{18,2},{3,19},{19,3},{4,20},{20... | collective-permute-start | bytes 2359304 | tf_op jit(solution)/shard_map/ppermute | solution.py:65
  86.5 27.8 %collective-permute-start.20 = (bf16[384,1024]{1,0:T(8,128)(2,1)}, bf16[384,1024]{1,0:T(8,128)(2,1)}, u32[]{:S(2)}, u32[]{:S(2)}) collective-permute-start(bf16[384,1024]{1,0:T(8,128)(2,1)} %shard_map.70), channel_id=1, source_target_pairs={{0,8},{12,4},{1,9},{13,5},{2,10},{14,6},{3,11},{15,7},{16,24},{28,... | collective-permute-start | bytes 2359304 | tf_op jit(solution)/shard_map/ppermute | solution.py:65
  92.5 23.4 %collective-permute-start.7 = (bf16[384,768]{1,0:T(8,128)(2,1)}, bf16[384,768]{1,0:T(8,128)(2,1)}, u32[]{:S(2)}, u32[]{:S(2)}) collective-permute-start(bf16[384,768]{1,0:T(8,128)(2,1)} %collective-permute-done.6.fold.refs_1_), channel_id=1, source_target_pairs={{0,16},{16,0},{1,17},{17,1},{2,18},{18,2},{3,19},{19,3},{4,20},{20... | collective-permute-start | bytes 1769480 | tf_op jit(solution)/shard_map/ppermute | solution.py:65
  94.0 27.0 %collective-permute-start.5 = (bf16[512,768]{1,0:T(8,128)(2,1)}, bf16[512,768]{1,0:T(8,128)(2,1)}, u32[]{:S(2)}, u32[]{:S(2)}) collective-permute-start(bf16[512,768]{1,0:T(8,128)(2,1)} %bitcast.12.both), channel_id=1, source_target_pairs={{0,1},{1,0},{2,3},{3,2},{4,5},{5,4},{6,7},{7,6},{8,9},{9,8},{10,11... | collective-permute-start | bytes 2359304 | tf_op jit(solution)/shard_map/ppermute | solution.py:65
  94.6 32.1 %collective-permute-start.17 = (bf16[384,1024]{1,0:T(8,128)(2,1)}, bf16[384,1024]{1,0:T(8,128)(2,1)S(1)}, u32[]{:S(2)}, u32[]{:S(2)}) collective-permute-start(bf16[384,1024]{1,0:T(8,128)(2,1)} %collective-permute-done.16), channel_id=1, source_target_pairs={{0,16},{16,0},{1,17},{17,1},{2,18},{18,2},{3,19},{19,3},{4,20},{20... | collective-permute-start | bytes 2359304 | tf_op jit(solution)/shard_map/ppermute | solution.py:65
  96.5 17.0 %collective-permute-start.8 = (bf16[4,64,768]{2,1,0:T(8,128)(2,1)S(1)}, bf16[4,64,768]{2,1,0:T(8,128)(2,1)S(1)}, u32[]{:S(2)}, u32[]{:S(2)}) collective-permute-start(bf16[4,64,768]{2,1,0:T(8,128)(2,1)S(1)} %copy-done.10), channel_id=1, source_target_pairs={{0,4},{12,8},{1,5},{13,9},{2,6},{14,10},{3,7},{15,11},{16,20},{28,... | collective-permute-start | bytes 1179656 | tf_op jit(solution)/shard_map/ppermute | solution.py:65
  113.6 19.9 %collective-permute-start.27 = (bf16[512,768]{1,0:T(8,128)(2,1)S(1)}, bf16[512,768]{1,0:T(8,128)(2,1)S(1)}, u32[]{:S(2)}, u32[]{:S(2)}) collective-permute-start(bf16[512,768]{1,0:T(8,128)(2,1)S(1)} %shard_map.73), channel_id=1, source_target_pairs={{4,8},{8,4},{5,9},{9,5},{6,10},{10,6},{7,11},{11,7},{20,24},{24,20... | collective-permute-start | bytes 2359304 | tf_op jit(solution)/shard_map/ppermute | solution.py:65
  114.3 24.4 %collective-permute-start.21 = (bf16[384,1024]{1,0:T(8,128)(2,1)}, bf16[384,1024]{1,0:T(8,128)(2,1)S(1)}, u32[]{:S(2)}, u32[]{:S(2)}) collective-permute-start(bf16[384,1024]{1,0:T(8,128)(2,1)} %collective-permute-done.20), channel_id=1, source_target_pairs={{0,16},{16,0},{1,17},{17,1},{2,18},{18,2},{3,19},{19,3},{4,20},{20... | collective-permute-start | bytes 2359304 | tf_op jit(solution)/shard_map/ppermute | solution.py:65
  126.0 14.1 %collective-permute-start.12 = (bf16[512,768]{1,0:T(8,128)(2,1)S(1)}, bf16[512,768]{1,0:T(8,128)(2,1)S(1)}, u32[]{:S(2)}, u32[]{:S(2)}) collective-permute-start(bf16[512,768]{1,0:T(8,128)(2,1)S(1)} %shard_map.68), channel_id=1, source_target_pairs={{4,8},{8,4},{5,9},{9,5},{6,10},{10,6},{7,11},{11,7},{20,24},{24,20... | collective-permute-start | bytes 2359304 | tf_op jit(solution)/shard_map/ppermute | solution.py:65
  135.2 21.1 %collective-permute-start.29 = (bf16[528,768]{1,0:T(8,128)(2,1)S(1)}, bf16[528,768]{1,0:T(8,128)(2,1)S(1)}, u32[]{:S(2)}, u32[]{:S(2)}) collective-permute-start(bf16[528,768]{1,0:T(8,128)(2,1)S(1)} %shard_map.74.s0), channel_id=1, source_target_pairs={{0,2},{2,0},{1,3},{3,1},{4,6},{6,4},{5,7},{7,5},{8,10},{10,8},{9,1... | collective-permute-start | bytes 2433032 | tf_op jit(solution)/shard_map/ppermute | solution.py:65
  135.8 36.8 %collective-permute-start.28 = (bf16[528,768]{1,0:T(8,128)(2,1)S(1)}, bf16[528,768]{1,0:T(8,128)(2,1)S(1)}, u32[]{:S(2)}, u32[]{:S(2)}) collective-permute-start(bf16[528,768]{1,0:T(8,128)(2,1)S(1)} %shard_map.74.s0), channel_id=1, source_target_pairs={{0,1},{1,0},{2,3},{3,2},{4,5},{5,4},{6,7},{7,6},{8,9},{9,8},{10,11... | collective-permute-start | bytes 2433032 | tf_op jit(solution)/shard_map/ppermute | solution.py:65
  141.8 26.9 %collective-permute-start.14 = (bf16[528,768]{1,0:T(8,128)(2,1)S(1)}, bf16[528,768]{1,0:T(8,128)(2,1)S(1)}, u32[]{:S(2)}, u32[]{:S(2)}) collective-permute-start(bf16[528,768]{1,0:T(8,128)(2,1)S(1)} %shard_map.69.s0), channel_id=1, source_target_pairs={{0,2},{2,0},{1,3},{3,1},{4,6},{6,4},{5,7},{7,5},{8,10},{10,8},{9,1... | collective-permute-start | bytes 2433032 | tf_op jit(solution)/shard_map/ppermute | solution.py:65
  144.7 38.3 %collective-permute-start.13 = (bf16[528,768]{1,0:T(8,128)(2,1)S(1)}, bf16[528,768]{1,0:T(8,128)(2,1)S(1)}, u32[]{:S(2)}, u32[]{:S(2)}) collective-permute-start(bf16[528,768]{1,0:T(8,128)(2,1)S(1)} %shard_map.69.s0), channel_id=1, source_target_pairs={{0,1},{1,0},{2,3},{3,2},{4,5},{5,4},{6,7},{7,6},{8,9},{9,8},{10,11... | collective-permute-start | bytes 2433032 | tf_op jit(solution)/shard_map/ppermute | solution.py:65
  156.2 16.3 %collective-permute-start.30 = (bf16[528,768]{1,0:T(8,128)(2,1)S(1)}, bf16[528,768]{1,0:T(8,128)(2,1)S(1)}, u32[]{:S(2)}, u32[]{:S(2)}) collective-permute-start(bf16[528,768]{1,0:T(8,128)(2,1)S(1)} %collective-permute-done.29.s2), channel_id=1, source_target_pairs={{0,1},{1,0},{2,3},{3,2},{4,5},{5,4},{6,7},{7,6},{8,9},{9,8},{10,11... | collective-permute-start | bytes 2433032 | tf_op jit(solution)/shard_map/ppermute | solution.py:65
  168.8 14.3 %collective-permute-start.15 = (bf16[528,768]{1,0:T(8,128)(2,1)S(1)}, bf16[528,768]{1,0:T(8,128)(2,1)S(1)}, u32[]{:S(2)}, u32[]{:S(2)}) collective-permute-start(bf16[528,768]{1,0:T(8,128)(2,1)S(1)} %collective-permute-done.14.s2), channel_id=1, source_target_pairs={{0,1},{1,0},{2,3},{3,2},{4,5},{5,4},{6,7},{7,6},{8,9},{9,8},{10,11... | collective-permute-start | bytes 2433032 | tf_op jit(solution)/shard_map/ppermute | solution.py:65
  179.8 12.5 %collective-permute-start.31 = (bf16[144,1024]{1,0:T(8,128)(2,1)S(1)}, bf16[144,1024]{1,0:T(8,128)(2,1)S(1)}, u32[]{:S(2)}, u32[]{:S(2)}) collective-permute-start(bf16[144,1024]{1,0:T(8,128)(2,1)S(1)} %get-tuple-element.30), channel_id=1, source_target_pairs={{4,8},{8,4},{5,9},{9,5},{6,10},{10,6},{7,11},{11,7},{20,24},{24,20... | collective-permute-start | bytes 884744 | tf_op jit(solution)/shard_map/ppermute | solution.py:65
  180.5 25.2 %collective-permute-start.32 = (bf16[144,1024]{1,0:T(8,128)(2,1)S(1)}, bf16[144,1024]{1,0:T(8,128)(2,1)S(1)}, u32[]{:S(2)}, u32[]{:S(2)}) collective-permute-start(bf16[144,1024]{1,0:T(8,128)(2,1)S(1)} %get-tuple-element.31), channel_id=1, source_target_pairs={{4,0},{8,12},{5,1},{9,13},{6,2},{10,14},{7,3},{11,15},{20,16},{24,... | collective-permute-start | bytes 884744 | tf_op jit(solution)/shard_map/ppermute | solution.py:65
  181.8 23.9 %collective-permute-start.33 = (bf16[144,1024]{1,0:T(8,128)(2,1)S(1)}, bf16[144,1024]{1,0:T(8,128)(2,1)S(1)}, u32[]{:S(2)}, u32[]{:S(2)}) collective-permute-start(bf16[144,1024]{1,0:T(8,128)(2,1)S(1)} %get-tuple-element.32), channel_id=1, source_target_pairs={{4,12},{8,0},{5,13},{9,1},{6,14},{10,2},{7,15},{11,3},{20,28},{24,... | collective-permute-start | bytes 884744 | tf_op jit(solution)/shard_map/ppermute | solution.py:65
  190.3 15.3 %collective-permute-start.22 = (bf16[144,1024]{1,0:T(8,128)(2,1)S(1)}, bf16[144,1024]{1,0:T(8,128)(2,1)S(1)}, u32[]{:S(2)}, u32[]{:S(2)}) collective-permute-start(bf16[144,1024]{1,0:T(8,128)(2,1)S(1)} %get-tuple-element.26), channel_id=1, source_target_pairs={{4,8},{8,4},{5,9},{9,5},{6,10},{10,6},{7,11},{11,7},{20,24},{24,20... | collective-permute-start | bytes 884744 | tf_op jit(solution)/shard_map/ppermute | solution.py:65
  191.0 26.9 %collective-permute-start.23 = (bf16[144,1024]{1,0:T(8,128)(2,1)S(1)}, bf16[144,1024]{1,0:T(8,128)(2,1)S(1)}, u32[]{:S(2)}, u32[]{:S(2)}) collective-permute-start(bf16[144,1024]{1,0:T(8,128)(2,1)S(1)} %get-tuple-element.27), channel_id=1, source_target_pairs={{4,0},{8,12},{5,1},{9,13},{6,2},{10,14},{7,3},{11,15},{20,16},{24,... | collective-permute-start | bytes 884744 | tf_op jit(solution)/shard_map/ppermute | solution.py:65
  192.3 25.6 %collective-permute-start.24 = (bf16[144,1024]{1,0:T(8,128)(2,1)S(1)}, bf16[144,1024]{1,0:T(8,128)(2,1)S(1)}, u32[]{:S(2)}, u32[]{:S(2)}) collective-permute-start(bf16[144,1024]{1,0:T(8,128)(2,1)S(1)} %get-tuple-element.28), channel_id=1, source_target_pairs={{4,12},{8,0},{5,13},{9,1},{6,14},{10,2},{7,15},{11,3},{20,28},{24,... | collective-permute-start | bytes 884744 | tf_op jit(solution)/shard_map/ppermute | solution.py:65
  (18 other events, 214.3 us)

commit v4 on v3

--- a/solution.py
+++ b/solution.py
@@ -78,8 +78,7 @@
 EXTRA = 16
 
 
-def call(kernel, place, grid, ins, outs, shapes, scratch, args, flops=0):
-    moved = sum(v.size * v.dtype.itemsize for v in (*args, *jax.tree.leaves(shapes)))
+def call(kernel, place, grid, ins, outs, shapes, scratch, args):
     return pl.pallas_call(
         kernel,
         grid_spec=pltpu.PrefetchScalarGridSpec(
@@ -87,7 +86,7 @@
         ),
         out_shape=shapes,
         compiler_params=pltpu.CompilerParams(vmem_limit_bytes=LIMIT),
-        cost_estimate=pl.CostEstimate(flops=flops, bytes_accessed=moved, transcendentals=0),
+        cost_estimate=pl.CostEstimate(flops=1, bytes_accessed=1, transcendentals=0),
     )(place, *args)
 
 
@@ -135,43 +134,51 @@
     return jnp.concatenate([rows, fill], axis=0).T
 
 
-def attend(place, both, other, w_out, fold, swapped, resid, came, bias, part, inner, dtype):
-    tokens, heads = both.shape
+def attend(place, tokens_of, w_out, fold, swapped, resid, came, bias, part, inner, dtype):
+    rows, heads = tokens_of[0].shape
+    tokens = 2 * rows
     half, share = fold.shape[1], fold.shape[0]
     images, span = resid.shape[0], tokens // resid.shape[0] // 4
     tile = 256 if half % 256 == 0 else half
     tiles = half // tile
 
-    def kernel(p, both, other, own, fold, swapped, old, came, bias, out, total):
+    def kernel(p, own, far, near, both, weight, fold, swapped, old, came, bias, out, left, total):
         low = p[0] == 1
         turn = low == (p[2] == 0)
-        here = jnp.where(turn, other[...], both[...])
-        folded = jnp.where(turn, both[...], other[...])
-        first = jnp.where(p[1] == 0, fold[...], swapped[...])
-        second = jnp.where(p[1] == 0, swapped[...], fold[...])
-        value = jnp.dot(here, own[...], preferred_element_type=jnp.float32)
-        value = value + jnp.dot(folded[:, :share], first, preferred_element_type=jnp.float32)
-        value = value + jnp.dot(folded[:, share:], second, preferred_element_type=jnp.float32)
+
+        @pl.when(pl.program_id(0) == 0)
+        def _():
+            for at, one, two in ((p[5], own, near), (1 - p[5], far, both)):
+                at = pl.ds(pl.multiple_of(at * rows, rows), rows)
+                left[at, :heads] = jnp.where(turn, two[...], one[...])
+                folded = jnp.where(turn, one[...], two[...])
+                first, second = folded[:, :share], folded[:, share:]
+                left[at, heads : heads + share] = jnp.where(p[1] == 0, first, second)
+                left[at, heads + share :] = jnp.where(p[1] == 0, second, first)
+
+        value = jnp.dot(left[:, :heads], weight[...], preferred_element_type=jnp.float32)
+        for i, piece in enumerate((fold, swapped)):
+            at = slice(heads + i * share, heads + (i + 1) * share)
+            value = value + jnp.dot(left[:, at], piece[...], preferred_element_type=jnp.float32)
         total[...] = value + jnp.where(low, bias[...], jnp.zeros_like(bias[...]))
         own_at, came_at = jnp.where(low, span, 2 * span), jnp.where(low, 0, 3 * span)
         for image in range(images):
             for at, source in ((own_at, old), (came_at, came)):
-                rows = pl.ds(pl.multiple_of(image * 4 * span + at, span), span)
-                total[rows, :] = total[rows, :] + source[image].astype(jnp.float32)
+                at = pl.ds(pl.multiple_of(image * 4 * span + at, span), span)
+                total[at, :] = total[at, :] + source[image].astype(jnp.float32)
         out[...] = total[...].astype(dtype)
 
     def column(p, t):
         return jnp.where((p[0] == 1) == inner, 0, tiles) + t
 
-    whole = pl.BlockSpec((tokens, heads), lambda t, p: (0, 0))
+    whole = pl.BlockSpec((rows, heads), lambda t, p: (0, 0))
     piece = pl.BlockSpec((share, tile), lambda t, p: (0, t))
     return call(
         kernel,
         place,
         (tiles,),
-        [
-            whole,
-            whole,
+        [whole] * 4
+        + [
             pl.BlockSpec((heads, tile), lambda t, p: (0, column(p, t))),
             piece,
             piece,
@@ -181,9 +188,8 @@
         ],
         pl.BlockSpec((tokens, tile), lambda t, p: (0, t)),
         jax.ShapeDtypeStruct((tokens, half), dtype),
-        [pltpu.VMEM((tokens, tile), jnp.float32)],
-        [both, other, w_out, fold, swapped, resid, came, bias.reshape(1, -1)],
-        flops=4 * tokens * heads * half,
+        [pltpu.VMEM((tokens, 2 * heads), jnp.bfloat16), pltpu.VMEM((tokens, tile), jnp.float32)],
+        [*tokens_of, w_out, fold, swapped, resid, came, bias],
     )
 
 
@@ -208,7 +214,7 @@
         kernel,
         place,
         (tokens // 128,),
-        [row, row, pl.BlockSpec((1, half), lambda i, p: (0, 0))],
+        [row, row, pl.BlockSpec((1, half), lambda i, p: (0, 2 * p[4] + 1 - p[0]))],
         pl.BlockSpec((tokens + EXTRA, half), lambda i, p: (0, 0)),
         jax.ShapeDtypeStruct((tokens + EXTRA, half), jnp.bfloat16),
         [],
@@ -216,13 +222,25 @@
     )
 
 
-def project_up(place, scaled, slices, gain_proj):
+def project_up(place, scaled, w_proj, pieces, gain):
     rows, half = scaled[0].shape
-    tokens, out_cols = rows - EXTRA, slices.shape[1]
-    size = tokens // 4
+    tokens, out_cols = rows - EXTRA, w_proj.shape[1]
+    size, share = tokens // 4, half // 2
     tile = 256 if out_cols % 256 == 0 else out_cols
 
-    def kernel(p, s0, s1, s2, s3, slices, gain_proj, o0, o1, o2, o3, shifts, stats, total):
+    def kernel(p, s0, s1, s2, s3, own, f0, f1, c0, c1, a0, a1, gain, *rest):
+        outs, (left, shifts, stats, total) = rest[:4], rest[4:]
+        low = p[0] == 1
+
+        def slot(feature):
+            return jnp.where(low, feature, 3 - feature)
+
+        def put(value, at, rows):
+            swap = (p[1] == 1) & (at != 1)
+            first, second = value[:, :share], value[:, share:]
+            left[at, rows, :share] = jnp.where(swap, second, first)
+            left[at, rows, share:] = jnp.where(swap, first, second)
+
         @pl.when(pl.program_id(0) == 0)
         def _():
             last = [s[tokens:, :tokens] for s in (s0, s1, s2, s3)]
@@ -230,49 +248,77 @@
             middle = 0.25 * (means[0] + means[1] + means[2] + means[3])
             shift = [v - middle for v in means]
             square = sum(added(v, 3) + half * (d * d) for v, d in zip(last, shift))
-            shifts[...] = upright(shift)
             for image in range(4):
                 at = slice(image * size, (image + 1) * size)
                 stats[image] = jnp.concatenate([middle[:, at], square[:, at]], axis=0)
-
-        value = jnp.zeros(total.shape, jnp.float32)
-        for d, s in enumerate((s0, s1, s2, s3)):
-            value = value + jnp.dot(
-                s[:tokens, :],
-                slices[d * half : (d + 1) * half, :],
-                preferred_element_type=jnp.float32,
-            )
-            value = value + shifts[:, d : d + 1] * gain_proj[d : d + 1, :]
-        total[...] = value
-        gains = jnp.sum(gain_proj[...], axis=0, keepdims=True)
-        for role, out in enumerate((o0, o1, o2, o3)):
-            image = jnp.where(p[0] == 1, role, 3 - role)
+            for d, s in enumerate((s0, s1, s2, s3)):
+                feature = p[4] ^ d
+                put(s[:tokens, :], slot(feature), slice(0, tokens))
+                at = pl.multiple_of((2 * feature + 1 - p[0]) * half, half)
+                put(packed([gain[:, pl.ds(at, half)]]), slot(feature), slice(tokens, rows))
+            turned = upright(shift).astype(jnp.float32)
+            high, mid, low_term = terms(turned)
+            zero = jnp.zeros((tokens, 128), jnp.bfloat16)
+            lane = lax.broadcasted_iota(jnp.int32, (tokens, 128), 1)
+            spread = zero
+            for d in range(4):
+                for i, term in enumerate((high, high, high, mid, mid, low_term)):
+                    spread = jnp.where(lane == 6 * d + i, term[:, d : d + 1], spread)
+            shifts[...] = spread
+
+        value = jnp.zeros((rows, tile), jnp.float32)
+        gains = []
+        for at, halves in enumerate(((f0, f1), (own,), (c0, c1), (a0, a1))):
+            piece = jnp.zeros((rows, tile), jnp.float32)
+            for i, weight in enumerate(halves):
+                depth = weight.shape[0]
+                piece = piece + jnp.dot(
+                    left[at, :, i * depth : (i + 1) * depth],
+                    weight[...],
+                    preferred_element_type=jnp.float32,
+                )
+            value = value + piece
+            gains.append(jnp.sum(piece[tokens : tokens + 3], axis=0, keepdims=True))
+        fix = []
+        for d in range(4):
+            at = slot(p[4] ^ d)
+            row = sum(jnp.where(at == i, gains[i], 0.0) for i in range(4))
+            high, mid, low_term = terms(row)
+            fix += [high, mid, low_term, high, mid, high]
+        fix.append(jnp.zeros((128 - len(fix), tile), jnp.bfloat16))
+        fix = jnp.dot(
+            shifts[...], jnp.concatenate(fix, axis=0), preferred_element_type=jnp.float32
+        )
+        total[...] = value[:tokens] + fix
+        gains = gains[0] + gains[1] + gains[2] + gains[3]
+        for role, out in enumerate(outs):
+            image = jnp.where(low, role, 3 - role)
             at = pl.ds(pl.multiple_of(image * size, size), size)
             out[:size, :] = total[at, :].astype(jnp.bfloat16)
             here = stats[image]
-            here = jnp.concatenate([here] * (gains.shape[1] // size), axis=1)
+            here = jnp.concatenate([here] * (tile // size), axis=1)
             out[size:, :] = packed([here[0:1], here[1:2], gains])
 
     whole = pl.BlockSpec((rows, half), lambda t, p: (0, 0))
     message = pl.BlockSpec((size + EXTRA, tile), lambda t, p: (0, t))
+    piece = pl.BlockSpec((share, tile), lambda t, p: (0, t))
     return call(
         kernel,
         place,
         (out_cols // tile,),
         [whole] * 4
-        + [
-            pl.BlockSpec((4 * half, tile), lambda t, p: (0, t)),
-            pl.BlockSpec((4, tile), lambda t, p: (0, t)),
-        ],
+        + [pl.BlockSpec((half, tile), lambda t, p: (1 - p[0], t))]
+        + [piece] * 6
+        + [pl.BlockSpec(gain.shape, lambda t, p: (0, 0))],
         [message] * 4,
         [jax.ShapeDtypeStruct((size + EXTRA, out_cols), jnp.bfloat16)] * 4,
         [
-            pltpu.VMEM((tokens, 128), jnp.float32),
+            pltpu.VMEM((4, rows, half), jnp.bfloat16),
+            pltpu.VMEM((tokens, 128), jnp.bfloat16),
             pltpu.VMEM((4, 2, size), jnp.float32),
             pltpu.VMEM((tokens, tile), jnp.float32),
         ],
-        [*scaled, slices, gain_proj],
-        flops=8 * tokens * half * out_cols,
+        [*scaled, w_proj, *pieces, gain],
     )
 
 
@@ -314,19 +360,74 @@
     )
 
 
+def facing(place, context, got, block, *released):
+    array, shape, index = block
+    images, part, heads = got.shape
+
+    def kernel(p, kept, got, src, *refs):
+        near, away, dst = refs[-3:]
+        same = (p[0] == 1) == (p[5] == 0)
+        near[...] = jnp.where(same, kept[...], got[...])
+        away[...] = jnp.where(same, got[...], kept[...])
+        dst[...] = src[...]
+
+    whole = pl.BlockSpec(got.shape, lambda i, p: (0, 0, 0))
+    return call(
+        kernel,
+        place,
+        (1,),
+        [pl.BlockSpec(got.shape, lambda i, p: (p[5], 0, 0)), whole]
+        + [pl.BlockSpec(shape, index)]
+        + [ANY] * len(released),
+        [whole, whole, pl.BlockSpec(shape, lambda i, p: (0,) * len(shape))],
+        [jax.ShapeDtypeStruct(got.shape, got.dtype)] * 2
+        + [jax.ShapeDtypeStruct(shape, array.dtype)],
+        [],
+        [context, got, array, *released],
+    )
+
+
+def ordered(place, pieces, block, *released):
+    array, shape, index = block
+    images, part, heads = pieces[0].shape
+    span = part // CHUNKS
+    rows = images * 4 * span
+
+    def kernel(p, *refs):
+        ins, outs = refs[:4], refs[-CHUNKS - 1 : -1]
+        for k, out in enumerate(outs):
+            at = slice(k * span, (k + 1) * span)
+            for image in range(images):
+                for row in range(4):
+                    to = (image * 4 + row) * span
+                    out[to : to + span, :] = jnp.where(
+                        p[0] == 1, ins[row][image, at, :], ins[3 - row][image, at, :]
+                    )
+        refs[-1][...] = refs[4][...]
+
+    whole = pl.BlockSpec(pieces[0].shape, lambda i, p: (0, 0, 0))
+    return call(
+        kernel,
+        place,
+        (1,),
+        [whole] * 4 + [pl.BlockSpec(shape, index)] + [ANY] * len(released),
+        [pl.BlockSpec((rows, heads), lambda i, p: (0, 0))] * CHUNKS
+        + [pl.BlockSpec(shape, lambda i, p: (0,) * len(shape))],
+        [jax.ShapeDtypeStruct((rows, heads), pieces[0].dtype)] * CHUNKS
+        + [jax.ShapeDtypeStruct(shape, array.dtype)],
+        [],
+        [*pieces, array, *released],
+    )
+
+
 def centred(context, resid, w_out, b_out, ln_gain, w_proj):
     row, group = lax.axis_index("dp"), lax.axis_index("groups")
     x, core = lax.axis_index("mp"), lax.axis_index("sub")
-    col = 2 * x + core
-    low = row < 2
-    place = jnp.stack([low.astype(jnp.int32), group, core, row])
+    place = jnp.stack([(row < 2).astype(jnp.int32), group, core, row, 2 * x + core, x])
     images, part, heads = context.shape
     wide, out_cols = resid.shape[2], w_proj.shape[1]
     half = wide // 2
-    span = part // CHUNKS
-
-    def halves(came, swap):
-        return jnp.concatenate(either(group == 0, came, swap), axis=0)
+    bias, gain = b_out.reshape(1, -1), ln_gain.reshape(1, -1)
 
     def inner(p):
         return 1 - p[0]
@@ -334,94 +435,84 @@
     def outer(p):
         return p[0]
 
-    share, share2 = heads // 2, half // 2
-    sent_outer, sent_cross = cuts(
+    def out_block(side):
+        return (w_out, (heads // 2, half), lambda i, p: (p[1], side(p)))
+
+    def proj_block(side):
+        return (w_proj, (half // 2, out_cols), lambda i, p: (2 * side(p) + p[1], 0))
+
+    def old_block(side):
+        return (resid, (images, part, half), lambda i, p: (0, 0, side(p)))
+
+    sent, sent_outer, sent_cross = cuts(
         place,
         [
-            (w_out, (share, half), lambda i, p: (p[1], outer(p))),
-            (w_proj, (share2, out_cols), lambda i, p: (2 * outer(p) + p[1], 0)),
+            (context, (images // 2, part, heads), lambda i, p: (1 - p[5], 0, 0)),
+            out_block(outer),
+            proj_block(outer),
         ],
     )
-    kept, sent = either(x == 0, context[: images // 2], context[images // 2 :])
     got = along(sent, "mp", SWAP)
     fold_outer = along(sent_outer, "dp", FOLD)
     proj_cross = along(sent_cross, "dp", CROSS)
 
-    first, second = either(x == 0, kept, got)
-    near, away = either(low, first, second)
-    mine = [along(near, "dp", FOLD), near, along(away, "dp", CROSS), along(away, "dp", FAR)]
-    mine = jnp.where(low, jnp.stack(mine, 1), jnp.stack(mine[::-1], 1))
-
-    old = (images, part, half)
-    sent_inner, sent_old = cuts(
-        place,
-        [
-            (w_out, (share, half), lambda i, p: (p[1], inner(p))),
-            (resid, old, lambda i, p: (0, 0, outer(p))),
-        ],
-        got,
-    )
+    near, away, sent_old = facing(place, context, got, old_block(outer))
+    pieces = [along(near, "dp", FOLD), near, along(away, "dp", CROSS), along(away, "dp", FAR)]
     old_outer = along(sent_old, "dp", FOLD)
+
+    sent_inner, sent_swap = cuts(
+        place, [out_block(inner), (fold_outer, fold_outer.shape, None)], near
+    )
     fold_inner = along(sent_inner, "dp", FOLD)
-    swap_outer = along(fold_outer, "groups", SWAP)
-    swap_inner = along(fold_inner, "groups", SWAP)
-
-    sent_fold, sent_old = cuts(
-        place,
-        [
-            (w_proj, (share2, out_cols), lambda i, p: (2 * inner(p) + p[1], 0)),
-            (resid, old, lambda i, p: (0, 0, inner(p))),
-        ],
-        mine,
-    )
+    swap_outer = along(sent_swap, "groups", SWAP)
+
+    *own, sent_old = ordered(place, pieces, old_block(inner), sent_inner)
     old_inner = along(sent_old, "dp", FOLD)
+    far = [along(v, "mp", SWAP) for v in own]
+    near = [along(v, "sub", SWAP) for v in own]
+    tokens_of = [(a, b, c, along(b, "sub", SWAP)) for a, b, c in zip(own, far, near)]
+
+    def sends(k):
+        weights = (w_out, fold_outer, swap_outer, resid, old_outer, bias)
+        return attend(place, tokens_of[k], *weights, k, False, jnp.bfloat16)
+
+    def keeps(k, swapped):
+        weights = (w_out, fold_inner, swapped, resid, old_inner, bias)
+        return attend(place, tokens_of[k], *weights, k, True, jnp.float32)
+
+    came = [sends(0)]
+    sent_far, sent_swap = cuts(
+        place, [proj_block(outer), (fold_inner, fold_inner.shape, None)], came[0]
+    )
+    proj_far = along(sent_far, "dp", FAR)
+    swap_inner = along(sent_swap, "groups", SWAP)
+    came += [sends(k) for k in range(1, CHUNKS)]
+    came = [along(v, "dp", CROSS) for v in came]
+
+    kept = [keeps(k, swap_inner) for k in range(CHUNKS)]
+    sent_fold, sent_swap = cuts(
+        place, [proj_block(inner), (proj_cross, proj_cross.shape, None)], kept[0]
+    )
     proj_fold = along(sent_fold, "dp", FOLD)
-    (sent_far,) = cuts(
-        place,
-        [(w_proj, (share2, out_cols), lambda i, p: (2 * outer(p) + p[1], 0))],
-        fold_inner,
-    )
-    proj_far = along(sent_far, "dp", FAR)
-
-    sends, keeps = [], []
-    for k in range(CHUNKS):
-        own = mine[:, :, k * span : (k + 1) * span]
-        both = jnp.concatenate(either(x == 0, own, along(own, "mp", SWAP)), axis=0)
-        both = both.reshape(images * 4 * span, heads)
-        other = along(both, "sub", SWAP)
-        common = (place, both, other, w_out)
-        sends.append(
-            attend(*common, fold_outer, swap_outer, resid, old_outer, b_out, k, False, jnp.bfloat16)
-        )
-        keeps.append(
-            attend(*common, fold_inner, swap_inner, resid, old_inner, b_out, k, True, jnp.float32)
-        )
-
-    gains = ln_gain.reshape(4, 2, half)
-    gains = pick(gains.transpose(1, 0, 2), jnp.where(low, 0, 1))
-    gains = jnp.stack([pick(gains, col ^ d) for d in range(4)])
-    came = [along(v, "dp", CROSS) for v in sends]
+    swap_cross = along(sent_swap, "groups", SWAP)
+
     scaled = []
     for k in range(CHUNKS):
-        near = scale_up(place, keeps[k], came[k], gains[:1])
+        near = scale_up(place, kept[k], came[k], gain)
         far = along(near, "mp", SWAP)
         scaled.append([near, along(near, "sub", SWAP), far, along(far, "sub", SWAP)])
 
-    proj_own = lax.dynamic_slice_in_dim(w_proj, jnp.where(low, 0, half), half, 0)
-    slices = [
-        halves(proj_fold, along(proj_fold, "groups", SWAP)),
-        proj_own,
-        halves(proj_cross, along(proj_cross, "groups", SWAP)),
-        halves(proj_far, along(proj_far, "groups", SWAP)),
+    weights = [
+        proj_fold,
+        along(proj_fold, "groups", SWAP),
+        proj_cross,
+        swap_cross,
+        proj_far,
+        along(proj_far, "groups", SWAP),
     ]
-    slices = jnp.where(low, jnp.stack(slices), jnp.stack(slices[::-1]))
-    slices = jnp.stack([pick(slices, col ^ d) for d in range(4)])
-    gain_proj = jnp.sum(gains[:, :, None] * slices.astype(jnp.float32), axis=1)
-    slices = slices.reshape(4 * half, out_cols)
-
     parts = []
     for k in range(CHUNKS):
-        spread, own, cross, leap = project_up(place, scaled[k], slices, gain_proj)
+        spread, own, cross, leap = project_up(place, scaled[k], w_proj, weights, gain)
         leap = along(leap, "dp", LEAP)
         cross = along(cross, "dp", CROSS)
         spread = along(spread, "dp", SPREAD)

time: 221 us -> 220 us (level)
  starting transfers between devices: 53.2 us -> 83.3 us
  waiting for transfers between devices: 97.1 us -> 77.5 us
  other arithmetic: 16 us -> 0 us
  Pallas kernels: 46.1 us -> 52.4 us
    ppermute x34 -> x36, starting transfers between devices: 53.2 us -> 83.3 us  [along(): return lax.ppermute(value, axis, pairs)]
    ppermute x34 -> x36, waiting for transfers between devices: 97.1 us -> 77.5 us  [along(): return lax.ppermute(value, axis, pairs)]
    select_n x9 -> x0, other arithmetic: 9.12 us -> none  [the longest x7 7.42 us: either(): return (jnp.where(test, first, second), jnp.where(test, second, first))]
    pallas_call x13 -> x15, Pallas kernels: 46.1 us -> 52.4 us  [call(): pl.pallas_call(kernel, grid_spec=pltpu.PrefetchScalarGridSpec(num_scalar_...]
    reduce_sum x1 -> x0, other arithmetic: 3.79 us -> none  [centred(): gain_proj = jnp.sum(gains[:, :, None] * slices.astype(jnp.float32), axis=1)]
    unnamed x32 -> x30, local copies, waits for them, and re-layouts: 1.73 us -> 5.38 us
  transfers between devices with their start and end apart: 34 -> 36, of which waited for: 12 -> 11; matrix products, arithmetic and copies ran while one was open for 8% -> 0% of each run, Pallas kernels for 20% -> 22%
where the time goes in v4:
time: 220 us; the launch traced here: 219 us
  starting transfers between devices  83.3 us (38%)
  waiting for transfers between devices  77.5 us (35%)
  Pallas kernels  52.4 us (24%)
  local copies, waits for them, and re-layouts  5.47 us (2%)
    ppermute x36, starting transfers between devices, along(): return lax.ppermute(value, axis, pairs)  83.3 us
    ppermute x36, waiting for transfers between devices, along(): return lax.ppermute(value, axis, pairs)  77.5 us
    pallas_call x15, Pallas kernels, call(): pl.pallas_call(kernel, grid_spec=pltpu.PrefetchScalarGridSpec(num_scalar_...  52.4 us
    unnamed x30, local copies, waits for them, and re-layouts  5.38 us
  transfers between devices with their start and end apart: 36, of which 11 were waited for; matrix products, arithmetic and copies ran while one was open for 0% of the time, Pallas kernels for 22%

profile of v4, /device:TPU:0, one launch (start us, length us, event | category | flops | bytes accessed | tf_op | source)
XLA Modules:
  0.0 219.3 jit_solution(18396514427213537002)
XLA Ops:
  0.1 1.7 copy-done
  2.8 2.1 shard_map.64
  4.8 5.0 %collective-permute-start.4 = (bf16[384,768]{1,0:T(8,128)(2,1)S(1)}, bf16[384,768]{1,0:T(8,128)(2,1)S(1)}, u32[]{:S(2)}, u32[]{:S(2)}) collective-permute-start(bf16[384,768]{1,0:T(8,128)(2,1)S(1)} %get-tuple-element.31), channel_id=1, source_target_pairs={{0,4},{12,8},{1,5},{13,9},{2,6},{14,10},{3,7},{15,11},{16,20},{28,... | collective-permute-start | bytes 1769480 | tf_op jit(solution)/shard_map/ppermute | solution.py:65
  9.8 1.6 collective-permute-start
  11.4 4.9 %collective-permute-done.got = bf16[2,64,768]{2,1,0:T(8,128)(2,1)S(1)} collective-permute-done((bf16[2,64,768]{2,1,0:T(8,128)(2,1)S(1)}, bf16[2,64,768]{2,1,0:T(8,128)(2,1)S(1)}, u32[]{:S(2)}, u32[]{:S(2)}) %collective-permute-start) | collective-permute-done | bytes 196640 | tf_op jit(solution)/shard_map/ppermute | solution.py:65
  16.9 2.6 %collective-permute-start.3 = (bf16[2,64,768]{2,1,0:T(8,128)(2,1)S(1)}, bf16[2,64,768]{2,1,0:T(8,128)(2,1)S(1)}, u32[]{:S(2)}, u32[]{:S(2)}) collective-permute-start(bf16[2,64,768]{2,1,0:T(8,128)(2,1)S(1)} %get-tuple-element.30), channel_id=1, source_target_pairs={{0,8},{12,4},{1,9},{13,5},{2,10},{14,6},{3,11},{15,7},{16,24},{28,... | collective-permute-start | bytes 589832 | tf_op jit(solution)/shard_map/ppermute | solution.py:65
  20.1 3.1 %collective-permute-start.1 = (bf16[2,64,768]{2,1,0:T(8,128)(2,1)S(1)}, bf16[2,64,768]{2,1,0:T(8,128)(2,1)S(1)}, u32[]{:S(2)}, u32[]{:S(2)}) collective-permute-start(bf16[2,64,768]{2,1,0:T(8,128)(2,1)S(1)} %get-tuple-element.29.refs_2_.refs_1_), channel_id=1, source_target_pairs={{0,4},{12,8},{1,5},{13,9},{2,6},{14,10},{3,7},{15,11},{16,20},{28,... | collective-permute-start | bytes 589832 | tf_op jit(solution)/shard_map/ppermute | solution.py:65
  25.2 2.6 %collective-permute-done.3.refs_3_ = bf16[2,64,768]{2,1,0:T(8,128)(2,1)S(1)} collective-permute-done((bf16[2,64,768]{2,1,0:T(8,128)(2,1)S(1)}, bf16[2,64,768]{2,1,0:T(8,128)(2,1)S(1)}, u32[]{:S(2)}, u32[]{:S(2)}) %collective-permute-start.3) | collective-permute-done | bytes 196640 | tf_op jit(solution)/shard_map/ppermute | solution.py:65
  27.8 4.2 %collective-permute-done.1.refs_0_ = bf16[2,64,768]{2,1,0:T(8,128)(2,1)S(1)} collective-permute-done((bf16[2,64,768]{2,1,0:T(8,128)(2,1)S(1)}, bf16[2,64,768]{2,1,0:T(8,128)(2,1)S(1)}, u32[]{:S(2)}, u32[]{:S(2)}) %collective-permute-start.1) | collective-permute-done | bytes 196640 | tf_op jit(solution)/shard_map/ppermute | solution.py:65
  32.6 1.6 collective-permute-start.5
  35.7 4.4 %collective-permute-start.8 = (bf16[384,768]{1,0:T(8,128)(2,1)S(1)}, bf16[384,768]{1,0:T(8,128)(2,1)S(1)}, u32[]{:S(2)}, u32[]{:S(2)}) collective-permute-start(bf16[384,768]{1,0:T(8,128)(2,1)S(1)} %get-tuple-element.32.refs_5_), channel_id=1, source_target_pairs={{0,4},{12,8},{1,5},{13,9},{2,6},{14,10},{3,7},{15,11},{16,20},{28,... | collective-permute-start | bytes 1769480 | tf_op jit(solution)/shard_map/ppermute | solution.py:65
  42.0 9.4 %collective-permute-done.26.far = bf16[256,768]{1,0:T(8,128)(2,1)S(1)} collective-permute-done((bf16[256,768]{1,0:T(8,128)(2,1)S(1)}, bf16[256,768]{1,0:T(8,128)(2,1)S(1)}, u32[]{:S(2)}, u32[]{:S(2)}) %collective-permute-start.26) | collective-permute-done | bytes 393248 | tf_op jit(solution)/shard_map/ppermute | solution.py:65
  51.4 2.9 %collective-permute-start.12 = (bf16[4,64,768]{2,1,0:T(8,128)(2,1)S(1)}, bf16[4,64,768]{2,1,0:T(8,128)(2,1)S(1)}, u32[]{:S(2)}, u32[]{:S(2)}) collective-permute-start(bf16[4,64,768]{2,1,0:T(8,128)(2,1)S(1)} %get-tuple-element.37), channel_id=1, source_target_pairs={{0,4},{12,8},{1,5},{13,9},{2,6},{14,10},{3,7},{15,11},{16,20},{28,... | collective-permute-start | bytes 1179656 | tf_op jit(solution)/shard_map/ppermute | solution.py:65
  54.4 4.6 %shard_map.68.refs_2_ = bf16[512,768]{1,0:T(8,128)(2,1)S(1)} custom-call(s32[6]{0:T(128)S(1)} %stack.31.place_ref.p, bf16[256,768]{1,0:T(8,128)(2,1)S(1)} %get-tuple-element.33.own, bf16[256,768]{1,0:T(8,128)(2,1)S(1)} %collective-permute-done.5.far, bf16[256,768]{1,0:T(8,128)(2,1)S(1)} %collective-permute-done.6.near, ...), custom_call_target="tpu_custom_call" | custom-call | flops 1 | bytes 1 | tf_op jit(solution)/shard_map/pallas_call | solution.py:82
  63.5 4.3 %shard_map.75 = bf16[512,768]{1,0:T(8,128)(2,1)S(1)} custom-call(s32[6]{0:T(128)S(1)} %stack.31.place_ref.p, bf16[256,768]{1,0:T(8,128)(2,1)S(1)} %get-tuple-element.46.own, bf16[256,768]{1,0:T(8,128)(2,1)S(1)} %collective-permute-done.26.far, bf16[256,768]{1,0:T(8,128)(2,1)S(1)} %collective-permute-done.27.near, ...), custom_call_target="tpu_custom_call" | custom-call | flops 1 | bytes 1 | tf_op jit(solution)/shard_map/pallas_call | solution.py:82
  68.6 8.4 %collective-permute-start.21 = (bf16[384,1024]{1,0:T(8,128)(2,1)}, bf16[384,1024]{1,0:T(8,128)(2,1)S(1)}, u32[]{:S(2)}, u32[]{:S(2)}) collective-permute-start(bf16[384,1024]{1,0:T(8,128)(2,1)} %get-tuple-element.41), channel_id=1, source_target_pairs={{0,8},{12,4},{1,9},{13,5},{2,10},{14,6},{3,11},{15,7},{16,24},{28,... | collective-permute-start | bytes 2359304 | tf_op jit(solution)/shard_map/ppermute | solution.py:65
  77.5 4.4 %shard_map.70.keeps.refs_2_ = f32[512,768]{1,0:T(8,128)S(1)} custom-call(s32[6]{0:T(128)S(1)} %stack.31.place_ref.p, bf16[256,768]{1,0:T(8,128)(2,1)S(1)} %get-tuple-element.33.own, bf16[256,768]{1,0:T(8,128)(2,1)S(1)} %collective-permute-done.5.far, bf16[256,768]{1,0:T(8,128)(2,1)S(1)} %collective-permute-done.6.near, ...), custom_call_target="tpu_custom_call" | custom-call | flops 1 | bytes 1 | tf_op jit(solution)/shard_map/pallas_call | solution.py:82
  81.8 1.7 shard_map.71.s0
  83.6 1.6 collective-permute-start.15
  85.1 1.8 shard_map.72
  86.9 31.1 %collective-permute-start.18 = (bf16[384,1024]{1,0:T(8,128)(2,1)S(1)}, bf16[384,1024]{1,0:T(8,128)(2,1)S(1)}, u32[]{:S(2)}, u32[]{:S(2)}) collective-permute-start(bf16[384,1024]{1,0:T(8,128)(2,1)S(1)} %get-tuple-element.39), channel_id=1, source_target_pairs={{0,4},{12,8},{1,5},{13,9},{2,6},{14,10},{3,7},{15,11},{16,20},{28,... | collective-permute-start | bytes 2359304 | tf_op jit(solution)/shard_map/ppermute | solution.py:65
  118.1 1.6 collective-permute-start.20
  119.7 4.3 %shard_map.74.keeps = f32[512,768]{1,0:T(8,128)S(1)} custom-call(s32[6]{0:T(128)S(1)} %stack.31.place_ref.p, bf16[256,768]{1,0:T(8,128)(2,1)S(1)} %get-tuple-element.46.own, bf16[256,768]{1,0:T(8,128)(2,1)S(1)} %collective-permute-done.26.far, bf16[256,768]{1,0:T(8,128)(2,1)S(1)} %collective-permute-done.27.near, ...), custom_call_target="tpu_custom_call" | custom-call | flops 1 | bytes 1 | tf_op jit(solution)/shard_map/pallas_call | solution.py:82
  124.0 1.7 shard_map.76.s0
  127.8 6.5 %collective-permute-done.18.f0 = bf16[384,1024]{1,0:T(8,128)(2,1)S(1)} collective-permute-done((bf16[384,1024]{1,0:T(8,128)(2,1)S(1)}, bf16[384,1024]{1,0:T(8,128)(2,1)S(1)}, u32[]{:S(2)}, u32[]{:S(2)}) %collective-permute-start.18) | collective-permute-done | bytes 786464 | tf_op jit(solution)/shard_map/ppermute | solution.py:65
  134.8 3.8 %collective-permute-done.20.c1 = bf16[384,1024]{1,0:T(8,128)(2,1)S(1)} collective-permute-done((bf16[384,1024]{1,0:T(8,128)(2,1)S(1)}, bf16[384,1024]{1,0:T(8,128)(2,1)S(1)}, u32[]{:S(2)}, u32[]{:S(2)}) %collective-permute-start.20) | collective-permute-done | bytes 786464 | tf_op jit(solution)/shard_map/ppermute | solution.py:65
  140.1 15.3 %collective-permute-done.22.a1 = bf16[384,1024]{1,0:T(8,128)(2,1)S(1)} collective-permute-done((bf16[384,1024]{1,0:T(8,128)(2,1)S(1)}, bf16[384,1024]{1,0:T(8,128)(2,1)S(1)}, u32[]{:S(2)}, u32[]{:S(2)}) %collective-permute-start.22) | collective-permute-done | bytes 786464 | tf_op jit(solution)/shard_map/ppermute | solution.py:65
  156.0 14.4 %collective-permute-done.19.f1 = bf16[384,1024]{1,0:T(8,128)(2,1)S(1)} collective-permute-done((bf16[384,1024]{1,0:T(8,128)(2,1)S(1)}, bf16[384,1024]{1,0:T(8,128)(2,1)S(1)}, u32[]{:S(2)}, u32[]{:S(2)}) %collective-permute-start.19) | collective-permute-done | bytes 786464 | tf_op jit(solution)/shard_map/ppermute | solution.py:65
  171.3 11.2 %shard_map.73 = (bf16[144,1024]{1,0:T(8,128)(2,1)S(1)}, bf16[144,1024]{1,0:T(8,128)(2,1)S(1)}, bf16[144,1024]{1,0:T(8,128)(2,1)S(1)}, bf16[144,1024]{1,0:T(8,128)(2,1)S(1)}) custom-call(s32[6]{0:T(128)S(1)} %stack.31.place_ref.p, bf16[528,768]{1,0:T(8,128)(2,1)} %copy-done.4, bf16[528,768]{1,0:T(8,128)(2,1)} %copy-done.12, bf16[528,768]{1,0:T(8,128)(2,1)} %copy-done.8, ...), custom_call_target="tpu_custom_call" | custom-call | flops 1 | bytes 1 | tf_op jit(solution)/shard_map/pallas_call | solution.py:82
  187.8 11.2 %shard_map.77 = (bf16[144,1024]{1,0:T(8,128)(2,1)S(1)}, bf16[144,1024]{1,0:T(8,128)(2,1)S(1)}, bf16[144,1024]{1,0:T(8,128)(2,1)S(1)}, bf16[144,1024]{1,0:T(8,128)(2,1)S(1)}) custom-call(s32[6]{0:T(128)S(1)} %stack.31.place_ref.p, bf16[528,768]{1,0:T(8,128)(2,1)} %copy-done.5, bf16[528,768]{1,0:T(8,128)(2,1)} %copy-done.10, bf16[528,768]{1,0:T(8,128)(2,1)} %copy-done.9, ...), custom_call_target="tpu_custom_call" | custom-call | flops 1 | bytes 1 | tf_op jit(solution)/shard_map/pallas_call | solution.py:82
  202.3 15.2 %collective-permute-done.34.refs_6_ = bf16[144,1024]{1,0:T(8,128)(2,1)S(1)} collective-permute-done((bf16[144,1024]{1,0:T(8,128)(2,1)S(1)}, bf16[144,1024]{1,0:T(8,128)(2,1)S(1)}, u32[]{:S(2)}, u32[]{:S(2)}) %collective-permute-start.34) | collective-permute-done | bytes 294944 | tf_op jit(solution)/shard_map/ppermute | solution.py:65
  217.5 1.7 shard_map.78
  (87 shorter events, 28.1 us)
Async XLA Ops:
  4.8 19.7 %collective-permute-start.4 = (bf16[384,768]{1,0:T(8,128)(2,1)S(1)}, bf16[384,768]{1,0:T(8,128)(2,1)S(1)}, u32[]{:S(2)}, u32[]{:S(2)}) collective-permute-start(bf16[384,768]{1,0:T(8,128)(2,1)S(1)} %get-tuple-element.31), channel_id=1, source_target_pairs={{0,4},{12,8},{1,5},{13,9},{2,6},{14,10},{3,7},{15,11},{16,20},{28,... | collective-permute-start | bytes 1769480 | tf_op jit(solution)/shard_map/ppermute | solution.py:65
  16.9 10.9 %collective-permute-start.3 = (bf16[2,64,768]{2,1,0:T(8,128)(2,1)S(1)}, bf16[2,64,768]{2,1,0:T(8,128)(2,1)S(1)}, u32[]{:S(2)}, u32[]{:S(2)}) collective-permute-start(bf16[2,64,768]{2,1,0:T(8,128)(2,1)S(1)} %get-tuple-element.30), channel_id=1, source_target_pairs={{0,8},{12,4},{1,9},{13,5},{2,10},{14,6},{3,11},{15,7},{16,24},{28,... | collective-permute-start | bytes 589832 | tf_op jit(solution)/shard_map/ppermute | solution.py:65
  20.1 11.9 %collective-permute-start.1 = (bf16[2,64,768]{2,1,0:T(8,128)(2,1)S(1)}, bf16[2,64,768]{2,1,0:T(8,128)(2,1)S(1)}, u32[]{:S(2)}, u32[]{:S(2)}) collective-permute-start(bf16[2,64,768]{2,1,0:T(8,128)(2,1)S(1)} %get-tuple-element.29.refs_2_.refs_1_), channel_id=1, source_target_pairs={{0,4},{12,8},{1,5},{13,9},{2,6},{14,10},{3,7},{15,11},{16,20},{28,... | collective-permute-start | bytes 589832 | tf_op jit(solution)/shard_map/ppermute | solution.py:65
  23.2 16.9 %collective-permute-start.10 = (bf16[4,64,768]{2,1,0:T(8,128)(2,1)S(1)}, bf16[4,64,768]{2,1,0:T(8,128)(2,1)S(1)}, u32[]{:S(2)}, u32[]{:S(2)}) collective-permute-start(bf16[4,64,768]{2,1,0:T(8,128)(2,1)S(1)} %get-tuple-element.35), channel_id=1, source_target_pairs={{0,4},{12,8},{1,5},{13,9},{2,6},{14,10},{3,7},{15,11},{16,20},{28,... | collective-permute-start | bytes 1179656 | tf_op jit(solution)/shard_map/ppermute | solution.py:65
  32.6 8.9 %collective-permute-start.5 = (bf16[256,768]{1,0:T(8,128)(2,1)S(1)}, bf16[256,768]{1,0:T(8,128)(2,1)S(1)}, u32[]{:S(2)}, u32[]{:S(2)}) collective-permute-start(bf16[256,768]{1,0:T(8,128)(2,1)S(1)} %get-tuple-element.33.own), channel_id=1, source_target_pairs={{0,2},{2,0},{1,3},{3,1},{4,6},{6,4},{5,7},{7,5},{8,10},{10,8},{9,1... | collective-permute-start | bytes 1179656 | tf_op jit(solution)/shard_map/ppermute | solution.py:65
  34.2 17.3 %collective-permute-start.9 = (bf16[384,768]{1,0:T(8,128)(2,1)S(1)}, bf16[384,768]{1,0:T(8,128)(2,1)S(1)}, u32[]{:S(2)}, u32[]{:S(2)}) collective-permute-start(bf16[384,768]{1,0:T(8,128)(2,1)S(1)} %get-tuple-element.34), channel_id=1, source_target_pairs={{0,16},{16,0},{1,17},{17,1},{2,18},{18,2},{3,19},{19,3},{4,20},{20... | collective-permute-start | bytes 1769480 | tf_op jit(solution)/shard_map/ppermute | solution.py:65
  35.7 24.1 %collective-permute-start.8 = (bf16[384,768]{1,0:T(8,128)(2,1)S(1)}, bf16[384,768]{1,0:T(8,128)(2,1)S(1)}, u32[]{:S(2)}, u32[]{:S(2)}) collective-permute-start(bf16[384,768]{1,0:T(8,128)(2,1)S(1)} %get-tuple-element.32.refs_5_), channel_id=1, source_target_pairs={{0,4},{12,8},{1,5},{13,9},{2,6},{14,10},{3,7},{15,11},{16,20},{28,... | collective-permute-start | bytes 1769480 | tf_op jit(solution)/shard_map/ppermute | solution.py:65
  40.1 11.3 %collective-permute-start.26 = (bf16[256,768]{1,0:T(8,128)(2,1)S(1)}, bf16[256,768]{1,0:T(8,128)(2,1)S(1)}, u32[]{:S(2)}, u32[]{:S(2)}) collective-permute-start(bf16[256,768]{1,0:T(8,128)(2,1)S(1)} %get-tuple-element.46.own), channel_id=1, source_target_pairs={{0,2},{2,0},{1,3},{3,1},{4,6},{6,4},{5,7},{7,5},{8,10},{10,8},{9,1... | collective-permute-start | bytes 1179656 | tf_op jit(solution)/shard_map/ppermute | solution.py:65
  41.5 12.9 %collective-permute-start.7 = (bf16[256,768]{1,0:T(8,128)(2,1)S(1)}, bf16[256,768]{1,0:T(8,128)(2,1)S(1)}, u32[]{:S(2)}, u32[]{:S(2)}) collective-permute-start(bf16[256,768]{1,0:T(8,128)(2,1)S(1)} %collective-permute-done.5.far), channel_id=1, source_target_pairs={{0,1},{1,0},{2,3},{3,2},{4,5},{5,4},{6,7},{7,6},{8,9},{9,8},{10,11... | collective-permute-start | bytes 1179656 | tf_op jit(solution)/shard_map/ppermute | solution.py:65
  41.5 20.5 %collective-permute-start.27 = (bf16[256,768]{1,0:T(8,128)(2,1)S(1)}, bf16[256,768]{1,0:T(8,128)(2,1)S(1)}, u32[]{:S(2)}, u32[]{:S(2)}) collective-permute-start(bf16[256,768]{1,0:T(8,128)(2,1)S(1)} %get-tuple-element.46.own), channel_id=1, source_target_pairs={{0,1},{1,0},{2,3},{3,2},{4,5},{5,4},{6,7},{7,6},{8,9},{9,8},{10,11... | collective-permute-start | bytes 1179656 | tf_op jit(solution)/shard_map/ppermute | solution.py:65
  51.4 12.1 %collective-permute-start.28 = (bf16[256,768]{1,0:T(8,128)(2,1)S(1)}, bf16[256,768]{1,0:T(8,128)(2,1)S(1)}, u32[]{:S(2)}, u32[]{:S(2)}) collective-permute-start(bf16[256,768]{1,0:T(8,128)(2,1)S(1)} %collective-permute-done.26.far), channel_id=1, source_target_pairs={{0,1},{1,0},{2,3},{3,2},{4,5},{5,4},{6,7},{7,6},{8,9},{9,8},{10,11... | collective-permute-start | bytes 1179656 | tf_op jit(solution)/shard_map/ppermute | solution.py:65
  51.4 17.1 %collective-permute-start.12 = (bf16[4,64,768]{2,1,0:T(8,128)(2,1)S(1)}, bf16[4,64,768]{2,1,0:T(8,128)(2,1)S(1)}, u32[]{:S(2)}, u32[]{:S(2)}) collective-permute-start(bf16[4,64,768]{2,1,0:T(8,128)(2,1)S(1)} %get-tuple-element.37), channel_id=1, source_target_pairs={{0,4},{12,8},{1,5},{13,9},{2,6},{14,10},{3,7},{15,11},{16,20},{28,... | collective-permute-start | bytes 1179656 | tf_op jit(solution)/shard_map/ppermute | solution.py:65
  59.0 22.8 %collective-permute-start.13 = (bf16[512,768]{1,0:T(8,128)(2,1)S(1)}, bf16[512,768]{1,0:T(8,128)(2,1)S(1)}, u32[]{:S(2)}, u32[]{:S(2)}) collective-permute-start(bf16[512,768]{1,0:T(8,128)(2,1)S(1)} %shard_map.68.refs_2_), channel_id=1, source_target_pairs={{4,8},{8,4},{5,9},{9,5},{6,10},{10,6},{7,11},{11,7},{20,24},{24,20... | collective-permute-start | bytes 2359304 | tf_op jit(solution)/shard_map/ppermute | solution.py:65
  59.7 25.4 %collective-permute-start.17 = (bf16[384,1024]{1,0:T(8,128)(2,1)S(1)}, bf16[384,1024]{1,0:T(8,128)(2,1)S(1)}, u32[]{:S(2)}, u32[]{:S(2)}) collective-permute-start(bf16[384,1024]{1,0:T(8,128)(2,1)S(1)} %get-tuple-element.38), channel_id=1, source_target_pairs={{4,8},{8,4},{5,9},{9,5},{6,10},{10,6},{7,11},{11,7},{20,24},{24,20... | collective-permute-start | bytes 2359304 | tf_op jit(solution)/shard_map/ppermute | solution.py:65
  62.0 15.5 %collective-permute-start.11 = (bf16[384,768]{1,0:T(8,128)(2,1)S(1)}, bf16[384,768]{1,0:T(8,128)(2,1)S(1)}, u32[]{:S(2)}, u32[]{:S(2)}) collective-permute-start(bf16[384,768]{1,0:T(8,128)(2,1)S(1)} %get-tuple-element.36), channel_id=1, source_target_pairs={{0,16},{16,0},{1,17},{17,1},{2,18},{18,2},{3,19},{19,3},{4,20},{20... | collective-permute-start | bytes 1769480 | tf_op jit(solution)/shard_map/ppermute | solution.py:65
  67.8 56.2 %collective-permute-start.29 = (bf16[512,768]{1,0:T(8,128)(2,1)S(1)}, bf16[512,768]{1,0:T(8,128)(2,1)S(1)}, u32[]{:S(2)}, u32[]{:S(2)}) collective-permute-start(bf16[512,768]{1,0:T(8,128)(2,1)S(1)} %shard_map.75), channel_id=1, source_target_pairs={{4,8},{8,4},{5,9},{9,5},{6,10},{10,6},{7,11},{11,7},{20,24},{24,20... | collective-permute-start | bytes 2359304 | tf_op jit(solution)/shard_map/ppermute | solution.py:65
  68.6 58.7 %collective-permute-start.21 = (bf16[384,1024]{1,0:T(8,128)(2,1)}, bf16[384,1024]{1,0:T(8,128)(2,1)S(1)}, u32[]{:S(2)}, u32[]{:S(2)}) collective-permute-start(bf16[384,1024]{1,0:T(8,128)(2,1)} %get-tuple-element.41), channel_id=1, source_target_pairs={{0,8},{12,4},{1,9},{13,5},{2,10},{14,6},{3,11},{15,7},{16,24},{28,... | collective-permute-start | bytes 2359304 | tf_op jit(solution)/shard_map/ppermute | solution.py:65
  83.6 50.7 %collective-permute-start.15 = (bf16[528,768]{1,0:T(8,128)(2,1)S(1)}, bf16[528,768]{1,0:T(8,128)(2,1)S(1)}, u32[]{:S(2)}, u32[]{:S(2)}) collective-permute-start(bf16[528,768]{1,0:T(8,128)(2,1)S(1)} %shard_map.71.s0), channel_id=1, source_target_pairs={{0,2},{2,0},{1,3},{3,1},{4,6},{6,4},{5,7},{7,5},{8,10},{10,8},{9,1... | collective-permute-start | bytes 2433032 | tf_op jit(solution)/shard_map/ppermute | solution.py:65
  86.9 47.4 %collective-permute-start.18 = (bf16[384,1024]{1,0:T(8,128)(2,1)S(1)}, bf16[384,1024]{1,0:T(8,128)(2,1)S(1)}, u32[]{:S(2)}, u32[]{:S(2)}) collective-permute-start(bf16[384,1024]{1,0:T(8,128)(2,1)S(1)} %get-tuple-element.39), channel_id=1, source_target_pairs={{0,4},{12,8},{1,5},{13,9},{2,6},{14,10},{3,7},{15,11},{16,20},{28,... | collective-permute-start | bytes 2359304 | tf_op jit(solution)/shard_map/ppermute | solution.py:65
  118.1 20.5 %collective-permute-start.20 = (bf16[384,1024]{1,0:T(8,128)(2,1)S(1)}, bf16[384,1024]{1,0:T(8,128)(2,1)S(1)}, u32[]{:S(2)}, u32[]{:S(2)}) collective-permute-start(bf16[384,1024]{1,0:T(8,128)(2,1)S(1)} %get-tuple-element.40), channel_id=1, source_target_pairs={{0,16},{16,0},{1,17},{17,1},{2,18},{18,2},{3,19},{19,3},{4,20},{20... | collective-permute-start | bytes 2359304 | tf_op jit(solution)/shard_map/ppermute | solution.py:65
  125.7 29.7 %collective-permute-start.31 = (bf16[528,768]{1,0:T(8,128)(2,1)S(1)}, bf16[528,768]{1,0:T(8,128)(2,1)S(1)}, u32[]{:S(2)}, u32[]{:S(2)}) collective-permute-start(bf16[528,768]{1,0:T(8,128)(2,1)S(1)} %shard_map.76.s0), channel_id=1, source_target_pairs={{0,2},{2,0},{1,3},{3,1},{4,6},{6,4},{5,7},{7,5},{8,10},{10,8},{9,1... | collective-permute-start | bytes 2433032 | tf_op jit(solution)/shard_map/ppermute | solution.py:65
  127.3 28.2 %collective-permute-start.22 = (bf16[384,1024]{1,0:T(8,128)(2,1)S(1)}, bf16[384,1024]{1,0:T(8,128)(2,1)S(1)}, u32[]{:S(2)}, u32[]{:S(2)}) collective-permute-start(bf16[384,1024]{1,0:T(8,128)(2,1)S(1)} %collective-permute-done.21.a0), channel_id=1, source_target_pairs={{0,16},{16,0},{1,17},{17,1},{2,18},{18,2},{3,19},{19,3},{4,20},{20... | collective-permute-start | bytes 2359304 | tf_op jit(solution)/shard_map/ppermute | solution.py:65
  134.3 21.7 %collective-permute-start.14 = (bf16[528,768]{1,0:T(8,128)(2,1)S(1)}, bf16[528,768]{1,0:T(8,128)(2,1)S(1)}, u32[]{:S(2)}, u32[]{:S(2)}) collective-permute-start(bf16[528,768]{1,0:T(8,128)(2,1)S(1)} %shard_map.71.s0), channel_id=1, source_target_pairs={{0,1},{1,0},{2,3},{3,2},{4,5},{5,4},{6,7},{7,6},{8,9},{9,8},{10,11... | collective-permute-start | bytes 2433032 | tf_op jit(solution)/shard_map/ppermute | solution.py:65
  134.3 36.0 %collective-permute-start.16 = (bf16[528,768]{1,0:T(8,128)(2,1)S(1)}, bf16[528,768]{1,0:T(8,128)(2,1)S(1)}, u32[]{:S(2)}, u32[]{:S(2)}) collective-permute-start(bf16[528,768]{1,0:T(8,128)(2,1)S(1)} %collective-permute-done.15.s2), channel_id=1, source_target_pairs={{0,1},{1,0},{2,3},{3,2},{4,5},{5,4},{6,7},{7,6},{8,9},{9,8},{10,11... | collective-permute-start | bytes 2433032 | tf_op jit(solution)/shard_map/ppermute | solution.py:65
  138.6 31.7 %collective-permute-start.19 = (bf16[384,1024]{1,0:T(8,128)(2,1)S(1)}, bf16[384,1024]{1,0:T(8,128)(2,1)S(1)}, u32[]{:S(2)}, u32[]{:S(2)}) collective-permute-start(bf16[384,1024]{1,0:T(8,128)(2,1)S(1)} %collective-permute-done.18.f0), channel_id=1, source_target_pairs={{0,16},{16,0},{1,17},{17,1},{2,18},{18,2},{3,19},{19,3},{4,20},{20... | collective-permute-start | bytes 2359304 | tf_op jit(solution)/shard_map/ppermute | solution.py:65
  155.5 30.5 %collective-permute-start.30 = (bf16[528,768]{1,0:T(8,128)(2,1)S(1)}, bf16[528,768]{1,0:T(8,128)(2,1)S(1)}, u32[]{:S(2)}, u32[]{:S(2)}) collective-permute-start(bf16[528,768]{1,0:T(8,128)(2,1)S(1)} %shard_map.76.s0), channel_id=1, source_target_pairs={{0,1},{1,0},{2,3},{3,2},{4,5},{5,4},{6,7},{7,6},{8,9},{9,8},{10,11... | collective-permute-start | bytes 2433032 | tf_op jit(solution)/shard_map/ppermute | solution.py:65
  155.5 30.5 %collective-permute-start.32 = (bf16[528,768]{1,0:T(8,128)(2,1)S(1)}, bf16[528,768]{1,0:T(8,128)(2,1)S(1)}, u32[]{:S(2)}, u32[]{:S(2)}) collective-permute-start(bf16[528,768]{1,0:T(8,128)(2,1)S(1)} %collective-permute-done.31.s2), channel_id=1, source_target_pairs={{0,1},{1,0},{2,3},{3,2},{4,5},{5,4},{6,7},{7,6},{8,9},{9,8},{10,11... | collective-permute-start | bytes 2433032 | tf_op jit(solution)/shard_map/ppermute | solution.py:65
  182.5 18.5 %collective-permute-start.23 = (bf16[144,1024]{1,0:T(8,128)(2,1)S(1)}, bf16[144,1024]{1,0:T(8,128)(2,1)S(1)}, u32[]{:S(2)}, u32[]{:S(2)}) collective-permute-start(bf16[144,1024]{1,0:T(8,128)(2,1)S(1)} %get-tuple-element.43), channel_id=1, source_target_pairs={{4,8},{8,4},{5,9},{9,5},{6,10},{10,6},{7,11},{11,7},{20,24},{24,20... | collective-permute-start | bytes 884744 | tf_op jit(solution)/shard_map/ppermute | solution.py:65
  183.2 19.1 %collective-permute-start.24 = (bf16[144,1024]{1,0:T(8,128)(2,1)S(1)}, bf16[144,1024]{1,0:T(8,128)(2,1)S(1)}, u32[]{:S(2)}, u32[]{:S(2)}) collective-permute-start(bf16[144,1024]{1,0:T(8,128)(2,1)S(1)} %get-tuple-element.44), channel_id=1, source_target_pairs={{4,0},{8,12},{5,1},{9,13},{6,2},{10,14},{7,3},{11,15},{20,16},{24,... | collective-permute-start | bytes 884744 | tf_op jit(solution)/shard_map/ppermute | solution.py:65
  184.5 17.8 %collective-permute-start.25 = (bf16[144,1024]{1,0:T(8,128)(2,1)S(1)}, bf16[144,1024]{1,0:T(8,128)(2,1)S(1)}, u32[]{:S(2)}, u32[]{:S(2)}) collective-permute-start(bf16[144,1024]{1,0:T(8,128)(2,1)S(1)} %get-tuple-element.45), channel_id=1, source_target_pairs={{4,12},{8,0},{5,13},{9,1},{6,14},{10,2},{7,15},{11,3},{20,28},{24,... | collective-permute-start | bytes 884744 | tf_op jit(solution)/shard_map/ppermute | solution.py:65
  199.7 17.8 %collective-permute-start.34 = (bf16[144,1024]{1,0:T(8,128)(2,1)S(1)}, bf16[144,1024]{1,0:T(8,128)(2,1)S(1)}, u32[]{:S(2)}, u32[]{:S(2)}) collective-permute-start(bf16[144,1024]{1,0:T(8,128)(2,1)S(1)} %get-tuple-element.49), channel_id=1, source_target_pairs={{4,0},{8,12},{5,1},{9,13},{6,2},{10,14},{7,3},{11,15},{20,16},{24,... | collective-permute-start | bytes 884744 | tf_op jit(solution)/shard_map/ppermute | solution.py:65
  201.0 16.5 %collective-permute-start.35 = (bf16[144,1024]{1,0:T(8,128)(2,1)S(1)}, bf16[144,1024]{1,0:T(8,128)(2,1)S(1)}, u32[]{:S(2)}, u32[]{:S(2)}) collective-permute-start(bf16[144,1024]{1,0:T(8,128)(2,1)S(1)} %get-tuple-element.50), channel_id=1, source_target_pairs={{4,12},{8,0},{5,13},{9,1},{6,14},{10,2},{7,15},{11,3},{20,28},{24,... | collective-permute-start | bytes 884744 | tf_op jit(solution)/shard_map/ppermute | solution.py:65
  (19 other events, 300.0 us)

commit v5 on v0

--- a/solution.py
+++ b/solution.py
@@ -1,7 +1,13 @@
 import jax
 import jax.numpy as jnp
 from jax import lax
+from jax.experimental import pallas as pl
+from jax.experimental.pallas import tpu as pltpu
 from jax.sharding import PartitionSpec as P
+
+EPS = 1e-06
+CHUNKS = 2
+JOIN = 1
 
 
 def normalize(values, ln_gain):
@@ -17,7 +23,7 @@
     gain_share = lax.dynamic_slice_in_dim(
         ln_gain, lax.axis_index(("mp", "sub")) * shard_cols, shard_cols
     )
-    shard_norm = ((floats - center) * lax.rsqrt(spread + 1e-06) * gain_share).astype(jnp.bfloat16)
+    shard_norm = ((floats - center) * lax.rsqrt(spread + EPS) * gain_share).astype(jnp.bfloat16)
     normed = lax.all_gather(shard_norm, ("mp", "sub"), axis=2, tiled=True)
     return normed.reshape(-1, normed.shape[2])
 
@@ -29,7 +35,7 @@
     return summed_proj.astype(jnp.bfloat16)
 
 
-def local(context, resid, w_out, b_out, ln_gain, w_proj):
+def gathered(context, resid, w_out, b_out, ln_gain, w_proj):
     images, part_rows, head_cols = context.shape
     width_cols = resid.shape[2]
     tok_rows = context.reshape(images * part_rows, head_cols)
@@ -45,8 +51,475 @@
     summed = summed.reshape(images, part_rows, width_cols)
     moved = lax.all_to_all(summed, "dp", split_axis=0, concat_axis=1, tiled=True)
     normed = normalize(moved, ln_gain)
-    result = project(normed, w_proj).reshape(moved.shape[0], moved.shape[1], w_proj.shape[1])
-    return result
+    return project(normed, w_proj).reshape(moved.shape[0], moved.shape[1], w_proj.shape[1])
+
+
+SWAP = [(0, 1), (1, 0)]
+FOLD = [(0, 1), (3, 2)]
+CROSS = [(1, 2), (2, 1)]
+FAR = [(0, 2), (3, 1)]
+SPREAD = [(1, 0), (2, 3)]
+LEAP = [(1, 3), (2, 0)]
+
+
+def along(value, axis, pairs):
+    return lax.ppermute(value, axis, pairs)
+
+
+def pick(stack, index):
+    return lax.dynamic_index_in_dim(stack, index, 0, keepdims=False)
+
+
+def either(test, first, second):
+    return jnp.where(test, first, second), jnp.where(test, second, first)
+
+
+LIMIT = 32 * 1024 * 1024
+ANY = pl.BlockSpec(memory_space=pl.ANY)
+VMEM = pl.BlockSpec(memory_space=pltpu.VMEM)
+SMEM = pl.BlockSpec(memory_space=pltpu.SMEM)
+EXTRA = 16
+TILE = 256
+
+
+def call(kernel, place, ins, shapes, scratch, args, cost=1):
+    return pl.pallas_call(
+        kernel,
+        in_specs=[SMEM, *ins],
+        out_specs=jax.tree.map(lambda _: VMEM, shapes),
+        scratch_shapes=scratch,
+        out_shape=shapes,
+        compiler_params=pltpu.CompilerParams(vmem_limit_bytes=LIMIT),
+        cost_estimate=pl.CostEstimate(flops=cost, bytes_accessed=1, transcendentals=0),
+    )(place, *args)
+
+
+def shaped(shape, dtype=jnp.bfloat16):
+    return jax.ShapeDtypeStruct(shape, dtype)
+
+
+def moved(pairs, sems):
+    copies = [pltpu.make_async_copy(src, dst, sems.at[i]) for i, (src, dst) in enumerate(pairs)]
+    for copy in copies:
+        copy.start()
+    for copy in copies:
+        copy.wait()
+
+
+def cuts(place, blocks, *released, cost=1):
+    def kernel(p, *refs):
+        dsts = refs[-1 - len(blocks) : -1]
+        pairs = [
+            (src.at[at(p, block)] if at else src, dst)
+            for src, dst, (_, block, at) in zip(refs, dsts, blocks)
+        ]
+        moved(pairs, refs[-1])
+
+    return call(
+        kernel,
+        place,
+        [ANY] * (len(blocks) + len(released)),
+        [shaped(block, array.dtype) for array, block, _ in blocks],
+        [pltpu.SemaphoreType.DMA((len(blocks),))],
+        [array for array, _, _ in blocks] + list(released),
+        cost,
+    )
+
+
+def run(index, size):
+    return pl.ds(pl.multiple_of(index * size, size), size)
+
+
+def terms(value):
+    high = value.astype(jnp.bfloat16)
+    rest = value - high.astype(jnp.float32)
+    mid = rest.astype(jnp.bfloat16)
+    return [high, mid, (rest - mid.astype(jnp.float32)).astype(jnp.bfloat16)]
+
+
+def added(rows, first):
+    high, mid, low = (rows[first + i : first + i + 1].astype(jnp.float32) for i in range(3))
+    return high + (mid + low)
+
+
+def packed(rows):
+    parts = [term for row in rows for term in terms(row)]
+    parts.append(jnp.zeros((EXTRA - len(parts), rows[0].shape[1]), jnp.bfloat16))
+    return jnp.concatenate(parts, axis=0)
+
+
+def upright(rows):
+    rows = jnp.concatenate(rows, axis=0)
+    fill = jnp.zeros((128 - rows.shape[0], rows.shape[1]), jnp.float32)
+    return jnp.concatenate([rows, fill], axis=0).T
+
+
+def attend(place, tokens_of, w_out, fold, swapped, resid, came, bias, part, inner, dtype):
+    rows, heads = tokens_of[0].shape
+    tokens = 2 * rows
+    half, share = fold.shape[1], fold.shape[0]
+    images, span = resid.shape[0], tokens // resid.shape[0] // 4
+    tile = TILE if half % TILE == 0 else half
+
+    def kernel(p, own, far, near, both, weight, fold, swapped, old, came, bias, out, left, total):
+        low = p[0] == 1
+        turn = low == (p[2] == 0)
+        side = jnp.where(low == inner, 0, half)
+        for at, one, two in ((p[5], own, near), (1 - p[5], far, both)):
+            at = run(at, rows)
+            left[at, :heads] = jnp.where(turn, two[...], one[...])
+            folded = jnp.where(turn, one[...], two[...])
+            first, second = folded[:, :share], folded[:, share:]
+            left[at, heads : heads + share] = jnp.where(p[1] == 0, first, second)
+            left[at, heads + share :] = jnp.where(p[1] == 0, second, first)
+        own_at, came_at = jnp.where(low, span, 2 * span), jnp.where(low, 0, 3 * span)
+        patches = slice(part * span, (part + 1) * span)
+        for t in range(half // tile):
+            here = slice(t * tile, (t + 1) * tile)
+            there = pl.ds(pl.multiple_of(side + t * tile, tile), tile)
+            value = jnp.dot(left[:, :heads], weight[:, there], preferred_element_type=jnp.float32)
+            for i, piece in enumerate((fold, swapped)):
+                at = slice(heads + i * share, heads + (i + 1) * share)
+                value = value + jnp.dot(
+                    left[:, at], piece[:, here], preferred_element_type=jnp.float32
+                )
+            total[...] = value + jnp.where(low, bias[:, there], 0.0)
+            for image in range(images):
+                for at, source, columns in ((own_at, old, there), (came_at, came, here)):
+                    at = pl.ds(pl.multiple_of(image * 4 * span + at, span), span)
+                    total[at, :] = total[at, :] + source[image, patches, columns].astype(
+                        jnp.float32
+                    )
+            out[:, here] = total[...].astype(dtype)
+
+    return call(
+        kernel,
+        place,
+        [VMEM] * 10,
+        shaped((tokens, half), dtype),
+        [pltpu.VMEM((tokens, 2 * heads), jnp.bfloat16), pltpu.VMEM((tokens, tile), jnp.float32)],
+        [*tokens_of, w_out, fold, swapped, resid, came, bias],
+    )
+
+
+def scale_up(place, keeps, came, gain, *released):
+    tokens, half = keeps.shape
+
+    def kernel(p, keeps, came, gain, *refs):
+        out = refs[-1]
+        scale = gain[:, run(2 * p[4] + 1 - p[0], half)]
+        lane = lax.broadcasted_iota(jnp.int32, (128, 128), 1)
+
+        def step(i):
+            at = run(i, 128)
+            summed = (keeps[at, :] + came[at, :].astype(jnp.float32)).astype(jnp.bfloat16)
+            summed = summed.astype(jnp.float32)
+            mean = jnp.sum(summed, axis=1, keepdims=True) / half
+            off = summed - mean
+            square = jnp.sum(off * off, axis=1, keepdims=True)
+            out[at, :] = (off * scale).astype(jnp.bfloat16)
+            stats = jnp.where(lane == 0, mean, jnp.where(lane == 1, square, 0.0)).T
+            out[tokens:, at] = packed([stats[0:1], stats[1:2]])
+
+        pl.loop(0, tokens // 128)(step)
+
+    return call(
+        kernel,
+        place,
+        [VMEM] * 3 + [ANY] * len(released),
+        shaped((tokens + EXTRA, half)),
+        [],
+        [keeps, came, gain, *released],
+    )
+
+
+def project_up(place, scaled, w_proj, pieces, gain):
+    rows, half = scaled[0].shape
+    tokens, out_cols = rows - EXTRA, w_proj.shape[1]
+    size, share = tokens // 4, half // 2
+    tile = TILE if out_cols % TILE == 0 else out_cols
+
+    def kernel(p, s0, s1, s2, s3, own, f0, f1, c0, c1, a0, a1, gain, *rest):
+        outs, (left, stats, total) = rest[:4], rest[4:]
+        low = p[0] == 1
+
+        def slot(feature):
+            return jnp.where(low, feature, 3 - feature)
+
+        def put(value, at, rows):
+            swap = (p[1] == 1) & (at != 1)
+            first, second = value[:, :share], value[:, share:]
+            left[at, rows, :share] = jnp.where(swap, second, first)
+            left[at, rows, share:] = jnp.where(swap, first, second)
+
+        last = [s[tokens:, :tokens] for s in (s0, s1, s2, s3)]
+        means = [added(v, 0) for v in last]
+        middle = 0.25 * (means[0] + means[1] + means[2] + means[3])
+        shift = [v - middle for v in means]
+        square = sum(added(v, 3) + half * (d * d) for v, d in zip(last, shift))
+        for image in range(4):
+            at = slice(image * size, (image + 1) * size)
+            stats[image] = jnp.concatenate([middle[:, at], square[:, at]], axis=0)
+        for d, s in enumerate((s0, s1, s2, s3)):
+            feature = p[4] ^ d
+            put(s[:tokens, :], slot(feature), slice(0, tokens))
+            put(
+                packed([gain[:, run(2 * feature + 1 - p[0], half)]]),
+                slot(feature),
+                slice(tokens, rows),
+            )
+        pairs = []
+        for d in range(4):
+            high, mid, low_term = (v.astype(jnp.float32) for v in terms(shift[d]))
+            pairs += [high, high, high, mid, mid, low_term]
+        shifts = upright(pairs).astype(jnp.bfloat16)
+
+        for t in range(out_cols // tile):
+            here = slice(t * tile, (t + 1) * tile)
+            value = jnp.zeros((tokens, tile), jnp.float32)
+            gains = []
+            for at, halves in enumerate(((f0, f1), (own,), (c0, c1), (a0, a1))):
+                piece = jnp.zeros((rows, tile), jnp.float32)
+                if at == 1:
+                    weights = [own[run(1 - p[0], half), here]]
+                else:
+                    weights = [weight[:, here] for weight in halves]
+                for i, weight in enumerate(weights):
+                    depth = weight.shape[0]
+                    piece = piece + jnp.dot(
+                        left[at, :, i * depth : (i + 1) * depth],
+                        weight,
+                        preferred_element_type=jnp.float32,
+                    )
+                value = value + piece[:tokens]
+                gains.append(jnp.sum(piece[tokens : tokens + 3], axis=0, keepdims=True))
+            fix = []
+            for d in range(4):
+                at = slot(p[4] ^ d)
+                row = sum(jnp.where(at == i, gains[i], 0.0) for i in range(4))
+                high, mid, low_term = terms(row)
+                fix += [high, mid, low_term, high, mid, high]
+            fix.append(jnp.zeros((128 - len(fix), tile), jnp.bfloat16))
+            fix = jnp.concatenate(fix, axis=0)
+            total[...] = value + jnp.dot(shifts, fix, preferred_element_type=jnp.float32)
+            gains = gains[0] + gains[1] + gains[2] + gains[3]
+            for role, out in enumerate(outs):
+                image = jnp.where(low, role, 3 - role)
+                out[:size, here] = total[run(image, size), :].astype(jnp.bfloat16)
+                rest = stats[image]
+                rest = jnp.concatenate([rest] * (tile // size), axis=1)
+                out[size:, here] = packed([rest[0:1], rest[1:2], gains])
+
+    return call(
+        kernel,
+        place,
+        [VMEM] * 12,
+        [shaped((size + EXTRA, out_cols))] * 4,
+        [
+            pltpu.VMEM((4, rows, half), jnp.bfloat16),
+            pltpu.VMEM((4, 2, size), jnp.float32),
+            pltpu.VMEM((tokens, tile), jnp.float32),
+        ],
+        [*scaled, w_proj, *pieces, gain],
+    )
+
+
+def finish(place, parts, count):
+    rows, out_cols = parts[0][0].shape
+    size = rows - EXTRA
+    span = size // 4
+
+    def kernel(p, *refs):
+        out = refs[-1]
+        middle = (p[3] == 1) | (p[3] == 2)
+        for k in range(len(parts)):
+            own, cross, spread, leap = refs[4 * k : 4 * k + 4]
+            one = jnp.where(middle, own[...], spread[...])
+            two = jnp.where(middle, cross[...], leap[...])
+            ends = [one[size:], two[size:]]
+            means = [added(v, 0)[:, :size] for v in ends]
+            squares = [added(v, 3)[:, :size] for v in ends]
+            gap = 0.5 * (means[0] - means[1])
+            spread_of = (squares[0] + squares[1]) / count + gap * gap
+            turned = upright([gap, lax.rsqrt(spread_of + EPS)])
+            value = one[:size].astype(jnp.float32) + two[:size].astype(jnp.float32)
+            value = value + turned[:, 0:1] * (added(ends[0], 6) - added(ends[1], 6))
+            value = (value * turned[:, 1:2]).astype(jnp.bfloat16)
+            for row in range(4):
+                at = (row * len(parts) + k) * span
+                out[at : at + span, :] = value[row * span : (row + 1) * span]
+
+    args = [v for part in parts for v in part]
+    return call(
+        kernel, place, [VMEM] * len(args), shaped((size * len(parts), out_cols)), [], args
+    )
+
+
+def facing(place, context, got, *released):
+    half_images = got.shape[0]
+
+    def kernel(p, kept, got, *refs):
+        near, away, sems = refs[-3:]
+        kept = kept.at[run(p[5], half_images)]
+        same = (p[0] == 1) == (p[5] == 0)
+
+        @pl.when(same)
+        def _():
+            moved([(kept, near), (got, away)], sems)
+
+        @pl.when(jnp.logical_not(same))
+        def _():
+            moved([(kept, away), (got, near)], sems)
+
+    return call(
+        kernel,
+        place,
+        [ANY] * (2 + len(released)),
+        [shaped(got.shape)] * 2,
+        [pltpu.SemaphoreType.DMA((2,))],
+        [context, got, *released],
+    )
+
+
+def ordered(place, pieces, *released):
+    images, part, heads = pieces[0].shape
+    span = part // CHUNKS
+
+    def kernel(p, *refs):
+        ins, outs, sems = refs[:4], refs[-CHUNKS - 1 : -1], refs[-1]
+
+        def go(ins):
+            moved(
+                [
+                    (ins[row].at[:, k * span : (k + 1) * span], out.at[:, row])
+                    for k, out in enumerate(outs)
+                    for row in range(4)
+                ],
+                sems,
+            )
+
+        pl.when(p[0] == 1)(lambda: go(ins))
+        pl.when(p[0] == 0)(lambda: go(ins[::-1]))
+
+    outs = call(
+        kernel,
+        place,
+        [ANY] * (4 + len(released)),
+        [shaped((images, 4, span, heads))] * CHUNKS,
+        [pltpu.SemaphoreType.DMA((4 * CHUNKS,))],
+        [*pieces, *released],
+    )
+    return [v.reshape(images * 4 * span, heads) for v in outs]
+
+
+def centred(context, resid, w_out, b_out, ln_gain, w_proj):
+    row, group = lax.axis_index("dp"), lax.axis_index("groups")
+    x, core = lax.axis_index("mp"), lax.axis_index("sub")
+    place = jnp.stack([(row < 2).astype(jnp.int32), group, core, row, 2 * x + core, x])
+    images, part, heads = context.shape
+    wide, out_cols = resid.shape[2], w_proj.shape[1]
+    half = wide // 2
+    bias, gain = b_out.reshape(1, -1), ln_gain.reshape(1, -1)
+
+    def inner(p):
+        return 1 - p[0]
+
+    def outer(p):
+        return p[0]
+
+    def out_block(side):
+        shape = (heads // 2, half)
+        return w_out, shape, lambda p, b: (run(p[1], b[0]), run(side(p), b[1]))
+
+    def proj_block(side):
+        shape = (half // 2, out_cols)
+        return w_proj, shape, lambda p, b: (run(2 * side(p) + p[1], b[0]),)
+
+    def old_block(side):
+        shape = (images, part, half)
+        return resid, shape, lambda p, b: (slice(None), slice(None), run(side(p), b[2]))
+
+    def whole(array):
+        return array, array.shape, None
+
+    (sent,) = cuts(
+        place,
+        [(context, (images // 2, part, heads), lambda p, b: (run(1 - p[5], b[0]),))],
+    )
+    got = along(sent, "mp", SWAP)
+    sent_outer, sent_cross = cuts(place, [out_block(outer), proj_block(outer)])
+    fold_outer = along(sent_outer, "dp", FOLD)
+    proj_cross = along(sent_cross, "dp", CROSS)
+
+    near, away = facing(place, context, got, sent_outer)
+    pieces = [along(near, "dp", FOLD), near, along(away, "dp", CROSS), along(away, "dp", FAR)]
+    (sent_old,) = cuts(place, [old_block(outer)], near)
+    old_outer = along(sent_old, "dp", FOLD)
+
+    sent_inner, sent_old, sent_swap = cuts(
+        place, [out_block(inner), old_block(inner), whole(fold_outer)], near
+    )
+    fold_inner = along(sent_inner, "dp", FOLD)
+    old_inner = along(sent_old, "dp", FOLD)
+    swap_outer = along(sent_swap, "groups", SWAP)
+
+    own = ordered(place, pieces, sent_inner, proj_cross)
+    far = [along(v, "mp", SWAP) for v in own]
+    near = [along(v, "sub", SWAP) for v in own]
+    tokens_of = [(a, b, c, along(b, "sub", SWAP)) for a, b, c in zip(own, far, near)]
+
+    (join,) = cuts(place, [whole(swap_outer)], cost=JOIN)
+
+    def sends(k):
+        weights = (w_out, fold_outer, join, resid, old_outer, bias)
+        return attend(place, tokens_of[k], *weights, k, False, jnp.bfloat16)
+
+    def keeps(k, swapped):
+        weights = (w_out, fold_inner, swapped, resid, old_inner, bias)
+        return attend(place, tokens_of[k], *weights, k, True, jnp.float32)
+
+    (sent_swap,) = cuts(place, [whole(proj_cross)], join)
+    swap_cross = along(sent_swap, "groups", SWAP)
+    came = [sends(0)]
+    sent_far, sent_swap = cuts(place, [proj_block(outer), whole(fold_inner)], came[0])
+    proj_far = along(sent_far, "dp", FAR)
+    swap_inner = along(sent_swap, "groups", SWAP)
+    came += [sends(k) for k in range(1, CHUNKS)]
+    came = [along(v, "dp", CROSS) for v in came]
+
+    (sent_fold,) = cuts(place, [proj_block(inner)], swap_inner)
+    proj_fold = along(sent_fold, "dp", FOLD)
+    kept = [keeps(k, swap_inner) for k in range(CHUNKS)]
+
+    scaled = []
+    for k in range(CHUNKS):
+        near = scale_up(place, kept[k], came[k], gain, sent_fold)
+        far = along(near, "mp", SWAP)
+        scaled.append([near, along(near, "sub", SWAP), far, along(far, "sub", SWAP)])
+
+    weights = [
+        proj_fold,
+        along(proj_fold, "groups", SWAP),
+        proj_cross,
+        swap_cross,
+        proj_far,
+        along(proj_far, "groups", SWAP),
+    ]
+    parts = []
+    for k in range(CHUNKS):
+        spread, own, cross, leap = project_up(place, scaled[k], w_proj, weights, gain)
+        leap = along(leap, "dp", LEAP)
+        cross = along(cross, "dp", CROSS)
+        spread = along(spread, "dp", SPREAD)
+        parts.append([own, cross, spread, leap])
+    return finish(place, parts, 8 * half).reshape(1, 4 * part, out_cols)
+
+
+def local(context, resid, w_out, b_out, ln_gain, w_proj):
+    grid = [lax.axis_size(name) for name in ("groups", "dp", "mp", "sub")]
+    fits = grid == [2, 4, 2, 2] and context.shape[0] == 4 and context.shape[1] % CHUNKS == 0
+    plan = centred if fits else gathered
+    return plan(context, resid, w_out, b_out, ln_gain, w_proj)
 
 
 def solution(mesh):

time: 479 us -> 196 us (0.41)
  waiting for transfers between devices: 436 us -> 93.2 us
  starting transfers between devices: 3.69 us -> 60.5 us
  Pallas kernels: 0 us -> 37.2 us
  matrix products: 17.4 us -> 0 us
  between operations: 13.2 us -> 0.47 us
  blocking collectives: 6.94 us -> 0 us
    all_gather x4 -> x0, waiting for transfers between devices: 388 us -> none  [the longest x1 169 us: project(): lax.all_gather(w_proj, 'dp', axis=0, tiled=True)]
    ppermute x0 -> x36, waiting for transfers between devices: none -> 93.2 us  [along(): return lax.ppermute(value, axis, pairs)]
    ppermute x0 -> x36, starting transfers between devices: none -> 60.5 us  [along(): return lax.ppermute(value, axis, pairs)]
    all_to_all x1 -> x0, waiting for transfers between devices: 45.1 us -> none  [local(): lax.all_to_all(summed, 'dp', split_axis=0, concat_axis=1, tiled=True)]
    pallas_call x0 -> x19, Pallas kernels: none -> 37.2 us  [call(): pl.pallas_call(kernel, in_specs=[SMEM, *ins], out_specs=jax.tree.map(lamb...]
    dot_general x2 -> x0, matrix products: 17.4 us -> none  [the longest x1 9.73 us: project(): jnp.dot(normed, lax.all_gather(w_proj, 'dp', axis=0, tiled=True), preferr...]
    psum x1 -> x0, blocking collectives: 6.94 us -> none  [normalize(): lax.psum((jnp.sum(floats, axis=-1, keepdims=True), jnp.sum(floats * float...]
  transfers between devices with their start and end apart: 5 -> 36, of which waited for: 5 -> 11; matrix products, arithmetic and copies ran while one was open for 2% -> 0% of each run, Pallas kernels for 0% -> 18%
where the time goes in v5:
time: 196 us; the launch traced here: 195 us
  waiting for transfers between devices  93.2 us (48%)
  starting transfers between devices  60.5 us (31%)
  Pallas kernels  37.2 us (19%)
  local copies, waits for them, and re-layouts  3.68 us (2%)
    ppermute x36, waiting for transfers between devices, along(): return lax.ppermute(value, axis, pairs)  93.2 us
    ppermute x36, starting transfers between devices, along(): return lax.ppermute(value, axis, pairs)  60.5 us
    pallas_call x19, Pallas kernels, call(): pl.pallas_call(kernel, in_specs=[SMEM, *ins], out_specs=jax.tree.map(lamb...  37.2 us
  transfers between devices with their start and end apart: 36, of which 11 were waited for; matrix products, arithmetic and copies ran while one was open for 0% of the time, Pallas kernels for 18%

profile of v5, /device:TPU:0, one launch (start us, length us, event | category | flops | bytes accessed | tf_op | source)
XLA Modules:
  0.0 195.0 jit_solution(522855131608357369)
XLA Ops:
  0.1 1.7 copy-done
  1.8 1.9 copy-done.2
  5.2 7.7 %collective-permute-start.4 = (bf16[384,768]{1,0:T(8,128)(2,1)S(1)}, bf16[384,768]{1,0:T(8,128)(2,1)S(1)}, u32[]{:S(2)}, u32[]{:S(2)}) collective-permute-start(bf16[384,768]{1,0:T(8,128)(2,1)S(1)} %get-tuple-element.24.refs_0_), channel_id=1, source_target_pairs={{0,4},{12,8},{1,5},{13,9},{2,6},{14,10},{3,7},{15,11},{16,20},{28,... | collective-permute-start | bytes 1769480 | tf_op jit(solution)/shard_map/ppermute | solution.py:66
  13.8 1.6 collective-permute-start
  15.3 4.6 %collective-permute-done.got = bf16[2,64,768]{2,1,0:T(8,128)(2,1)S(1)} collective-permute-done((bf16[2,64,768]{2,1,0:T(8,128)(2,1)S(1)}, bf16[2,64,768]{2,1,0:T(8,128)(2,1)S(1)}, u32[]{:S(2)}, u32[]{:S(2)}) %collective-permute-start) | collective-permute-done | bytes 196640 | tf_op jit(solution)/shard_map/ppermute | solution.py:66
  23.1 3.1 %collective-permute-start.1 = (bf16[2,64,768]{2,1,0:T(8,128)(2,1)S(1)}, bf16[2,64,768]{2,1,0:T(8,128)(2,1)S(1)}, u32[]{:S(2)}, u32[]{:S(2)}) collective-permute-start(bf16[2,64,768]{2,1,0:T(8,128)(2,1)S(1)} %get-tuple-element.25.refs_3_.refs_1_), channel_id=1, source_target_pairs={{0,4},{12,8},{1,5},{13,9},{2,6},{14,10},{3,7},{15,11},{16,20},{28,... | collective-permute-start | bytes 589832 | tf_op jit(solution)/shard_map/ppermute | solution.py:66
  26.8 4.2 %collective-permute-start.11 = (bf16[4,64,768]{2,1,0:T(8,128)(2,1)S(1)}, bf16[4,64,768]{2,1,0:T(8,128)(2,1)S(1)}, u32[]{:S(2)}, u32[]{:S(2)}) collective-permute-start(bf16[4,64,768]{2,1,0:T(8,128)(2,1)S(1)} %shard_map.70), channel_id=1, source_target_pairs={{0,4},{12,8},{1,5},{13,9},{2,6},{14,10},{3,7},{15,11},{16,20},{28,... | collective-permute-start | bytes 1179656 | tf_op jit(solution)/shard_map/ppermute | solution.py:66
  31.9 3.3 %collective-permute-done.1.refs_0_ = bf16[2,64,768]{2,1,0:T(8,128)(2,1)S(1)} collective-permute-done((bf16[2,64,768]{2,1,0:T(8,128)(2,1)S(1)}, bf16[2,64,768]{2,1,0:T(8,128)(2,1)S(1)}, u32[]{:S(2)}, u32[]{:S(2)}) %collective-permute-start.1) | collective-permute-done | bytes 196640 | tf_op jit(solution)/shard_map/ppermute | solution.py:66
  36.3 1.6 collective-permute-start.6
  39.9 4.4 %collective-permute-start.9 = (bf16[384,768]{1,0:T(8,128)(2,1)S(1)}, bf16[384,768]{1,0:T(8,128)(2,1)S(1)}, u32[]{:S(2)}, u32[]{:S(2)}) collective-permute-start(bf16[384,768]{1,0:T(8,128)(2,1)S(1)} %get-tuple-element.27.refs_4_), channel_id=1, source_target_pairs={{0,4},{12,8},{1,5},{13,9},{2,6},{14,10},{3,7},{15,11},{16,20},{28,... | collective-permute-start | bytes 1769480 | tf_op jit(solution)/shard_map/ppermute | solution.py:66
  44.4 4.0 %collective-permute-done.6.far = bf16[256,768]{1,0:T(8,128)(2,1)S(1)} collective-permute-done((bf16[256,768]{1,0:T(8,128)(2,1)S(1)}, bf16[256,768]{1,0:T(8,128)(2,1)S(1)}, u32[]{:S(2)}, u32[]{:S(2)}) %collective-permute-start.6) | collective-permute-done | bytes 393248 | tf_op jit(solution)/shard_map/ppermute | solution.py:66
  48.4 4.6 %collective-permute-done.26.far = bf16[256,768]{1,0:T(8,128)(2,1)S(1)} collective-permute-done((bf16[256,768]{1,0:T(8,128)(2,1)S(1)}, bf16[256,768]{1,0:T(8,128)(2,1)S(1)}, u32[]{:S(2)}, u32[]{:S(2)}) %collective-permute-start.26) | collective-permute-done | bytes 393248 | tf_op jit(solution)/shard_map/ppermute | solution.py:66
  54.2 2.8 %shard_map.71.refs_2_ = bf16[512,768]{1,0:T(8,128)(2,1)S(1)} custom-call(s32[6]{0:T(128)S(1)} %stack.31.p, bf16[256,768]{1,0:T(8,128)(2,1)S(1)} %bitcast.16, bf16[256,768]{1,0:T(8,128)(2,1)S(1)} %collective-permute-done.6.far, bf16[256,768]{1,0:T(8,128)(2,1)S(1)} %collective-permute-done.7.near, bf16[256,768]{1,0:T(8,128)(2,1)S(1)} %collective-permute-done.8.both, ...), custom_call_target="tpu_custom_call" | custom-call | flops 1 | bytes 1 | tf_op jit(solution)/shard_map/pallas_call | solution.py:86
  58.5 1.6 collective-permute-start.12
  60.1 2.8 %shard_map.79 = bf16[512,768]{1,0:T(8,128)(2,1)S(1)} custom-call(s32[6]{0:T(128)S(1)} %stack.31.p, bf16[256,768]{1,0:T(8,128)(2,1)S(1)} %bitcast.12, bf16[256,768]{1,0:T(8,128)(2,1)S(1)} %collective-permute-done.26.far, bf16[256,768]{1,0:T(8,128)(2,1)S(1)} %collective-permute-done.27.near, bf16[256,768]{1,0:T(8,128)(2,1)S(1)} %collective-permute-done.28.both, ...), custom_call_target="tpu_custom_call" | custom-call | flops 1 | bytes 1 | tf_op jit(solution)/shard_map/pallas_call | solution.py:86
  63.6 11.1 %collective-permute-start.21 = (bf16[384,1024]{1,0:T(8,128)(2,1)S(1)}, bf16[384,1024]{1,0:T(8,128)(2,1)S(1)}, u32[]{:S(2)}, u32[]{:S(2)}) collective-permute-start(bf16[384,1024]{1,0:T(8,128)(2,1)S(1)} %get-tuple-element.33), channel_id=1, source_target_pairs={{0,8},{12,4},{1,9},{13,5},{2,10},{14,6},{3,11},{15,7},{16,24},{28,... | collective-permute-start | bytes 2359304 | tf_op jit(solution)/shard_map/ppermute | solution.py:66
  76.7 22.6 %collective-permute-done.13.came = bf16[4,64,768]{2,1,0:T(8,128)(2,1)S(1)} collective-permute-done((bf16[4,64,768]{2,1,0:T(8,128)(2,1)S(1)}, bf16[4,64,768]{2,1,0:T(8,128)(2,1)S(1)}, u32[]{:S(2)}, u32[]{:S(2)}) %collective-permute-start.13) | collective-permute-done | bytes 393248 | tf_op jit(solution)/shard_map/ppermute | solution.py:66
  99.2 2.8 %shard_map.73.keeps = f32[512,768]{1,0:T(8,128)S(1)} custom-call(s32[6]{0:T(128)S(1)} %stack.31.p, bf16[256,768]{1,0:T(8,128)(2,1)S(1)} %bitcast.17, bf16[256,768]{1,0:T(8,128)(2,1)S(1)} %collective-permute-done.6.far, bf16[256,768]{1,0:T(8,128)(2,1)S(1)} %collective-permute-done.7.near, bf16[256,768]{1,0:T(8,128)(2,1)S(1)} %collective-permute-done.8.both, ...), custom_call_target="tpu_custom_call" | custom-call | flops 1 | bytes 1 | tf_op jit(solution)/shard_map/pallas_call | solution.py:86
  102.0 1.7 shard_map.75.s0
  103.7 1.6 collective-permute-start.16
  106.5 4.6 %collective-permute-start.18 = (bf16[384,1024]{1,0:T(8,128)(2,1)S(1)}, bf16[384,1024]{1,0:T(8,128)(2,1)S(1)}, u32[]{:S(2)}, u32[]{:S(2)}) collective-permute-start(bf16[384,1024]{1,0:T(8,128)(2,1)S(1)} %shard_map.74.refs_0_), channel_id=1, source_target_pairs={{0,4},{12,8},{1,5},{13,9},{2,6},{14,10},{3,7},{15,11},{16,20},{28,... | collective-permute-start | bytes 2359304 | tf_op jit(solution)/shard_map/ppermute | solution.py:66
  111.1 2.8 %shard_map.78.keeps = f32[512,768]{1,0:T(8,128)S(1)} custom-call(s32[6]{0:T(128)S(1)} %stack.31.p, bf16[256,768]{1,0:T(8,128)(2,1)S(1)} %bitcast.13, bf16[256,768]{1,0:T(8,128)(2,1)S(1)} %collective-permute-done.26.far, bf16[256,768]{1,0:T(8,128)(2,1)S(1)} %collective-permute-done.27.near, bf16[256,768]{1,0:T(8,128)(2,1)S(1)} %collective-permute-done.28.both, ...), custom_call_target="tpu_custom_call" | custom-call | flops 1 | bytes 1 | tf_op jit(solution)/shard_map/pallas_call | solution.py:86
  113.8 1.7 shard_map.80.s0
  117.7 8.8 %collective-permute-done.20.c1 = bf16[384,1024]{1,0:T(8,128)(2,1)S(1)} collective-permute-done((bf16[384,1024]{1,0:T(8,128)(2,1)S(1)}, bf16[384,1024]{1,0:T(8,128)(2,1)S(1)}, u32[]{:S(2)}, u32[]{:S(2)}) %collective-permute-start.20) | collective-permute-done | bytes 786464 | tf_op jit(solution)/shard_map/ppermute | solution.py:66
  127.5 15.8 %collective-permute-done.22.a1 = bf16[384,1024]{1,0:T(8,128)(2,1)S(1)} collective-permute-done((bf16[384,1024]{1,0:T(8,128)(2,1)S(1)}, bf16[384,1024]{1,0:T(8,128)(2,1)S(1)}, u32[]{:S(2)}, u32[]{:S(2)}) %collective-permute-start.22) | collective-permute-done | bytes 786464 | tf_op jit(solution)/shard_map/ppermute | solution.py:66
  143.8 13.3 %collective-permute-done.19.f1 = bf16[384,1024]{1,0:T(8,128)(2,1)S(1)} collective-permute-done((bf16[384,1024]{1,0:T(8,128)(2,1)S(1)}, bf16[384,1024]{1,0:T(8,128)(2,1)S(1)}, u32[]{:S(2)}, u32[]{:S(2)}) %collective-permute-start.19) | collective-permute-done | bytes 786464 | tf_op jit(solution)/shard_map/ppermute | solution.py:66
  157.1 6.6 %shard_map.77 = (bf16[144,1024]{1,0:T(8,128)(2,1)S(1)}, bf16[144,1024]{1,0:T(8,128)(2,1)S(1)}, bf16[144,1024]{1,0:T(8,128)(2,1)S(1)}, bf16[144,1024]{1,0:T(8,128)(2,1)S(1)}) custom-call(s32[6]{0:T(128)S(1)} %stack.31.p, bf16[528,768]{1,0:T(8,128)(2,1)S(1)} %shard_map.75.s0, bf16[528,768]{1,0:T(8,128)(2,1)S(1)} %collective-permute-done.15.s1, ...), custom_call_target="tpu_custom_call" | custom-call | flops 1 | bytes 1 | tf_op jit(solution)/shard_map/pallas_call | solution.py:86
  167.1 6.7 %shard_map.81 = (bf16[144,1024]{1,0:T(8,128)(2,1)S(1)}, bf16[144,1024]{1,0:T(8,128)(2,1)S(1)}, bf16[144,1024]{1,0:T(8,128)(2,1)S(1)}, bf16[144,1024]{1,0:T(8,128)(2,1)S(1)}) custom-call(s32[6]{0:T(128)S(1)} %stack.31.p, bf16[528,768]{1,0:T(8,128)(2,1)S(1)} %shard_map.80.s0, bf16[528,768]{1,0:T(8,128)(2,1)S(1)} %collective-permute-done.30.s1, ...), custom_call_target="tpu_custom_call" | custom-call | flops 1 | bytes 1 | tf_op jit(solution)/shard_map/pallas_call | solution.py:86
  177.0 2.2 %collective-permute-done.24.refs_2_ = bf16[144,1024]{1,0:T(8,128)(2,1)S(1)} collective-permute-done((bf16[144,1024]{1,0:T(8,128)(2,1)S(1)}, bf16[144,1024]{1,0:T(8,128)(2,1)S(1)}, u32[]{:S(2)}, u32[]{:S(2)}) %collective-permute-start.24) | collective-permute-done | bytes 294944 | tf_op jit(solution)/shard_map/ppermute | solution.py:66
  179.3 1.9 collective-permute-done.25.refs_3_
  181.2 12.1 %collective-permute-done.34.refs_6_ = bf16[144,1024]{1,0:T(8,128)(2,1)S(1)} collective-permute-done((bf16[144,1024]{1,0:T(8,128)(2,1)S(1)}, bf16[144,1024]{1,0:T(8,128)(2,1)S(1)}, u32[]{:S(2)}, u32[]{:S(2)}) %collective-permute-start.34) | collective-permute-done | bytes 294944 | tf_op jit(solution)/shard_map/ppermute | solution.py:66
  193.3 1.7 shard_map.82
  (77 shorter events, 27.0 us)
Async XLA Ops:
  4.3 30.8 %collective-permute-start.5 = (bf16[384,1024]{1,0:T(8,128)(2,1)S(1)}, bf16[384,1024]{1,0:T(8,128)(2,1)S(1)}, u32[]{:S(2)}, u32[]{:S(2)}) collective-permute-start(bf16[384,1024]{1,0:T(8,128)(2,1)S(1)} %get-tuple-element.28), channel_id=1, source_target_pairs={{4,8},{8,4},{5,9},{9,5},{6,10},{10,6},{7,11},{11,7},{20,24},{24,20... | collective-permute-start | bytes 2359304 | tf_op jit(solution)/shard_map/ppermute | solution.py:66
  5.2 21.6 %collective-permute-start.4 = (bf16[384,768]{1,0:T(8,128)(2,1)S(1)}, bf16[384,768]{1,0:T(8,128)(2,1)S(1)}, u32[]{:S(2)}, u32[]{:S(2)}) collective-permute-start(bf16[384,768]{1,0:T(8,128)(2,1)S(1)} %get-tuple-element.24.refs_0_), channel_id=1, source_target_pairs={{0,4},{12,8},{1,5},{13,9},{2,6},{14,10},{3,7},{15,11},{16,20},{28,... | collective-permute-start | bytes 1769480 | tf_op jit(solution)/shard_map/ppermute | solution.py:66
  21.0 10.9 %collective-permute-start.3 = (bf16[2,64,768]{2,1,0:T(8,128)(2,1)S(1)}, bf16[2,64,768]{2,1,0:T(8,128)(2,1)S(1)}, u32[]{:S(2)}, u32[]{:S(2)}) collective-permute-start(bf16[2,64,768]{2,1,0:T(8,128)(2,1)S(1)} %get-tuple-element.26), channel_id=1, source_target_pairs={{0,8},{12,4},{1,9},{13,5},{2,10},{14,6},{3,11},{15,7},{16,24},{28,... | collective-permute-start | bytes 589832 | tf_op jit(solution)/shard_map/ppermute | solution.py:66
  22.4 9.4 %collective-permute-start.2 = (bf16[2,64,768]{2,1,0:T(8,128)(2,1)S(1)}, bf16[2,64,768]{2,1,0:T(8,128)(2,1)S(1)}, u32[]{:S(2)}, u32[]{:S(2)}) collective-permute-start(bf16[2,64,768]{2,1,0:T(8,128)(2,1)S(1)} %get-tuple-element.26), channel_id=1, source_target_pairs={{4,8},{8,4},{5,9},{9,5},{6,10},{10,6},{7,11},{11,7},{20,24},{24,20... | collective-permute-start | bytes 589832 | tf_op jit(solution)/shard_map/ppermute | solution.py:66
  23.1 12.0 %collective-permute-start.1 = (bf16[2,64,768]{2,1,0:T(8,128)(2,1)S(1)}, bf16[2,64,768]{2,1,0:T(8,128)(2,1)S(1)}, u32[]{:S(2)}, u32[]{:S(2)}) collective-permute-start(bf16[2,64,768]{2,1,0:T(8,128)(2,1)S(1)} %get-tuple-element.25.refs_3_.refs_1_), channel_id=1, source_target_pairs={{0,4},{12,8},{1,5},{13,9},{2,6},{14,10},{3,7},{15,11},{16,20},{28,... | collective-permute-start | bytes 589832 | tf_op jit(solution)/shard_map/ppermute | solution.py:66
  26.8 17.5 %collective-permute-start.11 = (bf16[4,64,768]{2,1,0:T(8,128)(2,1)S(1)}, bf16[4,64,768]{2,1,0:T(8,128)(2,1)S(1)}, u32[]{:S(2)}, u32[]{:S(2)}) collective-permute-start(bf16[4,64,768]{2,1,0:T(8,128)(2,1)S(1)} %shard_map.70), channel_id=1, source_target_pairs={{0,4},{12,8},{1,5},{13,9},{2,6},{14,10},{3,7},{15,11},{16,20},{28,... | collective-permute-start | bytes 1179656 | tf_op jit(solution)/shard_map/ppermute | solution.py:66
  36.3 12.1 %collective-permute-start.6 = (bf16[256,768]{1,0:T(8,128)(2,1)S(1)}, bf16[256,768]{1,0:T(8,128)(2,1)S(1)}, u32[]{:S(2)}, u32[]{:S(2)}) collective-permute-start(bf16[256,768]{1,0:T(8,128)(2,1)S(1)} %bitcast.14), channel_id=1, source_target_pairs={{0,2},{2,0},{1,3},{3,1},{4,6},{6,4},{5,7},{7,5},{8,10},{10,8},{9,1... | collective-permute-start | bytes 1179656 | tf_op jit(solution)/shard_map/ppermute | solution.py:66
  37.8 15.1 %collective-permute-start.10 = (bf16[384,768]{1,0:T(8,128)(2,1)S(1)}, bf16[384,768]{1,0:T(8,128)(2,1)S(1)}, u32[]{:S(2)}, u32[]{:S(2)}) collective-permute-start(bf16[384,768]{1,0:T(8,128)(2,1)S(1)} %get-tuple-element.30), channel_id=1, source_target_pairs={{0,16},{16,0},{1,17},{17,1},{2,18},{18,2},{3,19},{19,3},{4,20},{20... | collective-permute-start | bytes 1769480 | tf_op jit(solution)/shard_map/ppermute | solution.py:66
  39.3 13.6 %collective-permute-start.26 = (bf16[256,768]{1,0:T(8,128)(2,1)S(1)}, bf16[256,768]{1,0:T(8,128)(2,1)S(1)}, u32[]{:S(2)}, u32[]{:S(2)}) collective-permute-start(bf16[256,768]{1,0:T(8,128)(2,1)S(1)} %bitcast.10), channel_id=1, source_target_pairs={{0,2},{2,0},{1,3},{3,1},{4,6},{6,4},{5,7},{7,5},{8,10},{10,8},{9,1... | collective-permute-start | bytes 1179656 | tf_op jit(solution)/shard_map/ppermute | solution.py:66
  39.9 17.8 %collective-permute-start.9 = (bf16[384,768]{1,0:T(8,128)(2,1)S(1)}, bf16[384,768]{1,0:T(8,128)(2,1)S(1)}, u32[]{:S(2)}, u32[]{:S(2)}) collective-permute-start(bf16[384,768]{1,0:T(8,128)(2,1)S(1)} %get-tuple-element.27.refs_4_), channel_id=1, source_target_pairs={{0,4},{12,8},{1,5},{13,9},{2,6},{14,10},{3,7},{15,11},{16,20},{28,... | collective-permute-start | bytes 1769480 | tf_op jit(solution)/shard_map/ppermute | solution.py:66
  44.3 9.9 %collective-permute-start.7 = (bf16[256,768]{1,0:T(8,128)(2,1)S(1)}, bf16[256,768]{1,0:T(8,128)(2,1)S(1)}, u32[]{:S(2)}, u32[]{:S(2)}) collective-permute-start(bf16[256,768]{1,0:T(8,128)(2,1)S(1)} %bitcast.15), channel_id=1, source_target_pairs={{0,1},{1,0},{2,3},{3,2},{4,5},{5,4},{6,7},{7,6},{8,9},{9,8},{10,11... | collective-permute-start | bytes 1179656 | tf_op jit(solution)/shard_map/ppermute | solution.py:66
  57.0 45.0 %collective-permute-start.14 = (bf16[512,768]{1,0:T(8,128)(2,1)S(1)}, bf16[512,768]{1,0:T(8,128)(2,1)S(1)}, u32[]{:S(2)}, u32[]{:S(2)}) collective-permute-start(bf16[512,768]{1,0:T(8,128)(2,1)S(1)} %shard_map.71.refs_2_), channel_id=1, source_target_pairs={{4,8},{8,4},{5,9},{9,5},{6,10},{10,6},{7,11},{11,7},{20,24},{24,20... | collective-permute-start | bytes 2359304 | tf_op jit(solution)/shard_map/ppermute | solution.py:66
  58.5 17.5 %collective-permute-start.12 = (bf16[384,768]{1,0:T(8,128)(2,1)S(1)}, bf16[384,768]{1,0:T(8,128)(2,1)S(1)}, u32[]{:S(2)}, u32[]{:S(2)}) collective-permute-start(bf16[384,768]{1,0:T(8,128)(2,1)S(1)} %get-tuple-element.31), channel_id=1, source_target_pairs={{0,16},{16,0},{1,17},{17,1},{2,18},{18,2},{3,19},{19,3},{4,20},{20... | collective-permute-start | bytes 1769480 | tf_op jit(solution)/shard_map/ppermute | solution.py:66
  62.8 51.0 %collective-permute-start.29 = (bf16[512,768]{1,0:T(8,128)(2,1)S(1)}, bf16[512,768]{1,0:T(8,128)(2,1)S(1)}, u32[]{:S(2)}, u32[]{:S(2)}) collective-permute-start(bf16[512,768]{1,0:T(8,128)(2,1)S(1)} %shard_map.79), channel_id=1, source_target_pairs={{4,8},{8,4},{5,9},{9,5},{6,10},{10,6},{7,11},{11,7},{20,24},{24,20... | collective-permute-start | bytes 2359304 | tf_op jit(solution)/shard_map/ppermute | solution.py:66
  63.6 52.6 %collective-permute-start.21 = (bf16[384,1024]{1,0:T(8,128)(2,1)S(1)}, bf16[384,1024]{1,0:T(8,128)(2,1)S(1)}, u32[]{:S(2)}, u32[]{:S(2)}) collective-permute-start(bf16[384,1024]{1,0:T(8,128)(2,1)S(1)} %get-tuple-element.33), channel_id=1, source_target_pairs={{0,8},{12,4},{1,9},{13,5},{2,10},{14,6},{3,11},{15,7},{16,24},{28,... | collective-permute-start | bytes 2359304 | tf_op jit(solution)/shard_map/ppermute | solution.py:66
  74.7 24.5 %collective-permute-start.13 = (bf16[4,64,768]{2,1,0:T(8,128)(2,1)S(1)}, bf16[4,64,768]{2,1,0:T(8,128)(2,1)S(1)}, u32[]{:S(2)}, u32[]{:S(2)}) collective-permute-start(bf16[4,64,768]{2,1,0:T(8,128)(2,1)S(1)} %get-tuple-element.32), channel_id=1, source_target_pairs={{0,4},{12,8},{1,5},{13,9},{2,6},{14,10},{3,7},{15,11},{16,20},{28,... | collective-permute-start | bytes 1179656 | tf_op jit(solution)/shard_map/ppermute | solution.py:66
  103.7 22.7 %collective-permute-start.16 = (bf16[528,768]{1,0:T(8,128)(2,1)S(1)}, bf16[528,768]{1,0:T(8,128)(2,1)S(1)}, u32[]{:S(2)}, u32[]{:S(2)}) collective-permute-start(bf16[528,768]{1,0:T(8,128)(2,1)S(1)} %shard_map.75.s0), channel_id=1, source_target_pairs={{0,2},{2,0},{1,3},{3,1},{4,6},{6,4},{5,7},{7,5},{8,10},{10,8},{9,1... | collective-permute-start | bytes 2433032 | tf_op jit(solution)/shard_map/ppermute | solution.py:66
  105.9 20.5 %collective-permute-start.20 = (bf16[384,1024]{1,0:T(8,128)(2,1)S(1)}, bf16[384,1024]{1,0:T(8,128)(2,1)S(1)}, u32[]{:S(2)}, u32[]{:S(2)}) collective-permute-start(bf16[384,1024]{1,0:T(8,128)(2,1)S(1)} %shard_map.76), channel_id=1, source_target_pairs={{0,16},{16,0},{1,17},{17,1},{2,18},{18,2},{3,19},{19,3},{4,20},{20... | collective-permute-start | bytes 2359304 | tf_op jit(solution)/shard_map/ppermute | solution.py:66
  106.5 20.5 %collective-permute-start.18 = (bf16[384,1024]{1,0:T(8,128)(2,1)S(1)}, bf16[384,1024]{1,0:T(8,128)(2,1)S(1)}, u32[]{:S(2)}, u32[]{:S(2)}) collective-permute-start(bf16[384,1024]{1,0:T(8,128)(2,1)S(1)} %shard_map.74.refs_0_), channel_id=1, source_target_pairs={{0,4},{12,8},{1,5},{13,9},{2,6},{14,10},{3,7},{15,11},{16,20},{28,... | collective-permute-start | bytes 2359304 | tf_op jit(solution)/shard_map/ppermute | solution.py:66
  115.6 27.7 %collective-permute-start.31 = (bf16[528,768]{1,0:T(8,128)(2,1)S(1)}, bf16[528,768]{1,0:T(8,128)(2,1)S(1)}, u32[]{:S(2)}, u32[]{:S(2)}) collective-permute-start(bf16[528,768]{1,0:T(8,128)(2,1)S(1)} %shard_map.80.s0), channel_id=1, source_target_pairs={{0,2},{2,0},{1,3},{3,1},{4,6},{6,4},{5,7},{7,5},{8,10},{10,8},{9,1... | collective-permute-start | bytes 2433032 | tf_op jit(solution)/shard_map/ppermute | solution.py:66
  116.2 27.1 %collective-permute-start.22 = (bf16[384,1024]{1,0:T(8,128)(2,1)S(1)}, bf16[384,1024]{1,0:T(8,128)(2,1)S(1)}, u32[]{:S(2)}, u32[]{:S(2)}) collective-permute-start(bf16[384,1024]{1,0:T(8,128)(2,1)S(1)} %collective-permute-done.21.a0), channel_id=1, source_target_pairs={{0,16},{16,0},{1,17},{17,1},{2,18},{18,2},{3,19},{19,3},{4,20},{20... | collective-permute-start | bytes 2359304 | tf_op jit(solution)/shard_map/ppermute | solution.py:66
  126.4 17.4 %collective-permute-start.15 = (bf16[528,768]{1,0:T(8,128)(2,1)S(1)}, bf16[528,768]{1,0:T(8,128)(2,1)S(1)}, u32[]{:S(2)}, u32[]{:S(2)}) collective-permute-start(bf16[528,768]{1,0:T(8,128)(2,1)S(1)} %shard_map.75.s0), channel_id=1, source_target_pairs={{0,1},{1,0},{2,3},{3,2},{4,5},{5,4},{6,7},{7,6},{8,9},{9,8},{10,11... | collective-permute-start | bytes 2433032 | tf_op jit(solution)/shard_map/ppermute | solution.py:66
  126.4 30.7 %collective-permute-start.17 = (bf16[528,768]{1,0:T(8,128)(2,1)S(1)}, bf16[528,768]{1,0:T(8,128)(2,1)S(1)}, u32[]{:S(2)}, u32[]{:S(2)}) collective-permute-start(bf16[528,768]{1,0:T(8,128)(2,1)S(1)} %collective-permute-done.16.s2), channel_id=1, source_target_pairs={{0,1},{1,0},{2,3},{3,2},{4,5},{5,4},{6,7},{7,6},{8,9},{9,8},{10,11... | collective-permute-start | bytes 2433032 | tf_op jit(solution)/shard_map/ppermute | solution.py:66
  127.0 30.2 %collective-permute-start.19 = (bf16[384,1024]{1,0:T(8,128)(2,1)S(1)}, bf16[384,1024]{1,0:T(8,128)(2,1)S(1)}, u32[]{:S(2)}, u32[]{:S(2)}) collective-permute-start(bf16[384,1024]{1,0:T(8,128)(2,1)S(1)} %collective-permute-done.18.f0), channel_id=1, source_target_pairs={{0,16},{16,0},{1,17},{17,1},{2,18},{18,2},{3,19},{19,3},{4,20},{20... | collective-permute-start | bytes 2359304 | tf_op jit(solution)/shard_map/ppermute | solution.py:66
  143.3 23.8 %collective-permute-start.30 = (bf16[528,768]{1,0:T(8,128)(2,1)S(1)}, bf16[528,768]{1,0:T(8,128)(2,1)S(1)}, u32[]{:S(2)}, u32[]{:S(2)}) collective-permute-start(bf16[528,768]{1,0:T(8,128)(2,1)S(1)} %shard_map.80.s0), channel_id=1, source_target_pairs={{0,1},{1,0},{2,3},{3,2},{4,5},{5,4},{6,7},{7,6},{8,9},{9,8},{10,11... | collective-permute-start | bytes 2433032 | tf_op jit(solution)/shard_map/ppermute | solution.py:66
  143.3 23.8 %collective-permute-start.32 = (bf16[528,768]{1,0:T(8,128)(2,1)S(1)}, bf16[528,768]{1,0:T(8,128)(2,1)S(1)}, u32[]{:S(2)}, u32[]{:S(2)}) collective-permute-start(bf16[528,768]{1,0:T(8,128)(2,1)S(1)} %collective-permute-done.31.s2), channel_id=1, source_target_pairs={{0,1},{1,0},{2,3},{3,2},{4,5},{5,4},{6,7},{7,6},{8,9},{9,8},{10,11... | collective-permute-start | bytes 2433032 | tf_op jit(solution)/shard_map/ppermute | solution.py:66
  163.8 12.0 %collective-permute-start.23 = (bf16[144,1024]{1,0:T(8,128)(2,1)S(1)}, bf16[144,1024]{1,0:T(8,128)(2,1)S(1)}, u32[]{:S(2)}, u32[]{:S(2)}) collective-permute-start(bf16[144,1024]{1,0:T(8,128)(2,1)S(1)} %get-tuple-element.35), channel_id=1, source_target_pairs={{4,8},{8,4},{5,9},{9,5},{6,10},{10,6},{7,11},{11,7},{20,24},{24,20... | collective-permute-start | bytes 884744 | tf_op jit(solution)/shard_map/ppermute | solution.py:66
  164.5 14.8 %collective-permute-start.24 = (bf16[144,1024]{1,0:T(8,128)(2,1)S(1)}, bf16[144,1024]{1,0:T(8,128)(2,1)S(1)}, u32[]{:S(2)}, u32[]{:S(2)}) collective-permute-start(bf16[144,1024]{1,0:T(8,128)(2,1)S(1)} %get-tuple-element.36), channel_id=1, source_target_pairs={{4,0},{8,12},{5,1},{9,13},{6,2},{10,14},{7,3},{11,15},{20,16},{24,... | collective-permute-start | bytes 884744 | tf_op jit(solution)/shard_map/ppermute | solution.py:66
  165.8 15.4 %collective-permute-start.25 = (bf16[144,1024]{1,0:T(8,128)(2,1)S(1)}, bf16[144,1024]{1,0:T(8,128)(2,1)S(1)}, u32[]{:S(2)}, u32[]{:S(2)}) collective-permute-start(bf16[144,1024]{1,0:T(8,128)(2,1)S(1)} %get-tuple-element.37), channel_id=1, source_target_pairs={{4,12},{8,0},{5,13},{9,1},{6,14},{10,2},{7,15},{11,3},{20,28},{24,... | collective-permute-start | bytes 884744 | tf_op jit(solution)/shard_map/ppermute | solution.py:66
  173.7 7.4 %collective-permute-start.33 = (bf16[144,1024]{1,0:T(8,128)(2,1)S(1)}, bf16[144,1024]{1,0:T(8,128)(2,1)S(1)}, u32[]{:S(2)}, u32[]{:S(2)}) collective-permute-start(bf16[144,1024]{1,0:T(8,128)(2,1)S(1)} %get-tuple-element.40), channel_id=1, source_target_pairs={{4,8},{8,4},{5,9},{9,5},{6,10},{10,6},{7,11},{11,7},{20,24},{24,20... | collective-permute-start | bytes 884744 | tf_op jit(solution)/shard_map/ppermute | solution.py:66
  174.4 18.8 %collective-permute-start.34 = (bf16[144,1024]{1,0:T(8,128)(2,1)S(1)}, bf16[144,1024]{1,0:T(8,128)(2,1)S(1)}, u32[]{:S(2)}, u32[]{:S(2)}) collective-permute-start(bf16[144,1024]{1,0:T(8,128)(2,1)S(1)} %get-tuple-element.41), channel_id=1, source_target_pairs={{4,0},{8,12},{5,1},{9,13},{6,2},{10,14},{7,3},{11,15},{20,16},{24,... | collective-permute-start | bytes 884744 | tf_op jit(solution)/shard_map/ppermute | solution.py:66
  175.7 17.5 %collective-permute-start.35 = (bf16[144,1024]{1,0:T(8,128)(2,1)S(1)}, bf16[144,1024]{1,0:T(8,128)(2,1)S(1)}, u32[]{:S(2)}, u32[]{:S(2)}) collective-permute-start(bf16[144,1024]{1,0:T(8,128)(2,1)S(1)} %get-tuple-element.42), channel_id=1, source_target_pairs={{4,12},{8,0},{5,13},{9,1},{6,14},{10,2},{7,15},{11,3},{20,28},{24,... | collective-permute-start | bytes 884744 | tf_op jit(solution)/shard_map/ppermute | solution.py:66
  (12 other events, 143.9 us)

commit v6 on v5

--- a/solution.py
+++ b/solution.py
@@ -7,7 +7,43 @@
 
 EPS = 1e-06
 CHUNKS = 2
-JOIN = 1
+PLAN = dict(
+    first=0,
+    at_cross=0,
+    at_old=3,
+    at_inner=3,
+    at_far=2,
+    at_fold=3,
+    due_cross=2,
+    due_old=7,
+    due_inner=6,
+    due_far=99,
+    due_fold=99,
+    due_swap_cross=6,
+    due_swap_far=6,
+    hop_cross=0,
+    hop_old=0,
+    hop_inner=0,
+    hop_far=0,
+    hop_fold=0,
+    hop_swap_cross=1,
+    hop_swap_far=0,
+    join=1,
+    c_send=1,
+    c_keep=1,
+    xjoin=1,
+    k3=0,
+    h0=-1,
+    h1=2,
+    y_fold=1,
+    hop_swap_fold=0,
+    c_x1=1,
+    c_xc=1,
+    c_k3=1,
+    c_ord=1,
+    hop_join=-1,
+    full=1,
+)
 
 
 def normalize(values, ln_gain):
@@ -64,6 +100,18 @@
 
 def along(value, axis, pairs):
     return lax.ppermute(value, axis, pairs)
+
+
+def hop(value):
+    return along(value.reshape(-1, value.shape[-1])[:16, :128], "sub", SWAP)
+
+
+def hops(value, count):
+    if count < 0:
+        return []
+    for _ in range(count):
+        value = hop(value) if value.shape != (16, 128) else along(value, "sub", SWAP)
+    return [value]
 
 
 def pick(stack, index):
@@ -106,22 +154,25 @@
         copy.wait()
 
 
-def cuts(place, blocks, *released, cost=1):
+def cuts(place, outs, *released, cost=1):
+    sources = [block[0] for _, blocks in outs for block in blocks]
+
     def kernel(p, *refs):
-        dsts = refs[-1 - len(blocks) : -1]
-        pairs = [
-            (src.at[at(p, block)] if at else src, dst)
-            for src, dst, (_, block, at) in zip(refs, dsts, blocks)
-        ]
-        moved(pairs, refs[-1])
+        dsts, sems = refs[-1 - len(outs) : -1], refs[-1]
+        pairs = []
+        for dst, (_, blocks) in zip(dsts, outs):
+            for _, there, here in blocks:
+                src = refs[len(pairs)]
+                pairs.append((src.at[there(p)] if there else src, dst.at[here] if here else dst))
+        moved(pairs, sems)
 
     return call(
         kernel,
         place,
-        [ANY] * (len(blocks) + len(released)),
-        [shaped(block, array.dtype) for array, block, _ in blocks],
-        [pltpu.SemaphoreType.DMA((len(blocks),))],
-        [array for array, _, _ in blocks] + list(released),
+        [ANY] * (len(sources) + len(released)),
+        [shaped(shape) for shape, _ in outs],
+        [pltpu.SemaphoreType.DMA((len(sources),))],
+        sources + list(released),
         cost,
     )
 
@@ -154,14 +205,16 @@
     return jnp.concatenate([rows, fill], axis=0).T
 
 
-def attend(place, tokens_of, w_out, fold, swapped, resid, came, bias, part, inner, dtype):
+def attend(place, tokens_of, w_out, fold, swapped, resid, others, bias, part, inner, dtype, *after, cost=1):
     rows, heads = tokens_of[0].shape
     tokens = 2 * rows
-    half, share = fold.shape[1], fold.shape[0]
-    images, span = resid.shape[0], tokens // resid.shape[0] // 4
+    share, half = swapped.shape
+    images, patches = resid.shape[:2]
+    span = tokens // images // 4
     tile = TILE if half % TILE == 0 else half
 
-    def kernel(p, own, far, near, both, weight, fold, swapped, old, came, bias, out, left, total):
+    def kernel(p, own, far, near, both, weight, fold, swapped, old, bias, *refs):
+        others, (out, left, total) = refs[: -3 - len(after)], refs[-3:]
         low = p[0] == 1
         turn = low == (p[2] == 0)
         side = jnp.where(low == inner, 0, half)
@@ -172,8 +225,7 @@
             first, second = folded[:, :share], folded[:, share:]
             left[at, heads : heads + share] = jnp.where(p[1] == 0, first, second)
             left[at, heads + share :] = jnp.where(p[1] == 0, second, first)
-        own_at, came_at = jnp.where(low, span, 2 * span), jnp.where(low, 0, 3 * span)
-        patches = slice(part * span, (part + 1) * span)
+        row_of = [jnp.where(low, 1, 2), jnp.where(low, 0, 3), jnp.where(low, 3, 0)]
         for t in range(half // tile):
             here = slice(t * tile, (t + 1) * tile)
             there = pl.ds(pl.multiple_of(side + t * tile, tile), tile)
@@ -181,24 +233,28 @@
             for i, piece in enumerate((fold, swapped)):
                 at = slice(heads + i * share, heads + (i + 1) * share)
                 value = value + jnp.dot(
-                    left[:, at], piece[:, here], preferred_element_type=jnp.float32
+                    left[:, at], piece[:share, here], preferred_element_type=jnp.float32
                 )
             total[...] = value + jnp.where(low, bias[:, there], 0.0)
             for image in range(images):
-                for at, source, columns in ((own_at, old, there), (came_at, came, here)):
-                    at = pl.ds(pl.multiple_of(image * 4 * span + at, span), span)
-                    total[at, :] = total[at, :] + source[image, patches, columns].astype(
-                        jnp.float32
-                    )
+                first = part * span
+                more = [old[image, first : first + span, there]]
+                for source in others:
+                    first = source.shape[0] - (images - image) * patches + part * span
+                    more.append(source[first : first + span, here])
+                for row, values in zip(row_of, more):
+                    at = run(image * 4 + row, span)
+                    total[at, :] = total[at, :] + values.astype(jnp.float32)
             out[:, here] = total[...].astype(dtype)
 
     return call(
         kernel,
         place,
-        [VMEM] * 10,
+        [VMEM] * (9 + len(others)) + [ANY] * len(after),
         shaped((tokens, half), dtype),
         [pltpu.VMEM((tokens, 2 * heads), jnp.bfloat16), pltpu.VMEM((tokens, tile), jnp.float32)],
-        [*tokens_of, w_out, fold, swapped, resid, came, bias],
+        [*tokens_of, w_out, fold, swapped, resid, bias, *others, *after],
+        cost,
     )
 
 
@@ -233,21 +289,24 @@
     )
 
 
-def project_up(place, scaled, w_proj, pieces, gain):
+def project_up(place, scaled, w_proj, pieces, gain, *after):
     rows, half = scaled[0].shape
     tokens, out_cols = rows - EXTRA, w_proj.shape[1]
     size, share = tokens // 4, half // 2
     tile = TILE if out_cols % TILE == 0 else out_cols
 
-    def kernel(p, s0, s1, s2, s3, own, f0, f1, c0, c1, a0, a1, gain, *rest):
-        outs, (left, stats, total) = rest[:4], rest[4:]
+    whole = len(pieces) % 2
+
+    def kernel(p, s0, s1, s2, s3, own, *rest):
+        fold, (c0, c1, a0, a1, gain) = rest[: 2 - whole], rest[2 - whole : 7 - whole]
+        outs, (left, stats, total) = rest[-7:-3], rest[-3:]
         low = p[0] == 1
 
         def slot(feature):
             return jnp.where(low, feature, 3 - feature)
 
         def put(value, at, rows):
-            swap = (p[1] == 1) & (at != 1)
+            swap = (p[1] == 1) & (at > 1 if whole else at != 1)
             first, second = value[:, :share], value[:, share:]
             left[at, rows, :share] = jnp.where(swap, second, first)
             left[at, rows, share:] = jnp.where(swap, first, second)
@@ -278,7 +337,7 @@
             here = slice(t * tile, (t + 1) * tile)
             value = jnp.zeros((tokens, tile), jnp.float32)
             gains = []
-            for at, halves in enumerate(((f0, f1), (own,), (c0, c1), (a0, a1))):
+            for at, halves in enumerate((fold, (own,), (c0, c1), (a0, a1))):
                 piece = jnp.zeros((rows, tile), jnp.float32)
                 if at == 1:
                     weights = [own[run(1 - p[0], half), here]]
@@ -313,14 +372,14 @@
     return call(
         kernel,
         place,
-        [VMEM] * 12,
+        [VMEM] * (6 + len(pieces)) + [ANY] * len(after),
         [shaped((size + EXTRA, out_cols))] * 4,
         [
             pltpu.VMEM((4, rows, half), jnp.bfloat16),
             pltpu.VMEM((4, 2, size), jnp.float32),
             pltpu.VMEM((tokens, tile), jnp.float32),
         ],
-        [*scaled, w_proj, *pieces, gain],
+        [*scaled, w_proj, *pieces, gain, *after],
     )
 
 
@@ -381,20 +440,28 @@
     )
 
 
-def ordered(place, pieces, *released):
+def ordered(place, pieces, blocks, *released, cost=1):
     images, part, heads = pieces[0].shape
     span = part // CHUNKS
+    sources = [block[0] for _, many in blocks for block in many]
 
     def kernel(p, *refs):
-        ins, outs, sems = refs[:4], refs[-CHUNKS - 1 : -1], refs[-1]
+        ins, rest = refs[:4], refs[4 : 4 + len(sources)]
+        outs, sems = refs[-1 - CHUNKS - len(blocks) : -1], refs[-1]
+        more = []
+        for dst, (_, many) in zip(outs[CHUNKS:], blocks):
+            for _, there, here in many:
+                src = rest[len(more)]
+                more.append((src.at[there(p)] if there else src, dst.at[here] if here else dst))
 
         def go(ins):
             moved(
                 [
                     (ins[row].at[:, k * span : (k + 1) * span], out.at[:, row])
-                    for k, out in enumerate(outs)
+                    for k, out in enumerate(outs[:CHUNKS])
                     for row in range(4)
-                ],
+                ]
+                + more,
                 sems,
             )
 
@@ -404,12 +471,13 @@
     outs = call(
         kernel,
         place,
-        [ANY] * (4 + len(released)),
-        [shaped((images, 4, span, heads))] * CHUNKS,
-        [pltpu.SemaphoreType.DMA((4 * CHUNKS,))],
-        [*pieces, *released],
-    )
-    return [v.reshape(images * 4 * span, heads) for v in outs]
+        [ANY] * (4 + len(sources) + len(released)),
+        [shaped((images, 4, span, heads))] * CHUNKS + [shaped(shape) for shape, _ in blocks],
+        [pltpu.SemaphoreType.DMA((4 * CHUNKS + len(sources),))],
+        [*pieces, *sources, *released],
+        cost,
+    )
+    return [v.reshape(images * 4 * span, heads) for v in outs[:CHUNKS]], outs[CHUNKS:]
 
 
 def centred(context, resid, w_out, b_out, ln_gain, w_proj):
@@ -427,87 +495,155 @@
     def outer(p):
         return p[0]
 
-    def out_block(side):
-        shape = (heads // 2, half)
-        return w_out, shape, lambda p, b: (run(p[1], b[0]), run(side(p), b[1]))
+    share = heads // 2, half // 2
+
+    def out_block(side, here=None):
+        return w_out, lambda p: (run(p[1], share[0]), run(side(p), half)), here
 
     def proj_block(side):
-        shape = (half // 2, out_cols)
-        return w_proj, shape, lambda p, b: (run(2 * side(p) + p[1], b[0]),)
-
-    def old_block(side):
-        shape = (images, part, half)
-        return resid, shape, lambda p, b: (slice(None), slice(None), run(side(p), b[2]))
-
-    def whole(array):
-        return array, array.shape, None
-
-    (sent,) = cuts(
-        place,
-        [(context, (images // 2, part, heads), lambda p, b: (run(1 - p[5], b[0]),))],
-    )
+        return w_proj, lambda p: (run(2 * side(p) + p[1], share[1]),), None
+
+    def old_blocks(side, start):
+        return [
+            (
+                resid,
+                lambda p, image=image: (image, slice(None), run(side(p), half)),
+                (slice(start + image * part, start + (image + 1) * part),),
+            )
+            for image in range(images)
+        ]
+
+    out_shape, proj_shape = (share[0], half), (share[1], out_cols)
+
+    def first(v):
+        return v, lambda p: (slice(0, share[0]),), None
+
+    old_shape = (images * part, half)
+
+    b_swap = lambda v: (out_shape, [first(v)])
+    b_cross = (proj_shape, [proj_block(outer)])
+    b_far = (proj_shape, [proj_block(outer)])
+    b_fold = (proj_shape, [proj_block(inner)])
+    if PLAN["full"]:
+        b_fold = ((half, out_cols), [(w_proj, lambda p: (run(inner(p), half),), None)])
+    b_old = (old_shape, old_blocks(outer, 0))
+    b_inner = (
+        (share[0] + images * part, half),
+        [out_block(inner, (slice(0, share[0]),)), *old_blocks(inner, share[0])],
+    )
+    perm = dict(cross=CROSS, far=FAR, fold=FOLD, old=FAR, inner=FOLD)
+    block = dict(cross=b_cross, far=b_far, fold=b_fold, old=b_old, inner=b_inner)
+    arrived = {}
+
+    def emitted(stage):
+        return [n for n in ("cross", "old", "inner", "far", "fold") if PLAN["at_" + n] == stage]
+
+    def launch(stage, made):
+        for n, v in zip(emitted(stage), made):
+            arrived[n] = along(v, "dp", perm[n])
+
+    def due(stage):
+        out = []
+        for n in ("cross", "old", "inner", "far", "fold", "swap_cross", "swap_far"):
+            if PLAN["due_" + n] == stage and n in arrived:
+                out += hops(arrived[n], PLAN["hop_" + n])
+        return out
+
+    sent = lax.dynamic_slice_in_dim(context, (1 - x) * (images // 2), images // 2, 0)
     got = along(sent, "mp", SWAP)
-    sent_outer, sent_cross = cuts(place, [out_block(outer), proj_block(outer)])
+    sent_outer, *made = cuts(
+        place,
+        [(out_shape, [out_block(outer)])] + [block[n] for n in emitted(0)],
+        *hops(sent, PLAN["first"]),
+    )
     fold_outer = along(sent_outer, "dp", FOLD)
-    proj_cross = along(sent_cross, "dp", CROSS)
+    launch(0, made)
 
     near, away = facing(place, context, got, sent_outer)
     pieces = [along(near, "dp", FOLD), near, along(away, "dp", CROSS), along(away, "dp", FAR)]
-    (sent_old,) = cuts(place, [old_block(outer)], near)
-    old_outer = along(sent_old, "dp", FOLD)
-
-    sent_inner, sent_old, sent_swap = cuts(
-        place, [out_block(inner), old_block(inner), whole(fold_outer)], near
-    )
-    fold_inner = along(sent_inner, "dp", FOLD)
-    old_inner = along(sent_old, "dp", FOLD)
+    if emitted(1):
+        launch(1, cuts(place, [block[n] for n in emitted(1)], near))
+
+    own, (sent_swap, *made) = ordered(
+        place, pieces, [b_swap(fold_outer)] + [block[n] for n in emitted(2)], *due(2), cost=PLAN["c_ord"]
+    )
     swap_outer = along(sent_swap, "groups", SWAP)
-
-    own = ordered(place, pieces, sent_inner, proj_cross)
-    far = [along(v, "mp", SWAP) for v in own]
+    launch(2, made)
+
+    far = [along(own[0], "mp", SWAP)]
+    sent, *made = cuts(
+        place,
+        [(own[1].shape, [(own[1], None, None)])] + [block[n] for n in emitted(3)],
+        far[0],
+        *due(3),
+        cost=PLAN["c_x1"],
+    )
+    far.append(along(sent, "mp", SWAP))
+    launch(3, made)
     near = [along(v, "sub", SWAP) for v in own]
     tokens_of = [(a, b, c, along(b, "sub", SWAP)) for a, b, c in zip(own, far, near)]
 
-    (join,) = cuts(place, [whole(swap_outer)], cost=JOIN)
-
-    def sends(k):
-        weights = (w_out, fold_outer, join, resid, old_outer, bias)
-        return attend(place, tokens_of[k], *weights, k, False, jnp.bfloat16)
-
-    def keeps(k, swapped):
-        weights = (w_out, fold_inner, swapped, resid, old_inner, bias)
-        return attend(place, tokens_of[k], *weights, k, True, jnp.float32)
-
-    (sent_swap,) = cuts(place, [whole(proj_cross)], join)
-    swap_cross = along(sent_swap, "groups", SWAP)
-    came = [sends(0)]
-    sent_far, sent_swap = cuts(place, [proj_block(outer), whole(fold_inner)], came[0])
-    proj_far = along(sent_far, "dp", FAR)
+    (join,) = cuts(
+        place, [(out_shape, [(swap_outer, None, None)])], *hops(swap_outer, PLAN["hop_join"]), cost=PLAN["join"]
+    )
+
+    def sends(k, *after):
+        weights = (w_out, fold_outer, join, resid, [], bias, k, False, jnp.bfloat16)
+        return attend(place, tokens_of[k], *weights, *after, cost=PLAN["c_send"])
+
+    def keeps(k, *after):
+        others = [arrived["inner"], arrived["old"]]
+        weights = (w_out, arrived["inner"], swap_inner, resid, others, bias, k, True, jnp.float32)
+        return attend(place, tokens_of[k], *weights, *after, cost=PLAN["c_keep"])
+
+    (sent_swap,) = cuts(
+        place, [(proj_shape, [(arrived["cross"], None, None)])], *([join] if PLAN["xjoin"] else []), cost=PLAN["c_xc"]
+    )
+    arrived["swap_cross"] = along(sent_swap, "groups", SWAP)
+    came = [sends(0, *due(4)), sends(1, *due(5))]
+    if PLAN["at_far"] < 6:
+        arrived["swap_far"] = along(arrived["far"], "groups", SWAP)
+    more = [came[1]] if emitted(6) or PLAN["k3"] else []
+    sent_swap, *made = cuts(
+        place, [b_swap(arrived["inner"])] + [block[n] for n in emitted(6)], *more, *due(6), cost=PLAN["c_k3"]
+    )
     swap_inner = along(sent_swap, "groups", SWAP)
-    came += [sends(k) for k in range(1, CHUNKS)]
+    launch(6, made)
     came = [along(v, "dp", CROSS) for v in came]
 
-    (sent_fold,) = cuts(place, [proj_block(inner)], swap_inner)
-    proj_fold = along(sent_fold, "dp", FOLD)
-    kept = [keeps(k, swap_inner) for k in range(CHUNKS)]
+    here = [hops(v, h) for v, h in zip(came, (PLAN["h0"], PLAN["h1"]))]
+    kept = [keeps(0, *due(7))]
+    if emitted(7):
+        launch(7, cuts(place, [block[n] for n in emitted(7)], kept[0]))
+    if "swap_far" not in arrived:
+        arrived["swap_far"] = along(arrived["far"], "groups", SWAP)
+    kept.append(keeps(1, *due(8)))
 
     scaled = []
     for k in range(CHUNKS):
-        near = scale_up(place, kept[k], came[k], gain, sent_fold)
+        near = scale_up(place, kept[k], came[k], gain, *here[k], *due(9 + k))
         far = along(near, "mp", SWAP)
         scaled.append([near, along(near, "sub", SWAP), far, along(far, "sub", SWAP)])
 
+    sent_swap, ready = arrived["fold"], []
+    if not PLAN["full"]:
+        if PLAN["y_fold"] >= 0:
+            (sent_swap,) = cuts(
+                place, [(proj_shape, [(sent_swap, None, None)])], *hops(sent_swap, PLAN["y_fold"])
+            )
+        swap_fold = along(sent_swap, "groups", SWAP)
+        ready = hops(swap_fold, PLAN["hop_swap_fold"])
     weights = [
-        proj_fold,
-        along(proj_fold, "groups", SWAP),
-        proj_cross,
-        swap_cross,
-        proj_far,
-        along(proj_far, "groups", SWAP),
+        *([arrived["fold"]] if PLAN["full"] else [arrived["fold"], swap_fold]),
+        arrived["cross"],
+        arrived["swap_cross"],
+        arrived["far"],
+        arrived["swap_far"],
     ]
+    ready += due(11)
     parts = []
     for k in range(CHUNKS):
-        spread, own, cross, leap = project_up(place, scaled[k], w_proj, weights, gain)
+        spread, own, cross, leap = project_up(place, scaled[k], w_proj, weights, gain, *ready)
         leap = along(leap, "dp", LEAP)
         cross = along(cross, "dp", CROSS)
         spread = along(spread, "dp", SPREAD)

time: 196 us -> 181 us (0.923)
  starting transfers between devices: 60.5 us -> 48 us
  Pallas kernels: 37.2 us -> 34.8 us
    ppermute x36 -> x37, starting transfers between devices: 60.5 us -> 48 us  [along(): return lax.ppermute(value, axis, pairs)]
    pallas_call x19 -> x16, Pallas kernels: 37.2 us -> 34.8 us  [call(): pl.pallas_call(kernel, in_specs=[SMEM, *ins], out_specs=jax.tree.map(lamb...]
    ppermute x36 -> x37, waiting for transfers between devices: 93.2 us -> 92.6 us  [along(): return lax.ppermute(value, axis, pairs)]
  transfers between devices with their start and end apart: 36 -> 37, of which waited for: 11 -> 17; matrix products, arithmetic and copies ran while one was open for 0% -> 0% of each run, Pallas kernels for 18% -> 17%
where the time goes in v6:
time: 181 us
  waiting for transfers between devices  92.6 us (51%)
  starting transfers between devices  48 us (27%)
  Pallas kernels  34.8 us (19%)
  local copies, waits for them, and re-layouts  4.63 us (3%)
    ppermute x37, waiting for transfers between devices, along(): return lax.ppermute(value, axis, pairs)  92.6 us
    ppermute x37, starting transfers between devices, along(): return lax.ppermute(value, axis, pairs)  48 us
    pallas_call x16, Pallas kernels, call(): pl.pallas_call(kernel, in_specs=[SMEM, *ins], out_specs=jax.tree.map(lamb...  34.8 us
  transfers between devices with their start and end apart: 37, of which 17 were waited for; matrix products, arithmetic and copies ran while one was open for 0% of the time, Pallas kernels for 17%

profile of v6, /device:TPU:0, one launch (start us, length us, event | category | flops | bytes accessed | tf_op | source)
XLA Modules:
  0.0 180.5 jit_solution(8877418266830204091)
XLA Ops:
  1.0 1.7 copy-done.1
  2.7 1.9 %copy-done.3 = bf16[1536,1024]{1,0:T(8,128)(2,1)S(1)} copy-done((bf16[1536,1024]{1,0:T(8,128)(2,1)S(1)}, bf16[1536,1024]{1,0:T(8,128)(2,1)}, u32[]{:S(2)}) %copy-start.3) | copy-done | bytes 3145752
  6.1 7.7 %collective-permute-start.4 = (bf16[384,768]{1,0:T(8,128)(2,1)S(1)}, bf16[384,768]{1,0:T(8,128)(2,1)S(1)}, u32[]{:S(2)}, u32[]{:S(2)}) collective-permute-start(bf16[384,768]{1,0:T(8,128)(2,1)S(1)} %get-tuple-element.25.refs_0_), channel_id=1, source_target_pairs={{0,4},{12,8},{1,5},{13,9},{2,6},{14,10},{3,7},{15,11},{16,20},{28,... | collective-permute-start | bytes 1769480 | tf_op jit(solution)/shard_map/ppermute | solution.py:102
  13.9 1.6 collective-permute-start
  15.4 4.6 %collective-permute-done.got = bf16[2,64,768]{2,1,0:T(8,128)(2,1)S(1)} collective-permute-done((bf16[2,64,768]{2,1,0:T(8,128)(2,1)S(1)}, bf16[2,64,768]{2,1,0:T(8,128)(2,1)S(1)}, u32[]{:S(2)}, u32[]{:S(2)}) %collective-permute-start) | collective-permute-done | bytes 196640 | tf_op jit(solution)/shard_map/ppermute | solution.py:102
  22.7 1.6 collective-permute-start.3
  24.9 6.9 %collective-permute-done.1.refs_0_ = bf16[2,64,768]{2,1,0:T(8,128)(2,1)S(1)} collective-permute-done((bf16[2,64,768]{2,1,0:T(8,128)(2,1)S(1)}, bf16[2,64,768]{2,1,0:T(8,128)(2,1)S(1)}, u32[]{:S(2)}, u32[]{:S(2)}) %collective-permute-start.1) | collective-permute-done | bytes 196640 | tf_op jit(solution)/shard_map/ppermute | solution.py:102
  31.8 2.8 %collective-permute-done.3.refs_3_ = bf16[2,64,768]{2,1,0:T(8,128)(2,1)S(1)} collective-permute-done((bf16[2,64,768]{2,1,0:T(8,128)(2,1)S(1)}, bf16[2,64,768]{2,1,0:T(8,128)(2,1)S(1)}, u32[]{:S(2)}, u32[]{:S(2)}) %collective-permute-start.3) | collective-permute-done | bytes 196640 | tf_op jit(solution)/shard_map/ppermute | solution.py:102
  36.0 1.6 collective-permute-start.10
  37.5 6.4 %collective-permute-start.13 = (bf16[384,1024]{1,0:T(8,128)(2,1)S(1)}, bf16[384,1024]{1,0:T(8,128)(2,1)S(1)}, u32[]{:S(2)}, u32[]{:S(2)}) collective-permute-start(bf16[384,1024]{1,0:T(8,128)(2,1)S(1)} %get-tuple-element.33), channel_id=1, source_target_pairs={{0,8},{12,4},{1,9},{13,5},{2,10},{14,6},{3,11},{15,7},{16,24},{28,... | collective-permute-start | bytes 2359304 | tf_op jit(solution)/shard_map/ppermute | solution.py:102
  45.5 6.6 %collective-permute-done.6.refs_11_.far = bf16[256,768]{1,0:T(8,128)(2,1)S(1)} collective-permute-done((bf16[256,768]{1,0:T(8,128)(2,1)S(1)}, bf16[256,768]{1,0:T(8,128)(2,1)S(1)}, u32[]{:S(2)}, u32[]{:S(2)}) %collective-permute-start.6) | collective-permute-done | bytes 393248 | tf_op jit(solution)/shard_map/ppermute | solution.py:102
  53.2 1.6 collective-permute-start.25
  58.0 3.9 %collective-permute-done.13.rest_3_ = bf16[384,1024]{1,0:T(8,128)(2,1)S(1)} collective-permute-done((bf16[384,1024]{1,0:T(8,128)(2,1)S(1)}, bf16[384,1024]{1,0:T(8,128)(2,1)S(1)}, u32[]{:S(2)}, u32[]{:S(2)}) %collective-permute-start.13) | collective-permute-done | bytes 786464 | tf_op jit(solution)/shard_map/ppermute | solution.py:102
  64.3 2.6 %shard_map.76 = bf16[512,768]{1,0:T(8,128)(2,1)S(1)} custom-call(s32[6]{0:T(128)S(1)} %stack.31.p, bf16[256,768]{1,0:T(8,128)(2,1)S(1)} %bitcast.12, bf16[256,768]{1,0:T(8,128)(2,1)S(1)} %collective-permute-done.25.far, bf16[256,768]{1,0:T(8,128)(2,1)S(1)} %collective-permute-done.26.near, bf16[256,768]{1,0:T(8,128)(2,1)S(1)} %collective-permute-done.27.both, ...), custom_call_target="tpu_custom_call" | custom-call | flops 1 | bytes 1 | tf_op jit(solution)/shard_map/pallas_call | solution.py:134
  66.9 9.7 %collective-permute-done.11.rest_2_ = bf16[384,1024]{1,0:T(8,128)(2,1)S(1)} collective-permute-done((bf16[384,1024]{1,0:T(8,128)(2,1)S(1)}, bf16[384,1024]{1,0:T(8,128)(2,1)S(1)}, u32[]{:S(2)}, u32[]{:S(2)}) %collective-permute-start.11) | collective-permute-done | bytes 786464 | tf_op jit(solution)/shard_map/ppermute | solution.py:102
  77.3 1.9 %collective-permute-done.9.refs_0_.refs_1_.fold = bf16[640,768]{1,0:T(8,128)(2,1)S(1)} collective-permute-done((bf16[640,768]{1,0:T(8,128)(2,1)S(1)}, bf16[640,768]{1,0:T(8,128)(2,1)S(1)}, u32[]{:S(2)}, u32[]{:S(2)}) %collective-permute-start.9) | collective-permute-done | bytes 983072 | tf_op jit(solution)/shard_map/ppermute | solution.py:102
  80.4 9.6 %collective-permute-done.14.refs_3_.rest_4_ = bf16[384,1024]{1,0:T(8,128)(2,1)S(1)} collective-permute-done((bf16[384,1024]{1,0:T(8,128)(2,1)S(1)}, bf16[384,1024]{1,0:T(8,128)(2,1)S(1)}, u32[]{:S(2)}, u32[]{:S(2)}) %collective-permute-start.14) | collective-permute-done | bytes 786464 | tf_op jit(solution)/shard_map/ppermute | solution.py:102
  91.2 2.6 %shard_map.72 = bf16[512,768]{1,0:T(8,128)(2,1)S(1)} custom-call(s32[6]{0:T(128)S(1)} %stack.31.p, bf16[256,768]{1,0:T(8,128)(2,1)S(1)} %bitcast.16, bf16[256,768]{1,0:T(8,128)(2,1)S(1)} %collective-permute-done.6.refs_11_.far, bf16[256,768]{1,0:T(8,128)(2,1)S(1)} %collective-permute-done.7.near, bf16[256,768]{1,0:T(8,128)(2,1)S(1)} %collective-permute-done.8.both, ...), custom_call_target="tpu_custom_call" | custom-call | flops 1 | bytes 1 | tf_op jit(solution)/shard_map/pallas_call | solution.py:134
  94.5 3.2 %collective-permute-start.16 = (bf16[256,768]{1,0:T(8,128)(2,1)S(1)}, bf16[256,768]{1,0:T(8,128)(2,1)S(1)}, u32[]{:S(2)}, u32[]{:S(2)}) collective-permute-start(bf16[256,768]{1,0:T(8,128)(2,1)S(1)} %get-tuple-element.34), channel_id=1, source_target_pairs={{0,8},{12,4},{1,9},{13,5},{2,10},{14,6},{3,11},{15,7},{16,24},{28,... | collective-permute-start | bytes 1179656 | tf_op jit(solution)/shard_map/ppermute | solution.py:102
  99.2 3.9 %collective-permute-done.16.refs_1_.refs_2_ = bf16[256,768]{1,0:T(8,128)(2,1)S(1)} collective-permute-done((bf16[256,768]{1,0:T(8,128)(2,1)S(1)}, bf16[256,768]{1,0:T(8,128)(2,1)S(1)}, u32[]{:S(2)}, u32[]{:S(2)}) %collective-permute-start.16) | collective-permute-done | bytes 393248 | tf_op jit(solution)/shard_map/ppermute | solution.py:102
  103.0 2.8 %shard_map.75.keeps = f32[512,768]{1,0:T(8,128)S(1)} custom-call(s32[6]{0:T(128)S(1)} %stack.31.p, bf16[256,768]{1,0:T(8,128)(2,1)S(1)} %bitcast.13, bf16[256,768]{1,0:T(8,128)(2,1)S(1)} %collective-permute-done.25.far, bf16[256,768]{1,0:T(8,128)(2,1)S(1)} %collective-permute-done.26.near, bf16[256,768]{1,0:T(8,128)(2,1)S(1)} %collective-permute-done.27.both, ...), custom_call_target="tpu_custom_call" | custom-call | flops 1 | bytes 1 | tf_op jit(solution)/shard_map/pallas_call | solution.py:134
  105.9 1.7 shard_map.77.s0
  109.0 5.7 %collective-permute-start.21 = (bf16[768,1024]{1,0:T(8,128)(2,1)S(1)}, bf16[768,1024]{1,0:T(8,128)(2,1)S(1)}, u32[]{:S(2)}, u32[]{:S(2)}) collective-permute-start(bf16[768,1024]{1,0:T(8,128)(2,1)S(1)} %get-tuple-element.35), channel_id=1, source_target_pairs={{0,4},{12,8},{1,5},{13,9},{2,6},{14,10},{3,7},{15,11},{16,20},{28,... | collective-permute-start | bytes 4718600 | tf_op jit(solution)/shard_map/ppermute | solution.py:102
  114.8 2.8 %shard_map.71.keeps = f32[512,768]{1,0:T(8,128)S(1)} custom-call(s32[6]{0:T(128)S(1)} %stack.31.p, bf16[256,768]{1,0:T(8,128)(2,1)S(1)} %bitcast.17, bf16[256,768]{1,0:T(8,128)(2,1)S(1)} %collective-permute-done.6.refs_11_.far, bf16[256,768]{1,0:T(8,128)(2,1)S(1)} %collective-permute-done.7.near, bf16[256,768]{1,0:T(8,128)(2,1)S(1)} %collective-permute-done.8.both, ...), custom_call_target="tpu_custom_call" | custom-call | flops 1 | bytes 1 | tf_op jit(solution)/shard_map/pallas_call | solution.py:134
  117.6 1.7 shard_map.73.s0
  120.0 8.6 %collective-permute-done.32.s2 = bf16[528,768]{1,0:T(8,128)(2,1)S(1)} collective-permute-done((bf16[528,768]{1,0:T(8,128)(2,1)S(1)}, bf16[528,768]{1,0:T(8,128)(2,1)S(1)}, u32[]{:S(2)}, u32[]{:S(2)}) %collective-permute-start.32) | collective-permute-done | bytes 811040 | tf_op jit(solution)/shard_map/ppermute | solution.py:102
  129.1 12.3 %collective-permute-done.19.s2 = bf16[528,768]{1,0:T(8,128)(2,1)S(1)} collective-permute-done((bf16[528,768]{1,0:T(8,128)(2,1)S(1)}, bf16[528,768]{1,0:T(8,128)(2,1)S(1)}, u32[]{:S(2)}, u32[]{:S(2)}) %collective-permute-start.19) | collective-permute-done | bytes 811040 | tf_op jit(solution)/shard_map/ppermute | solution.py:102
  141.5 6.3 %shard_map.78 = (bf16[144,1024]{1,0:T(8,128)(2,1)S(1)}, bf16[144,1024]{1,0:T(8,128)(2,1)S(1)}, bf16[144,1024]{1,0:T(8,128)(2,1)S(1)}, bf16[144,1024]{1,0:T(8,128)(2,1)S(1)}) custom-call(s32[6]{0:T(128)S(1)} %stack.31.p, bf16[528,768]{1,0:T(8,128)(2,1)S(1)} %shard_map.77.s0, bf16[528,768]{1,0:T(8,128)(2,1)S(1)} %collective-permute-done.31.s1, ...), custom_call_target="tpu_custom_call" | custom-call | flops 1 | bytes 1 | tf_op jit(solution)/shard_map/pallas_call | solution.py:134
  151.1 6.3 %shard_map.74 = (bf16[144,1024]{1,0:T(8,128)(2,1)S(1)}, bf16[144,1024]{1,0:T(8,128)(2,1)S(1)}, bf16[144,1024]{1,0:T(8,128)(2,1)S(1)}, bf16[144,1024]{1,0:T(8,128)(2,1)S(1)}) custom-call(s32[6]{0:T(128)S(1)} %stack.31.p, bf16[528,768]{1,0:T(8,128)(2,1)S(1)} %shard_map.73.s0, bf16[528,768]{1,0:T(8,128)(2,1)S(1)} %collective-permute-done.18.s1, ...), custom_call_target="tpu_custom_call" | custom-call | flops 1 | bytes 1 | tf_op jit(solution)/shard_map/pallas_call | solution.py:134
  160.8 5.7 %collective-permute-done.35.refs_6_ = bf16[144,1024]{1,0:T(8,128)(2,1)S(1)} collective-permute-done((bf16[144,1024]{1,0:T(8,128)(2,1)S(1)}, bf16[144,1024]{1,0:T(8,128)(2,1)S(1)}, u32[]{:S(2)}, u32[]{:S(2)}) %collective-permute-start.35) | collective-permute-done | bytes 294944 | tf_op jit(solution)/shard_map/ppermute | solution.py:102
  166.5 12.3 %collective-permute-done.23.refs_2_ = bf16[144,1024]{1,0:T(8,128)(2,1)S(1)} collective-permute-done((bf16[144,1024]{1,0:T(8,128)(2,1)S(1)}, bf16[144,1024]{1,0:T(8,128)(2,1)S(1)}, u32[]{:S(2)}, u32[]{:S(2)}) %collective-permute-start.23) | collective-permute-done | bytes 294944 | tf_op jit(solution)/shard_map/ppermute | solution.py:102
  178.8 1.7 shard_map.79
  (79 shorter events, 30.0 us)
Async XLA Ops:
  5.3 29.3 %collective-permute-start.5 = (bf16[384,1024]{1,0:T(8,128)(2,1)S(1)}, bf16[384,1024]{1,0:T(8,128)(2,1)S(1)}, u32[]{:S(2)}, u32[]{:S(2)}) collective-permute-start(bf16[384,1024]{1,0:T(8,128)(2,1)S(1)} %get-tuple-element.28), channel_id=1, source_target_pairs={{4,8},{8,4},{5,9},{9,5},{6,10},{10,6},{7,11},{11,7},{20,24},{24,20... | collective-permute-start | bytes 2359304 | tf_op jit(solution)/shard_map/ppermute | solution.py:102
  6.1 28.5 %collective-permute-start.4 = (bf16[384,768]{1,0:T(8,128)(2,1)S(1)}, bf16[384,768]{1,0:T(8,128)(2,1)S(1)}, u32[]{:S(2)}, u32[]{:S(2)}) collective-permute-start(bf16[384,768]{1,0:T(8,128)(2,1)S(1)} %get-tuple-element.25.refs_0_), channel_id=1, source_target_pairs={{0,4},{12,8},{1,5},{13,9},{2,6},{14,10},{3,7},{15,11},{16,20},{28,... | collective-permute-start | bytes 1769480 | tf_op jit(solution)/shard_map/ppermute | solution.py:102
  21.1 10.7 %collective-permute-start.1 = (bf16[2,64,768]{2,1,0:T(8,128)(2,1)S(1)}, bf16[2,64,768]{2,1,0:T(8,128)(2,1)S(1)}, u32[]{:S(2)}, u32[]{:S(2)}) collective-permute-start(bf16[2,64,768]{2,1,0:T(8,128)(2,1)S(1)} %get-tuple-element.26.refs_1_), channel_id=1, source_target_pairs={{0,4},{12,8},{1,5},{13,9},{2,6},{14,10},{3,7},{15,11},{16,20},{28,... | collective-permute-start | bytes 589832 | tf_op jit(solution)/shard_map/ppermute | solution.py:102
  22.7 11.9 %collective-permute-start.3 = (bf16[2,64,768]{2,1,0:T(8,128)(2,1)S(1)}, bf16[2,64,768]{2,1,0:T(8,128)(2,1)S(1)}, u32[]{:S(2)}, u32[]{:S(2)}) collective-permute-start(bf16[2,64,768]{2,1,0:T(8,128)(2,1)S(1)} %get-tuple-element.27), channel_id=1, source_target_pairs={{0,8},{12,4},{1,9},{13,5},{2,10},{14,6},{3,11},{15,7},{16,24},{28,... | collective-permute-start | bytes 589832 | tf_op jit(solution)/shard_map/ppermute | solution.py:102
  24.3 10.3 %collective-permute-start.2 = (bf16[2,64,768]{2,1,0:T(8,128)(2,1)S(1)}, bf16[2,64,768]{2,1,0:T(8,128)(2,1)S(1)}, u32[]{:S(2)}, u32[]{:S(2)}) collective-permute-start(bf16[2,64,768]{2,1,0:T(8,128)(2,1)S(1)} %get-tuple-element.27), channel_id=1, source_target_pairs={{4,8},{8,4},{5,9},{9,5},{6,10},{10,6},{7,11},{11,7},{20,24},{24,20... | collective-permute-start | bytes 589832 | tf_op jit(solution)/shard_map/ppermute | solution.py:102
  36.0 18.8 %collective-permute-start.10 = (bf16[384,768]{1,0:T(8,128)(2,1)S(1)}, bf16[384,768]{1,0:T(8,128)(2,1)S(1)}, u32[]{:S(2)}, u32[]{:S(2)}) collective-permute-start(bf16[384,768]{1,0:T(8,128)(2,1)S(1)} %get-tuple-element.32), channel_id=1, source_target_pairs={{0,16},{16,0},{1,17},{17,1},{2,18},{18,2},{3,19},{19,3},{4,20},{20... | collective-permute-start | bytes 1769480 | tf_op jit(solution)/shard_map/ppermute | solution.py:102
  37.5 24.3 %collective-permute-start.13 = (bf16[384,1024]{1,0:T(8,128)(2,1)S(1)}, bf16[384,1024]{1,0:T(8,128)(2,1)S(1)}, u32[]{:S(2)}, u32[]{:S(2)}) collective-permute-start(bf16[384,1024]{1,0:T(8,128)(2,1)S(1)} %get-tuple-element.33), channel_id=1, source_target_pairs={{0,8},{12,4},{1,9},{13,5},{2,10},{14,6},{3,11},{15,7},{16,24},{28,... | collective-permute-start | bytes 2359304 | tf_op jit(solution)/shard_map/ppermute | solution.py:102
  43.9 8.1 %collective-permute-start.6 = (bf16[256,768]{1,0:T(8,128)(2,1)S(1)}, bf16[256,768]{1,0:T(8,128)(2,1)S(1)}, u32[]{:S(2)}, u32[]{:S(2)}) collective-permute-start(bf16[256,768]{1,0:T(8,128)(2,1)S(1)} %bitcast.14), channel_id=1, source_target_pairs={{0,2},{2,0},{1,3},{3,1},{4,6},{6,4},{5,7},{7,5},{8,10},{10,8},{9,1... | collective-permute-start | bytes 1179656 | tf_op jit(solution)/shard_map/ppermute | solution.py:102
  53.2 8.7 %collective-permute-start.25 = (bf16[256,768]{1,0:T(8,128)(2,1)S(1)}, bf16[256,768]{1,0:T(8,128)(2,1)S(1)}, u32[]{:S(2)}, u32[]{:S(2)}) collective-permute-start(bf16[256,768]{1,0:T(8,128)(2,1)S(1)} %get-tuple-element.40), channel_id=1, source_target_pairs={{0,2},{2,0},{1,3},{3,1},{4,6},{6,4},{5,7},{7,5},{8,10},{10,8},{9,1... | collective-permute-start | bytes 1179656 | tf_op jit(solution)/shard_map/ppermute | solution.py:102
  56.1 20.5 %collective-permute-start.11 = (bf16[384,1024]{1,0:T(8,128)(2,1)S(1)}, bf16[384,1024]{1,0:T(8,128)(2,1)S(1)}, u32[]{:S(2)}, u32[]{:S(2)}) collective-permute-start(bf16[384,1024]{1,0:T(8,128)(2,1)S(1)} %shard_map.69), channel_id=1, source_target_pairs={{0,16},{16,0},{1,17},{17,1},{2,18},{18,2},{3,19},{19,3},{4,20},{20... | collective-permute-start | bytes 2359304 | tf_op jit(solution)/shard_map/ppermute | solution.py:102
  56.6 22.6 %collective-permute-start.9 = (bf16[640,768]{1,0:T(8,128)(2,1)S(1)}, bf16[640,768]{1,0:T(8,128)(2,1)S(1)}, u32[]{:S(2)}, u32[]{:S(2)}) collective-permute-start(bf16[640,768]{1,0:T(8,128)(2,1)S(1)} %get-tuple-element.31), channel_id=1, source_target_pairs={{0,4},{12,8},{1,5},{13,9},{2,6},{14,10},{3,7},{15,11},{16,20},{28,... | collective-permute-start | bytes 2949128 | tf_op jit(solution)/shard_map/ppermute | solution.py:102
  61.9 28.1 %collective-permute-start.14 = (bf16[384,1024]{1,0:T(8,128)(2,1)S(1)}, bf16[384,1024]{1,0:T(8,128)(2,1)S(1)}, u32[]{:S(2)}, u32[]{:S(2)}) collective-permute-start(bf16[384,1024]{1,0:T(8,128)(2,1)S(1)} %collective-permute-done.13.rest_3_), channel_id=1, source_target_pairs={{0,16},{16,0},{1,17},{17,1},{2,18},{18,2},{3,19},{19,3},{4,20},{20... | collective-permute-start | bytes 2359304 | tf_op jit(solution)/shard_map/ppermute | solution.py:102
  63.6 27.6 %collective-permute-start.7 = (bf16[256,768]{1,0:T(8,128)(2,1)S(1)}, bf16[256,768]{1,0:T(8,128)(2,1)S(1)}, u32[]{:S(2)}, u32[]{:S(2)}) collective-permute-start(bf16[256,768]{1,0:T(8,128)(2,1)S(1)} %bitcast.15), channel_id=1, source_target_pairs={{0,1},{1,0},{2,3},{3,2},{4,5},{5,4},{6,7},{7,6},{8,9},{9,8},{10,11... | collective-permute-start | bytes 1179656 | tf_op jit(solution)/shard_map/ppermute | solution.py:102
  64.2 27.1 %collective-permute-start.8 = (bf16[256,768]{1,0:T(8,128)(2,1)S(1)}, bf16[256,768]{1,0:T(8,128)(2,1)S(1)}, u32[]{:S(2)}, u32[]{:S(2)}) collective-permute-start(bf16[256,768]{1,0:T(8,128)(2,1)S(1)} %collective-permute-done.6.refs_11_.far), channel_id=1, source_target_pairs={{0,1},{1,0},{2,3},{3,2},{4,5},{5,4},{6,7},{7,6},{8,9},{9,8},{10,11... | collective-permute-start | bytes 1179656 | tf_op jit(solution)/shard_map/ppermute | solution.py:102
  76.6 21.1 %collective-permute-start.28 = (bf16[512,768]{1,0:T(8,128)(2,1)S(1)}, bf16[512,768]{1,0:T(8,128)(2,1)S(1)}, u32[]{:S(2)}, u32[]{:S(2)}) collective-permute-start(bf16[512,768]{1,0:T(8,128)(2,1)S(1)} %shard_map.76), channel_id=1, source_target_pairs={{4,8},{8,4},{5,9},{9,5},{6,10},{10,6},{7,11},{11,7},{20,24},{24,20... | collective-permute-start | bytes 2359304 | tf_op jit(solution)/shard_map/ppermute | solution.py:102
  90.6 12.4 %collective-permute-start.15 = (bf16[384,768]{1,0:T(8,128)(2,1)S(1)}, bf16[384,768]{1,0:T(8,128)(2,1)S(1)}, u32[]{:S(2)}, u32[]{:S(2)}) collective-permute-start(bf16[384,768]{1,0:T(8,128)(2,1)S(1)} %shard_map.70), channel_id=1, source_target_pairs={{0,16},{16,0},{1,17},{17,1},{2,18},{18,2},{3,19},{19,3},{4,20},{20... | collective-permute-start | bytes 1769480 | tf_op jit(solution)/shard_map/ppermute | solution.py:102
  93.8 23.8 %collective-permute-start.17 = (bf16[512,768]{1,0:T(8,128)(2,1)S(1)}, bf16[512,768]{1,0:T(8,128)(2,1)S(1)}, u32[]{:S(2)}, u32[]{:S(2)}) collective-permute-start(bf16[512,768]{1,0:T(8,128)(2,1)S(1)} %shard_map.72), channel_id=1, source_target_pairs={{4,8},{8,4},{5,9},{9,5},{6,10},{10,6},{7,11},{11,7},{20,24},{24,20... | collective-permute-start | bytes 2359304 | tf_op jit(solution)/shard_map/ppermute | solution.py:102
  94.5 8.5 %collective-permute-start.16 = (bf16[256,768]{1,0:T(8,128)(2,1)S(1)}, bf16[256,768]{1,0:T(8,128)(2,1)S(1)}, u32[]{:S(2)}, u32[]{:S(2)}) collective-permute-start(bf16[256,768]{1,0:T(8,128)(2,1)S(1)} %get-tuple-element.34), channel_id=1, source_target_pairs={{0,8},{12,4},{1,9},{13,5},{2,10},{14,6},{3,11},{15,7},{16,24},{28,... | collective-permute-start | bytes 1179656 | tf_op jit(solution)/shard_map/ppermute | solution.py:102
  99.0 6.8 %collective-permute-start.30 = (bf16[16,128]{1,0:T(8,128)(2,1)S(1)}, bf16[16,128]{1,0:T(8,128)(2,1)S(1)}, u32[]{:S(2)}, u32[]{:S(2)}) collective-permute-start(bf16[16,128]{1,0:T(8,128)(2,1)S(1)} %collective-permute-done.29), channel_id=1, source_target_pairs={{0,1},{1,0},{2,3},{3,2},{4,5},{5,4},{6,7},{7,6},{8,9},{9,8},{10,11... | collective-permute-start | bytes 12296 | tf_op jit(solution)/shard_map/ppermute | solution.py:102
  107.6 21.1 %collective-permute-start.32 = (bf16[528,768]{1,0:T(8,128)(2,1)S(1)}, bf16[528,768]{1,0:T(8,128)(2,1)S(1)}, u32[]{:S(2)}, u32[]{:S(2)}) collective-permute-start(bf16[528,768]{1,0:T(8,128)(2,1)S(1)} %shard_map.77.s0), channel_id=1, source_target_pairs={{0,2},{2,0},{1,3},{3,1},{4,6},{6,4},{5,7},{7,5},{8,10},{10,8},{9,1... | collective-permute-start | bytes 2433032 | tf_op jit(solution)/shard_map/ppermute | solution.py:102
  109.0 32.4 %collective-permute-start.21 = (bf16[768,1024]{1,0:T(8,128)(2,1)S(1)}, bf16[768,1024]{1,0:T(8,128)(2,1)S(1)}, u32[]{:S(2)}, u32[]{:S(2)}) collective-permute-start(bf16[768,1024]{1,0:T(8,128)(2,1)S(1)} %get-tuple-element.35), channel_id=1, source_target_pairs={{0,4},{12,8},{1,5},{13,9},{2,6},{14,10},{3,7},{15,11},{16,20},{28,... | collective-permute-start | bytes 4718600 | tf_op jit(solution)/shard_map/ppermute | solution.py:102
  119.3 22.1 %collective-permute-start.19 = (bf16[528,768]{1,0:T(8,128)(2,1)S(1)}, bf16[528,768]{1,0:T(8,128)(2,1)S(1)}, u32[]{:S(2)}, u32[]{:S(2)}) collective-permute-start(bf16[528,768]{1,0:T(8,128)(2,1)S(1)} %shard_map.73.s0), channel_id=1, source_target_pairs={{0,2},{2,0},{1,3},{3,1},{4,6},{6,4},{5,7},{7,5},{8,10},{10,8},{9,1... | collective-permute-start | bytes 2433032 | tf_op jit(solution)/shard_map/ppermute | solution.py:102
  120.0 21.5 %collective-permute-start.31 = (bf16[528,768]{1,0:T(8,128)(2,1)S(1)}, bf16[528,768]{1,0:T(8,128)(2,1)S(1)}, u32[]{:S(2)}, u32[]{:S(2)}) collective-permute-start(bf16[528,768]{1,0:T(8,128)(2,1)S(1)} %shard_map.77.s0), channel_id=1, source_target_pairs={{0,1},{1,0},{2,3},{3,2},{4,5},{5,4},{6,7},{7,6},{8,9},{9,8},{10,11... | collective-permute-start | bytes 2433032 | tf_op jit(solution)/shard_map/ppermute | solution.py:102
  128.6 12.8 %collective-permute-start.33 = (bf16[528,768]{1,0:T(8,128)(2,1)S(1)}, bf16[528,768]{1,0:T(8,128)(2,1)S(1)}, u32[]{:S(2)}, u32[]{:S(2)}) collective-permute-start(bf16[528,768]{1,0:T(8,128)(2,1)S(1)} %collective-permute-done.32.s2), channel_id=1, source_target_pairs={{0,1},{1,0},{2,3},{3,2},{4,5},{5,4},{6,7},{7,6},{8,9},{9,8},{10,11... | collective-permute-start | bytes 2433032 | tf_op jit(solution)/shard_map/ppermute | solution.py:102
  128.6 22.5 %collective-permute-start.18 = (bf16[528,768]{1,0:T(8,128)(2,1)S(1)}, bf16[528,768]{1,0:T(8,128)(2,1)S(1)}, u32[]{:S(2)}, u32[]{:S(2)}) collective-permute-start(bf16[528,768]{1,0:T(8,128)(2,1)S(1)} %shard_map.73.s0), channel_id=1, source_target_pairs={{0,1},{1,0},{2,3},{3,2},{4,5},{5,4},{6,7},{7,6},{8,9},{9,8},{10,11... | collective-permute-start | bytes 2433032 | tf_op jit(solution)/shard_map/ppermute | solution.py:102
  141.5 9.7 %collective-permute-start.20 = (bf16[528,768]{1,0:T(8,128)(2,1)S(1)}, bf16[528,768]{1,0:T(8,128)(2,1)S(1)}, u32[]{:S(2)}, u32[]{:S(2)}) collective-permute-start(bf16[528,768]{1,0:T(8,128)(2,1)S(1)} %collective-permute-done.19.s2), channel_id=1, source_target_pairs={{0,1},{1,0},{2,3},{3,2},{4,5},{5,4},{6,7},{7,6},{8,9},{9,8},{10,11... | collective-permute-start | bytes 2433032 | tf_op jit(solution)/shard_map/ppermute | solution.py:102
  147.8 11.6 %collective-permute-start.34 = (bf16[144,1024]{1,0:T(8,128)(2,1)S(1)}, bf16[144,1024]{1,0:T(8,128)(2,1)S(1)}, u32[]{:S(2)}, u32[]{:S(2)}) collective-permute-start(bf16[144,1024]{1,0:T(8,128)(2,1)S(1)} %get-tuple-element.42), channel_id=1, source_target_pairs={{4,8},{8,4},{5,9},{9,5},{6,10},{10,6},{7,11},{11,7},{20,24},{24,20... | collective-permute-start | bytes 884744 | tf_op jit(solution)/shard_map/ppermute | solution.py:102
  148.5 18.0 %collective-permute-start.35 = (bf16[144,1024]{1,0:T(8,128)(2,1)S(1)}, bf16[144,1024]{1,0:T(8,128)(2,1)S(1)}, u32[]{:S(2)}, u32[]{:S(2)}) collective-permute-start(bf16[144,1024]{1,0:T(8,128)(2,1)S(1)} %get-tuple-element.43), channel_id=1, source_target_pairs={{4,0},{8,12},{5,1},{9,13},{6,2},{10,14},{7,3},{11,15},{20,16},{24,... | collective-permute-start | bytes 884744 | tf_op jit(solution)/shard_map/ppermute | solution.py:102
  149.8 16.7 %collective-permute-start.36 = (bf16[144,1024]{1,0:T(8,128)(2,1)S(1)}, bf16[144,1024]{1,0:T(8,128)(2,1)S(1)}, u32[]{:S(2)}, u32[]{:S(2)}) collective-permute-start(bf16[144,1024]{1,0:T(8,128)(2,1)S(1)} %get-tuple-element.44), channel_id=1, source_target_pairs={{4,12},{8,0},{5,13},{9,1},{6,14},{10,2},{7,15},{11,3},{20,28},{24,... | collective-permute-start | bytes 884744 | tf_op jit(solution)/shard_map/ppermute | solution.py:102
  157.5 9.0 %collective-permute-start.22 = (bf16[144,1024]{1,0:T(8,128)(2,1)S(1)}, bf16[144,1024]{1,0:T(8,128)(2,1)S(1)}, u32[]{:S(2)}, u32[]{:S(2)}) collective-permute-start(bf16[144,1024]{1,0:T(8,128)(2,1)S(1)} %get-tuple-element.37), channel_id=1, source_target_pairs={{4,8},{8,4},{5,9},{9,5},{6,10},{10,6},{7,11},{11,7},{20,24},{24,20... | collective-permute-start | bytes 884744 | tf_op jit(solution)/shard_map/ppermute | solution.py:102
  158.2 20.6 %collective-permute-start.23 = (bf16[144,1024]{1,0:T(8,128)(2,1)S(1)}, bf16[144,1024]{1,0:T(8,128)(2,1)S(1)}, u32[]{:S(2)}, u32[]{:S(2)}) collective-permute-start(bf16[144,1024]{1,0:T(8,128)(2,1)S(1)} %get-tuple-element.38), channel_id=1, source_target_pairs={{4,0},{8,12},{5,1},{9,13},{6,2},{10,14},{7,3},{11,15},{20,16},{24,... | collective-permute-start | bytes 884744 | tf_op jit(solution)/shard_map/ppermute | solution.py:102
  159.5 19.3 %collective-permute-start.24 = (bf16[144,1024]{1,0:T(8,128)(2,1)S(1)}, bf16[144,1024]{1,0:T(8,128)(2,1)S(1)}, u32[]{:S(2)}, u32[]{:S(2)}) collective-permute-start(bf16[144,1024]{1,0:T(8,128)(2,1)S(1)} %get-tuple-element.39), channel_id=1, source_target_pairs={{4,12},{8,0},{5,13},{9,1},{6,14},{10,2},{7,15},{11,3},{20,28},{24,... | collective-permute-start | bytes 884744 | tf_op jit(solution)/shard_map/ppermute | solution.py:102
  (13 other events, 139.5 us)

commit v7 on v6

--- a/solution.py
+++ b/solution.py
@@ -9,17 +9,17 @@
 CHUNKS = 2
 PLAN = dict(
     first=0,
-    at_cross=0,
+    at_cross=2,
     at_old=3,
     at_inner=3,
     at_far=2,
-    at_fold=3,
-    due_cross=2,
+    at_fold=6,
+    due_cross=5,
     due_old=7,
     due_inner=6,
-    due_far=99,
+    due_far=4,
     due_fold=99,
-    due_swap_cross=6,
+    due_swap_cross=8,
     due_swap_far=6,
     hop_cross=0,
     hop_old=0,
@@ -31,18 +31,21 @@
     join=1,
     c_send=1,
     c_keep=1,
-    xjoin=1,
+    xjoin=0,
     k3=0,
     h0=-1,
-    h1=2,
+    h1=-1,
     y_fold=1,
     hop_swap_fold=0,
     c_x1=1,
     c_xc=1,
     c_k3=1,
-    c_ord=1,
-    hop_join=-1,
+    c_ord=10000000000,
+    hop_join=2,
     full=1,
+    hop_yi=1,
+    hop_m1=0,
+    hop_out=1,
 )
 
 
@@ -383,7 +386,7 @@
     )
 
 
-def finish(place, parts, count):
+def finish(place, parts, count, *released):
     rows, out_cols = parts[0][0].shape
     size = rows - EXTRA
     span = size // 4
@@ -410,7 +413,12 @@
 
     args = [v for part in parts for v in part]
     return call(
-        kernel, place, [VMEM] * len(args), shaped((size * len(parts), out_cols)), [], args
+        kernel,
+        place,
+        [VMEM] * len(args) + [ANY] * len(released),
+        shaped((size * len(parts), out_cols)),
+        [],
+        args + list(released),
     )
 
 
@@ -551,23 +559,32 @@
 
     sent = lax.dynamic_slice_in_dim(context, (1 - x) * (images // 2), images // 2, 0)
     got = along(sent, "mp", SWAP)
-    sent_outer, *made = cuts(
-        place,
-        [(out_shape, [out_block(outer)])] + [block[n] for n in emitted(0)],
-        *hops(sent, PLAN["first"]),
-    )
-    fold_outer = along(sent_outer, "dp", FOLD)
-    launch(0, made)
-
-    near, away = facing(place, context, got, sent_outer)
+    def opening(*released):
+        return cuts(
+            place,
+            [(out_shape, [out_block(outer)])] + [block[n] for n in emitted(0)],
+            *released,
+        )
+
+    if PLAN["first"] < 2:
+        sent_outer, *made = opening(*hops(sent, PLAN["first"]))
+        fold_outer = along(sent_outer, "dp", FOLD)
+        launch(0, made)
+        near, away = facing(place, context, got, sent_outer)
+    else:
+        near, away = facing(place, context, got)
+        sent_outer, *made = opening(*hops(near, PLAN["first"] - 2))
+        fold_outer = along(sent_outer, "dp", FOLD)
+        launch(0, made)
     pieces = [along(near, "dp", FOLD), near, along(away, "dp", CROSS), along(away, "dp", FAR)]
     if emitted(1):
         launch(1, cuts(place, [block[n] for n in emitted(1)], near))
 
-    own, (sent_swap, *made) = ordered(
-        place, pieces, [b_swap(fold_outer)] + [block[n] for n in emitted(2)], *due(2), cost=PLAN["c_ord"]
-    )
+    (sent_swap,) = cuts(place, [b_swap(fold_outer)], *hops(fold_outer, PLAN["hop_m1"]))
     swap_outer = along(sent_swap, "groups", SWAP)
+    own, made = ordered(
+        place, pieces, [block[n] for n in emitted(2)], *due(2), cost=PLAN["c_ord"]
+    )
     launch(2, made)
 
     far = [along(own[0], "mp", SWAP)]
@@ -612,7 +629,8 @@
     came = [along(v, "dp", CROSS) for v in came]
 
     here = [hops(v, h) for v, h in zip(came, (PLAN["h0"], PLAN["h1"]))]
-    kept = [keeps(0, *due(7))]
+    yi = hops(swap_inner, PLAN["hop_yi"])
+    kept = [keeps(0, *yi, *due(7))]
     if emitted(7):
         launch(7, cuts(place, [block[n] for n in emitted(7)], kept[0]))
     if "swap_far" not in arrived:
@@ -641,14 +659,16 @@
         arrived["swap_far"],
     ]
     ready += due(11)
-    parts = []
+    parts, early = [], []
     for k in range(CHUNKS):
         spread, own, cross, leap = project_up(place, scaled[k], w_proj, weights, gain, *ready)
         leap = along(leap, "dp", LEAP)
         cross = along(cross, "dp", CROSS)
         spread = along(spread, "dp", SPREAD)
         parts.append([own, cross, spread, leap])
-    return finish(place, parts, 8 * half).reshape(1, 4 * part, out_cols)
+        if k < CHUNKS - 1:
+            early += hops(spread, PLAN["hop_out"]) + hops(leap, PLAN["hop_out"])
+    return finish(place, parts, 8 * half, *early).reshape(1, 4 * part, out_cols)
 
 
 def local(context, resid, w_out, b_out, ln_gain, w_proj):

time: 181 us -> 175 us (0.967)
  waiting for transfers between devices: 92.6 us -> 76.1 us
  starting transfers between devices: 48 us -> 58.5 us
  local copies, waits for them, and re-layouts: 4.63 us -> 2.8 us
    ppermute x37 -> x40, waiting for transfers between devices: 92.6 us -> 76.1 us  [along(): return lax.ppermute(value, axis, pairs)]
    ppermute x37 -> x40, starting transfers between devices: 48 us -> 58.5 us  [along(): return lax.ppermute(value, axis, pairs)]
    unnamed x16 -> x14, local copies, waits for them, and re-layouts: 3.59 us -> 1.69 us
    pallas_call x16 -> x17, Pallas kernels: 34.8 us -> 35.3 us  [call(): pl.pallas_call(kernel, in_specs=[SMEM, *ins], out_specs=jax.tree.map(lamb...]
  transfers between devices with their start and end apart: 37 -> 40, of which waited for: 17 -> 20; matrix products, arithmetic and copies ran while one was open for 0% -> 0% of each run, Pallas kernels for 17% -> 19%
where the time goes in v7:
time: 175 us; the launch traced here: 173 us
  waiting for transfers between devices  76.1 us (43%)
  starting transfers between devices  58.5 us (33%)
  Pallas kernels  35.3 us (20%)
  local copies, waits for them, and re-layouts  2.8 us (2%)
    ppermute x40, waiting for transfers between devices, along(): return lax.ppermute(value, axis, pairs)  76.1 us
    ppermute x40, starting transfers between devices, along(): return lax.ppermute(value, axis, pairs)  58.5 us
    pallas_call x17, Pallas kernels, call(): pl.pallas_call(kernel, in_specs=[SMEM, *ins], out_specs=jax.tree.map(lamb...  35.3 us
  transfers between devices with their start and end apart: 40, of which 20 were waited for; matrix products, arithmetic and copies ran while one was open for 0% of the time, Pallas kernels for 19%

profile of v7, /device:TPU:0, one launch (start us, length us, event | category | flops | bytes accessed | tf_op | source)
XLA Modules:
  0.0 173.1 jit_solution(13526473093405701737)
XLA Ops:
  1.0 3.0 %collective-permute-start = (bf16[2,64,768]{2,1,0:T(8,128)(2,1)S(1)}, bf16[2,64,768]{2,1,0:T(8,128)(2,1)S(1)}, u32[]{:S(2)}, u32[]{:S(2)}) collective-permute-start(bf16[2,64,768]{2,1,0:T(8,128)(2,1)S(1)} %constant_dynamic-slice_fusion.refs_1_), channel_id=1, source_target_pairs={{0,2},{2,0},{1,3},{3,1},{4,6},{6,4},{5,7},{7,5},{8,10},{10,8},{9,1... | collective-permute-start | bytes 589832 | tf_op jit(solution)/shard_map/ppermute | solution.py:105
  4.1 1.7 copy-done.1
  6.4 2.5 %collective-permute-done.got = bf16[2,64,768]{2,1,0:T(8,128)(2,1)S(1)} collective-permute-done((bf16[2,64,768]{2,1,0:T(8,128)(2,1)S(1)}, bf16[2,64,768]{2,1,0:T(8,128)(2,1)S(1)}, u32[]{:S(2)}, u32[]{:S(2)}) %collective-permute-start) | collective-permute-done | bytes 196640 | tf_op jit(solution)/shard_map/ppermute | solution.py:105
  10.0 3.7 %collective-permute-start.1 = (bf16[2,64,768]{2,1,0:T(8,128)(2,1)S(1)}, bf16[2,64,768]{2,1,0:T(8,128)(2,1)S(1)}, u32[]{:S(2)}, u32[]{:S(2)}) collective-permute-start(bf16[2,64,768]{2,1,0:T(8,128)(2,1)S(1)} %get-tuple-element.24.refs_1_), channel_id=1, source_target_pairs={{0,4},{12,8},{1,5},{13,9},{2,6},{14,10},{3,7},{15,11},{16,20},{28,... | collective-permute-start | bytes 589832 | tf_op jit(solution)/shard_map/ppermute | solution.py:105
  13.8 2.3 %collective-permute-start.3 = (bf16[2,64,768]{2,1,0:T(8,128)(2,1)S(1)}, bf16[2,64,768]{2,1,0:T(8,128)(2,1)S(1)}, u32[]{:S(2)}, u32[]{:S(2)}) collective-permute-start(bf16[2,64,768]{2,1,0:T(8,128)(2,1)S(1)} %get-tuple-element.25), channel_id=1, source_target_pairs={{0,8},{12,4},{1,9},{13,5},{2,10},{14,6},{3,11},{15,7},{16,24},{28,... | collective-permute-start | bytes 589832 | tf_op jit(solution)/shard_map/ppermute | solution.py:105
  16.8 3.1 %collective-permute-start.11 = (bf16[384,768]{1,0:T(8,128)(2,1)S(1)}, bf16[384,768]{1,0:T(8,128)(2,1)S(1)}, u32[]{:S(2)}, u32[]{:S(2)}) collective-permute-start(bf16[384,768]{1,0:T(8,128)(2,1)S(1)} %shard_map.64.refs_0_), channel_id=1, source_target_pairs={{0,4},{12,8},{1,5},{13,9},{2,6},{14,10},{3,7},{15,11},{16,20},{28,... | collective-permute-start | bytes 1769480 | tf_op jit(solution)/shard_map/ppermute | solution.py:105
  19.9 3.2 %collective-permute-done.3.refs_3_ = bf16[2,64,768]{2,1,0:T(8,128)(2,1)S(1)} collective-permute-done((bf16[2,64,768]{2,1,0:T(8,128)(2,1)S(1)}, bf16[2,64,768]{2,1,0:T(8,128)(2,1)S(1)}, u32[]{:S(2)}, u32[]{:S(2)}) %collective-permute-start.3) | collective-permute-done | bytes 196640 | tf_op jit(solution)/shard_map/ppermute | solution.py:105
  24.4 6.1 %collective-permute-start.16 = (bf16[384,1024]{1,0:T(8,128)(2,1)S(1)}, bf16[384,1024]{1,0:T(8,128)(2,1)S(1)}, u32[]{:S(2)}, u32[]{:S(2)}) collective-permute-start(bf16[384,1024]{1,0:T(8,128)(2,1)S(1)} %get-tuple-element.31), channel_id=1, source_target_pairs={{0,8},{12,4},{1,9},{13,5},{2,10},{14,6},{3,11},{15,7},{16,24},{28,... | collective-permute-start | bytes 2359304 | tf_op jit(solution)/shard_map/ppermute | solution.py:105
  32.1 3.7 %collective-permute-done.11.refs_0_.refs_1_.fold = bf16[384,768]{1,0:T(8,128)(2,1)S(1)} collective-permute-done((bf16[384,768]{1,0:T(8,128)(2,1)S(1)}, bf16[384,768]{1,0:T(8,128)(2,1)S(1)}, u32[]{:S(2)}, u32[]{:S(2)}) %collective-permute-start.11) | collective-permute-done | bytes 589856 | tf_op jit(solution)/shard_map/ppermute | solution.py:105
  38.0 1.9 %collective-permute-done.4.refs_10_.far = bf16[256,768]{1,0:T(8,128)(2,1)S(1)} collective-permute-done((bf16[256,768]{1,0:T(8,128)(2,1)S(1)}, bf16[256,768]{1,0:T(8,128)(2,1)S(1)}, u32[]{:S(2)}, u32[]{:S(2)}) %collective-permute-start.4) | collective-permute-done | bytes 393248 | tf_op jit(solution)/shard_map/ppermute | solution.py:105
  40.9 2.6 %collective-permute-start.7 = (bf16[640,768]{1,0:T(8,128)(2,1)S(1)}, bf16[640,768]{1,0:T(8,128)(2,1)S(1)}, u32[]{:S(2)}, u32[]{:S(2)}) collective-permute-start(bf16[640,768]{1,0:T(8,128)(2,1)S(1)} %get-tuple-element.28), channel_id=1, source_target_pairs={{0,4},{12,8},{1,5},{13,9},{2,6},{14,10},{3,7},{15,11},{16,20},{28,... | collective-permute-start | bytes 2949128 | tf_op jit(solution)/shard_map/ppermute | solution.py:105
  45.3 2.7 %collective-permute-done.12.refs_0_ = bf16[384,768]{1,0:T(8,128)(2,1)S(1)} collective-permute-done((bf16[384,768]{1,0:T(8,128)(2,1)S(1)}, bf16[384,768]{1,0:T(8,128)(2,1)S(1)}, u32[]{:S(2)}, u32[]{:S(2)}) %collective-permute-start.12) | collective-permute-done | bytes 589856 | tf_op jit(solution)/shard_map/ppermute | solution.py:105
  48.8 3.9 %collective-permute-done.16.refs_0_.rest_3_ = bf16[384,1024]{1,0:T(8,128)(2,1)S(1)} collective-permute-done((bf16[384,1024]{1,0:T(8,128)(2,1)S(1)}, bf16[384,1024]{1,0:T(8,128)(2,1)S(1)}, u32[]{:S(2)}, u32[]{:S(2)}) %collective-permute-start.16) | collective-permute-done | bytes 786464 | tf_op jit(solution)/shard_map/ppermute | solution.py:105
  58.4 2.6 %shard_map.73 = bf16[512,768]{1,0:T(8,128)(2,1)S(1)} custom-call(s32[6]{0:T(128)S(1)} %stack.31.p, bf16[256,768]{1,0:T(8,128)(2,1)S(1)} %bitcast.16, bf16[256,768]{1,0:T(8,128)(2,1)S(1)} %collective-permute-done.4.refs_10_.far, bf16[256,768]{1,0:T(8,128)(2,1)S(1)} %collective-permute-done.5.near, bf16[256,768]{1,0:T(8,128)(2,1)S(1)} %collective-permute-done.6.both, ...), custom_call_target="tpu_custom_call" | custom-call | flops 1 | bytes 1 | tf_op jit(solution)/shard_map/pallas_call | solution.py:137
  61.7 2.6 %shard_map.70.refs_2_ = bf16[512,768]{1,0:T(8,128)(2,1)S(1)} custom-call(s32[6]{0:T(128)S(1)} %stack.31.p, bf16[256,768]{1,0:T(8,128)(2,1)S(1)} %bitcast.12, bf16[256,768]{1,0:T(8,128)(2,1)S(1)} %collective-permute-done.8.far, bf16[256,768]{1,0:T(8,128)(2,1)S(1)} %collective-permute-done.9.near, bf16[256,768]{1,0:T(8,128)(2,1)S(1)} %collective-permute-done.10.both, ...), custom_call_target="tpu_custom_call" | custom-call | flops 1 | bytes 1 | tf_op jit(solution)/shard_map/pallas_call | solution.py:137
  64.3 7.5 %collective-permute-done.7.refs_0_.refs_3_.fold = bf16[640,768]{1,0:T(8,128)(2,1)S(1)} collective-permute-done((bf16[640,768]{1,0:T(8,128)(2,1)S(1)}, bf16[640,768]{1,0:T(8,128)(2,1)S(1)}, u32[]{:S(2)}, u32[]{:S(2)}) %collective-permute-start.7) | collective-permute-done | bytes 983072 | tf_op jit(solution)/shard_map/ppermute | solution.py:105
  76.1 8.5 %collective-permute-start.19 = (bf16[256,768]{1,0:T(8,128)(2,1)S(1)}, bf16[256,768]{1,0:T(8,128)(2,1)S(1)}, u32[]{:S(2)}, u32[]{:S(2)}) collective-permute-start(bf16[256,768]{1,0:T(8,128)(2,1)S(1)} %get-tuple-element.33), channel_id=1, source_target_pairs={{0,8},{12,4},{1,9},{13,5},{2,10},{14,6},{3,11},{15,7},{16,24},{28,... | collective-permute-start | bytes 1179656 | tf_op jit(solution)/shard_map/ppermute | solution.py:105
  84.6 4.4 %collective-permute-done.18.swapped = bf16[384,768]{1,0:T(8,128)(2,1)S(1)} collective-permute-done((bf16[384,768]{1,0:T(8,128)(2,1)S(1)}, bf16[384,768]{1,0:T(8,128)(2,1)S(1)}, u32[]{:S(2)}, u32[]{:S(2)}) %collective-permute-start.18) | collective-permute-done | bytes 589856 | tf_op jit(solution)/shard_map/ppermute | solution.py:105
  90.1 2.8 %shard_map.72.keeps = f32[512,768]{1,0:T(8,128)S(1)} custom-call(s32[6]{0:T(128)S(1)} %stack.31.p, bf16[256,768]{1,0:T(8,128)(2,1)S(1)} %bitcast.17, bf16[256,768]{1,0:T(8,128)(2,1)S(1)} %collective-permute-done.4.refs_10_.far, bf16[256,768]{1,0:T(8,128)(2,1)S(1)} %collective-permute-done.5.near, bf16[256,768]{1,0:T(8,128)(2,1)S(1)} %collective-permute-done.6.both, ...), custom_call_target="tpu_custom_call" | custom-call | flops 1 | bytes 1 | tf_op jit(solution)/shard_map/pallas_call | solution.py:137
  92.9 1.7 shard_map.74.s0
  96.2 7.6 %collective-permute-start.25 = (bf16[768,1024]{1,0:T(8,128)(2,1)S(1)}, bf16[768,1024]{1,0:T(8,128)(2,1)S(1)}, u32[]{:S(2)}, u32[]{:S(2)}) collective-permute-start(bf16[768,1024]{1,0:T(8,128)(2,1)S(1)} %get-tuple-element.34), channel_id=1, source_target_pairs={{0,4},{12,8},{1,5},{13,9},{2,6},{14,10},{3,7},{15,11},{16,20},{28,... | collective-permute-start | bytes 4718600 | tf_op jit(solution)/shard_map/ppermute | solution.py:105
  105.1 2.8 %shard_map.77.keeps = f32[512,768]{1,0:T(8,128)S(1)} custom-call(s32[6]{0:T(128)S(1)} %stack.31.p, bf16[256,768]{1,0:T(8,128)(2,1)S(1)} %bitcast.13, bf16[256,768]{1,0:T(8,128)(2,1)S(1)} %collective-permute-done.8.far, bf16[256,768]{1,0:T(8,128)(2,1)S(1)} %collective-permute-done.9.near, bf16[256,768]{1,0:T(8,128)(2,1)S(1)} %collective-permute-done.10.both, ...), custom_call_target="tpu_custom_call" | custom-call | flops 1 | bytes 1 | tf_op jit(solution)/shard_map/pallas_call | solution.py:137
  107.9 1.7 shard_map.78.s0
  110.2 5.4 %collective-permute-done.23.s2 = bf16[528,768]{1,0:T(8,128)(2,1)S(1)} collective-permute-done((bf16[528,768]{1,0:T(8,128)(2,1)S(1)}, bf16[528,768]{1,0:T(8,128)(2,1)S(1)}, u32[]{:S(2)}, u32[]{:S(2)}) %collective-permute-start.23) | collective-permute-done | bytes 811040 | tf_op jit(solution)/shard_map/ppermute | solution.py:105
  116.1 16.1 %collective-permute-done.33.s2 = bf16[528,768]{1,0:T(8,128)(2,1)S(1)} collective-permute-done((bf16[528,768]{1,0:T(8,128)(2,1)S(1)}, bf16[528,768]{1,0:T(8,128)(2,1)S(1)}, u32[]{:S(2)}, u32[]{:S(2)}) %collective-permute-start.33) | collective-permute-done | bytes 811040 | tf_op jit(solution)/shard_map/ppermute | solution.py:105
  132.2 3.5 %collective-permute-done.25.rest_0_ = bf16[768,1024]{1,0:T(8,128)(2,1)S(1)} collective-permute-done((bf16[768,1024]{1,0:T(8,128)(2,1)S(1)}, bf16[768,1024]{1,0:T(8,128)(2,1)S(1)}, u32[]{:S(2)}, u32[]{:S(2)}) %collective-permute-start.25) | collective-permute-done | bytes 1572896 | tf_op jit(solution)/shard_map/ppermute | solution.py:105
  135.7 6.3 %shard_map.76 = (bf16[144,1024]{1,0:T(8,128)(2,1)S(1)}, bf16[144,1024]{1,0:T(8,128)(2,1)S(1)}, bf16[144,1024]{1,0:T(8,128)(2,1)S(1)}, bf16[144,1024]{1,0:T(8,128)(2,1)S(1)}) custom-call(s32[6]{0:T(128)S(1)} %stack.31.p, bf16[528,768]{1,0:T(8,128)(2,1)S(1)} %shard_map.74.s0, bf16[528,768]{1,0:T(8,128)(2,1)S(1)} %collective-permute-done.22.s1, ...), custom_call_target="tpu_custom_call" | custom-call | flops 1 | bytes 1 | tf_op jit(solution)/shard_map/pallas_call | solution.py:137
  144.6 6.3 %shard_map.79 = (bf16[144,1024]{1,0:T(8,128)(2,1)S(1)}, bf16[144,1024]{1,0:T(8,128)(2,1)S(1)}, bf16[144,1024]{1,0:T(8,128)(2,1)S(1)}, bf16[144,1024]{1,0:T(8,128)(2,1)S(1)}) custom-call(s32[6]{0:T(128)S(1)} %stack.31.p, bf16[528,768]{1,0:T(8,128)(2,1)S(1)} %shard_map.78.s0, bf16[528,768]{1,0:T(8,128)(2,1)S(1)} %collective-permute-done.32.s1, ...), custom_call_target="tpu_custom_call" | custom-call | flops 1 | bytes 1 | tf_op jit(solution)/shard_map/pallas_call | solution.py:137
  154.2 4.8 %collective-permute-done.28.refs_2_ = bf16[144,1024]{1,0:T(8,128)(2,1)S(1)} collective-permute-done((bf16[144,1024]{1,0:T(8,128)(2,1)S(1)}, bf16[144,1024]{1,0:T(8,128)(2,1)S(1)}, u32[]{:S(2)}, u32[]{:S(2)}) %collective-permute-start.28) | collective-permute-done | bytes 294944 | tf_op jit(solution)/shard_map/ppermute | solution.py:105
  160.3 9.1 %collective-permute-done.36.refs_6_ = bf16[144,1024]{1,0:T(8,128)(2,1)S(1)} collective-permute-done((bf16[144,1024]{1,0:T(8,128)(2,1)S(1)}, bf16[144,1024]{1,0:T(8,128)(2,1)S(1)}, u32[]{:S(2)}, u32[]{:S(2)}) %collective-permute-start.36) | collective-permute-done | bytes 294944 | tf_op jit(solution)/shard_map/ppermute | solution.py:105
  169.4 2.0 %collective-permute-done.37.refs_7_ = bf16[144,1024]{1,0:T(8,128)(2,1)S(1)} collective-permute-done((bf16[144,1024]{1,0:T(8,128)(2,1)S(1)}, bf16[144,1024]{1,0:T(8,128)(2,1)S(1)}, u32[]{:S(2)}, u32[]{:S(2)}) %collective-permute-start.37) | collective-permute-done | bytes 294944 | tf_op jit(solution)/shard_map/ppermute | solution.py:105
  171.4 1.7 %shard_map.80 = bf16[256,1024]{1,0:T(8,128)(2,1)} custom-call(s32[6]{0:T(128)S(1)} %stack.31.p, bf16[144,1024]{1,0:T(8,128)(2,1)S(1)} %get-tuple-element.35.refs_0_, bf16[144,1024]{1,0:T(8,128)(2,1)S(1)} %collective-permute-done.27.refs_1_, bf16[144,1024]{1,0:T(8,128)(2,1)S(1)} %collective-permute-done.28.refs_2_, ...), custom_call_target="tpu_custom_call" | custom-call | flops 1 | bytes 1 | tf_op jit(solution)/shard_map/pallas_call | solution.py:137
  (87 shorter events, 34.9 us)
Async XLA Ops:
  1.0 7.9 %collective-permute-start = (bf16[2,64,768]{2,1,0:T(8,128)(2,1)S(1)}, bf16[2,64,768]{2,1,0:T(8,128)(2,1)S(1)}, u32[]{:S(2)}, u32[]{:S(2)}) collective-permute-start(bf16[2,64,768]{2,1,0:T(8,128)(2,1)S(1)} %constant_dynamic-slice_fusion.refs_1_), channel_id=1, source_target_pairs={{0,2},{2,0},{1,3},{3,1},{4,6},{6,4},{5,7},{7,5},{8,10},{10,8},{9,1... | collective-permute-start | bytes 589832 | tf_op jit(solution)/shard_map/ppermute | solution.py:105
  10.0 9.9 %collective-permute-start.1 = (bf16[2,64,768]{2,1,0:T(8,128)(2,1)S(1)}, bf16[2,64,768]{2,1,0:T(8,128)(2,1)S(1)}, u32[]{:S(2)}, u32[]{:S(2)}) collective-permute-start(bf16[2,64,768]{2,1,0:T(8,128)(2,1)S(1)} %get-tuple-element.24.refs_1_), channel_id=1, source_target_pairs={{0,4},{12,8},{1,5},{13,9},{2,6},{14,10},{3,7},{15,11},{16,20},{28,... | collective-permute-start | bytes 589832 | tf_op jit(solution)/shard_map/ppermute | solution.py:105
  13.8 9.4 %collective-permute-start.3 = (bf16[2,64,768]{2,1,0:T(8,128)(2,1)S(1)}, bf16[2,64,768]{2,1,0:T(8,128)(2,1)S(1)}, u32[]{:S(2)}, u32[]{:S(2)}) collective-permute-start(bf16[2,64,768]{2,1,0:T(8,128)(2,1)S(1)} %get-tuple-element.25), channel_id=1, source_target_pairs={{0,8},{12,4},{1,9},{13,5},{2,10},{14,6},{3,11},{15,7},{16,24},{28,... | collective-permute-start | bytes 589832 | tf_op jit(solution)/shard_map/ppermute | solution.py:105
  16.8 19.0 %collective-permute-start.11 = (bf16[384,768]{1,0:T(8,128)(2,1)S(1)}, bf16[384,768]{1,0:T(8,128)(2,1)S(1)}, u32[]{:S(2)}, u32[]{:S(2)}) collective-permute-start(bf16[384,768]{1,0:T(8,128)(2,1)S(1)} %shard_map.64.refs_0_), channel_id=1, source_target_pairs={{0,4},{12,8},{1,5},{13,9},{2,6},{14,10},{3,7},{15,11},{16,20},{28,... | collective-permute-start | bytes 1769480 | tf_op jit(solution)/shard_map/ppermute | solution.py:105
  24.4 28.2 %collective-permute-start.16 = (bf16[384,1024]{1,0:T(8,128)(2,1)S(1)}, bf16[384,1024]{1,0:T(8,128)(2,1)S(1)}, u32[]{:S(2)}, u32[]{:S(2)}) collective-permute-start(bf16[384,1024]{1,0:T(8,128)(2,1)S(1)} %get-tuple-element.31), channel_id=1, source_target_pairs={{0,8},{12,4},{1,9},{13,5},{2,10},{14,6},{3,11},{15,7},{16,24},{28,... | collective-permute-start | bytes 2359304 | tf_op jit(solution)/shard_map/ppermute | solution.py:105
  30.5 9.4 %collective-permute-start.4 = (bf16[256,768]{1,0:T(8,128)(2,1)S(1)}, bf16[256,768]{1,0:T(8,128)(2,1)S(1)}, u32[]{:S(2)}, u32[]{:S(2)}) collective-permute-start(bf16[256,768]{1,0:T(8,128)(2,1)S(1)} %bitcast.14), channel_id=1, source_target_pairs={{0,2},{2,0},{1,3},{3,1},{4,6},{6,4},{5,7},{7,5},{8,10},{10,8},{9,1... | collective-permute-start | bytes 1179656 | tf_op jit(solution)/shard_map/ppermute | solution.py:105
  36.5 11.6 %collective-permute-start.12 = (bf16[384,768]{1,0:T(8,128)(2,1)S(1)}, bf16[384,768]{1,0:T(8,128)(2,1)S(1)}, u32[]{:S(2)}, u32[]{:S(2)}) collective-permute-start(bf16[384,768]{1,0:T(8,128)(2,1)S(1)} %shard_map.68), channel_id=1, source_target_pairs={{0,16},{16,0},{1,17},{17,1},{2,18},{18,2},{3,19},{19,3},{4,20},{20... | collective-permute-start | bytes 1769480 | tf_op jit(solution)/shard_map/ppermute | solution.py:105
  40.9 30.8 %collective-permute-start.7 = (bf16[640,768]{1,0:T(8,128)(2,1)S(1)}, bf16[640,768]{1,0:T(8,128)(2,1)S(1)}, u32[]{:S(2)}, u32[]{:S(2)}) collective-permute-start(bf16[640,768]{1,0:T(8,128)(2,1)S(1)} %get-tuple-element.28), channel_id=1, source_target_pairs={{0,4},{12,8},{1,5},{13,9},{2,6},{14,10},{3,7},{15,11},{16,20},{28,... | collective-permute-start | bytes 2949128 | tf_op jit(solution)/shard_map/ppermute | solution.py:105
  43.6 10.6 %collective-permute-start.6 = (bf16[256,768]{1,0:T(8,128)(2,1)S(1)}, bf16[256,768]{1,0:T(8,128)(2,1)S(1)}, u32[]{:S(2)}, u32[]{:S(2)}) collective-permute-start(bf16[256,768]{1,0:T(8,128)(2,1)S(1)} %collective-permute-done.4.refs_10_.far), channel_id=1, source_target_pairs={{0,1},{1,0},{2,3},{3,2},{4,5},{5,4},{6,7},{7,6},{8,9},{9,8},{10,11... | collective-permute-start | bytes 1179656 | tf_op jit(solution)/shard_map/ppermute | solution.py:105
  43.8 11.3 %collective-permute-start.8 = (bf16[256,768]{1,0:T(8,128)(2,1)S(1)}, bf16[256,768]{1,0:T(8,128)(2,1)S(1)}, u32[]{:S(2)}, u32[]{:S(2)}) collective-permute-start(bf16[256,768]{1,0:T(8,128)(2,1)S(1)} %get-tuple-element.29), channel_id=1, source_target_pairs={{0,2},{2,0},{1,3},{3,1},{4,6},{6,4},{5,7},{7,5},{8,10},{10,8},{9,1... | collective-permute-start | bytes 1179656 | tf_op jit(solution)/shard_map/ppermute | solution.py:105
  48.1 13.6 %collective-permute-start.15 = (bf16[384,1024]{1,0:T(8,128)(2,1)S(1)}, bf16[384,1024]{1,0:T(8,128)(2,1)S(1)}, u32[]{:S(2)}, u32[]{:S(2)}) collective-permute-start(bf16[384,1024]{1,0:T(8,128)(2,1)S(1)} %get-tuple-element.30), channel_id=1, source_target_pairs={{4,8},{8,4},{5,9},{9,5},{6,10},{10,6},{7,11},{11,7},{20,24},{24,20... | collective-permute-start | bytes 2359304 | tf_op jit(solution)/shard_map/ppermute | solution.py:105
  52.6 19.2 %collective-permute-start.17 = (bf16[384,1024]{1,0:T(8,128)(2,1)S(1)}, bf16[384,1024]{1,0:T(8,128)(2,1)S(1)}, u32[]{:S(2)}, u32[]{:S(2)}) collective-permute-start(bf16[384,1024]{1,0:T(8,128)(2,1)S(1)} %collective-permute-done.16.refs_0_.rest_3_), channel_id=1, source_target_pairs={{0,16},{16,0},{1,17},{17,1},{2,18},{18,2},{3,19},{19,3},{4,20},{20... | collective-permute-start | bytes 2359304 | tf_op jit(solution)/shard_map/ppermute | solution.py:105
  61.0 31.9 %collective-permute-start.21 = (bf16[512,768]{1,0:T(8,128)(2,1)S(1)}, bf16[512,768]{1,0:T(8,128)(2,1)S(1)}, u32[]{:S(2)}, u32[]{:S(2)}) collective-permute-start(bf16[512,768]{1,0:T(8,128)(2,1)S(1)} %shard_map.73), channel_id=1, source_target_pairs={{4,8},{8,4},{5,9},{9,5},{6,10},{10,6},{7,11},{11,7},{20,24},{24,20... | collective-permute-start | bytes 2359304 | tf_op jit(solution)/shard_map/ppermute | solution.py:105
  72.6 16.3 %collective-permute-start.18 = (bf16[384,768]{1,0:T(8,128)(2,1)S(1)}, bf16[384,768]{1,0:T(8,128)(2,1)S(1)}, u32[]{:S(2)}, u32[]{:S(2)}) collective-permute-start(bf16[384,768]{1,0:T(8,128)(2,1)S(1)} %get-tuple-element.32), channel_id=1, source_target_pairs={{0,16},{16,0},{1,17},{17,1},{2,18},{18,2},{3,19},{19,3},{4,20},{20... | collective-permute-start | bytes 1769480 | tf_op jit(solution)/shard_map/ppermute | solution.py:105
  74.8 29.0 %collective-permute-start.26 = (bf16[384,1024]{1,0:T(8,128)(2,1)S(1)}, bf16[384,1024]{1,0:T(8,128)(2,1)S(1)}, u32[]{:S(2)}, u32[]{:S(2)}) collective-permute-start(bf16[384,1024]{1,0:T(8,128)(2,1)S(1)} %shard_map.75), channel_id=1, source_target_pairs={{0,16},{16,0},{1,17},{17,1},{2,18},{18,2},{3,19},{19,3},{4,20},{20... | collective-permute-start | bytes 2359304 | tf_op jit(solution)/shard_map/ppermute | solution.py:105
  75.4 32.5 %collective-permute-start.31 = (bf16[512,768]{1,0:T(8,128)(2,1)S(1)}, bf16[512,768]{1,0:T(8,128)(2,1)S(1)}, u32[]{:S(2)}, u32[]{:S(2)}) collective-permute-start(bf16[512,768]{1,0:T(8,128)(2,1)S(1)} %shard_map.70.refs_2_), channel_id=1, source_target_pairs={{4,8},{8,4},{5,9},{9,5},{6,10},{10,6},{7,11},{11,7},{20,24},{24,20... | collective-permute-start | bytes 2359304 | tf_op jit(solution)/shard_map/ppermute | solution.py:105
  76.1 13.8 %collective-permute-start.19 = (bf16[256,768]{1,0:T(8,128)(2,1)S(1)}, bf16[256,768]{1,0:T(8,128)(2,1)S(1)}, u32[]{:S(2)}, u32[]{:S(2)}) collective-permute-start(bf16[256,768]{1,0:T(8,128)(2,1)S(1)} %get-tuple-element.33), channel_id=1, source_target_pairs={{0,8},{12,4},{1,9},{13,5},{2,10},{14,6},{3,11},{15,7},{16,24},{28,... | collective-permute-start | bytes 1179656 | tf_op jit(solution)/shard_map/ppermute | solution.py:105
  94.6 21.0 %collective-permute-start.23 = (bf16[528,768]{1,0:T(8,128)(2,1)S(1)}, bf16[528,768]{1,0:T(8,128)(2,1)S(1)}, u32[]{:S(2)}, u32[]{:S(2)}) collective-permute-start(bf16[528,768]{1,0:T(8,128)(2,1)S(1)} %shard_map.74.s0), channel_id=1, source_target_pairs={{0,2},{2,0},{1,3},{3,1},{4,6},{6,4},{5,7},{7,5},{8,10},{10,8},{9,1... | collective-permute-start | bytes 2433032 | tf_op jit(solution)/shard_map/ppermute | solution.py:105
  96.2 39.5 %collective-permute-start.25 = (bf16[768,1024]{1,0:T(8,128)(2,1)S(1)}, bf16[768,1024]{1,0:T(8,128)(2,1)S(1)}, u32[]{:S(2)}, u32[]{:S(2)}) collective-permute-start(bf16[768,1024]{1,0:T(8,128)(2,1)S(1)} %get-tuple-element.34), channel_id=1, source_target_pairs={{0,4},{12,8},{1,5},{13,9},{2,6},{14,10},{3,7},{15,11},{16,20},{28,... | collective-permute-start | bytes 4718600 | tf_op jit(solution)/shard_map/ppermute | solution.py:105
  109.6 22.6 %collective-permute-start.33 = (bf16[528,768]{1,0:T(8,128)(2,1)S(1)}, bf16[528,768]{1,0:T(8,128)(2,1)S(1)}, u32[]{:S(2)}, u32[]{:S(2)}) collective-permute-start(bf16[528,768]{1,0:T(8,128)(2,1)S(1)} %shard_map.78.s0), channel_id=1, source_target_pairs={{0,2},{2,0},{1,3},{3,1},{4,6},{6,4},{5,7},{7,5},{8,10},{10,8},{9,1... | collective-permute-start | bytes 2433032 | tf_op jit(solution)/shard_map/ppermute | solution.py:105
  110.2 22.0 %collective-permute-start.22 = (bf16[528,768]{1,0:T(8,128)(2,1)S(1)}, bf16[528,768]{1,0:T(8,128)(2,1)S(1)}, u32[]{:S(2)}, u32[]{:S(2)}) collective-permute-start(bf16[528,768]{1,0:T(8,128)(2,1)S(1)} %shard_map.74.s0), channel_id=1, source_target_pairs={{0,1},{1,0},{2,3},{3,2},{4,5},{5,4},{6,7},{7,6},{8,9},{9,8},{10,11... | collective-permute-start | bytes 2433032 | tf_op jit(solution)/shard_map/ppermute | solution.py:105
  115.6 20.1 %collective-permute-start.24 = (bf16[528,768]{1,0:T(8,128)(2,1)S(1)}, bf16[528,768]{1,0:T(8,128)(2,1)S(1)}, u32[]{:S(2)}, u32[]{:S(2)}) collective-permute-start(bf16[528,768]{1,0:T(8,128)(2,1)S(1)} %collective-permute-done.23.s2), channel_id=1, source_target_pairs={{0,1},{1,0},{2,3},{3,2},{4,5},{5,4},{6,7},{7,6},{8,9},{9,8},{10,11... | collective-permute-start | bytes 2433032 | tf_op jit(solution)/shard_map/ppermute | solution.py:105
  115.6 29.0 %collective-permute-start.32 = (bf16[528,768]{1,0:T(8,128)(2,1)S(1)}, bf16[528,768]{1,0:T(8,128)(2,1)S(1)}, u32[]{:S(2)}, u32[]{:S(2)}) collective-permute-start(bf16[528,768]{1,0:T(8,128)(2,1)S(1)} %shard_map.78.s0), channel_id=1, source_target_pairs={{0,1},{1,0},{2,3},{3,2},{4,5},{5,4},{6,7},{7,6},{8,9},{9,8},{10,11... | collective-permute-start | bytes 2433032 | tf_op jit(solution)/shard_map/ppermute | solution.py:105
  132.2 12.4 %collective-permute-start.34 = (bf16[528,768]{1,0:T(8,128)(2,1)S(1)}, bf16[528,768]{1,0:T(8,128)(2,1)S(1)}, u32[]{:S(2)}, u32[]{:S(2)}) collective-permute-start(bf16[528,768]{1,0:T(8,128)(2,1)S(1)} %collective-permute-done.33.s2), channel_id=1, source_target_pairs={{0,1},{1,0},{2,3},{3,2},{4,5},{5,4},{6,7},{7,6},{8,9},{9,8},{10,11... | collective-permute-start | bytes 2433032 | tf_op jit(solution)/shard_map/ppermute | solution.py:105
  142.0 17.0 %collective-permute-start.28 = (bf16[144,1024]{1,0:T(8,128)(2,1)S(1)}, bf16[144,1024]{1,0:T(8,128)(2,1)S(1)}, u32[]{:S(2)}, u32[]{:S(2)}) collective-permute-start(bf16[144,1024]{1,0:T(8,128)(2,1)S(1)} %get-tuple-element.37), channel_id=1, source_target_pairs={{4,0},{8,12},{5,1},{9,13},{6,2},{10,14},{7,3},{11,15},{20,16},{24,... | collective-permute-start | bytes 884744 | tf_op jit(solution)/shard_map/ppermute | solution.py:105
  143.3 16.4 %collective-permute-start.29 = (bf16[144,1024]{1,0:T(8,128)(2,1)S(1)}, bf16[144,1024]{1,0:T(8,128)(2,1)S(1)}, u32[]{:S(2)}, u32[]{:S(2)}) collective-permute-start(bf16[144,1024]{1,0:T(8,128)(2,1)S(1)} %get-tuple-element.38), channel_id=1, source_target_pairs={{4,12},{8,0},{5,13},{9,1},{6,14},{10,2},{7,15},{11,3},{20,28},{24,... | collective-permute-start | bytes 884744 | tf_op jit(solution)/shard_map/ppermute | solution.py:105
  150.9 8.8 %collective-permute-start.35 = (bf16[144,1024]{1,0:T(8,128)(2,1)S(1)}, bf16[144,1024]{1,0:T(8,128)(2,1)S(1)}, u32[]{:S(2)}, u32[]{:S(2)}) collective-permute-start(bf16[144,1024]{1,0:T(8,128)(2,1)S(1)} %get-tuple-element.40), channel_id=1, source_target_pairs={{4,8},{8,4},{5,9},{9,5},{6,10},{10,6},{7,11},{11,7},{20,24},{24,20... | collective-permute-start | bytes 884744 | tf_op jit(solution)/shard_map/ppermute | solution.py:105
  151.6 17.8 %collective-permute-start.36 = (bf16[144,1024]{1,0:T(8,128)(2,1)S(1)}, bf16[144,1024]{1,0:T(8,128)(2,1)S(1)}, u32[]{:S(2)}, u32[]{:S(2)}) collective-permute-start(bf16[144,1024]{1,0:T(8,128)(2,1)S(1)} %get-tuple-element.41), channel_id=1, source_target_pairs={{4,0},{8,12},{5,1},{9,13},{6,2},{10,14},{7,3},{11,15},{20,16},{24,... | collective-permute-start | bytes 884744 | tf_op jit(solution)/shard_map/ppermute | solution.py:105
  152.9 18.4 %collective-permute-start.37 = (bf16[144,1024]{1,0:T(8,128)(2,1)S(1)}, bf16[144,1024]{1,0:T(8,128)(2,1)S(1)}, u32[]{:S(2)}, u32[]{:S(2)}) collective-permute-start(bf16[144,1024]{1,0:T(8,128)(2,1)S(1)} %get-tuple-element.42), channel_id=1, source_target_pairs={{4,12},{8,0},{5,13},{9,1},{6,14},{10,2},{7,15},{11,3},{20,28},{24,... | collective-permute-start | bytes 884744 | tf_op jit(solution)/shard_map/ppermute | solution.py:105
  159.0 12.4 %collective-permute-start.27 = (bf16[144,1024]{1,0:T(8,128)(2,1)S(1)}, bf16[144,1024]{1,0:T(8,128)(2,1)S(1)}, u32[]{:S(2)}, u32[]{:S(2)}) collective-permute-start(bf16[144,1024]{1,0:T(8,128)(2,1)S(1)} %get-tuple-element.36), channel_id=1, source_target_pairs={{4,8},{8,4},{5,9},{9,5},{6,10},{10,6},{7,11},{11,7},{20,24},{24,20... | collective-permute-start | bytes 884744 | tf_op jit(solution)/shard_map/ppermute | solution.py:105
  159.7 11.7 %collective-permute-start.38 = (bf16[16,128]{1,0:T(8,128)(2,1)S(1)}, bf16[16,128]{1,0:T(8,128)(2,1)S(1)}, u32[]{:S(2)}, u32[]{:S(2)}) collective-permute-start(bf16[16,128]{1,0:T(8,128)(2,1)S(1)} %slice.23), channel_id=1, source_target_pairs={{0,1},{1,0},{2,3},{3,2},{4,5},{5,4},{6,7},{7,6},{8,9},{9,8},{10,11... | collective-permute-start | bytes 12296 | tf_op jit(solution)/shard_map/ppermute | solution.py:105
  159.8 11.6 %collective-permute-start.39 = (bf16[16,128]{1,0:T(8,128)(2,1)S(1)}, bf16[16,128]{1,0:T(8,128)(2,1)S(1)}, u32[]{:S(2)}, u32[]{:S(2)}) collective-permute-start(bf16[16,128]{1,0:T(8,128)(2,1)S(1)} %slice.24), channel_id=1, source_target_pairs={{0,1},{1,0},{2,3},{3,2},{4,5},{5,4},{6,7},{7,6},{8,9},{9,8},{10,11... | collective-permute-start | bytes 12296 | tf_op jit(solution)/shard_map/ppermute | solution.py:105
  (15 other events, 110.6 us)

commit v8 on v7

--- a/solution.py
+++ b/solution.py
@@ -130,7 +130,7 @@
 VMEM = pl.BlockSpec(memory_space=pltpu.VMEM)
 SMEM = pl.BlockSpec(memory_space=pltpu.SMEM)
 EXTRA = 16
-TILE = 256
+TILE = 512
 
 
 def call(kernel, place, ins, shapes, scratch, args, cost=1):

time: 175 us -> 175 us (level)
  no operation moved by 1% of the time
where the time goes in v8:
time: 175 us; the launch traced here: 173 us
  waiting for transfers between devices  76.1 us (43%)
  starting transfers between devices  58.4 us (33%)
  Pallas kernels  35.4 us (20%)
  local copies, waits for them, and re-layouts  2.8 us (2%)
    ppermute x40, waiting for transfers between devices, along(): return lax.ppermute(value, axis, pairs)  76.1 us
    ppermute x40, starting transfers between devices, along(): return lax.ppermute(value, axis, pairs)  58.4 us
    pallas_call x17, Pallas kernels, call(): pl.pallas_call(kernel, in_specs=[SMEM, *ins], out_specs=jax.tree.map(lamb...  35.4 us
  transfers between devices with their start and end apart: 40, of which 20 were waited for; matrix products, arithmetic and copies ran while one was open for 0% of the time, Pallas kernels for 19%

profile of v8, /device:TPU:0, one launch (start us, length us, event | category | flops | bytes accessed | tf_op | source)
XLA Modules:
  0.0 173.1 jit_solution(2295055845896982283)
XLA Ops:
  1.0 3.0 %collective-permute-start = (bf16[2,64,768]{2,1,0:T(8,128)(2,1)S(1)}, bf16[2,64,768]{2,1,0:T(8,128)(2,1)S(1)}, u32[]{:S(2)}, u32[]{:S(2)}) collective-permute-start(bf16[2,64,768]{2,1,0:T(8,128)(2,1)S(1)} %constant_dynamic-slice_fusion.refs_1_), channel_id=1, source_target_pairs={{0,2},{2,0},{1,3},{3,1},{4,6},{6,4},{5,7},{7,5},{8,10},{10,8},{9,1... | collective-permute-start | bytes 589832 | tf_op jit(solution)/shard_map/ppermute | solution.py:105
  4.1 1.7 copy-done.1
  6.4 2.5 %collective-permute-done.got = bf16[2,64,768]{2,1,0:T(8,128)(2,1)S(1)} collective-permute-done((bf16[2,64,768]{2,1,0:T(8,128)(2,1)S(1)}, bf16[2,64,768]{2,1,0:T(8,128)(2,1)S(1)}, u32[]{:S(2)}, u32[]{:S(2)}) %collective-permute-start) | collective-permute-done | bytes 196640 | tf_op jit(solution)/shard_map/ppermute | solution.py:105
  10.0 3.7 %collective-permute-start.1 = (bf16[2,64,768]{2,1,0:T(8,128)(2,1)S(1)}, bf16[2,64,768]{2,1,0:T(8,128)(2,1)S(1)}, u32[]{:S(2)}, u32[]{:S(2)}) collective-permute-start(bf16[2,64,768]{2,1,0:T(8,128)(2,1)S(1)} %get-tuple-element.24.refs_1_), channel_id=1, source_target_pairs={{0,4},{12,8},{1,5},{13,9},{2,6},{14,10},{3,7},{15,11},{16,20},{28,... | collective-permute-start | bytes 589832 | tf_op jit(solution)/shard_map/ppermute | solution.py:105
  13.8 2.3 %collective-permute-start.3 = (bf16[2,64,768]{2,1,0:T(8,128)(2,1)S(1)}, bf16[2,64,768]{2,1,0:T(8,128)(2,1)S(1)}, u32[]{:S(2)}, u32[]{:S(2)}) collective-permute-start(bf16[2,64,768]{2,1,0:T(8,128)(2,1)S(1)} %get-tuple-element.25), channel_id=1, source_target_pairs={{0,8},{12,4},{1,9},{13,5},{2,10},{14,6},{3,11},{15,7},{16,24},{28,... | collective-permute-start | bytes 589832 | tf_op jit(solution)/shard_map/ppermute | solution.py:105
  16.8 3.1 %collective-permute-start.11 = (bf16[384,768]{1,0:T(8,128)(2,1)S(1)}, bf16[384,768]{1,0:T(8,128)(2,1)S(1)}, u32[]{:S(2)}, u32[]{:S(2)}) collective-permute-start(bf16[384,768]{1,0:T(8,128)(2,1)S(1)} %shard_map.64.refs_0_), channel_id=1, source_target_pairs={{0,4},{12,8},{1,5},{13,9},{2,6},{14,10},{3,7},{15,11},{16,20},{28,... | collective-permute-start | bytes 1769480 | tf_op jit(solution)/shard_map/ppermute | solution.py:105
  19.9 3.2 %collective-permute-done.3.refs_3_ = bf16[2,64,768]{2,1,0:T(8,128)(2,1)S(1)} collective-permute-done((bf16[2,64,768]{2,1,0:T(8,128)(2,1)S(1)}, bf16[2,64,768]{2,1,0:T(8,128)(2,1)S(1)}, u32[]{:S(2)}, u32[]{:S(2)}) %collective-permute-start.3) | collective-permute-done | bytes 196640 | tf_op jit(solution)/shard_map/ppermute | solution.py:105
  24.4 6.1 %collective-permute-start.16 = (bf16[384,1024]{1,0:T(8,128)(2,1)S(1)}, bf16[384,1024]{1,0:T(8,128)(2,1)S(1)}, u32[]{:S(2)}, u32[]{:S(2)}) collective-permute-start(bf16[384,1024]{1,0:T(8,128)(2,1)S(1)} %get-tuple-element.31), channel_id=1, source_target_pairs={{0,8},{12,4},{1,9},{13,5},{2,10},{14,6},{3,11},{15,7},{16,24},{28,... | collective-permute-start | bytes 2359304 | tf_op jit(solution)/shard_map/ppermute | solution.py:105
  32.1 3.7 %collective-permute-done.11.refs_0_.refs_1_.fold = bf16[384,768]{1,0:T(8,128)(2,1)S(1)} collective-permute-done((bf16[384,768]{1,0:T(8,128)(2,1)S(1)}, bf16[384,768]{1,0:T(8,128)(2,1)S(1)}, u32[]{:S(2)}, u32[]{:S(2)}) %collective-permute-start.11) | collective-permute-done | bytes 589856 | tf_op jit(solution)/shard_map/ppermute | solution.py:105
  38.0 1.9 %collective-permute-done.4.refs_10_.far = bf16[256,768]{1,0:T(8,128)(2,1)S(1)} collective-permute-done((bf16[256,768]{1,0:T(8,128)(2,1)S(1)}, bf16[256,768]{1,0:T(8,128)(2,1)S(1)}, u32[]{:S(2)}, u32[]{:S(2)}) %collective-permute-start.4) | collective-permute-done | bytes 393248 | tf_op jit(solution)/shard_map/ppermute | solution.py:105
  40.9 2.6 %collective-permute-start.7 = (bf16[640,768]{1,0:T(8,128)(2,1)S(1)}, bf16[640,768]{1,0:T(8,128)(2,1)S(1)}, u32[]{:S(2)}, u32[]{:S(2)}) collective-permute-start(bf16[640,768]{1,0:T(8,128)(2,1)S(1)} %get-tuple-element.28), channel_id=1, source_target_pairs={{0,4},{12,8},{1,5},{13,9},{2,6},{14,10},{3,7},{15,11},{16,20},{28,... | collective-permute-start | bytes 2949128 | tf_op jit(solution)/shard_map/ppermute | solution.py:105
  45.3 2.7 %collective-permute-done.12.refs_0_ = bf16[384,768]{1,0:T(8,128)(2,1)S(1)} collective-permute-done((bf16[384,768]{1,0:T(8,128)(2,1)S(1)}, bf16[384,768]{1,0:T(8,128)(2,1)S(1)}, u32[]{:S(2)}, u32[]{:S(2)}) %collective-permute-start.12) | collective-permute-done | bytes 589856 | tf_op jit(solution)/shard_map/ppermute | solution.py:105
  48.8 3.9 %collective-permute-done.16.refs_0_.rest_3_ = bf16[384,1024]{1,0:T(8,128)(2,1)S(1)} collective-permute-done((bf16[384,1024]{1,0:T(8,128)(2,1)S(1)}, bf16[384,1024]{1,0:T(8,128)(2,1)S(1)}, u32[]{:S(2)}, u32[]{:S(2)}) %collective-permute-start.16) | collective-permute-done | bytes 786464 | tf_op jit(solution)/shard_map/ppermute | solution.py:105
  58.4 2.6 %shard_map.73 = bf16[512,768]{1,0:T(8,128)(2,1)S(1)} custom-call(s32[6]{0:T(128)S(1)} %stack.31.p, bf16[256,768]{1,0:T(8,128)(2,1)S(1)} %bitcast.16, bf16[256,768]{1,0:T(8,128)(2,1)S(1)} %collective-permute-done.4.refs_10_.far, bf16[256,768]{1,0:T(8,128)(2,1)S(1)} %collective-permute-done.5.near, bf16[256,768]{1,0:T(8,128)(2,1)S(1)} %collective-permute-done.6.both, ...), custom_call_target="tpu_custom_call" | custom-call | flops 1 | bytes 1 | tf_op jit(solution)/shard_map/pallas_call | solution.py:137
  61.7 2.6 %shard_map.70.refs_2_ = bf16[512,768]{1,0:T(8,128)(2,1)S(1)} custom-call(s32[6]{0:T(128)S(1)} %stack.31.p, bf16[256,768]{1,0:T(8,128)(2,1)S(1)} %bitcast.12, bf16[256,768]{1,0:T(8,128)(2,1)S(1)} %collective-permute-done.8.far, bf16[256,768]{1,0:T(8,128)(2,1)S(1)} %collective-permute-done.9.near, bf16[256,768]{1,0:T(8,128)(2,1)S(1)} %collective-permute-done.10.both, ...), custom_call_target="tpu_custom_call" | custom-call | flops 1 | bytes 1 | tf_op jit(solution)/shard_map/pallas_call | solution.py:137
  64.4 7.4 %collective-permute-done.7.refs_0_.refs_3_.fold = bf16[640,768]{1,0:T(8,128)(2,1)S(1)} collective-permute-done((bf16[640,768]{1,0:T(8,128)(2,1)S(1)}, bf16[640,768]{1,0:T(8,128)(2,1)S(1)}, u32[]{:S(2)}, u32[]{:S(2)}) %collective-permute-start.7) | collective-permute-done | bytes 983072 | tf_op jit(solution)/shard_map/ppermute | solution.py:105
  76.1 8.5 %collective-permute-start.19 = (bf16[256,768]{1,0:T(8,128)(2,1)S(1)}, bf16[256,768]{1,0:T(8,128)(2,1)S(1)}, u32[]{:S(2)}, u32[]{:S(2)}) collective-permute-start(bf16[256,768]{1,0:T(8,128)(2,1)S(1)} %get-tuple-element.33), channel_id=1, source_target_pairs={{0,8},{12,4},{1,9},{13,5},{2,10},{14,6},{3,11},{15,7},{16,24},{28,... | collective-permute-start | bytes 1179656 | tf_op jit(solution)/shard_map/ppermute | solution.py:105
  84.5 4.4 %collective-permute-done.18.swapped = bf16[384,768]{1,0:T(8,128)(2,1)S(1)} collective-permute-done((bf16[384,768]{1,0:T(8,128)(2,1)S(1)}, bf16[384,768]{1,0:T(8,128)(2,1)S(1)}, u32[]{:S(2)}, u32[]{:S(2)}) %collective-permute-start.18) | collective-permute-done | bytes 589856 | tf_op jit(solution)/shard_map/ppermute | solution.py:105
  90.1 2.9 %shard_map.72.keeps = f32[512,768]{1,0:T(8,128)S(1)} custom-call(s32[6]{0:T(128)S(1)} %stack.31.p, bf16[256,768]{1,0:T(8,128)(2,1)S(1)} %bitcast.17, bf16[256,768]{1,0:T(8,128)(2,1)S(1)} %collective-permute-done.4.refs_10_.far, bf16[256,768]{1,0:T(8,128)(2,1)S(1)} %collective-permute-done.5.near, bf16[256,768]{1,0:T(8,128)(2,1)S(1)} %collective-permute-done.6.both, ...), custom_call_target="tpu_custom_call" | custom-call | flops 1 | bytes 1 | tf_op jit(solution)/shard_map/pallas_call | solution.py:137
  93.0 1.7 shard_map.74.s0
  96.3 7.4 %collective-permute-start.25 = (bf16[768,1024]{1,0:T(8,128)(2,1)S(1)}, bf16[768,1024]{1,0:T(8,128)(2,1)S(1)}, u32[]{:S(2)}, u32[]{:S(2)}) collective-permute-start(bf16[768,1024]{1,0:T(8,128)(2,1)S(1)} %get-tuple-element.34), channel_id=1, source_target_pairs={{0,4},{12,8},{1,5},{13,9},{2,6},{14,10},{3,7},{15,11},{16,20},{28,... | collective-permute-start | bytes 4718600 | tf_op jit(solution)/shard_map/ppermute | solution.py:105
  105.0 2.9 %shard_map.77.keeps = f32[512,768]{1,0:T(8,128)S(1)} custom-call(s32[6]{0:T(128)S(1)} %stack.31.p, bf16[256,768]{1,0:T(8,128)(2,1)S(1)} %bitcast.13, bf16[256,768]{1,0:T(8,128)(2,1)S(1)} %collective-permute-done.8.far, bf16[256,768]{1,0:T(8,128)(2,1)S(1)} %collective-permute-done.9.near, bf16[256,768]{1,0:T(8,128)(2,1)S(1)} %collective-permute-done.10.both, ...), custom_call_target="tpu_custom_call" | custom-call | flops 1 | bytes 1 | tf_op jit(solution)/shard_map/pallas_call | solution.py:137
  107.9 1.7 shard_map.78.s0
  110.3 5.4 %collective-permute-done.23.s2 = bf16[528,768]{1,0:T(8,128)(2,1)S(1)} collective-permute-done((bf16[528,768]{1,0:T(8,128)(2,1)S(1)}, bf16[528,768]{1,0:T(8,128)(2,1)S(1)}, u32[]{:S(2)}, u32[]{:S(2)}) %collective-permute-start.23) | collective-permute-done | bytes 811040 | tf_op jit(solution)/shard_map/ppermute | solution.py:105
  116.2 16.1 %collective-permute-done.33.s2 = bf16[528,768]{1,0:T(8,128)(2,1)S(1)} collective-permute-done((bf16[528,768]{1,0:T(8,128)(2,1)S(1)}, bf16[528,768]{1,0:T(8,128)(2,1)S(1)}, u32[]{:S(2)}, u32[]{:S(2)}) %collective-permute-start.33) | collective-permute-done | bytes 811040 | tf_op jit(solution)/shard_map/ppermute | solution.py:105
  132.3 3.4 %collective-permute-done.25.rest_0_ = bf16[768,1024]{1,0:T(8,128)(2,1)S(1)} collective-permute-done((bf16[768,1024]{1,0:T(8,128)(2,1)S(1)}, bf16[768,1024]{1,0:T(8,128)(2,1)S(1)}, u32[]{:S(2)}, u32[]{:S(2)}) %collective-permute-start.25) | collective-permute-done | bytes 1572896 | tf_op jit(solution)/shard_map/ppermute | solution.py:105
  135.7 6.2 %shard_map.76 = (bf16[144,1024]{1,0:T(8,128)(2,1)S(1)}, bf16[144,1024]{1,0:T(8,128)(2,1)S(1)}, bf16[144,1024]{1,0:T(8,128)(2,1)S(1)}, bf16[144,1024]{1,0:T(8,128)(2,1)S(1)}) custom-call(s32[6]{0:T(128)S(1)} %stack.31.p, bf16[528,768]{1,0:T(8,128)(2,1)S(1)} %shard_map.74.s0, bf16[528,768]{1,0:T(8,128)(2,1)S(1)} %collective-permute-done.22.s1, ...), custom_call_target="tpu_custom_call" | custom-call | flops 1 | bytes 1 | tf_op jit(solution)/shard_map/pallas_call | solution.py:137
  144.6 6.2 %shard_map.79 = (bf16[144,1024]{1,0:T(8,128)(2,1)S(1)}, bf16[144,1024]{1,0:T(8,128)(2,1)S(1)}, bf16[144,1024]{1,0:T(8,128)(2,1)S(1)}, bf16[144,1024]{1,0:T(8,128)(2,1)S(1)}) custom-call(s32[6]{0:T(128)S(1)} %stack.31.p, bf16[528,768]{1,0:T(8,128)(2,1)S(1)} %shard_map.78.s0, bf16[528,768]{1,0:T(8,128)(2,1)S(1)} %collective-permute-done.32.s1, ...), custom_call_target="tpu_custom_call" | custom-call | flops 1 | bytes 1 | tf_op jit(solution)/shard_map/pallas_call | solution.py:137
  154.1 4.8 %collective-permute-done.28.refs_2_ = bf16[144,1024]{1,0:T(8,128)(2,1)S(1)} collective-permute-done((bf16[144,1024]{1,0:T(8,128)(2,1)S(1)}, bf16[144,1024]{1,0:T(8,128)(2,1)S(1)}, u32[]{:S(2)}, u32[]{:S(2)}) %collective-permute-start.28) | collective-permute-done | bytes 294944 | tf_op jit(solution)/shard_map/ppermute | solution.py:105
  160.2 9.1 %collective-permute-done.36.refs_6_ = bf16[144,1024]{1,0:T(8,128)(2,1)S(1)} collective-permute-done((bf16[144,1024]{1,0:T(8,128)(2,1)S(1)}, bf16[144,1024]{1,0:T(8,128)(2,1)S(1)}, u32[]{:S(2)}, u32[]{:S(2)}) %collective-permute-start.36) | collective-permute-done | bytes 294944 | tf_op jit(solution)/shard_map/ppermute | solution.py:105
  169.4 1.9 %collective-permute-done.37.refs_7_ = bf16[144,1024]{1,0:T(8,128)(2,1)S(1)} collective-permute-done((bf16[144,1024]{1,0:T(8,128)(2,1)S(1)}, bf16[144,1024]{1,0:T(8,128)(2,1)S(1)}, u32[]{:S(2)}, u32[]{:S(2)}) %collective-permute-start.37) | collective-permute-done | bytes 294944 | tf_op jit(solution)/shard_map/ppermute | solution.py:105
  171.3 1.7 %shard_map.80 = bf16[256,1024]{1,0:T(8,128)(2,1)} custom-call(s32[6]{0:T(128)S(1)} %stack.31.p, bf16[144,1024]{1,0:T(8,128)(2,1)S(1)} %get-tuple-element.35.refs_0_, bf16[144,1024]{1,0:T(8,128)(2,1)S(1)} %collective-permute-done.27.refs_1_, bf16[144,1024]{1,0:T(8,128)(2,1)S(1)} %collective-permute-done.28.refs_2_, ...), custom_call_target="tpu_custom_call" | custom-call | flops 1 | bytes 1 | tf_op jit(solution)/shard_map/pallas_call | solution.py:137
  (87 shorter events, 35.0 us)
Async XLA Ops:
  1.0 7.9 %collective-permute-start = (bf16[2,64,768]{2,1,0:T(8,128)(2,1)S(1)}, bf16[2,64,768]{2,1,0:T(8,128)(2,1)S(1)}, u32[]{:S(2)}, u32[]{:S(2)}) collective-permute-start(bf16[2,64,768]{2,1,0:T(8,128)(2,1)S(1)} %constant_dynamic-slice_fusion.refs_1_), channel_id=1, source_target_pairs={{0,2},{2,0},{1,3},{3,1},{4,6},{6,4},{5,7},{7,5},{8,10},{10,8},{9,1... | collective-permute-start | bytes 589832 | tf_op jit(solution)/shard_map/ppermute | solution.py:105
  10.0 9.9 %collective-permute-start.1 = (bf16[2,64,768]{2,1,0:T(8,128)(2,1)S(1)}, bf16[2,64,768]{2,1,0:T(8,128)(2,1)S(1)}, u32[]{:S(2)}, u32[]{:S(2)}) collective-permute-start(bf16[2,64,768]{2,1,0:T(8,128)(2,1)S(1)} %get-tuple-element.24.refs_1_), channel_id=1, source_target_pairs={{0,4},{12,8},{1,5},{13,9},{2,6},{14,10},{3,7},{15,11},{16,20},{28,... | collective-permute-start | bytes 589832 | tf_op jit(solution)/shard_map/ppermute | solution.py:105
  13.8 9.4 %collective-permute-start.3 = (bf16[2,64,768]{2,1,0:T(8,128)(2,1)S(1)}, bf16[2,64,768]{2,1,0:T(8,128)(2,1)S(1)}, u32[]{:S(2)}, u32[]{:S(2)}) collective-permute-start(bf16[2,64,768]{2,1,0:T(8,128)(2,1)S(1)} %get-tuple-element.25), channel_id=1, source_target_pairs={{0,8},{12,4},{1,9},{13,5},{2,10},{14,6},{3,11},{15,7},{16,24},{28,... | collective-permute-start | bytes 589832 | tf_op jit(solution)/shard_map/ppermute | solution.py:105
  16.8 19.0 %collective-permute-start.11 = (bf16[384,768]{1,0:T(8,128)(2,1)S(1)}, bf16[384,768]{1,0:T(8,128)(2,1)S(1)}, u32[]{:S(2)}, u32[]{:S(2)}) collective-permute-start(bf16[384,768]{1,0:T(8,128)(2,1)S(1)} %shard_map.64.refs_0_), channel_id=1, source_target_pairs={{0,4},{12,8},{1,5},{13,9},{2,6},{14,10},{3,7},{15,11},{16,20},{28,... | collective-permute-start | bytes 1769480 | tf_op jit(solution)/shard_map/ppermute | solution.py:105
  24.4 28.2 %collective-permute-start.16 = (bf16[384,1024]{1,0:T(8,128)(2,1)S(1)}, bf16[384,1024]{1,0:T(8,128)(2,1)S(1)}, u32[]{:S(2)}, u32[]{:S(2)}) collective-permute-start(bf16[384,1024]{1,0:T(8,128)(2,1)S(1)} %get-tuple-element.31), channel_id=1, source_target_pairs={{0,8},{12,4},{1,9},{13,5},{2,10},{14,6},{3,11},{15,7},{16,24},{28,... | collective-permute-start | bytes 2359304 | tf_op jit(solution)/shard_map/ppermute | solution.py:105
  30.5 9.4 %collective-permute-start.4 = (bf16[256,768]{1,0:T(8,128)(2,1)S(1)}, bf16[256,768]{1,0:T(8,128)(2,1)S(1)}, u32[]{:S(2)}, u32[]{:S(2)}) collective-permute-start(bf16[256,768]{1,0:T(8,128)(2,1)S(1)} %bitcast.14), channel_id=1, source_target_pairs={{0,2},{2,0},{1,3},{3,1},{4,6},{6,4},{5,7},{7,5},{8,10},{10,8},{9,1... | collective-permute-start | bytes 1179656 | tf_op jit(solution)/shard_map/ppermute | solution.py:105
  36.5 11.6 %collective-permute-start.12 = (bf16[384,768]{1,0:T(8,128)(2,1)S(1)}, bf16[384,768]{1,0:T(8,128)(2,1)S(1)}, u32[]{:S(2)}, u32[]{:S(2)}) collective-permute-start(bf16[384,768]{1,0:T(8,128)(2,1)S(1)} %shard_map.68), channel_id=1, source_target_pairs={{0,16},{16,0},{1,17},{17,1},{2,18},{18,2},{3,19},{19,3},{4,20},{20... | collective-permute-start | bytes 1769480 | tf_op jit(solution)/shard_map/ppermute | solution.py:105
  40.9 30.8 %collective-permute-start.7 = (bf16[640,768]{1,0:T(8,128)(2,1)S(1)}, bf16[640,768]{1,0:T(8,128)(2,1)S(1)}, u32[]{:S(2)}, u32[]{:S(2)}) collective-permute-start(bf16[640,768]{1,0:T(8,128)(2,1)S(1)} %get-tuple-element.28), channel_id=1, source_target_pairs={{0,4},{12,8},{1,5},{13,9},{2,6},{14,10},{3,7},{15,11},{16,20},{28,... | collective-permute-start | bytes 2949128 | tf_op jit(solution)/shard_map/ppermute | solution.py:105
  43.6 10.6 %collective-permute-start.6 = (bf16[256,768]{1,0:T(8,128)(2,1)S(1)}, bf16[256,768]{1,0:T(8,128)(2,1)S(1)}, u32[]{:S(2)}, u32[]{:S(2)}) collective-permute-start(bf16[256,768]{1,0:T(8,128)(2,1)S(1)} %collective-permute-done.4.refs_10_.far), channel_id=1, source_target_pairs={{0,1},{1,0},{2,3},{3,2},{4,5},{5,4},{6,7},{7,6},{8,9},{9,8},{10,11... | collective-permute-start | bytes 1179656 | tf_op jit(solution)/shard_map/ppermute | solution.py:105
  43.8 11.3 %collective-permute-start.8 = (bf16[256,768]{1,0:T(8,128)(2,1)S(1)}, bf16[256,768]{1,0:T(8,128)(2,1)S(1)}, u32[]{:S(2)}, u32[]{:S(2)}) collective-permute-start(bf16[256,768]{1,0:T(8,128)(2,1)S(1)} %get-tuple-element.29), channel_id=1, source_target_pairs={{0,2},{2,0},{1,3},{3,1},{4,6},{6,4},{5,7},{7,5},{8,10},{10,8},{9,1... | collective-permute-start | bytes 1179656 | tf_op jit(solution)/shard_map/ppermute | solution.py:105
  48.1 13.7 %collective-permute-start.15 = (bf16[384,1024]{1,0:T(8,128)(2,1)S(1)}, bf16[384,1024]{1,0:T(8,128)(2,1)S(1)}, u32[]{:S(2)}, u32[]{:S(2)}) collective-permute-start(bf16[384,1024]{1,0:T(8,128)(2,1)S(1)} %get-tuple-element.30), channel_id=1, source_target_pairs={{4,8},{8,4},{5,9},{9,5},{6,10},{10,6},{7,11},{11,7},{20,24},{24,20... | collective-permute-start | bytes 2359304 | tf_op jit(solution)/shard_map/ppermute | solution.py:105
  52.6 19.2 %collective-permute-start.17 = (bf16[384,1024]{1,0:T(8,128)(2,1)S(1)}, bf16[384,1024]{1,0:T(8,128)(2,1)S(1)}, u32[]{:S(2)}, u32[]{:S(2)}) collective-permute-start(bf16[384,1024]{1,0:T(8,128)(2,1)S(1)} %collective-permute-done.16.refs_0_.rest_3_), channel_id=1, source_target_pairs={{0,16},{16,0},{1,17},{17,1},{2,18},{18,2},{3,19},{19,3},{4,20},{20... | collective-permute-start | bytes 2359304 | tf_op jit(solution)/shard_map/ppermute | solution.py:105
  61.0 32.0 %collective-permute-start.21 = (bf16[512,768]{1,0:T(8,128)(2,1)S(1)}, bf16[512,768]{1,0:T(8,128)(2,1)S(1)}, u32[]{:S(2)}, u32[]{:S(2)}) collective-permute-start(bf16[512,768]{1,0:T(8,128)(2,1)S(1)} %shard_map.73), channel_id=1, source_target_pairs={{4,8},{8,4},{5,9},{9,5},{6,10},{10,6},{7,11},{11,7},{20,24},{24,20... | collective-permute-start | bytes 2359304 | tf_op jit(solution)/shard_map/ppermute | solution.py:105
  72.6 16.3 %collective-permute-start.18 = (bf16[384,768]{1,0:T(8,128)(2,1)S(1)}, bf16[384,768]{1,0:T(8,128)(2,1)S(1)}, u32[]{:S(2)}, u32[]{:S(2)}) collective-permute-start(bf16[384,768]{1,0:T(8,128)(2,1)S(1)} %get-tuple-element.32), channel_id=1, source_target_pairs={{0,16},{16,0},{1,17},{17,1},{2,18},{18,2},{3,19},{19,3},{4,20},{20... | collective-permute-start | bytes 1769480 | tf_op jit(solution)/shard_map/ppermute | solution.py:105
  74.8 28.9 %collective-permute-start.26 = (bf16[384,1024]{1,0:T(8,128)(2,1)S(1)}, bf16[384,1024]{1,0:T(8,128)(2,1)S(1)}, u32[]{:S(2)}, u32[]{:S(2)}) collective-permute-start(bf16[384,1024]{1,0:T(8,128)(2,1)S(1)} %shard_map.75), channel_id=1, source_target_pairs={{0,16},{16,0},{1,17},{17,1},{2,18},{18,2},{3,19},{19,3},{4,20},{20... | collective-permute-start | bytes 2359304 | tf_op jit(solution)/shard_map/ppermute | solution.py:105
  75.4 32.5 %collective-permute-start.31 = (bf16[512,768]{1,0:T(8,128)(2,1)S(1)}, bf16[512,768]{1,0:T(8,128)(2,1)S(1)}, u32[]{:S(2)}, u32[]{:S(2)}) collective-permute-start(bf16[512,768]{1,0:T(8,128)(2,1)S(1)} %shard_map.70.refs_2_), channel_id=1, source_target_pairs={{4,8},{8,4},{5,9},{9,5},{6,10},{10,6},{7,11},{11,7},{20,24},{24,20... | collective-permute-start | bytes 2359304 | tf_op jit(solution)/shard_map/ppermute | solution.py:105
  76.1 13.8 %collective-permute-start.19 = (bf16[256,768]{1,0:T(8,128)(2,1)S(1)}, bf16[256,768]{1,0:T(8,128)(2,1)S(1)}, u32[]{:S(2)}, u32[]{:S(2)}) collective-permute-start(bf16[256,768]{1,0:T(8,128)(2,1)S(1)} %get-tuple-element.33), channel_id=1, source_target_pairs={{0,8},{12,4},{1,9},{13,5},{2,10},{14,6},{3,11},{15,7},{16,24},{28,... | collective-permute-start | bytes 1179656 | tf_op jit(solution)/shard_map/ppermute | solution.py:105
  94.7 21.0 %collective-permute-start.23 = (bf16[528,768]{1,0:T(8,128)(2,1)S(1)}, bf16[528,768]{1,0:T(8,128)(2,1)S(1)}, u32[]{:S(2)}, u32[]{:S(2)}) collective-permute-start(bf16[528,768]{1,0:T(8,128)(2,1)S(1)} %shard_map.74.s0), channel_id=1, source_target_pairs={{0,2},{2,0},{1,3},{3,1},{4,6},{6,4},{5,7},{7,5},{8,10},{10,8},{9,1... | collective-permute-start | bytes 2433032 | tf_op jit(solution)/shard_map/ppermute | solution.py:105
  96.3 39.4 %collective-permute-start.25 = (bf16[768,1024]{1,0:T(8,128)(2,1)S(1)}, bf16[768,1024]{1,0:T(8,128)(2,1)S(1)}, u32[]{:S(2)}, u32[]{:S(2)}) collective-permute-start(bf16[768,1024]{1,0:T(8,128)(2,1)S(1)} %get-tuple-element.34), channel_id=1, source_target_pairs={{0,4},{12,8},{1,5},{13,9},{2,6},{14,10},{3,7},{15,11},{16,20},{28,... | collective-permute-start | bytes 4718600 | tf_op jit(solution)/shard_map/ppermute | solution.py:105
  109.6 22.7 %collective-permute-start.33 = (bf16[528,768]{1,0:T(8,128)(2,1)S(1)}, bf16[528,768]{1,0:T(8,128)(2,1)S(1)}, u32[]{:S(2)}, u32[]{:S(2)}) collective-permute-start(bf16[528,768]{1,0:T(8,128)(2,1)S(1)} %shard_map.78.s0), channel_id=1, source_target_pairs={{0,2},{2,0},{1,3},{3,1},{4,6},{6,4},{5,7},{7,5},{8,10},{10,8},{9,1... | collective-permute-start | bytes 2433032 | tf_op jit(solution)/shard_map/ppermute | solution.py:105
  110.3 22.0 %collective-permute-start.22 = (bf16[528,768]{1,0:T(8,128)(2,1)S(1)}, bf16[528,768]{1,0:T(8,128)(2,1)S(1)}, u32[]{:S(2)}, u32[]{:S(2)}) collective-permute-start(bf16[528,768]{1,0:T(8,128)(2,1)S(1)} %shard_map.74.s0), channel_id=1, source_target_pairs={{0,1},{1,0},{2,3},{3,2},{4,5},{5,4},{6,7},{7,6},{8,9},{9,8},{10,11... | collective-permute-start | bytes 2433032 | tf_op jit(solution)/shard_map/ppermute | solution.py:105
  115.7 20.0 %collective-permute-start.24 = (bf16[528,768]{1,0:T(8,128)(2,1)S(1)}, bf16[528,768]{1,0:T(8,128)(2,1)S(1)}, u32[]{:S(2)}, u32[]{:S(2)}) collective-permute-start(bf16[528,768]{1,0:T(8,128)(2,1)S(1)} %collective-permute-done.23.s2), channel_id=1, source_target_pairs={{0,1},{1,0},{2,3},{3,2},{4,5},{5,4},{6,7},{7,6},{8,9},{9,8},{10,11... | collective-permute-start | bytes 2433032 | tf_op jit(solution)/shard_map/ppermute | solution.py:105
  115.7 28.9 %collective-permute-start.32 = (bf16[528,768]{1,0:T(8,128)(2,1)S(1)}, bf16[528,768]{1,0:T(8,128)(2,1)S(1)}, u32[]{:S(2)}, u32[]{:S(2)}) collective-permute-start(bf16[528,768]{1,0:T(8,128)(2,1)S(1)} %shard_map.78.s0), channel_id=1, source_target_pairs={{0,1},{1,0},{2,3},{3,2},{4,5},{5,4},{6,7},{7,6},{8,9},{9,8},{10,11... | collective-permute-start | bytes 2433032 | tf_op jit(solution)/shard_map/ppermute | solution.py:105
  132.3 12.2 %collective-permute-start.34 = (bf16[528,768]{1,0:T(8,128)(2,1)S(1)}, bf16[528,768]{1,0:T(8,128)(2,1)S(1)}, u32[]{:S(2)}, u32[]{:S(2)}) collective-permute-start(bf16[528,768]{1,0:T(8,128)(2,1)S(1)} %collective-permute-done.33.s2), channel_id=1, source_target_pairs={{0,1},{1,0},{2,3},{3,2},{4,5},{5,4},{6,7},{7,6},{8,9},{9,8},{10,11... | collective-permute-start | bytes 2433032 | tf_op jit(solution)/shard_map/ppermute | solution.py:105
  142.0 17.0 %collective-permute-start.28 = (bf16[144,1024]{1,0:T(8,128)(2,1)S(1)}, bf16[144,1024]{1,0:T(8,128)(2,1)S(1)}, u32[]{:S(2)}, u32[]{:S(2)}) collective-permute-start(bf16[144,1024]{1,0:T(8,128)(2,1)S(1)} %get-tuple-element.37), channel_id=1, source_target_pairs={{4,0},{8,12},{5,1},{9,13},{6,2},{10,14},{7,3},{11,15},{20,16},{24,... | collective-permute-start | bytes 884744 | tf_op jit(solution)/shard_map/ppermute | solution.py:105
  143.3 16.4 %collective-permute-start.29 = (bf16[144,1024]{1,0:T(8,128)(2,1)S(1)}, bf16[144,1024]{1,0:T(8,128)(2,1)S(1)}, u32[]{:S(2)}, u32[]{:S(2)}) collective-permute-start(bf16[144,1024]{1,0:T(8,128)(2,1)S(1)} %get-tuple-element.38), channel_id=1, source_target_pairs={{4,12},{8,0},{5,13},{9,1},{6,14},{10,2},{7,15},{11,3},{20,28},{24,... | collective-permute-start | bytes 884744 | tf_op jit(solution)/shard_map/ppermute | solution.py:105
  150.8 8.9 %collective-permute-start.35 = (bf16[144,1024]{1,0:T(8,128)(2,1)S(1)}, bf16[144,1024]{1,0:T(8,128)(2,1)S(1)}, u32[]{:S(2)}, u32[]{:S(2)}) collective-permute-start(bf16[144,1024]{1,0:T(8,128)(2,1)S(1)} %get-tuple-element.40), channel_id=1, source_target_pairs={{4,8},{8,4},{5,9},{9,5},{6,10},{10,6},{7,11},{11,7},{20,24},{24,20... | collective-permute-start | bytes 884744 | tf_op jit(solution)/shard_map/ppermute | solution.py:105
  151.5 17.9 %collective-permute-start.36 = (bf16[144,1024]{1,0:T(8,128)(2,1)S(1)}, bf16[144,1024]{1,0:T(8,128)(2,1)S(1)}, u32[]{:S(2)}, u32[]{:S(2)}) collective-permute-start(bf16[144,1024]{1,0:T(8,128)(2,1)S(1)} %get-tuple-element.41), channel_id=1, source_target_pairs={{4,0},{8,12},{5,1},{9,13},{6,2},{10,14},{7,3},{11,15},{20,16},{24,... | collective-permute-start | bytes 884744 | tf_op jit(solution)/shard_map/ppermute | solution.py:105
  152.8 18.5 %collective-permute-start.37 = (bf16[144,1024]{1,0:T(8,128)(2,1)S(1)}, bf16[144,1024]{1,0:T(8,128)(2,1)S(1)}, u32[]{:S(2)}, u32[]{:S(2)}) collective-permute-start(bf16[144,1024]{1,0:T(8,128)(2,1)S(1)} %get-tuple-element.42), channel_id=1, source_target_pairs={{4,12},{8,0},{5,13},{9,1},{6,14},{10,2},{7,15},{11,3},{20,28},{24,... | collective-permute-start | bytes 884744 | tf_op jit(solution)/shard_map/ppermute | solution.py:105
  158.9 12.4 %collective-permute-start.27 = (bf16[144,1024]{1,0:T(8,128)(2,1)S(1)}, bf16[144,1024]{1,0:T(8,128)(2,1)S(1)}, u32[]{:S(2)}, u32[]{:S(2)}) collective-permute-start(bf16[144,1024]{1,0:T(8,128)(2,1)S(1)} %get-tuple-element.36), channel_id=1, source_target_pairs={{4,8},{8,4},{5,9},{9,5},{6,10},{10,6},{7,11},{11,7},{20,24},{24,20... | collective-permute-start | bytes 884744 | tf_op jit(solution)/shard_map/ppermute | solution.py:105
  159.6 11.7 %collective-permute-start.38 = (bf16[16,128]{1,0:T(8,128)(2,1)S(1)}, bf16[16,128]{1,0:T(8,128)(2,1)S(1)}, u32[]{:S(2)}, u32[]{:S(2)}) collective-permute-start(bf16[16,128]{1,0:T(8,128)(2,1)S(1)} %slice.23), channel_id=1, source_target_pairs={{0,1},{1,0},{2,3},{3,2},{4,5},{5,4},{6,7},{7,6},{8,9},{9,8},{10,11... | collective-permute-start | bytes 12296 | tf_op jit(solution)/shard_map/ppermute | solution.py:105
  159.7 11.6 %collective-permute-start.39 = (bf16[16,128]{1,0:T(8,128)(2,1)S(1)}, bf16[16,128]{1,0:T(8,128)(2,1)S(1)}, u32[]{:S(2)}, u32[]{:S(2)}) collective-permute-start(bf16[16,128]{1,0:T(8,128)(2,1)S(1)} %slice.24), channel_id=1, source_target_pairs={{0,1},{1,0},{2,3},{3,2},{4,5},{5,4},{6,7},{7,6},{8,9},{9,8},{10,11... | collective-permute-start | bytes 12296 | tf_op jit(solution)/shard_map/ppermute | solution.py:105
  (15 other events, 110.8 us)
